TPU v7x, 32 devices: a whole 2x2x4 slice. The times are simulated.
32 devices in a mesh: groups: 2 (over x), grid: 16 (over z, y, core).
Axes of the slice: x: 2, y: 2, z: 4, core: 2. Of those that a mesh axis runs over, the one named last changes fastest.
Arguments:
- hist: float32 [768, 256, 256], P('groups', 'grid'), parts along dimension 0, may hold values from 0.2 to 2
- drift: float32 [2, 256, 256], P(None, 'grid'), may hold values from -0.5 to 0.5
- shocks: int32 [768, 2], P('groups'), parts along dimension 0, may hold values from 0 to 7
- shock_table: float32 [16, 2], P('groups'), parts along dimension 0, may hold values from -0.3 to 0.3
- first_weight: bfloat16 [131072, 2048], P(('groups', 'grid')), parts along dimension 0, may hold values from -0.03125 to 0.03125
- mid_weight: bfloat16 [4096, 2048], P('groups', 'grid'), parts along dimension 0, may hold values from -0.1875 to 0.1875
- head_weight: float32 [4096], P(('groups', 'grid')), parts along dimension 0, may hold values from -0.125 to 0.125
- cotangent: float32 [768], P('groups'), parts along dimension 0, may hold values from -6 to 6
Outputs:
- hist_next: float32 [768, 256, 256], P('groups', 'grid'), parts along dimension 0
- value: float32 [768], P('groups'), parts along dimension 0
- grad_first: bfloat16 [131072, 2048], P(('groups', 'grid')), parts along dimension 0
- grad_mid: bfloat16 [4096, 2048], P('groups', 'grid'), parts along dimension 0
- grad_head: float32 [4096], P(('groups', 'grid')), parts along dimension 0
There are 2 independent parts, one for each index of `groups`. A program takes and returns all parts, laid end to end along the dimension named above; an argument that names none is the same for every part. Nothing has to cross between parts.
All inputs are finite; a program needn't handle non-finite values.
Results may differ from a plain program's by a relative error of at most 0.0173.
Values may be sent and summed in bfloat16 or wider, within the bound.
No kernel may reach another device: no remote copies, remote signals or barrier semaphores. Data moves between devices by JAX's collectives and lax.ppermute only.
A program may use at most 128 MiB of HBM per device.

v0:
```python
import jax
import jax.numpy as jnp
from jax import lax
from jax.sharding import PartitionSpec as P

diffusion_rate = 0.24


def padded_2(block, sides, width):
    for axis, dim in sides:
        count = lax.axis_size(axis)
        forward = [(i, i + 1) for i in range(count - 1)]
        backward = [(target, source) for source, target in forward]
        low = lax.ppermute(
            lax.slice_in_dim(block, block.shape[dim] - width, None, axis=dim), axis, forward
        )
        high = lax.ppermute(lax.slice_in_dim(block, 0, width, axis=dim), axis, backward)
        block = jnp.concatenate([low, block, high], axis=dim)
    return block


def column_shift(values, offset):
    zero_col = jnp.zeros_like(values[..., :1])
    if offset > 0:
        return jnp.concatenate([values[..., 1:], zero_col], axis=-1)
    return jnp.concatenate([zero_col, values[..., :-1]], axis=-1)


def shock_shift(levels_now, table):
    level_ids = lax.iota(jnp.int32, table.shape[0])
    onehot = (levels_now[:, None] == level_ids[None, :]).astype(jnp.float32)
    return jnp.sum(onehot[:, :, None] * table[None, :, :], axis=1)


def kfe_step(padded, drift_rows, shift_x, shift_y):
    velocity_x = drift_rows[0][None] + shift_x[:, None, None]
    velocity_y = drift_rows[1][1:-1][None] + shift_y[:, None, None]
    flux_x = velocity_x * padded
    centre = padded[:, 1:-1]
    flux_y = velocity_y * centre
    spread = (
        padded[:, 2:]
        + padded[:, :-2]
        + column_shift(centre, 1)
        + column_shift(centre, -1)
        - 4.0 * centre
    )
    carried = 0.5 * (flux_x[:, 2:] - flux_x[:, :-2]) + 0.5 * (
        column_shift(flux_y, 1) - column_shift(flux_y, -1)
    )
    return centre + diffusion_rate * spread - carried


def local(hist, drift, shocks, shock_table, first_weight, mid_weight, head_weight, cotangent):
    scenarios, row_count, columns = hist.shape
    step_count = shocks.shape[1]
    density = hist
    drift_ext = padded_2(drift, (("grid", 1),), 1)
    for section_no in range(step_count):
        shifts = shock_shift(shocks[:, section_no], shock_table)
        padded = padded_2(density, (("grid", 1),), 1)
        density = kfe_step(padded, drift_ext, shifts[:, 0], shifts[:, 1])
    inputs = density.astype(jnp.bfloat16).reshape(scenarios, row_count * columns)
    partial_first = jnp.dot(inputs, first_weight, preferred_element_type=jnp.float32)
    first_pre = lax.psum(partial_first, "grid")
    first_act = jnp.tanh(first_pre).astype(jnp.bfloat16)
    second_pre = jnp.dot(first_act, mid_weight, preferred_element_type=jnp.float32)
    second_act = jnp.tanh(second_pre).astype(jnp.bfloat16)
    second_f = second_act.astype(jnp.float32)
    value_part = jnp.dot(second_f, head_weight, precision=lax.Precision.HIGHEST)
    value = lax.psum(value_part, "grid")
    grad_head = jnp.dot(cotangent, second_f, precision=lax.Precision.HIGHEST)
    back_second = (cotangent[:, None] * head_weight[None, :] * (1.0 - second_f * second_f)).astype(
        jnp.bfloat16
    )
    grad_mid = lax.dot_general(
        first_act, back_second, (((0,), (0,)), ((), ())), preferred_element_type=jnp.float32
    )
    back_part = lax.dot_general(
        back_second, mid_weight, (((1,), (1,)), ((), ())), preferred_element_type=jnp.float32
    )
    back_raw = lax.psum(back_part, "grid")
    first_f = first_act.astype(jnp.float32)
    back_first = (back_raw * (1.0 - first_f * first_f)).astype(jnp.bfloat16)
    grad_first = lax.dot_general(
        inputs, back_first, (((0,), (0,)), ((), ())), preferred_element_type=jnp.float32
    )
    return (
        density,
        value,
        grad_first.astype(jnp.bfloat16),
        grad_mid.astype(jnp.bfloat16),
        grad_head,
    )


def solution(mesh):
    in_specs = (
        P("groups", "grid", None),
        P(None, "grid", None),
        P("groups", None),
        P("groups", None),
        P(("groups", "grid"), None),
        P("groups", "grid"),
        P(("groups", "grid")),
        P("groups"),
    )
    out_specs = (
        P("groups", "grid", None),
        P("groups"),
        P(("groups", "grid"), None),
        P("groups", "grid"),
        P(("groups", "grid")),
    )
    return jax.shard_map(local, mesh=mesh, in_specs=in_specs, out_specs=out_specs, check_vma=False)
```

profile of v0, /device:TPU:0, one launch (start us, length us, event | category | flops | bytes accessed | tf_op | source)
XLA Modules:
  0.0 386.3 jit_solution(2880481211151766229)
XLA Ops:
  8.0 2.3 collective-permute-start.2
  11.7 3.4 fusion.35
  17.2 6.7 %collective-permute-start.1 = (f32[384,1,256]{2,0,1:T(8,128)}, f32[384,1,256]{2,0,1:T(8,128)}, u32[]{:S(2)}, u32[]{:S(2)}) collective-permute-start(f32[384,1,256]{2,0,1:T(8,128)} %copy.71), channel_id=1, source_target_pairs={{0,1},{1,2},{2,3},{3,4},{4,5},{5,6},{6,7},{7,8},{8,9},{9,10},{10,1... | collective-permute-start | bytes 1179656 | tf_op jit(solution)/shard_map/ppermute | solution.py:14
  23.9 6.6 %copy.58 = f32[384,16,256]{0,2,1:T(8,128)} copy(f32[384,16,256]{2,1,0:T(8,128)} %param.8) | data formatting | bytes 12582912 | tf_op args[0]
  30.6 10.8 %fusion.34 = (f32[384,16,255]{0,2,1:T(8,128)}, f32[384,16,255]{0,2,1:T(8,128)}) fusion(f32[384,16,256]{0,2,1:T(8,128)} %copy.58), kind=kLoop, calls=%fused_computation.63 | loop fusion | bytes 25067520 | tf_op jit(solution)/shard_map/slice | solution.py:25
  41.4 4.9 %add_multiply_fusion.1 = f32[384,16,256]{0,2,1:T(8,128)} fusion(f32[384,16,256]{0,2,1:T(8,128)} %copy.58, f32[384]{0:T(512)S(1)} %get-tuple-element.24, f32[16,256]{1,0:T(8,128)S(1)} %slice_bitcast_fusion), kind=kLoop, calls=%fused_computation.28 | loop fusion | flops 3145728 | bytes 12600832 | tf_op jit(solution)/shard_map/mul | solution.py:40
  46.3 10.8 %fusion.36 = (f32[384,16,255]{0,2,1:T(8,128)}, f32[384,16,255]{0,2,1:T(8,128)}) fusion(f32[384,16,256]{0,2,1:T(8,128)} %add_multiply_fusion.1), kind=kLoop, calls=%fused_computation.65 | loop fusion | bytes 25067520 | tf_op jit(solution)/shard_map/slice | solution.py:25
  58.7 6.0 %maximum_multiply_fusion = f32[384,18,256]{0,2,1:T(8,128)} fusion(f32[384,1,256]{0,2,1:T(8,128)S(1)} %copy.51, f32[384,16,256]{0,2,1:T(8,128)} %copy.58, f32[384,1,256]{0,2,1:T(8,128)S(1)} %copy.53, f32[384]{0:T(512)S(1)} %get-tuple-element.25, f32[18,256]{1,0:T(8,128)S(1)} %fusion.20), kind=kLoop, calls=%fused_computation.1 | loop fusion | flops 7077888 | bytes 14175744 | tf_op jit(solution)/shard_map/mul | solution.py:38
  64.7 2.4 slice-done.1
  67.2 14.2 %add_multiply_fusion = (f32[384,16,256]{0,2,1:T(8,128)}, f32[384,16,256]{0,2,1:T(8,128)S(1)}) fusion(f32[384]{0:T(512)S(1)} %get-tuple-element.20, f32[16,256]{1,0:T(8,128)S(1)} %slice_bitcast_fusion, f32[384,16,255]{0,2,1:T(8,128)} %get-tuple-element.43, f32[384,16,255]{0,2,1:T(8,128)} %get-tuple-element.42, f32[384,18,256]{0,2,1:T(8,128)} %maximum_multiply_fusion, ...), kind=kLoop, calls=%fused_computation.27 | loop fusion | flops 25165824 | bytes 57329152 | tf_op jit(solution)/shard_map/mul | solution.py:40
  81.4 2.6 copy-done.1
  84.1 10.8 %fusion.31 = (f32[384,16,255]{0,2,1:T(8,128)}, f32[384,16,255]{0,2,1:T(8,128)}) fusion(f32[384,16,256]{0,2,1:T(8,128)} %copy-done.1), kind=kLoop, calls=%fused_computation.60 | loop fusion | bytes 25067520 | tf_op jit(solution)/shard_map/slice | solution.py:25
  96.5 4.3 %collective-permute-start.5 = (f32[384,1,256]{2,0,1:T(8,128)S(1)}, f32[384,1,256]{2,0,1:T(8,128)}, u32[]{:S(2)}, u32[]{:S(2)}) collective-permute-start(f32[384,1,256]{2,0,1:T(8,128)S(1)} %copy.65), channel_id=1, source_target_pairs={{0,1},{1,2},{2,3},{3,4},{4,5},{5,6},{6,7},{7,8},{8,9},{9,10},{10,1... | collective-permute-start | bytes 1179656 | tf_op jit(solution)/shard_map/ppermute | solution.py:14
  100.8 10.7 %fusion.33 = (f32[384,16,255]{0,2,1:T(8,128)}, f32[384,16,255]{0,2,1:T(8,128)}) fusion(f32[384,16,256]{0,2,1:T(8,128)} %get-tuple-element.30), kind=kLoop, calls=%fused_computation.62 | loop fusion | bytes 25067520 | tf_op jit(solution)/shard_map/slice | solution.py:25
  113.0 5.5 %maximum_multiply_fusion.1 = f32[384,18,256]{0,2,1:T(8,128)} fusion(f32[384,1,256]{0,2,1:T(8,128)S(1)} %copy.64, f32[384,16,256]{0,2,1:T(8,128)} %copy-done.1, f32[384,1,256]{0,2,1:T(8,128)S(1)} %copy.66, f32[384]{0:T(512)S(1)} %get-tuple-element.21, f32[18,256]{1,0:T(8,128)S(1)} %fusion.20), kind=kLoop, calls=%fused_computation.2 | loop fusion | flops 7077888 | bytes 14175744 | tf_op jit(solution)/shard_map/mul | solution.py:38
  118.7 17.3 %fusion.28 = (bf16[384,16,256]{0,2,1:T(8,128)(2,1)S(1)}, f32[384,16,256]{0,2,1:T(8,128)}) fusion(f32[384,16,255]{0,2,1:T(8,128)} %get-tuple-element.37, f32[384,16,255]{0,2,1:T(8,128)} %get-tuple-element.36, f32[384,18,256]{0,2,1:T(8,128)} %maximum_multiply_fusion.1, f32[384,16,256]{0,2,1:T(8,128)S(1)} %bitcast.21, f32[384,16,255]{0,2,1:T(8,128)} %get-tuple-element.33, ...), kind=kLoop, calls=%fused_computation.59 | loop fusion | flops 23592960 | bytes 54165504 | tf_op jit(solution)/shard_map/convert_element_type | solution.py:63
  137.7 12.1 %fusion.38 = f32[384,2048]{1,0:T(8,128)} fusion(bf16[384,4096]{0,1:T(8,128)(2,1)S(1)} %bitcast.22, bf16[4096,2048]{1,0:T(8,128)(2,1)} %param.12), kind=kOutput, calls=%fused_computation.67 | convolution fusion | flops 6442450944 | bytes 23068672 | tf_op jit(solution)/shard_map/dot_general | solution.py:64
  149.8 106.4 %all-reduce.11.cloned.1.call-done = f32[384,2048]{1,0:T(8,128)} async-done(((f32[384,2048]{1,0:T(8,128)}), f32[384,2048]{1,0:T(8,128)}) %all-reduce.11.cloned.1.call-update) | async-done | bytes 3145744 | tf_op jit(solution)/shard_map/psum | solution.py:65
  256.2 2.5 fusion.19
  261.1 6.8 %copy.69 = f32[384,16,256]{2,1,0:T(8,128)} copy(f32[384,16,256]{0,2,1:T(8,128)} %get-tuple-element.29) | data formatting | bytes 12582912
  268.1 31.0 %psum.22 = f32[384]{0:T(512)} all-reduce(f32[384]{0:T(512)S(1)} %convolution_reduce_fusion), channel_id=1, replica_groups=mesh['groups'=2,'grid'=16] {'grid'}, use_global_device_ids=true, to_apply=%region_3.0 | all-reduce | flops 384 | bytes 3072 | tf_op jit(solution)/shard_map/psum | solution.py:71
  299.8 3.4 convolution_convert_fusion.1
  303.2 60.8 %all-reduce.13.cloned.1.call-done = f32[384,2048]{1,0:T(8,128)} async-done(((f32[384,2048]{1,0:T(8,128)}), f32[384,2048]{1,0:T(8,128)}) %all-reduce.13.cloned.1.call-update) | async-done | bytes 3145744 | tf_op jit(solution)/shard_map/psum | solution.py:82
  364.0 15.5 %convolution_convert_fusion = bf16[4096,2048]{1,0:T(8,128)(2,1)} fusion(bf16[384,4096]{0,1:T(8,128)(2,1)} %bitcast.23, f32[384,2048]{1,0:T(8,128)} %all-reduce.13.cloned.1.call-done, f32[384,2048]{1,0:T(8,128)} %all-reduce.11.cloned.1.call-done), kind=kOutput, calls=%fused_computation | convolution fusion | flops 6455558144 | bytes 26214400 | tf_op jit(solution)/shard_map/dot_general | solution.py:85
  (60 shorter events, 14.1 us)
Async XLA Ops:
  7.2 249.1 %copy-start = (bf16[2048,128]{1,0:T(8,128)(2,1)S(1)}, bf16[2048,128]{1,0:T(8,128)(2,1)}, u32[]{:S(2)}) copy-start(bf16[2048,128]{1,0:T(8,128)(2,1)} %param.13) | copy-start | bytes 1572868
  7.2 249.0 %all-reduce.11.cloned.1.call-start = ((), (), s32[]{:S(2)}) async-start(), calls=%async_computation | async-start | bytes 6291456 | tf_op jit(solution)/shard_map/psum | solution.py:65
  8.0 49.1 %collective-permute-start.2 = (f32[2,1,256]{2,1,0:T(1,128)S(1)}, f32[2,1,256]{2,1,0:T(1,128)S(1)}, u32[]{:S(2)}, u32[]{:S(2)}) collective-permute-start(f32[2,1,256]{2,1,0:T(1,128)S(1)} %get-tuple-element.44), channel_id=1, source_target_pairs={{0,1},{1,2},{2,3},{3,4},{4,5},{5,6},{6,7},{7,8},{8,9},{9,10},{10,1... | collective-permute-start | bytes 6152 | tf_op jit(solution)/shard_map/ppermute | solution.py:14
  10.4 46.8 %collective-permute-start.3 = (f32[2,1,256]{2,1,0:T(1,128)S(1)}, f32[2,1,256]{2,1,0:T(1,128)S(1)}, u32[]{:S(2)}, u32[]{:S(2)}) collective-permute-start(f32[2,1,256]{2,1,0:T(1,128)S(1)} %get-tuple-element.45), channel_id=1, source_target_pairs={{1,0},{2,1},{3,2},{4,3},{5,4},{6,5},{7,6},{8,7},{9,8},{10,9},{11,1... | collective-permute-start | bytes 6152 | tf_op jit(solution)/shard_map/ppermute | solution.py:17
  15.1 42.1 %collective-permute-start = (f32[384,1,256]{2,0,1:T(8,128)S(1)}, f32[384,1,256]{2,0,1:T(8,128)S(1)}, u32[]{:S(2)}, u32[]{:S(2)}) collective-permute-start(f32[384,1,256]{2,0,1:T(8,128)S(1)} %copy.70), channel_id=1, source_target_pairs={{1,0},{2,1},{3,2},{4,3},{5,4},{6,5},{7,6},{8,7},{9,8},{10,9},{11,1... | collective-permute-start | bytes 1179656 | tf_op jit(solution)/shard_map/ppermute | solution.py:17
  17.2 13.3 %copy-start.4 = (f32[2,16,256]{2,1,0:T(8,128)S(1)}, f32[2,16,256]{2,1,0:T(8,128)}, u32[]{:S(2)}) copy-start(f32[2,16,256]{2,1,0:T(8,128)} %param.9) | copy-start | bytes 98308
  17.2 13.3 %copy-start.7 = (s32[384,2]{0,1:T(2,128)S(1)}, s32[384,2]{0,1:T(2,128)}, u32[]{:S(2)}) copy-start(s32[384,2]{0,1:T(2,128)} %param.10) | copy-start | bytes 9220
  17.2 13.3 %copy-start.8 = (f32[8,2]{0,1:T(2,128)S(1)}, f32[8,2]{0,1:T(2,128)}, u32[]{:S(2)}) copy-start(f32[8,2]{0,1:T(2,128)} %param.11) | copy-start | bytes 196
  17.2 40.2 %collective-permute-start.1 = (f32[384,1,256]{2,0,1:T(8,128)}, f32[384,1,256]{2,0,1:T(8,128)}, u32[]{:S(2)}, u32[]{:S(2)}) collective-permute-start(f32[384,1,256]{2,0,1:T(8,128)} %copy.71), channel_id=1, source_target_pairs={{0,1},{1,2},{2,3},{3,4},{4,5},{5,6},{6,7},{7,8},{8,9},{9,10},{10,1... | collective-permute-start | bytes 1179656 | tf_op jit(solution)/shard_map/ppermute | solution.py:14
  57.2 7.5 %slice-start = ((s8[6291456]{0:T(1024)(128)(4,1)}), s8[2097152]{0:T(1024)(128)(4,1)S(1)}, s32[]{:S(2)}) async-start(s8[6291456]{0:T(1024)(128)(4,1)} %bitcast.18), calls=%async_computation.2 | async-start | bytes 4194304
  58.7 8.5 %slice-start.1 = ((s8[6291456]{0:T(1024)(128)(4,1)}), s8[4194304]{0:T(1024)(128)(4,1)S(1)}, s32[]{:S(2)}) async-start(s8[6291456]{0:T(1024)(128)(4,1)} %bitcast.18), calls=%async_computation.3 | async-start | bytes 8388608
  58.7 8.5 %copy-start.2 = (f32[384,16,255]{0,2,1:T(8,128)S(1)}, f32[384,16,255]{0,2,1:T(8,128)}, u32[]{:S(2)}) copy-start(f32[384,16,255]{0,2,1:T(8,128)} %get-tuple-element.38) | copy-start | bytes 18800644
  81.4 2.6 copy-start.1
  95.0 16.5 %collective-permute-start.4 = (f32[384,1,256]{2,0,1:T(8,128)S(1)}, f32[384,1,256]{2,0,1:T(8,128)S(1)}, u32[]{:S(2)}, u32[]{:S(2)}) collective-permute-start(f32[384,1,256]{2,0,1:T(8,128)S(1)} %copy.63), channel_id=1, source_target_pairs={{1,0},{2,1},{3,2},{4,3},{5,4},{6,5},{7,6},{8,7},{9,8},{10,9},{11,1... | collective-permute-start | bytes 1179656 | tf_op jit(solution)/shard_map/ppermute | solution.py:17
  96.5 15.2 %collective-permute-start.5 = (f32[384,1,256]{2,0,1:T(8,128)S(1)}, f32[384,1,256]{2,0,1:T(8,128)}, u32[]{:S(2)}, u32[]{:S(2)}) collective-permute-start(f32[384,1,256]{2,0,1:T(8,128)S(1)} %copy.65), channel_id=1, source_target_pairs={{0,1},{1,2},{2,3},{3,4},{4,5},{5,6},{6,7},{7,8},{8,9},{9,10},{10,1... | collective-permute-start | bytes 1179656 | tf_op jit(solution)/shard_map/ppermute | solution.py:14
  111.7 6.9 %slice-start.2 = ((s8[6291456]{0:T(1024)(128)(4,1)}), s8[2097152]{0:T(1024)(128)(4,1)S(1)}, s32[]{:S(2)}) async-start(s8[6291456]{0:T(1024)(128)(4,1)} %bitcast.20), calls=%async_computation.4 | async-start | bytes 4194304
  113.0 5.7 %slice-start.3 = ((s8[6291456]{0:T(1024)(128)(4,1)}), s8[4194304]{0:T(1024)(128)(4,1)S(1)}, s32[]{:S(2)}) async-start(s8[6291456]{0:T(1024)(128)(4,1)} %bitcast.20), calls=%async_computation.5 | async-start | bytes 8388608
  136.0 1.7 copy-start.3
  149.8 108.9 %copy-start.5 = (f32[384]{0:T(512)S(1)}, f32[384]{0:T(512)}, u32[]{:S(2)}) copy-start(f32[384]{0:T(512)} %param.15) | copy-start | bytes 4612
  149.8 109.0 %copy-start.6 = (f32[128]{0:T(128)S(1)}, f32[128]{0:T(128)}, u32[]{:S(2)}) copy-start(f32[128]{0:T(128)} %param.14) | copy-start | bytes 1540
  149.8 214.2 %all-reduce.13.cloned.1.call-start = ((), (), s32[]{:S(2)}) async-start(), calls=%async_computation.1 | async-start | bytes 6291456 | tf_op jit(solution)/shard_map/psum | solution.py:82
Sparse Core Ops, SparseCore 0:
  149.9 106.2 all-reduce.10
  261.2 102.8 all-reduce.12
where the time goes:
time: 387 us; the launch traced here: 386 us
  waiting for transfers between devices  167 us (43%)
  local copies, waits for them, and re-layouts  71.7 us (19%)
  other arithmetic  48.1 us (12%)
  matrix products  36.7 us (9%)
  blocking collectives  31 us (8%)
  starting transfers between devices  17.3 us (4%)
  between operations  14.3 us (4%)
    psum x1, waiting for transfers between devices, local(): first_pre = lax.psum(partial_first, 'grid')  106 us
    psum x1, waiting for transfers between devices, local(): back_raw = lax.psum(back_part, 'grid')  60.8 us
    slice x4, local copies, waits for them, and re-layouts, column_shift(): return jnp.concatenate([values[..., 1:], zero_col], axis=-1)  43.1 us
    psum x1, blocking collectives, local(): value = lax.psum(value_part, 'grid')  31 us
    unnamed x31, local copies, waits for them, and re-layouts  21 us
    mul x2, other arithmetic, kfe_step(): flux_y = velocity_y * centre  19.2 us
    convert_element_type x1, other arithmetic, local(): density.astype(jnp.bfloat16).reshape(scenarios, row_count * columns)  17.3 us
    dot_general x1, matrix products, local(): lax.dot_general(inputs, back_first, (((0,), (0,)), ((), ())), preferred_e...  15.5 us
  transfers between devices with their start and end apart: 8, of which 2 were waited for; matrix products, arithmetic and copies ran while one was open for 15% of the time, Pallas kernels for 0%

commit v1 on v0

v1 whole, which is shorter than its diff:
```python
import functools
import jax
import jax.numpy as jnp
from jax import lax
from jax.experimental import pallas as pl
from jax.experimental.pallas import tpu as pltpu
from jax.sharding import PartitionSpec as P

diffusion_rate = 0.24
VMEM_BYTES = 48 * 1024 * 1024
EXTRA = 16
bf16 = jnp.bfloat16
f32 = jnp.float32


def params():
    return pltpu.CompilerParams(vmem_limit_bytes=VMEM_BYTES)


def scenario_block(scenarios):
    for size in (64, 32, 16):
        if scenarios % size == 0:
            return size
    return scenarios


LANES = 128
SUBLANES = 8
GROUP = 16


def to_tiles(hist):
    scenarios, rows, columns = hist.shape
    high = min(rows, SUBLANES)
    tiles = hist.reshape(scenarios, rows // high, high, columns // LANES, LANES)
    return tiles.transpose(0, 1, 3, 2, 4).reshape(scenarios * rows * (columns // LANES), LANES)


def from_tiles(tiles, shape):
    scenarios, rows, columns = shape
    high = min(rows, SUBLANES)
    parts = tiles.reshape(scenarios, rows // high, columns // LANES, high, LANES)
    return parts.transpose(0, 1, 3, 2, 4).reshape(shape)


def tile_offset(row, lane_tile, rows, lane_tiles):
    high = min(rows, SUBLANES)
    return (row // high * lane_tiles + lane_tile) * high + row % high


def read_row(ref, first_scenario, count, row, rows, columns):
    lane_tiles = columns // LANES
    per = rows * lane_tiles
    return jnp.concatenate(
        [
            ref[pl.ds(first_scenario * per + tile_offset(row, t, rows, lane_tiles), count, stride=per), :]
            for t in range(lane_tiles)
        ],
        axis=1,
    )


def write_row(ref, first_scenario, count, row, rows, columns, values):
    lane_tiles = columns // LANES
    per = rows * lane_tiles
    for t in range(lane_tiles):
        place = pl.ds(first_scenario * per + tile_offset(row, t, rows, lane_tiles), count, stride=per)
        ref[place, :] = values[:, t * LANES : (t + 1) * LANES]


def edge_kernel(rows, size, hist_ref, drift_ref, first_ref, last_ref):
    step = pl.program_id(0)
    columns = drift_ref.shape[2]

    @pl.when(step == 0)
    def _():
        for out, start in ((first_ref, 0), (last_ref, rows - 2)):
            pieces = [
                jnp.concatenate([drift_ref[c, start : start + 1], drift_ref[c, start + 1 : start + 2]], axis=1)
                for c in range(2)
            ]
            exact = jnp.concatenate(pieces, axis=0)
            high = exact.astype(bf16)
            low = (exact - high.astype(f32)).astype(bf16)
            ones = jnp.ones((1, 2 * columns), bf16)
            zeros = jnp.zeros((EXTRA - 5, 2 * columns), bf16)
            out[pl.ds(out.shape[0] - EXTRA, EXTRA), :] = jnp.concatenate([high, low, ones, zeros], axis=0)

    where = pl.ds(pl.multiple_of(step * size, size), size)
    for out, start in ((first_ref, 0), (last_ref, rows - 2)):
        for k in range(2):
            out[where, pl.ds(k * columns, columns)] = read_row(hist_ref, 0, size, start + k, rows, columns).astype(bf16)


def edges(tiles, drift, scenarios):
    rows, columns = drift.shape[1:]
    per = tiles.shape[0] // scenarios
    size = scenario_block(scenarios)
    shape = jax.ShapeDtypeStruct((scenarios + EXTRA, 2 * columns), bf16)
    spec = pl.BlockSpec(shape.shape, lambda i: (0, 0))
    return pl.pallas_call(
        functools.partial(edge_kernel, rows, size),
        grid=(scenarios // size,),
        in_specs=[
            pl.BlockSpec((size * per, LANES), lambda i: (i, 0)),
            pl.BlockSpec(drift.shape, lambda i: (0, 0, 0)),
        ],
        out_specs=[spec, spec],
        out_shape=[shape, shape],
        compiler_params=params(),
        name="edge_rows",
    )(tiles, drift)


def stencil_kernel(rows, size, hist_ref, below_ref, above_ref, alpha_ref, valid_ref, shift_ref, next_ref, inputs_ref):
    columns = alpha_ref.shape[2]
    column = lax.broadcasted_iota(jnp.int32, (GROUP, columns), 1)
    not_first = column > 0
    not_last = column < columns - 1

    def sweep(values, first_row, shift_x, shift_y):
        up, down = [], []
        for k, density in enumerate(values):
            at = first_row + k + 2
            rising = density * (alpha_ref[0, at : at + 1, :] + shift_x)
            up.append(rising)
            down.append(2.0 * diffusion_rate * density - rising)
        results = []
        for k in range(1, len(values) - 1):
            density = values[k]
            at = first_row + k + 2
            rising = density * (alpha_ref[1, at : at + 1, :] + shift_y)
            falling = 2.0 * diffusion_rate * density - rising
            from_left = jnp.where(not_first, pltpu.roll(rising, 1, 1), 0.0)
            from_right = jnp.where(not_last, pltpu.roll(falling, columns - 1, 1), 0.0)
            results.append(
                (1.0 - 4.0 * diffusion_rate) * density + up[k - 1] + down[k + 1] + from_left + from_right
            )
        return results

    def group(g, carry):
        base = pl.multiple_of(g * GROUP, GROUP)
        shifts = shift_ref[pl.ds(base, GROUP), :]
        sh = [jnp.broadcast_to(shifts[:, k : k + 1], (GROUP, columns)) for k in range(4)]
        values = []
        for k in range(2):
            values.append(below_ref[pl.ds(base, GROUP), pl.ds(k * columns, columns)].astype(f32))
        for r in range(rows):
            values.append(read_row(hist_ref, base, GROUP, r, rows, columns))
        for k in range(2):
            values.append(above_ref[pl.ds(base, GROUP), pl.ds(k * columns, columns)].astype(f32))
        middle = sweep(values, -2, sh[0], sh[1])
        middle[0] = middle[0] * valid_ref[0, 0]
        middle[-1] = middle[-1] * valid_ref[0, 1]
        final = sweep(middle, -1, sh[2], sh[3])
        for r in range(rows):
            write_row(next_ref, base, GROUP, r, rows, columns, final[r])
            inputs_ref[pl.ds(base, GROUP), pl.ds(r * columns, columns)] = final[r].astype(bf16)
        return carry

    lax.fori_loop(0, size // GROUP, group, 0)


def stencil(tiles, below, above, alpha, valid, shift):
    scenarios = shift.shape[0]
    rows, columns = alpha.shape[1] - 4, alpha.shape[2]
    per = tiles.shape[0] // scenarios
    size = scenario_block(scenarios)
    block = pl.BlockSpec((size * per, LANES), lambda i: (i, 0))
    halo = pl.BlockSpec((size, 2 * columns), lambda i: (i, 0))
    return pl.pallas_call(
        functools.partial(stencil_kernel, rows, size),
        grid=(scenarios // size,),
        in_specs=[
            block,
            halo,
            halo,
            pl.BlockSpec(alpha.shape, lambda i: (0, 0, 0)),
            pl.BlockSpec(memory_space=pltpu.SMEM),
            pl.BlockSpec((size, 4), lambda i: (i, 0)),
        ],
        out_specs=[block, pl.BlockSpec((size, rows * columns), lambda i: (i, 0))],
        out_shape=[
            jax.ShapeDtypeStruct(tiles.shape, f32),
            jax.ShapeDtypeStruct((scenarios, rows * columns), bf16),
        ],
        compiler_params=params(),
        name="density_steps",
    )(tiles, below, above, alpha, valid, shift)


def middle_kernel(first_ref, mid_ref, head_ref, cot_ref, second_ref, back_ref, head_grad_ref, value_ref):
    parts, scenarios, width = first_ref.shape
    total = jnp.zeros((scenarios, mid_ref.shape[1]), f32)
    for p in range(parts):
        total += jnp.dot(first_ref[p], mid_ref[pl.ds(p * width, width), :], preferred_element_type=f32)
    second = jnp.tanh(total).astype(bf16).astype(f32)
    head = head_ref[...]
    cot = cot_ref[...]
    head_grad_ref[...] = jnp.sum(cot * second, axis=0, keepdims=True)
    value_ref[...] = jnp.sum(second * head, axis=1, keepdims=True)
    back = (cot * head * (1.0 - second * second)).astype(bf16)
    second_ref[...] = back
    for p in range(parts):
        back_ref[p] = lax.dot_general(
            back, mid_ref[pl.ds(p * width, width), :], (((1,), (1,)), ((), ())), preferred_element_type=f32
        ).astype(bf16)


def middle(first3, mid_weight, head, cot):
    parts, scenarios, width = first3.shape
    units = mid_weight.shape[1]
    return pl.pallas_call(
        middle_kernel,
        out_shape=[
            jax.ShapeDtypeStruct((scenarios, units), bf16),
            jax.ShapeDtypeStruct((parts, scenarios, width), bf16),
            jax.ShapeDtypeStruct((1, units), f32),
            jax.ShapeDtypeStruct((scenarios, 1), f32),
        ],
        compiler_params=params(),
        name="value_layers",
    )(first3, mid_weight, head, cot)


def mid_grad_kernel(first_ref, back_ref, out_ref):
    parts, scenarios, width = first_ref.shape
    for p in range(parts):
        out_ref[pl.ds(p * width, width), :] = lax.dot_general(
            first_ref[p], back_ref[...], (((0,), (0,)), ((), ())), preferred_element_type=f32
        ).astype(bf16)


def mid_grad(first3, back):
    parts, scenarios, width = first3.shape
    return pl.pallas_call(
        mid_grad_kernel,
        out_shape=jax.ShapeDtypeStruct((parts * width, back.shape[1]), bf16),
        compiler_params=params(),
        name="mid_gradient",
    )(first3, back)


def first_grad_kernel(inputs_ref, back_ref, out_ref):
    parts, _, width = back_ref.shape
    group = max(1, 256 // width)
    left = inputs_ref[...].T
    for p in range(0, parts, group):
        right = jnp.concatenate([back_ref[p + k] for k in range(group)], axis=1)
        out_ref[:, pl.ds(p * width, group * width)] = jnp.dot(left, right, preferred_element_type=f32).astype(bf16)


def first_grad(inputs, back3):
    scenarios, cells = inputs.shape
    parts, _, width = back3.shape
    size = min(cells, 512)
    return pl.pallas_call(
        first_grad_kernel,
        grid=(cells // size,),
        in_specs=[
            pl.BlockSpec((scenarios, size), lambda i: (0, i)),
            pl.BlockSpec(back3.shape, lambda i: (0, 0, 0)),
        ],
        out_specs=pl.BlockSpec((size, parts * width), lambda i: (i, 0)),
        out_shape=jax.ShapeDtypeStruct((cells, parts * width), bf16),
        compiler_params=params(),
        name="first_gradient",
    )(inputs, back3)


def shock_shift(levels_now, table):
    level_ids = lax.iota(jnp.int32, table.shape[0])
    onehot = (levels_now[:, None] == level_ids[None, :]).astype(f32)
    return jnp.sum(onehot[:, :, None] * table[None, :, :], axis=1)


def local(hist, drift, shocks, shock_table, first_weight, mid_weight, head_weight, cotangent):
    scenarios, rows, columns = hist.shape
    count = lax.axis_size("grid")
    hidden = first_weight.shape[1]
    width = hidden // count
    tiles = to_tiles(hist)

    first_rows, last_rows = edges(tiles, drift, scenarios)
    forward = [(i, i + 1) for i in range(count - 1)]
    backward = [(i + 1, i) for i in range(count - 1)]
    below = lax.ppermute(last_rows, "grid", forward)
    above = lax.ppermute(first_rows, "grid", backward)

    def drift_rows(payload):
        tail = payload[scenarios : scenarios + 4].astype(f32)
        return (tail[:2] + tail[2:]).reshape(2, 2, columns)

    drift_ext = jnp.concatenate([drift_rows(below), drift, drift_rows(above)], axis=1)
    alpha = diffusion_rate + 0.5 * drift_ext
    valid = jnp.stack([below[scenarios + 4, 0], above[scenarios + 4, 0]]).astype(f32).reshape(1, 2)
    shift = jnp.concatenate([0.5 * shock_shift(shocks[:, t], shock_table) for t in range(shocks.shape[1])], axis=1)
    density, inputs = stencil(tiles, below, above, alpha, valid, shift)

    partial = jnp.dot(inputs, first_weight, preferred_element_type=f32).astype(bf16)
    first_pre = lax.psum_scatter(partial, "grid", scatter_dimension=1, tiled=True)
    first_mine = jnp.tanh(first_pre.astype(f32)).astype(bf16)
    first3 = lax.all_gather(first_mine, "grid")
    back_second, back_part, grad_head, value_part = middle(
        first3, mid_weight, head_weight[None, :], cotangent[:, None]
    )
    back_raw = lax.psum_scatter(back_part, "grid", scatter_dimension=0)
    grad_mid = mid_grad(first3, back_second)
    first_f = first_mine.astype(f32)
    back_mine = (back_raw.astype(f32) * (1.0 - first_f * first_f)).astype(bf16)
    value = lax.psum(value_part[:, 0], "grid")
    back3 = lax.all_gather(back_mine, "grid")
    grad_first = first_grad(inputs, back3)
    return from_tiles(density, hist.shape), value, grad_first, grad_mid, grad_head[0]


def solution(mesh):
    in_specs = (
        P("groups", "grid", None),
        P(None, "grid", None),
        P("groups", None),
        P("groups", None),
        P(("groups", "grid"), None),
        P("groups", "grid"),
        P(("groups", "grid")),
        P("groups"),
    )
    out_specs = (
        P("groups", "grid", None),
        P("groups"),
        P(("groups", "grid"), None),
        P("groups", "grid"),
        P(("groups", "grid")),
    )
    return jax.shard_map(local, mesh=mesh, in_specs=in_specs, out_specs=out_specs, check_vma=False)
```

time: 387 us -> 289 us (0.75)
  local copies, waits for them, and re-layouts: 71.7 us -> 11.1 us
  other arithmetic: 48.1 us -> 3.93 us
  Pallas kernels: 0 us -> 37.5 us
  matrix products: 36.7 us -> 10.4 us
  starting transfers between devices: 17.3 us -> 3.84 us
  waiting for transfers between devices: 167 us -> 177 us
    psum x2 -> x0, waiting for transfers between devices: 167 us -> none  [the longest x1 106 us: local(): first_pre = lax.psum(partial_first, 'grid')]
    unnamed x2 -> x5, waiting for transfers between devices: 0.03 us -> 67.3 us
    reduce_scatter x0 -> x1, waiting for transfers between devices: none -> 58.5 us  [local(): back_raw = lax.psum_scatter(back_part, 'grid', scatter_dimension=0)]
    all_gather x0 -> x2, waiting for transfers between devices: none -> 47.4 us  [the longest x1 39.9 us: local(): first3 = lax.all_gather(first_mine, 'grid')]
    slice x12 -> x3, local copies, waits for them, and re-layouts: 47.7 us -> 1.05 us  [the longest x1 0.52 us: local(): below[scenarios + 4, 0]]
    pallas_call x0 -> x5, Pallas kernels: none -> 37.5 us  [the longest x1 16.6 us: stencil(): pl.pallas_call(functools.partial(stencil_kernel, rows, size), grid=(scena...]
    mul x4 -> x2, other arithmetic: 30.7 us -> 0.01 us  [local(): 0.5 * shock_shift(shocks[:, t], shock_table)]
    dot_general x7 -> x1, matrix products: 36.7 us -> 10.4 us  [local(): jnp.dot(inputs, first_weight, preferred_element_type=f32).astype(bf16)]
  transfers between devices with their start and end apart: 8 -> 6, of which waited for: 2 -> 5; matrix products, arithmetic and copies ran while one was open for 15% -> 0% of each run, Pallas kernels for 0% -> 0%
where the time goes in v1:
time: 289 us; the launch traced here: 288 us
  waiting for transfers between devices  177 us (61%)
  Pallas kernels  37.5 us (13%)
  blocking collectives  30.3 us (10%)
  between operations  13.9 us (5%)
  local copies, waits for them, and re-layouts  11.1 us (4%)
  matrix products  10.4 us (4%)
  other arithmetic  3.93 us (1%)
  starting transfers between devices  3.84 us (1%)
    unnamed x5, waiting for transfers between devices  67.3 us
    reduce_scatter x1, waiting for transfers between devices, local(): back_raw = lax.psum_scatter(back_part, 'grid', scatter_dimension=0)  58.5 us
    all_gather x1, waiting for transfers between devices, local(): first3 = lax.all_gather(first_mine, 'grid')  39.9 us
    psum x1, blocking collectives, local(): value = lax.psum(value_part[:, 0], 'grid')  30.3 us
    pallas_call x1, Pallas kernels, stencil(): pl.pallas_call(functools.partial(stencil_kernel, rows, size), grid=(scena...  16.6 us
    pallas_call x1, Pallas kernels, first_grad(): pl.pallas_call(first_grad_kernel, grid=(cells // size,), in_specs=[pl.Blo...  11.9 us
    dot_general x1, matrix products, local(): jnp.dot(inputs, first_weight, preferred_element_type=f32).astype(bf16)  10.4 us
    unnamed x26, local copies, waits for them, and re-layouts  9.73 us
  transfers between devices with their start and end apart: 6, of which 5 were waited for; matrix products, arithmetic and copies ran while one was open for 0% of the time, Pallas kernels for 0%

profile of v1, /device:TPU:0, one launch (start us, length us, event | category | flops | bytes accessed | tf_op | source)
XLA Modules:
  0.0 288.2 jit_solution(9079359380077605892)
XLA Ops:
  7.2 0.7 copy-done.6
  8.0 4.6 %edge_rows.1 = (bf16[400,512]{1,0:T(8,128)(2,1)S(1)}, bf16[400,512]{1,0:T(8,128)(2,1)S(1)}) custom-call(f32[12288,128]{1,0:T(8,128)} %bitcast.25, f32[2,16,256]{2,1,0:T(8,128)S(1)} %copy-done.6), custom_call_target="tpu_custom_call" | custom-call | tf_op jit(solution)/shard_map/edge_rows/pallas_call | solution.py:101
  12.6 2.4 collective-permute-start
  15.0 1.3 collective-permute-start.1
  16.7 4.1 %collective-permute-done.1.above_ref = bf16[400,512]{1,0:T(8,128)(2,1)S(1)} collective-permute-done((bf16[400,512]{1,0:T(8,128)(2,1)S(1)}, bf16[400,512]{1,0:T(8,128)(2,1)S(1)}, u32[]{:S(2)}, u32[]{:S(2)}) %collective-permute-start.1) | collective-permute-done | bytes 409632 | tf_op jit(solution)/shard_map/ppermute | solution.py:288
  21.8 1.4 maximum_convert_fusion.valid_ref
  23.2 16.6 %density_steps.1 = (f32[12288,128]{1,0:T(8,128)}, bf16[384,4096]{1,0:T(8,128)(2,1)S(1)}) custom-call(f32[12288,128]{1,0:T(8,128)} %bitcast.26, bf16[400,512]{1,0:T(8,128)(2,1)S(1)} %collective-permute-done.below_ref, bf16[400,512]{1,0:T(8,128)(2,1)S(1)} %collective-permute-done.1.above_ref, f32[2,20,256]{2,1,0:T(8,128)S(1)} %fusion.1.alpha_ref, ...), custom_call_target="tpu_custom_call" | custom-call | tf_op jit(solution)/shard_map/density_steps/pallas_call | solution.py:171
  39.8 10.4 %convolution_convert_fusion = bf16[384,2048]{1,0:T(8,128)(2,1)S(1)} fusion(bf16[384,4096]{1,0:T(8,128)(2,1)S(1)} %get-tuple-element.16.inputs_ref, bf16[4096,2048]{1,0:T(8,128)(2,1)} %param.12), kind=kOutput, calls=%fused_computation | convolution fusion | flops 6443237376 | bytes 21495808 | tf_op jit(solution)/shard_map/dot_general | solution.py:300
  50.2 1.7 copy-done.2
  51.9 1.6 copy.21
  53.6 67.3 %reduce-scatter.7.cloned.1.call-done = bf16[128,384]{1,0:T(8,128)(2,1)} async-done(((bf16[2048,384]{1,0:T(8,128)(2,1)}), bf16[128,384]{1,0:T(8,128)(2,1)}) %reduce-scatter.7.cloned.1.call-update) | async-done | bytes 98320
  120.8 1.0 copy.22
  121.8 0.7 tanh_convert_fusion
  122.7 39.9 %all-gather.5.cloned.1.call-done = bf16[6144,128]{1,0:T(8,128)(2,1)} async-done(((bf16[384,128]{1,0:T(8,128)(2,1)}), bf16[6144,128]{1,0:T(8,128)(2,1)}) %all-gather.5.cloned.1.call-update) | async-done | bytes 1572880 | tf_op jit(solution)/shard_map/all_gather | solution.py:303
  162.6 1.4 copy-done
  164.0 3.0 %value_layers.1 = (bf16[384,128]{1,0:T(8,128)(2,1)S(1)}, bf16[16,384,128]{2,1,0:T(8,128)(2,1)}, f32[1,128]{1,0:T(1,128)}, f32[384,1]{1,0:T(8,128)S(1)}) custom-call(bf16[16,384,128]{2,1,0:T(8,128)(2,1)S(1)} %bitcast.21, bf16[2048,128]{1,0:T(8,128)(2,1)S(1)} %copy-done.5, f32[1,128]{1,0:T(1,128)S(1)} %bitcast.24, f32[384,1]{1,0:T(8,128)S(1)} %broadcast_in_dim.6.cot_ref), custom_call_target="tpu_custom_call" | custom-call | tf_op jit(solution)/shard_map/value_layers/pallas_call | solution.py:213
  167.1 58.5 %reduce-scatter.5.cloned.1.call-done = bf16[1,384,128]{2,1,0:T(8,128)(2,1)} async-done(((bf16[16,384,128]{2,1,0:T(8,128)(2,1)}), bf16[1,384,128]{2,1,0:T(8,128)(2,1)}) %reduce-scatter.5.cloned.1.call-update) | async-done | bytes 98320 | tf_op jit(solution)/shard_map/reduce_scatter | solution.py:307
  225.6 1.6 fusion
  227.2 1.4 mid_gradient.1
  228.8 30.3 %psum.7 = f32[384]{0:T(512)} all-reduce(f32[384]{0:T(512)S(1)} %reduce.2), channel_id=1, replica_groups=mesh['groups'=2,'grid'=16] {'grid'}, use_global_device_ids=true, to_apply=%region_3.0 | all-reduce | flops 384 | bytes 3072 | tf_op jit(solution)/shard_map/psum | solution.py:311
  259.1 7.4 %all-gather.7.cloned.1.call-done = bf16[6144,128]{1,0:T(8,128)(2,1)} async-done(((bf16[384,128]{1,0:T(8,128)(2,1)}), bf16[6144,128]{1,0:T(8,128)(2,1)}) %all-gather.7.cloned.1.call-update) | async-done | bytes 1572880 | tf_op jit(solution)/shard_map/all_gather | solution.py:312
  266.5 1.9 copy-done.3
  268.4 1.4 copy-done.4
  269.8 11.9 %first_gradient.1 = bf16[4096,2048]{1,0:T(8,128)(2,1)} custom-call(bf16[384,4096]{1,0:T(8,128)(2,1)S(1)} %copy-done.3, bf16[16,384,128]{2,1,0:T(8,128)(2,1)S(1)} %bitcast.23), custom_call_target="tpu_custom_call" | custom-call | tf_op jit(solution)/shard_map/first_gradient/pallas_call | solution.py:257
  (46 shorter events, 1.9 us)
Async XLA Ops:
  7.2 113.7 %reduce-scatter.7.cloned.1.call-start = ((), (), s32[]{:S(2)}) async-start(), calls=%async_computation.5 | async-start | bytes 1671168
  7.2 0.8 copy-start.6
  8.0 8.4 %copy-start.9 = (s32[384,2]{0,1:T(2,128)S(1)}, s32[384,2]{0,1:T(2,128)}, u32[]{:S(2)}) copy-start(s32[384,2]{0,1:T(2,128)} %param.10) | copy-start | bytes 9220
  8.0 8.4 %copy-start.11 = (f32[8,2]{0,1:T(2,128)S(1)}, f32[8,2]{0,1:T(2,128)}, u32[]{:S(2)}) copy-start(f32[8,2]{0,1:T(2,128)} %param.11) | copy-start | bytes 196
  8.0 15.2 %copy-start.7 = (f32[2,16,256]{2,1,0:T(8,128)S(1)}, f32[2,16,256]{2,1,0:T(8,128)}, u32[]{:S(2)}) copy-start(f32[2,16,256]{2,1,0:T(8,128)} %drift_ref.1) | copy-start | bytes 98308
  12.6 4.0 %collective-permute-start = (bf16[400,512]{1,0:T(8,128)(2,1)S(1)}, bf16[400,512]{1,0:T(8,128)(2,1)S(1)}, u32[]{:S(2)}, u32[]{:S(2)}) collective-permute-start(bf16[400,512]{1,0:T(8,128)(2,1)S(1)} %get-tuple-element.13), channel_id=1, source_target_pairs={{0,1},{1,2},{2,3},{3,4},{4,5},{5,6},{6,7},{7,8},{8,9},{9,10},{10,1... | collective-permute-start | bytes 1228808 | tf_op jit(solution)/shard_map/ppermute | solution.py:287
  15.0 5.8 %collective-permute-start.1 = (bf16[400,512]{1,0:T(8,128)(2,1)S(1)}, bf16[400,512]{1,0:T(8,128)(2,1)S(1)}, u32[]{:S(2)}, u32[]{:S(2)}) collective-permute-start(bf16[400,512]{1,0:T(8,128)(2,1)S(1)} %get-tuple-element.14), channel_id=1, source_target_pairs={{1,0},{2,1},{3,2},{4,3},{5,4},{6,5},{7,6},{8,7},{9,8},{10,9},{11,1... | collective-permute-start | bytes 1228808 | tf_op jit(solution)/shard_map/ppermute | solution.py:288
  50.2 1.7 copy-start.2
  51.9 70.7 %copy-start.10 = (f32[384]{0:T(512)S(1)}, f32[384]{0:T(512)}, u32[]{:S(2)}) copy-start(f32[384]{0:T(512)} %param.15) | copy-start | bytes 4612
  51.9 110.7 %copy-start.5 = (bf16[2048,128]{1,0:T(8,128)(2,1)S(1)}, bf16[2048,128]{1,0:T(8,128)(2,1)}, u32[]{:S(2)}) copy-start(bf16[2048,128]{1,0:T(8,128)(2,1)} %mid_ref.1) | copy-start | bytes 1572868
  51.9 110.7 %copy-start.8 = (f32[128]{0:T(128)S(1)}, f32[128]{0:T(128)}, u32[]{:S(2)}) copy-start(f32[128]{0:T(128)} %param.14) | copy-start | bytes 1540
  53.5 109.1 %all-gather.5.cloned.1.call-start = ((), (), s32[]{:S(2)}) async-start(), calls=%async_computation.3 | async-start | bytes 1671168 | tf_op jit(solution)/shard_map/all_gather | solution.py:303
  122.5 103.1 %reduce-scatter.5.cloned.1.call-start = ((), (), s32[]{:S(2)}) async-start(), calls=%async_computation.2 | async-start | bytes 1671168 | tf_op jit(solution)/shard_map/reduce_scatter | solution.py:307
  162.6 1.4 copy-start
  164.0 63.2 %copy-start.1 = (bf16[6144,128]{1,0:T(8,128)(2,1)S(1)}, bf16[6144,128]{1,0:T(8,128)(2,1)}, u32[]{:S(2)}) copy-start(bf16[6144,128]{1,0:T(8,128)(2,1)} %all-gather.5.cloned.1.call-done) | copy-start | bytes 4718596
  167.1 99.4 %all-gather.7.cloned.1.call-start = ((), (), s32[]{:S(2)}) async-start(), calls=%async_computation.4 | async-start | bytes 1671168 | tf_op jit(solution)/shard_map/all_gather | solution.py:312
  266.5 1.9 copy-start.3
  268.4 1.4 copy-start.4
Sparse Core Ops, SparseCore 0:
  53.6 67.1 reduce-scatter.6
  123.9 38.6 all-gather.4
  167.2 58.3 reduce-scatter.4
  227.8 38.6 all-gather.6

commit v2 on v0

v2 whole, which is shorter than its diff:
```python
import functools
import jax
import jax.numpy as jnp
from jax import lax
from jax.experimental import pallas as pl
from jax.experimental.pallas import tpu as pltpu
from jax.sharding import PartitionSpec as P

diffusion_rate = 0.24
VMEM_BYTES = 48 * 1024 * 1024
EXTRA = 16
bf16 = jnp.bfloat16
f32 = jnp.float32


def params():
    return pltpu.CompilerParams(vmem_limit_bytes=VMEM_BYTES)


def scenario_block(scenarios):
    for size in (64, 32, 16):
        if scenarios % size == 0:
            return size
    return scenarios


LANES = 128
SUBLANES = 8
GROUP = 16
CHUNKS = 1


def to_tiles(hist):
    scenarios, rows, columns = hist.shape
    high = min(rows, SUBLANES)
    tiles = hist.reshape(scenarios, rows // high, high, columns // LANES, LANES)
    return tiles.transpose(0, 1, 3, 2, 4).reshape(scenarios * rows * (columns // LANES), LANES)


def from_tiles(tiles, shape):
    scenarios, rows, columns = shape
    high = min(rows, SUBLANES)
    parts = tiles.reshape(scenarios, rows // high, columns // LANES, high, LANES)
    return parts.transpose(0, 1, 3, 2, 4).reshape(shape)


def tile_offset(row, lane_tile, rows, lane_tiles):
    high = min(rows, SUBLANES)
    return (row // high * lane_tiles + lane_tile) * high + row % high


def read_row(ref, first_scenario, count, row, rows, columns):
    lane_tiles = columns // LANES
    per = rows * lane_tiles
    return jnp.concatenate(
        [
            ref[pl.ds(first_scenario * per + tile_offset(row, t, rows, lane_tiles), count, stride=per), :]
            for t in range(lane_tiles)
        ],
        axis=1,
    )


def write_row(ref, first_scenario, count, row, rows, columns, values):
    lane_tiles = columns // LANES
    per = rows * lane_tiles
    for t in range(lane_tiles):
        place = pl.ds(first_scenario * per + tile_offset(row, t, rows, lane_tiles), count, stride=per)
        ref[place, :] = values[:, t * LANES : (t + 1) * LANES]


def drift_tail(drift_ref, start):
    pieces = [
        jnp.concatenate([drift_ref[c, start : start + 1], drift_ref[c, start + 1 : start + 2]], axis=1)
        for c in range(2)
    ]
    high, low = two_halves(jnp.concatenate(pieces, axis=0))
    ones = jnp.ones((1, high.shape[1]), bf16)
    zeros = jnp.zeros((EXTRA - 5, high.shape[1]), bf16)
    return jnp.concatenate([high, low, ones, zeros], axis=0)


def half_shifts(levels, table_ref):
    results = []
    for t in range(levels.shape[1]):
        level = jnp.broadcast_to(levels[:, t : t + 1], (levels.shape[0], LANES))
        for c in range(2):
            shift = jnp.zeros(level.shape, f32)
            for n in range(table_ref.shape[0]):
                shift = jnp.where(level == n, 0.5 * table_ref[n, c], shift)
            results.append(shift)
    return results


def sweep_rows(read, coefficient, first, last, shift_x, shift_y, columns):
    lane_tiles = columns // LANES
    wide_x = jnp.concatenate([shift_x] * lane_tiles, axis=1)
    wide_y = jnp.concatenate([shift_y] * lane_tiles, axis=1)
    column = lax.broadcasted_iota(jnp.int32, wide_x.shape, 1)
    twice = 2.0 * diffusion_rate
    before = now = None
    for row in range(first, last + 1):
        density = read(row)
        up = density * (coefficient(0, row) + wide_x)
        coming = (density, up, twice * density - up)
        if before is not None:
            middle = now[0]
            rising = middle * (coefficient(1, row - 1) + wide_y)
            falling = twice * middle - rising
            from_left = jnp.where(column > 0, pltpu.roll(rising, 1, 1), 0.0)
            from_right = jnp.where(column < columns - 1, pltpu.roll(falling, columns - 1, 1), 0.0)
            result = (1.0 - 2.0 * twice) * middle + (before[1] + coming[2]) + (from_left + from_right)
            yield row - 1, result
        before, now = now, coming


def two_steps(read, coefficient, edge, first, last, shifts, columns, write):
    middle = sweep_rows(read, coefficient, first - 2, last + 2, shifts[0], shifts[1], columns)

    def read_middle(row):
        at, density = next(middle)
        assert at == row
        return edge(row, density)

    for row, density in sweep_rows(read_middle, coefficient, first - 1, last + 1, shifts[2], shifts[3], columns):
        write(row, density)


def inner_kernel(
    rows, size, hist_ref, drift_ref, levels_ref, table_ref, first_ref, next_ref, prev_ref, last_ref, inner_ref, work
):
    step = pl.program_id(0)
    columns = drift_ref.shape[2]

    @pl.when(step == 0)
    def _():
        for out, start in ((first_ref, 0), (last_ref, rows - 2)):
            out[pl.ds(out.shape[0] - EXTRA, EXTRA), :] = drift_tail(drift_ref, start)

    where = pl.ds(pl.multiple_of(step * size, size), size)
    for out, start in ((first_ref, 0), (next_ref, 2), (prev_ref, rows - 4), (last_ref, rows - 2)):
        for k in range(2):
            out[where, pl.ds(k * columns, columns)] = read_row(hist_ref, 0, size, start + k, rows, columns).astype(bf16)
    if rows <= 4:
        return

    def coefficient(c, row):
        return diffusion_rate + 0.5 * drift_ref[c, row : row + 1, :]

    def group(g, carry):
        base = pl.multiple_of(g * GROUP, GROUP)
        for half in range(GROUP // SUBLANES):
            at = base + half * SUBLANES
            shifts = half_shifts(levels_ref[pl.ds(pl.multiple_of(at, SUBLANES), SUBLANES), :], table_ref)

            def write(row, density):
                work[pl.ds(half * SUBLANES, SUBLANES), pl.ds((row - 2) * columns, columns)] = density

            two_steps(
                lambda row: read_row(hist_ref, at, SUBLANES, row, rows, columns),
                coefficient,
                lambda row, density: density,
                2,
                rows - 3,
                shifts,
                columns,
                write,
            )
        inner_ref[pl.ds(base, GROUP), :] = work[...].astype(bf16)
        return carry

    lax.fori_loop(0, size // GROUP, group, 0)


def inner_steps(tiles, drift, shocks, table):
    scenarios = shocks.shape[0]
    rows, columns = drift.shape[1:]
    per = tiles.shape[0] // scenarios
    size = scenario_block(scenarios)
    inner = max(rows - 4, 1) * columns
    edge = jax.ShapeDtypeStruct((scenarios, 2 * columns), bf16)
    sent = jax.ShapeDtypeStruct((scenarios + EXTRA, 2 * columns), bf16)
    whole = [pl.BlockSpec(shape.shape, lambda i: (0, 0)) for shape in (sent, edge, edge, sent)]
    return pl.pallas_call(
        functools.partial(inner_kernel, rows, size),
        grid=(scenarios // size,),
        in_specs=[
            pl.BlockSpec((size * per, LANES), lambda i: (i, 0)),
            pl.BlockSpec(drift.shape, lambda i: (0, 0, 0)),
            pl.BlockSpec((size, shocks.shape[1]), lambda i: (i, 0)),
            smem(),
        ],
        out_specs=whole + [pl.BlockSpec((size, inner), lambda i: (i, 0))],
        out_shape=[sent, edge, edge, sent, jax.ShapeDtypeStruct((scenarios, inner), bf16)],
        scratch_shapes=[pltpu.VMEM((GROUP, inner), f32)],
        compiler_params=params(),
        cost_estimate=pl.CostEstimate(flops=1, bytes_accessed=1, transcendentals=0),
        name="inner_density_steps",
    )(tiles, drift, shocks, table)


def halo_drift(ref, columns):
    tail = ref[pl.ds(ref.shape[0] - EXTRA, EXTRA), :].astype(f32)
    rows = [[tail[c : c + 1, k * columns : (k + 1) * columns] + tail[2 + c : 3 + c, k * columns : (k + 1) * columns] for k in range(2)] for c in range(2)]
    return rows, tail[4:5, :columns]


def coefficients(drift_ref, below, above, rows):
    def coefficient(c, row):
        if row < 0:
            drift = below[c][row + 2]
        elif row >= rows:
            drift = above[c][row - rows]
        else:
            drift = drift_ref[c, row : row + 1, :]
        return diffusion_rate + 0.5 * drift

    return coefficient


def edge_kernel(
    size, drift_ref, levels_ref, table_ref, first_ref, next_ref, prev_ref, last_ref, below_ref, above_ref, *refs
):
    low_ref, high_ref, work = refs[-3:]
    step = pl.program_id(0)
    rows, columns = drift_ref.shape[1:]
    below, below_valid = halo_drift(below_ref, columns)
    above, above_valid = halo_drift(above_ref, columns)
    coefficient = coefficients(drift_ref, below, above, rows)

    def edge(row, density):
        if row < 0:
            return density * below_valid
        if row >= rows:
            return density * above_valid
        return density

    start = pl.multiple_of(step * size, size)

    def group(g, carry):
        base = pl.multiple_of(g * GROUP, GROUP)
        every = pl.ds(pl.multiple_of(start + base, GROUP), GROUP)
        for out, refs, first in (
            (low_ref, (below_ref, first_ref, next_ref), 0),
            (high_ref, (prev_ref, last_ref, above_ref), rows - 2),
        ):
            wide = [ref[every, :].astype(f32) for ref in refs]
            for half in range(GROUP // SUBLANES):
                part = slice(half * SUBLANES, (half + 1) * SUBLANES)
                levels = levels_ref[pl.ds(pl.multiple_of(base + half * SUBLANES, SUBLANES), SUBLANES), :]

                def read(row):
                    at = row - (first - 2)
                    return wide[at // 2][part, at % 2 * columns : (at % 2 + 1) * columns]

                def write(row, density):
                    work[part, pl.ds((row - first) * columns, columns)] = density

                two_steps(
                    read, coefficient, edge, first, first + 1, half_shifts(levels, table_ref), columns, write
                )
            out[pl.ds(base, GROUP), :] = work[...].astype(bf16)
        return carry

    lax.fori_loop(0, size // GROUP, group, 0)


def edge_steps(drift, shocks, table, own, below, above, deps):
    scenarios = shocks.shape[0]
    columns = drift.shape[2]
    size = scenario_block(scenarios)
    edge = jax.ShapeDtypeStruct((scenarios, 2 * columns), bf16)
    spec = pl.BlockSpec((size, 2 * columns), lambda i: (i, 0))
    return pl.pallas_call(
        functools.partial(edge_kernel, size),
        grid=(scenarios // size,),
        in_specs=[
            pl.BlockSpec(drift.shape, lambda i: (0, 0, 0)),
            pl.BlockSpec((size, shocks.shape[1]), lambda i: (i, 0)),
            smem(),
        ]
        + [pl.BlockSpec(ref.shape, lambda i: (0, 0)) for ref in (*own, below, above)]
        + any_specs(deps),
        out_specs=[spec, spec],
        out_shape=[edge, edge],
        scratch_shapes=[pltpu.VMEM((GROUP, 2 * columns), f32)],
        compiler_params=params(),
        cost_estimate=pl.CostEstimate(flops=1, bytes_accessed=1, transcendentals=0),
        name="edge_density_steps",
    )(drift, shocks, table, *own, below, above, *deps)


def density_kernel(
    rows, size, first_step, hist_ref, drift_ref, levels_ref, table_ref, below_ref, above_ref, dep_ref, *refs
):
    next_ref = refs[-1]
    columns = drift_ref.shape[2]
    below, below_valid = halo_drift(below_ref, columns)
    above, above_valid = halo_drift(above_ref, columns)
    coefficient = coefficients(drift_ref, below, above, rows)
    start = (first_step + pl.program_id(0)) * size

    def edge(row, density):
        if row < 0:
            return density * below_valid
        if row >= rows:
            return density * above_valid
        return density

    def group(g, carry):
        base = pl.multiple_of(g * GROUP, GROUP)
        every = pl.ds(pl.multiple_of(start + base, GROUP), GROUP)
        wide = [ref[every, :].astype(f32) for ref in (below_ref, above_ref)]
        for half in range(GROUP // SUBLANES):
            part = slice(half * SUBLANES, (half + 1) * SUBLANES)
            at = pl.multiple_of(base + half * SUBLANES, SUBLANES)

            def read(row):
                if row < 0:
                    return wide[0][part, (row + 2) * columns : (row + 3) * columns]
                if row >= rows:
                    return wide[1][part, (row - rows) * columns : (row - rows + 1) * columns]
                return read_row(hist_ref, at, SUBLANES, row, rows, columns)

            shifts = half_shifts(levels_ref[pl.ds(at, SUBLANES), :], table_ref)
            two_steps(
                read,
                coefficient,
                edge,
                0,
                rows - 1,
                shifts,
                columns,
                lambda row, density: write_row(next_ref, at, SUBLANES, row, rows, columns, density),
            )
        return carry

    lax.fori_loop(0, size // GROUP, group, 0)


def density_steps(tiles, drift, shocks, table, below, above, dep, so_far, turn, turns):
    scenarios = shocks.shape[0]
    rows, columns = drift.shape[1:]
    per = tiles.shape[0] // scenarios
    size = GROUP * 2 if scenarios % (turns * GROUP * 2) == 0 else GROUP
    steps = scenarios // size // turns
    first = turn * steps
    block = pl.BlockSpec((size * per, LANES), lambda i: (first + i, 0))
    hidden = pl.BlockSpec(memory_space=pl.ANY)
    args = [tiles, drift, shocks, table, below, above, dep]
    in_specs = [
        block,
        pl.BlockSpec(drift.shape, lambda i: (0, 0, 0)),
        pl.BlockSpec((size, shocks.shape[1]), lambda i: (first + i, 0)),
        smem(),
        pl.BlockSpec(below.shape, lambda i: (0, 0)),
        pl.BlockSpec(above.shape, lambda i: (0, 0)),
        hidden,
    ]
    aliases = {}
    if so_far is not None:
        args.append(so_far)
        in_specs.append(hidden)
        aliases = {7: 0}
    return pl.pallas_call(
        functools.partial(density_kernel, rows, size, first),
        grid=(steps,),
        in_specs=in_specs,
        out_specs=block,
        out_shape=jax.ShapeDtypeStruct(tiles.shape, f32),
        input_output_aliases=aliases,
        compiler_params=params(),
        cost_estimate=pl.CostEstimate(flops=1, bytes_accessed=1, transcendentals=0),
        name="density_steps",
    )(*args)


def smem():
    return pl.BlockSpec(memory_space=pltpu.SMEM)


def swap(values, count, flip):
    return lax.ppermute(values, "grid", [(i, i ^ flip) for i in range(count)])


def inner_product_kernel(count, dep_count, *refs):
    inputs_ref = refs[0]
    weights = refs[1 : 1 + count]
    weight = jnp.concatenate([ref[...] for ref in weights], axis=0)
    refs[-1][0] = jnp.dot(inputs_ref[...], weight, preferred_element_type=f32)


def inner_product(inner, weight, width, deps):
    scenarios, cells = inner.shape
    total, hidden = weight.shape
    size = (total - cells) // 2
    count = cells // size
    hidden_spec = pl.BlockSpec(memory_space=pl.ANY)

    def spec(k):
        return pl.BlockSpec((size, width), lambda n: (1 + k, n))

    return pl.pallas_call(
        functools.partial(inner_product_kernel, count, len(deps)),
        grid=(hidden // width,),
        in_specs=[pl.BlockSpec(inner.shape, lambda n: (0, 0))]
        + [spec(k) for k in range(count)]
        + [hidden_spec] * len(deps),
        out_specs=pl.BlockSpec((1, scenarios, width), lambda n: (n, 0, 0)),
        out_shape=jax.ShapeDtypeStruct((hidden // width, scenarios, width), f32),
        compiler_params=params(),
        cost_estimate=pl.CostEstimate(flops=1, bytes_accessed=1, transcendentals=0),
        name="inner_product",
    )(inner, *([weight] * count), *deps)


def edge_product_kernel(block, with_inner, place_ref, low_ref, high_ref, top_ref, bottom_ref, *refs):
    keep_ref, send_ref, total = refs[-3:]
    left = jnp.concatenate([low_ref[...], high_ref[...]], axis=1)
    weight = jnp.concatenate([top_ref[...], bottom_ref[...]], axis=0)
    product = jnp.dot(left, weight, preferred_element_type=f32)
    total[...] = product + refs[0][0] if with_inner else product
    core = place_ref[0]
    for out, half in ((keep_ref, core), (send_ref, 1 - core)):
        for side in range(2):
            start = pl.multiple_of((2 * half + side) * block, block)
            out[side, 0] = total[pl.ds(start, block), :].astype(out.dtype)


def edge_product(place, low, high, weight, inner, parts, width, chunk):
    scenarios, size = low.shape
    block = scenarios // 4
    last = weight.shape[0] // size - 1
    shape = (2, parts, block, width)
    spec = pl.BlockSpec((2, 1, block, width), lambda n: (0, n, 0, 0))
    in_specs = [
        smem(),
        pl.BlockSpec(low.shape, lambda n: (0, 0)),
        pl.BlockSpec(low.shape, lambda n: (0, 0)),
        pl.BlockSpec((size, width), lambda n: (0, chunk * parts + n)),
        pl.BlockSpec((size, width), lambda n: (last, chunk * parts + n)),
    ]
    args = [place, low, high, weight, weight]
    if inner is not None:
        in_specs.append(pl.BlockSpec((1, scenarios, width), lambda n: (chunk * parts + n, 0, 0)))
        args.append(inner)
    return pl.pallas_call(
        functools.partial(edge_product_kernel, block, inner is not None),
        grid=(parts,),
        in_specs=in_specs,
        out_specs=[spec, spec],
        out_shape=[jax.ShapeDtypeStruct(shape, f32), jax.ShapeDtypeStruct(shape, bf16)],
        scratch_shapes=[pltpu.VMEM((scenarios, width), f32)],
        compiler_params=params(),
        cost_estimate=pl.CostEstimate(flops=1, bytes_accessed=1, transcendentals=0),
        name="edge_product",
    )(*args)


def add_side_kernel(place_ref, mine_ref, other_ref, *refs):
    keep_ref, send_ref = refs[-2:]
    side = place_ref[1]
    keep_ref[...] = mine_ref[side] + other_ref[side].astype(f32)
    send_ref[...] = (mine_ref[1 - side] + other_ref[1 - side].astype(f32)).astype(bf16)


def any_specs(deps):
    return [pl.BlockSpec(memory_space=pl.ANY)] * len(deps)


def add_side(place, mine, other, deps=()):
    shape = mine.shape[1:]
    return pl.pallas_call(
        add_side_kernel,
        in_specs=[smem()] + [pl.BlockSpec(memory_space=pltpu.VMEM)] * 2 + any_specs(deps),
        out_shape=[jax.ShapeDtypeStruct(shape, f32), jax.ShapeDtypeStruct(shape, bf16)],
        compiler_params=params(),
        cost_estimate=pl.CostEstimate(flops=1, bytes_accessed=1, transcendentals=0),
        name="add_side",
    )(place, mine, other, *deps)


def add_parts_kernel(dep_count, place_ref, mine_ref, other_ref, *refs):
    own_ref, *send_refs = refs[dep_count:]
    part = place_ref[2]
    own_ref[...] = mine_ref[part] + other_ref[part].astype(f32)
    for k, out in enumerate(send_refs):
        at = part ^ (k + 1)
        out[...] = (mine_ref[at] + other_ref[at].astype(f32)).astype(bf16)


def add_parts(place, mine, other, deps=()):
    parts = mine.shape[0]
    vmem = pl.BlockSpec(memory_space=pltpu.VMEM)
    return pl.pallas_call(
        functools.partial(add_parts_kernel, len(deps)),
        in_specs=[smem(), vmem, vmem] + any_specs(deps),
        out_shape=[jax.ShapeDtypeStruct(mine.shape[1:], f32)]
        + [jax.ShapeDtypeStruct(mine.shape[1:], bf16)] * (parts - 1),
        compiler_params=params(),
        cost_estimate=pl.CostEstimate(flops=1, bytes_accessed=1, transcendentals=0),
        name="add_parts",
    )(place, mine, other, *deps)


def activate_kernel(count, *refs):
    total = refs[0][...]
    for ref in refs[1 : 1 + count]:
        total = total + ref[...].astype(f32)
    refs[-1][...] = jnp.tanh(total).astype(bf16)


def activate(own, received, deps=()):
    return pl.pallas_call(
        functools.partial(activate_kernel, len(received)),
        in_specs=[pl.BlockSpec(memory_space=pltpu.VMEM)] * (1 + len(received)) + any_specs(deps),
        out_shape=jax.ShapeDtypeStruct(own.shape, bf16),
        compiler_params=params(),
        cost_estimate=pl.CostEstimate(flops=1, bytes_accessed=1, transcendentals=0),
        name="first_activation",
    )(own, *received, *deps)


def two_halves(exact):
    high = exact.astype(bf16)
    low = (exact - high.astype(f32)).astype(bf16)
    return high, low


def tail_rows(exact):
    high, low = two_halves(exact)
    zeros = jnp.zeros((EXTRA - 2, exact.shape[1]), bf16)
    return jnp.concatenate([high, low, zeros], axis=0)


def middle_kernel(chunks, parts, width, *refs):
    pieces = chunks * parts
    place_ref, cot_ref = refs[0], refs[1]
    first_refs = refs[2 : 2 + pieces]
    mid_refs = refs[2 + pieces : 6 + pieces]
    weight_refs = refs[6 + pieces : 10 + pieces]
    outs = refs[-(3 + parts) :]
    back_ref, own_ref, value_ref, head_ref = outs[:4]
    send_refs = outs[4:]
    part = place_ref[2]
    block = cot_ref.shape[0]

    def mid_rows(start):
        return jnp.concatenate([ref[pl.ds(start, width), :] for ref in mid_refs], axis=1)

    def start_of(c, k):
        return pl.multiple_of((c * parts + (part ^ k)) * width, width)

    total = None
    for c in range(chunks):
        for k in range(parts):
            term = jnp.dot(first_refs[c * parts + k][...], mid_rows(start_of(c, k)), preferred_element_type=f32)
            total = term if total is None else total + term
    second_low = jnp.tanh(total).astype(bf16)
    second = second_low.astype(f32)
    head = jnp.concatenate([ref[...] for ref in weight_refs], axis=1)
    heads = tail_rows(head)
    rows = lax.dot_general(heads, second_low, (((1,), (1,)), ((), ())), preferred_element_type=f32)
    value = rows[0:1] + rows[1:2]
    if width > block:
        value = jnp.concatenate([value, jnp.zeros((1, width - block), f32)], axis=1)
    value_ref[...] = value
    cot = cot_ref[...]
    head_ref[...] = jnp.sum(cot * second, axis=0, keepdims=True)
    back = (cot * head * (1.0 - second * second)).astype(bf16)
    back_ref[...] = back
    for k in range(parts):
        for c in range(chunks):
            piece = lax.dot_general(
                back, mid_rows(start_of(c, k)), (((1,), (1,)), ((), ())), preferred_element_type=f32
            )
            if k == 0:
                own_ref[pl.ds(c * block, block), :] = piece
            else:
                send_refs[k - 1][pl.ds(c * block, block), :] = piece.astype(bf16)
        if k > 0:
            send_refs[k - 1][pl.ds(chunks * block, EXTRA), :] = tail_rows(value)


def middle(place, cot, firsts, mids, heads, chunks, parts, width, deps=()):
    block = cot.shape[0]
    units = 4 * mids[0].shape[1]
    vmem = pl.BlockSpec(memory_space=pltpu.VMEM)
    return pl.pallas_call(
        functools.partial(middle_kernel, chunks, parts, width),
        in_specs=[smem()] + [vmem] * (1 + len(firsts) + 8) + any_specs(deps),
        out_shape=[
            jax.ShapeDtypeStruct((block, units), bf16),
            jax.ShapeDtypeStruct((chunks * block, width), f32),
            jax.ShapeDtypeStruct((1, width), f32),
            jax.ShapeDtypeStruct((1, units), f32),
        ]
        + [jax.ShapeDtypeStruct((chunks * block + EXTRA, width), bf16)] * (parts - 1),
        compiler_params=params(),
        cost_estimate=pl.CostEstimate(flops=1, bytes_accessed=1, transcendentals=0),
        name="value_layers",
    )(place, cot, *firsts, *mids, *heads, *deps)


def mid_grad_kernel(chunks, parts, width, *refs):
    pieces = chunks * parts
    place_ref, back_ref, head_ref = refs[:3]
    first_refs = refs[3 : 3 + pieces]
    keep_ref, send_ref = refs[-2:]
    part = place_ref[2]
    units = back_ref.shape[1] // 4
    for c in range(chunks):
        for k in range(parts):
            start = pl.multiple_of((c * parts + (part ^ k)) * width, width)
            product = lax.dot_general(
                first_refs[c * parts + k][...],
                back_ref[...],
                (((0,), (0,)), ((), ())),
                preferred_element_type=f32,
            ).astype(bf16)
            for p in range(4):
                out = (keep_ref, send_ref)[p % 2]
                out[p // 2, pl.ds(start, width), :] = product[:, p * units : (p + 1) * units]
    for p in range(4):
        out = (keep_ref, send_ref)[p % 2]
        out[p // 2, pl.ds(pieces * width, EXTRA), :] = tail_rows(head_ref[:, p * units : (p + 1) * units])


def mid_grad(place, back, head, firsts, chunks, parts, width, deps=()):
    units = back.shape[1] // 4
    vmem = pl.BlockSpec(memory_space=pltpu.VMEM)
    shape = jax.ShapeDtypeStruct((2, chunks * parts * width + EXTRA, units), bf16)
    return pl.pallas_call(
        functools.partial(mid_grad_kernel, chunks, parts, width),
        in_specs=[smem()] + [vmem] * (2 + len(firsts)) + any_specs(deps),
        out_shape=[shape, shape],
        compiler_params=params(),
        cost_estimate=pl.CostEstimate(flops=1, bytes_accessed=1, transcendentals=0),
        name="mid_gradient",
    )(place, back, head, *firsts, *deps)


def add_tail(left, right, hidden):
    body = left[:hidden].astype(f32) + right[:hidden].astype(f32)
    tails = left[hidden:].astype(f32) + right[hidden:].astype(f32)
    return body.astype(bf16), tails[0:1] + tails[1:2]


def mid_add_kernel(keep_ref, other_ref, *refs):
    own_ref, send_ref = refs[-2:]
    hidden = own_ref.shape[0] - EXTRA
    for at, out in enumerate((own_ref, send_ref)):
        body, tail = add_tail(keep_ref[at], other_ref[at], hidden)
        out[pl.ds(0, hidden), :] = body
        out[pl.ds(hidden, EXTRA), :] = tail_rows(tail)


def mid_add(keep, other, deps=()):
    shape = jax.ShapeDtypeStruct(keep.shape[1:], bf16)
    return pl.pallas_call(
        mid_add_kernel,
        in_specs=[pl.BlockSpec(memory_space=pltpu.VMEM)] * 2 + any_specs(deps),
        out_shape=[shape, shape],
        compiler_params=params(),
        cost_estimate=pl.CostEstimate(flops=1, bytes_accessed=1, transcendentals=0),
        name="mid_gradient_add",
    )(keep, other, *deps)


def mid_final_kernel(own_ref, other_ref, out_ref, head_ref):
    body, tail = add_tail(own_ref[...], other_ref[...], out_ref.shape[0])
    out_ref[...] = body
    head_ref[...] = tail


def mid_final(own, other):
    hidden = own.shape[0] - EXTRA
    return pl.pallas_call(
        mid_final_kernel,
        out_shape=[
            jax.ShapeDtypeStruct((hidden, own.shape[1]), bf16),
            jax.ShapeDtypeStruct((1, own.shape[1]), f32),
        ],
        compiler_params=params(),
        cost_estimate=pl.CostEstimate(flops=1, bytes_accessed=1, transcendentals=0),
        name="mid_gradient_final",
    )(own, other)


def back_first_kernel(chunks, count, *refs):
    own_ref, value_ref = refs[:2]
    received = refs[2 : 2 + count]
    first_refs = refs[2 + count : 2 + count + chunks]
    out_refs = refs[-1 - chunks : -1]
    tail_ref = refs[-1]
    block = first_refs[0].shape[0]
    value = value_ref[...]
    for ref in received:
        tail = ref[pl.ds(chunks * block, EXTRA), :].astype(f32)
        value = value + (tail[0:1] + tail[1:2])
    tail_ref[...] = tail_rows(value)
    for c in range(chunks):
        total = own_ref[pl.ds(c * block, block), :]
        for ref in received:
            total = total + ref[pl.ds(c * block, block), :].astype(f32)
        first = first_refs[c][...].astype(f32)
        out_refs[c][...] = (total * (1.0 - first * first)).astype(bf16)


def back_first(own, value, received, firsts, deps=()):
    chunks = len(firsts)
    shape = firsts[0].shape
    return pl.pallas_call(
        functools.partial(back_first_kernel, chunks, len(received)),
        in_specs=[pl.BlockSpec(memory_space=pltpu.VMEM)] * (2 + len(received) + chunks) + any_specs(deps),
        out_shape=[jax.ShapeDtypeStruct(shape, bf16)] * chunks
        + [jax.ShapeDtypeStruct((EXTRA, shape[1]), bf16)],
        compiler_params=params(),
        cost_estimate=pl.CostEstimate(flops=1, bytes_accessed=1, transcendentals=0),
        name="back_first",
    )(own, value, *received, *firsts, *deps)


def stack_kernel(count, *refs):
    at = 0
    for ref in refs[:count]:
        refs[-1][pl.ds(at, ref.shape[0]), :] = ref[...]
        at += ref.shape[0]


def stack(pieces, deps=()):
    rows = sum(piece.shape[0] for piece in pieces)
    return pl.pallas_call(
        functools.partial(stack_kernel, len(pieces)),
        in_specs=[pl.BlockSpec(memory_space=pltpu.VMEM)] * len(pieces) + any_specs(deps),
        out_shape=jax.ShapeDtypeStruct((rows, pieces[0].shape[1]), bf16),
        compiler_params=params(),
        cost_estimate=pl.CostEstimate(flops=1, bytes_accessed=1, transcendentals=0),
        name="stack_parts",
    )(*pieces, *deps)


def first_grad_kernel(parts, block, with_inner, with_value, with_output, *refs):
    place_ref, low_ref, high_ref = refs[:3]
    stacks = refs[3 + with_inner : 7 + with_inner]
    out_ref = refs[7 + with_inner + with_output]
    whole = refs[-1]
    width = stacks[0].shape[1]
    step = pl.program_id(0)

    @pl.when(step == 0)
    def _():
        part, mine = place_ref[2], place_ref[3]
        for t, ref in enumerate(stacks):
            at = mine ^ (2 * (t % 2) + t // 2)
            for k in range(parts):
                column = pl.multiple_of((part ^ k) * width, width)
                whole[pl.ds(pl.multiple_of(at * block, block), block), pl.ds(column, width)] = ref[
                    pl.ds(k * block, block), :
                ]
            if with_value:
                tail = ref[pl.ds(parts * block, EXTRA), :].astype(f32)
                refs[8 + with_inner + with_output][pl.ds(at, 1), :] = tail[0:1] + tail[1:2]

    def product(ref):
        out_ref[...] = jnp.dot(ref[...].T, whole[...], preferred_element_type=f32).astype(bf16)

    @pl.when(step == 0)
    def _():
        product(low_ref)

    if with_inner:

        @pl.when((step > 0) & (step < pl.num_programs(0) - 1))
        def _():
            product(refs[3])

    @pl.when(step == pl.num_programs(0) - 1)
    def _():
        product(high_ref)


def first_grad(place, low, inner, high, stacks, so_far, hidden, parts, block, chunk):
    scenarios, size = low.shape
    inner_steps = 0 if inner is None else inner.shape[1] // size
    cells = (inner_steps + 2) * size
    width = stacks[0].shape[1]
    with_value = chunk == 0
    with_output = so_far is not None
    in_specs = [smem()] + [pl.BlockSpec(low.shape, lambda i: (0, 0))] * 2
    args = [place, low, high]
    if inner is not None:
        in_specs.append(pl.BlockSpec((scenarios, size), lambda i: (0, jnp.clip(i - 1, 0, inner_steps - 1))))
        args.append(inner)
    in_specs += [pl.BlockSpec(ref.shape, lambda i: (0, 0)) for ref in stacks]
    args += stacks
    aliases = {}
    if with_output:
        aliases = {len(args): 0}
        in_specs.append(pl.BlockSpec(memory_space=pl.ANY))
        args.append(so_far)
    out_specs = [pl.BlockSpec((size, parts * width), lambda i: (i, chunk))]
    out_shape = [jax.ShapeDtypeStruct((cells, hidden), bf16)]
    if with_value:
        out_specs.append(pl.BlockSpec((4, width), lambda i: (0, 0)))
        out_shape.append(jax.ShapeDtypeStruct((4, width), f32))
    return pl.pallas_call(
        functools.partial(first_grad_kernel, parts, block, inner is not None, with_value, with_output),
        grid=(inner_steps + 2,),
        in_specs=in_specs,
        out_specs=out_specs,
        out_shape=out_shape,
        input_output_aliases=aliases,
        scratch_shapes=[pltpu.VMEM((scenarios, parts * width), bf16)],
        compiler_params=params(),
        cost_estimate=pl.CostEstimate(flops=1, bytes_accessed=1, transcendentals=0),
        name="first_gradient",
    )(*args)


def local(hist, drift, shocks, shock_table, first_weight, mid_weight, head_weight, cotangent):
    scenarios, rows, columns = hist.shape
    count = lax.axis_size("grid")
    hidden = first_weight.shape[1]
    units = mid_weight.shape[1]
    parts = count // 4
    chunks = CHUNKS if hidden % (parts * CHUNKS * LANES) == 0 else 1
    width = hidden // (parts * chunks)
    block = scenarios // 4
    index = lax.axis_index("grid")
    core, side, part = index % 2, index // 2 % 2, index // 4
    mine = 2 * core + side
    tiles = to_tiles(hist)

    place = jnp.stack([core, side, part, mine])
    cot = lax.dynamic_slice_in_dim(cotangent, mine * block, block)[:, None]
    heads = [head_weight[None, :]]
    mids = [mid_weight]

    *own_rows, inner = inner_steps(tiles, drift, shocks, shock_table)
    inner = inner if rows > 4 else None
    forward = [(i, i + 1) for i in range(count - 1)]
    backward = [(i + 1, i) for i in range(count - 1)]
    below = lax.ppermute(own_rows[3], "grid", forward)
    above = lax.ppermute(own_rows[0], "grid", backward)
    mids.append(swap(mids[0], count, 1))
    mids.append(swap(mids[0], count, 2))
    product = None if inner is None else inner_product(inner, first_weight, width, mids[1:])
    mids.append(swap(mids[2], count, 1))
    low, high = edge_steps(drift, shocks, shock_table, own_rows, below, above, [] if product is None else [product])

    def density_turn(turn, dep, so_far):
        return density_steps(tiles, drift, shocks, shock_table, below, above, dep, so_far, turn, 4)

    owned, firsts, density = [], [], None
    products = [edge_product(place, low, high, first_weight, product, parts, width, c) for c in range(chunks)]
    sums = []
    for c, (keep, send) in enumerate(products):
        keep, send = add_side(place, keep, swap(send, count, 1), [mids[3]])
        sums.append((keep, send, swap(send, count, 2)))
    density = density_turn(0, sums[-1][1], density)
    for c, (keep, send, other) in enumerate(sums):
        own, *sends = add_parts(place, keep, other, [density])
        received = [swap(piece, count, 4 * (k + 1)) for k, piece in enumerate(sends)]
        if c == chunks - 1:
            density = density_turn(1, sends[-1], density)
        owned.append(activate(own, received, [density]))
    for first in owned:
        firsts.append(first)
        firsts += [swap(first, count, 4 * k) for k in range(1, parts)]
    heads += [swap(heads[0], count, k) for k in range(1, 4)]
    density = density_turn(2, owned[-1], density)
    back_second, own, value, head_part, *sends = middle(
        place, cot, firsts, mids, heads, chunks, parts, width, [density]
    )
    received = [swap(piece, count, 4 * (k + 1)) for k, piece in enumerate(sends)]
    density = density_turn(3, received[0], density)
    keep, send = mid_grad(place, back_second, head_part, firsts, chunks, parts, width, [density])
    *backs, tail = back_first(own, value, received, owned, [density])
    keep, send = mid_add(keep, swap(send, count, 1), [received[-1]])
    grad_mid, grad_head = mid_final(keep, swap(send, count, 2))
    grad_first = None
    for c in range(chunks):
        pieces = [backs[c]] + [swap(backs[c], count, 4 * k) for k in range(1, parts)]
        mine_stack = stack(pieces + [tail] if c == 0 else pieces, [grad_mid])
        stacks = [mine_stack, swap(mine_stack, count, 1), swap(mine_stack, count, 2)]
        stacks.append(swap(stacks[2], count, 1))
        results = first_grad(place, low, inner, high, stacks, grad_first, hidden, parts, block, c)
        grad_first = results[0]
        if c == 0:
            value = results[1][:, :block].reshape(scenarios)
    return from_tiles(density, hist.shape), value, grad_first, grad_mid, grad_head[0]


def solution(mesh):
    in_specs = (
        P("groups", "grid", None),
        P(None, "grid", None),
        P("groups", None),
        P("groups", None),
        P(("groups", "grid"), None),
        P("groups", "grid"),
        P(("groups", "grid")),
        P("groups"),
    )
    out_specs = (
        P("groups", "grid", None),
        P("groups"),
        P(("groups", "grid"), None),
        P("groups", "grid"),
        P(("groups", "grid")),
    )
    return jax.shard_map(local, mesh=mesh, in_specs=in_specs, out_specs=out_specs, check_vma=False)
```

time: 387 us -> 166 us (0.43)
  waiting for transfers between devices: 167 us -> 29.6 us
  Pallas kernels: 0 us -> 90.6 us
  local copies, waits for them, and re-layouts: 71.7 us -> 7.08 us
  other arithmetic: 48.1 us -> 0.08 us
  matrix products: 36.7 us -> 0 us
  blocking collectives: 31 us -> 0 us
  starting transfers between devices: 17.3 us -> 36.9 us
  between operations: 14.3 us -> 0.96 us
    psum x2 -> x0, waiting for transfers between devices: 167 us -> none  [the longest x1 106 us: local(): first_pre = lax.psum(partial_first, 'grid')]
    pallas_call x0 -> x18, Pallas kernels: none -> 90.6 us  [the longest x4 29.2 us: density_steps(): pl.pallas_call(functools.partial(density_kernel, rows, size, first), grid...]
    slice x12 -> x1, local copies, waits for them, and re-layouts: 47.7 us -> 0.01 us  [local(): value = results[1][:, :block].reshape(scenarios)]
    dot_general x7 -> x0, matrix products: 36.7 us -> none  [the longest x1 15.5 us: local(): lax.dot_general(inputs, back_first, (((0,), (0,)), ((), ())), preferred_e...]
    psum x1 -> x0, blocking collectives: 31 us -> none  [local(): value = lax.psum(value_part, 'grid')]
    mul x4 -> x0, other arithmetic: 30.7 us -> none  [the longest x2 19.2 us: kfe_step(): flux_y = velocity_y * centre]
    ppermute x6 -> x27, waiting for transfers between devices: 0.02 us -> 29.6 us  [the longest x25 29.6 us: swap(): return lax.ppermute(values, 'grid', [(i, i ^ flip) for i in range(count)])]
    ppermute x6 -> x27, starting transfers between devices: 17.2 us -> 36.9 us  [the longest x25 33.6 us: swap(): return lax.ppermute(values, 'grid', [(i, i ^ flip) for i in range(count)])]
  transfers between devices with their start and end apart: 8 -> 27, of which waited for: 2 -> 10; matrix products, arithmetic and copies ran while one was open for 15% -> 1% of each run, Pallas kernels for 0% -> 30%
where the time goes in v2:
time: 166 us; the launch traced here: 165 us
  Pallas kernels  90.6 us (55%)
  starting transfers between devices  36.9 us (22%)
  waiting for transfers between devices  29.6 us (18%)
  local copies, waits for them, and re-layouts  7.08 us (4%)
    ppermute x25, starting transfers between devices, swap(): return lax.ppermute(values, 'grid', [(i, i ^ flip) for i in range(count)])  33.6 us
    ppermute x25, waiting for transfers between devices, swap(): return lax.ppermute(values, 'grid', [(i, i ^ flip) for i in range(count)])  29.6 us
    pallas_call x4, Pallas kernels, density_steps(): pl.pallas_call(functools.partial(density_kernel, rows, size, first), grid...  29.2 us
    pallas_call x1, Pallas kernels, inner_steps(): pl.pallas_call(functools.partial(inner_kernel, rows, size), grid=(scenari...  16.2 us
    pallas_call x1, Pallas kernels, first_grad(): pl.pallas_call(functools.partial(first_grad_kernel, parts, block, inner i...  12.8 us
    pallas_call x1, Pallas kernels, inner_product(): pl.pallas_call(functools.partial(inner_product_kernel, count, len(deps)),...  9.43 us
    pallas_call x1, Pallas kernels, edge_steps(): pl.pallas_call(functools.partial(edge_kernel, size), grid=(scenarios // s...  8.86 us
    unnamed x40, local copies, waits for them, and re-layouts  5.63 us
  transfers between devices with their start and end apart: 27, of which 10 were waited for; matrix products, arithmetic and copies ran while one was open for 1% of the time, Pallas kernels for 30%

profile of v2, /device:TPU:0, one launch (start us, length us, event | category | flops | bytes accessed | tf_op | source)
XLA Modules:
  0.0 165.2 jit_solution(2744392903368960266)
XLA Ops:
  1.2 2.6 %collective-permute-start.3 = (bf16[2048,128]{1,0:T(8,128)(2,1)}, bf16[2048,128]{1,0:T(8,128)(2,1)}, u32[]{:S(2)}, u32[]{:S(2)}) collective-permute-start(bf16[2048,128]{1,0:T(8,128)(2,1)} %refs_6_.3), channel_id=1, source_target_pairs={{0,2},{1,3},{2,0},{3,1},{4,6},{5,7},{6,4},{7,5},{8,10},{9,11},{10,... | collective-permute-start | bytes 1572872 | tf_op jit(solution)/shard_map/ppermute | solution.py:383
  6.1 16.2 %inner_density_steps.1 = (bf16[400,512]{1,0:T(8,128)(2,1)}, bf16[384,512]{1,0:T(8,128)(2,1)S(1)}, bf16[384,512]{1,0:T(8,128)(2,1)S(1)}, bf16[400,512]{1,0:T(8,128)(2,1)}, bf16[384,3072]{1,0:T(8,128)(2,1)S(1)}) custom-call(f32[12288,128]{1,0:T(8,128)} %bitcast.23, f32[2,16,256]{2,1,0:T(8,128)S(1)} %copy-done.7, s32[384,2]{1,0:T(8,128)S(1)} %copy.27.levels_ref, ...), custom_call_target="tpu_custom_call" | custom-call | flops 1 | bytes 1 | tf_op jit(solution)/shard_map/inner_density_steps/pallas_call | solution.py:184
  27.4 9.4 %inner_product.1.refs_0_ = f32[4,384,512]{2,1,0:T(8,128)} custom-call(bf16[384,3072]{1,0:T(8,128)(2,1)S(1)} %get-tuple-element.41.refs_0_.refs_3_, bf16[4096,2048]{1,0:T(8,128)(2,1)} %bottom_ref.1, bf16[4096,2048]{1,0:T(8,128)(2,1)} %bottom_ref.1, bf16[4096,2048]{1,0:T(8,128)(2,1)} %bottom_ref.1, bf16[4096,2048]{1,0:T(8,128)(2,1)} %bottom_ref.1, ...), custom_call_target="tpu_custom_call" | custom-call | flops 1 | bytes 1 | tf_op jit(solution)/shard_map/inner_product/pallas_call | solution.py:403
  36.9 8.9 %edge_density_steps.1 = (bf16[384,512]{1,0:T(8,128)(2,1)S(1)}, bf16[384,512]{1,0:T(8,128)(2,1)S(1)}) custom-call(f32[2,16,256]{2,1,0:T(8,128)S(1)} %copy-done.8, s32[384,2]{1,0:T(8,128)S(1)} %copy.27.levels_ref, f32[8,2]{1,0:T(8,128)S(1)} %copy.28.table_ref, bf16[400,512]{1,0:T(8,128)(2,1)} %get-tuple-element.38.first_ref, bf16[384,512]{1,0:T(8,128)(2,1)S(1)} %copy-done.12, ...), custom_call_target="tpu_custom_call" | custom-call | flops 1 | bytes 1 | tf_op jit(solution)/shard_map/edge_density_steps/pallas_call | solution.py:274
  45.8 5.4 %edge_product.1 = (f32[2,4,96,512]{3,2,1,0:T(8,128)S(1)}, bf16[2,4,96,512]{3,2,1,0:T(8,128)(2,1)S(1)}) custom-call(s32[4]{0:T(128)S(1)} %pad_add_fusion.place_ref.refs_0_, bf16[384,512]{1,0:T(8,128)(2,1)S(1)} %get-tuple-element.42.low_ref.refs_1_, bf16[384,512]{1,0:T(8,128)(2,1)S(1)} %get-tuple-element.43.high_ref.refs_2_, bf16[4096,2048]{1,0:T(8,128)(2,1)} %bottom_ref.1, ...), custom_call_target="tpu_custom_call" | custom-call | flops 1 | bytes 1 | tf_op jit(solution)/shard_map/edge_product/pallas_call | solution.py:447
  52.5 2.8 %collective-permute-done.5.refs_0_.refs_9_ = bf16[2048,128]{1,0:T(8,128)(2,1)S(1)} collective-permute-done((bf16[2048,128]{1,0:T(8,128)(2,1)}, bf16[2048,128]{1,0:T(8,128)(2,1)S(1)}, u32[]{:S(2)}, u32[]{:S(2)}) %collective-permute-start.5) | collective-permute-done | bytes 524320 | tf_op jit(solution)/shard_map/ppermute | solution.py:383
  56.0 2.5 %collective-permute-start.6 = (bf16[4,96,512]{2,1,0:T(8,128)(2,1)S(1)}, bf16[4,96,512]{2,1,0:T(8,128)(2,1)S(1)}, u32[]{:S(2)}, u32[]{:S(2)}) collective-permute-start(bf16[4,96,512]{2,1,0:T(8,128)(2,1)S(1)} %get-tuple-element.47.dep_ref), channel_id=1, source_target_pairs={{0,2},{1,3},{2,0},{3,1},{4,6},{5,7},{6,4},{7,5},{8,10},{9,11},{10,... | collective-permute-start | bytes 1179656 | tf_op jit(solution)/shard_map/ppermute | solution.py:383
  58.5 7.3 %density_steps.4.refs_0_ = f32[12288,128]{1,0:T(8,128)} custom-call(f32[12288,128]{1,0:T(8,128)} %bitcast.24, f32[2,16,256]{2,1,0:T(8,128)S(1)} %copy-done.8, s32[384,2]{1,0:T(8,128)S(1)} %copy.27.levels_ref, f32[8,2]{1,0:T(8,128)S(1)} %copy.28.table_ref, bf16[400,512]{1,0:T(8,128)(2,1)S(1)} %collective-permute-done.below_ref, ...), custom_call_target="tpu_custom_call" | custom-call | flops 1 | bytes 1 | tf_op jit(solution)/shard_map/density_steps/pallas_call | solution.py:365
  70.1 2.9 %collective-permute-start.7 = (bf16[96,512]{1,0:T(8,128)(2,1)}, bf16[96,512]{1,0:T(8,128)(2,1)}, u32[]{:S(2)}, u32[]{:S(2)}) collective-permute-start(bf16[96,512]{1,0:T(8,128)(2,1)} %get-tuple-element.49), channel_id=1, source_target_pairs={{0,4},{1,5},{2,6},{3,7},{4,0},{5,1},{6,2},{7,3},{8,12},{9,13},{10,... | collective-permute-start | bytes 294920 | tf_op jit(solution)/shard_map/ppermute | solution.py:383
  73.0 2.6 %collective-permute-start.8 = (bf16[96,512]{1,0:T(8,128)(2,1)}, bf16[96,512]{1,0:T(8,128)(2,1)}, u32[]{:S(2)}, u32[]{:S(2)}) collective-permute-start(bf16[96,512]{1,0:T(8,128)(2,1)} %get-tuple-element.50), channel_id=1, source_target_pairs={{0,8},{1,9},{2,10},{3,11},{4,12},{5,13},{6,14},{7,15},{8,0},{9,1},... | collective-permute-start | bytes 294920 | tf_op jit(solution)/shard_map/ppermute | solution.py:383
  76.2 7.3 %density_steps.5.refs_4_.refs_0_ = f32[12288,128]{1,0:T(8,128)} custom-call(f32[12288,128]{1,0:T(8,128)} %bitcast.25, f32[2,16,256]{2,1,0:T(8,128)S(1)} %copy-done.8, s32[384,2]{1,0:T(8,128)S(1)} %copy.27.levels_ref, f32[8,2]{1,0:T(8,128)S(1)} %copy.28.table_ref, ...), custom_call_target="tpu_custom_call", output_to_operand_aliasing={{}: (7, {})} | custom-call | flops 1 | bytes 1 | tf_op jit(solution)/shard_map/density_steps/pallas_call | solution.py:365
  85.8 3.9 %collective-permute-start.12 = (bf16[96,512]{1,0:T(8,128)(2,1)S(1)}, bf16[96,512]{1,0:T(8,128)(2,1)}, u32[]{:S(2)}, u32[]{:S(2)}) collective-permute-start(bf16[96,512]{1,0:T(8,128)(2,1)S(1)} %first_activation.1.dep_ref.refs_2_.refs_5_.refs_3_), channel_id=1, source_target_pairs={{0,12},{1,13},{2,14},{3,15},{4,8},{5,9},{6,10},{7,11},{8,4},{9,5},... | collective-permute-start | bytes 294920 | tf_op jit(solution)/shard_map/ppermute | solution.py:383
  91.2 7.4 %density_steps.6.refs_14_.refs_0_ = f32[12288,128]{1,0:T(8,128)} custom-call(f32[12288,128]{1,0:T(8,128)} %bitcast.26, f32[2,16,256]{2,1,0:T(8,128)S(1)} %copy-done.8, s32[384,2]{1,0:T(8,128)S(1)} %copy.27.levels_ref, f32[8,2]{1,0:T(8,128)S(1)} %copy.28.table_ref, ...), custom_call_target="tpu_custom_call", output_to_operand_aliasing={{}: (7, {})} | custom-call | flops 1 | bytes 1 | tf_op jit(solution)/shard_map/density_steps/pallas_call | solution.py:365
  98.6 2.6 %value_layers.1 = (bf16[96,512]{1,0:T(8,128)(2,1)S(1)}, f32[96,512]{1,0:T(8,128)S(1)}, f32[1,512]{1,0:T(1,128)S(1)}, f32[1,512]{1,0:T(1,128)S(1)}, bf16[112,512]...) custom-call(s32[4]{0:T(128)S(1)} %pad_add_fusion.place_ref.refs_0_, ...), custom_call_target="tpu_custom_call" | custom-call | flops 1 | bytes 1 | tf_op jit(solution)/shard_map/value_layers/pallas_call | solution.py:589
  102.7 3.4 %collective-permute-done.16.dep_ref.refs_2_ = bf16[112,512]{1,0:T(8,128)(2,1)S(1)} collective-permute-done((bf16[112,512]{1,0:T(8,128)(2,1)S(1)}, bf16[112,512]{1,0:T(8,128)(2,1)S(1)}, u32[]{:S(2)}, u32[]{:S(2)}) %collective-permute-start.16) | collective-permute-done | bytes 114720 | tf_op jit(solution)/shard_map/ppermute | solution.py:383
  106.1 7.3 %density_steps.7.refs_6_.refs_7_ = f32[12288,128]{1,0:T(8,128)} custom-call(f32[12288,128]{1,0:T(8,128)} %bitcast.27, f32[2,16,256]{2,1,0:T(8,128)S(1)} %copy-done.8, s32[384,2]{1,0:T(8,128)S(1)} %copy.27.levels_ref, f32[8,2]{1,0:T(8,128)S(1)} %copy.28.table_ref, ...), custom_call_target="tpu_custom_call", output_to_operand_aliasing={{}: (7, {})} | custom-call | flops 1 | bytes 1 | tf_op jit(solution)/shard_map/density_steps/pallas_call | solution.py:365
  115.2 3.8 %collective-permute-start.18 = (bf16[112,512]{1,0:T(8,128)(2,1)S(1)}, bf16[112,512]{1,0:T(8,128)(2,1)S(1)}, u32[]{:S(2)}, u32[]{:S(2)}) collective-permute-start(bf16[112,512]{1,0:T(8,128)(2,1)S(1)} %get-tuple-element.56), channel_id=1, source_target_pairs={{0,12},{1,13},{2,14},{3,15},{4,8},{5,9},{6,10},{7,11},{8,4},{9,5},... | collective-permute-start | bytes 344072 | tf_op jit(solution)/shard_map/ppermute | solution.py:383
  119.0 3.8 %collective-permute-done.18.refs_4_.refs_0_ = bf16[112,512]{1,0:T(8,128)(2,1)S(1)} collective-permute-done((bf16[112,512]{1,0:T(8,128)(2,1)S(1)}, bf16[112,512]{1,0:T(8,128)(2,1)S(1)}, u32[]{:S(2)}, u32[]{:S(2)}) %collective-permute-start.18) | collective-permute-done | bytes 114720 | tf_op jit(solution)/shard_map/ppermute | solution.py:383
  123.5 2.7 %collective-permute-start.17 = (bf16[112,512]{1,0:T(8,128)(2,1)S(1)}, bf16[112,512]{1,0:T(8,128)(2,1)S(1)}, u32[]{:S(2)}, u32[]{:S(2)}) collective-permute-start(bf16[112,512]{1,0:T(8,128)(2,1)S(1)} %get-tuple-element.55), channel_id=1, source_target_pairs={{0,8},{1,9},{2,10},{3,11},{4,12},{5,13},{6,14},{7,15},{8,0},{9,1},... | collective-permute-start | bytes 344072 | tf_op jit(solution)/shard_map/ppermute | solution.py:383
  126.2 5.1 %collective-permute-done.17.refs_3_ = bf16[112,512]{1,0:T(8,128)(2,1)S(1)} collective-permute-done((bf16[112,512]{1,0:T(8,128)(2,1)S(1)}, bf16[112,512]{1,0:T(8,128)(2,1)S(1)}, u32[]{:S(2)}, u32[]{:S(2)}) %collective-permute-start.17) | collective-permute-done | bytes 114720 | tf_op jit(solution)/shard_map/ppermute | solution.py:383
  131.5 3.8 %collective-permute-start.21 = (bf16[96,512]{1,0:T(8,128)(2,1)S(1)}, bf16[96,512]{1,0:T(8,128)(2,1)S(1)}, u32[]{:S(2)}, u32[]{:S(2)}) collective-permute-start(bf16[96,512]{1,0:T(8,128)(2,1)S(1)} %get-tuple-element.57.refs_0_), channel_id=1, source_target_pairs={{0,12},{1,13},{2,14},{3,15},{4,8},{5,9},{6,10},{7,11},{8,4},{9,5},... | collective-permute-start | bytes 294920 | tf_op jit(solution)/shard_map/ppermute | solution.py:383
  137.9 2.9 %collective-permute-done.20.refs_2_ = bf16[96,512]{1,0:T(8,128)(2,1)S(1)} collective-permute-done((bf16[96,512]{1,0:T(8,128)(2,1)S(1)}, bf16[96,512]{1,0:T(8,128)(2,1)S(1)}, u32[]{:S(2)}, u32[]{:S(2)}) %collective-permute-start.20) | collective-permute-done | bytes 98336 | tf_op jit(solution)/shard_map/ppermute | solution.py:383
  143.8 6.2 %collective-permute-done.25.refs_6_ = bf16[400,512]{1,0:T(8,128)(2,1)S(1)} collective-permute-done((bf16[400,512]{1,0:T(8,128)(2,1)S(1)}, bf16[400,512]{1,0:T(8,128)(2,1)S(1)}, u32[]{:S(2)}, u32[]{:S(2)}) %collective-permute-start.25) | collective-permute-done | bytes 409632 | tf_op jit(solution)/shard_map/ppermute | solution.py:383
  151.7 12.8 %first_gradient.1 = (bf16[4096,2048]{1,0:T(8,128)(2,1)}, f32[4,512]{1,0:T(4,128)S(1)}) custom-call(s32[4]{0:T(128)S(1)} %pad_add_fusion.place_ref.refs_0_, bf16[384,512]{1,0:T(8,128)(2,1)S(1)} %copy-done.4, bf16[384,512]{1,0:T(8,128)(2,1)S(1)} %copy-done.6, bf16[384,3072]{1,0:T(8,128)(2,1)S(1)} %get-tuple-element.41.refs_0_.refs_3_, ...), custom_call_target="tpu_custom_call" | custom-call | flops 1 | bytes 1 | tf_op jit(solution)/shard_map/first_gradient/pallas_call | solution.py:807
  (93 shorter events, 30.5 us)
Async XLA Ops:
  0.6 26.7 %collective-permute-start.2 = (bf16[2048,128]{1,0:T(8,128)(2,1)}, bf16[2048,128]{1,0:T(8,128)(2,1)}, u32[]{:S(2)}, u32[]{:S(2)}) collective-permute-start(bf16[2048,128]{1,0:T(8,128)(2,1)} %refs_6_.3), channel_id=1, source_target_pairs={{0,1},{1,0},{2,3},{3,2},{4,5},{5,4},{6,7},{7,6},{8,9},{9,8},{10,11... | collective-permute-start | bytes 1572872 | tf_op jit(solution)/shard_map/ppermute | solution.py:383
  1.2 26.2 %collective-permute-start.3 = (bf16[2048,128]{1,0:T(8,128)(2,1)}, bf16[2048,128]{1,0:T(8,128)(2,1)}, u32[]{:S(2)}, u32[]{:S(2)}) collective-permute-start(bf16[2048,128]{1,0:T(8,128)(2,1)} %refs_6_.3), channel_id=1, source_target_pairs={{0,2},{1,3},{2,0},{3,1},{4,6},{5,7},{6,4},{7,5},{8,10},{9,11},{10,... | collective-permute-start | bytes 1572872 | tf_op jit(solution)/shard_map/ppermute | solution.py:383
  23.9 13.0 %collective-permute-start = (bf16[400,512]{1,0:T(8,128)(2,1)}, bf16[400,512]{1,0:T(8,128)(2,1)S(1)}, u32[]{:S(2)}, u32[]{:S(2)}) collective-permute-start(bf16[400,512]{1,0:T(8,128)(2,1)} %get-tuple-element.37.last_ref), channel_id=1, source_target_pairs={{0,1},{1,2},{2,3},{3,4},{4,5},{5,6},{6,7},{7,8},{8,9},{9,10},{10,1... | collective-permute-start | bytes 1228808 | tf_op jit(solution)/shard_map/ppermute | solution.py:844
  26.0 10.9 %collective-permute-start.1 = (bf16[400,512]{1,0:T(8,128)(2,1)}, bf16[400,512]{1,0:T(8,128)(2,1)S(1)}, u32[]{:S(2)}, u32[]{:S(2)}) collective-permute-start(bf16[400,512]{1,0:T(8,128)(2,1)} %get-tuple-element.38.first_ref), channel_id=1, source_target_pairs={{1,0},{2,1},{3,2},{4,3},{5,4},{6,5},{7,6},{8,7},{9,8},{10,9},{11,1... | collective-permute-start | bytes 1228808 | tf_op jit(solution)/shard_map/ppermute | solution.py:845
  56.0 12.2 %collective-permute-start.6 = (bf16[4,96,512]{2,1,0:T(8,128)(2,1)S(1)}, bf16[4,96,512]{2,1,0:T(8,128)(2,1)S(1)}, u32[]{:S(2)}, u32[]{:S(2)}) collective-permute-start(bf16[4,96,512]{2,1,0:T(8,128)(2,1)S(1)} %get-tuple-element.47.dep_ref), channel_id=1, source_target_pairs={{0,2},{1,3},{2,0},{3,1},{4,6},{5,7},{6,4},{7,5},{8,10},{9,11},{10,... | collective-permute-start | bytes 1179656 | tf_op jit(solution)/shard_map/ppermute | solution.py:383
  70.1 13.5 %collective-permute-start.7 = (bf16[96,512]{1,0:T(8,128)(2,1)}, bf16[96,512]{1,0:T(8,128)(2,1)}, u32[]{:S(2)}, u32[]{:S(2)}) collective-permute-start(bf16[96,512]{1,0:T(8,128)(2,1)} %get-tuple-element.49), channel_id=1, source_target_pairs={{0,4},{1,5},{2,6},{3,7},{4,0},{5,1},{6,2},{7,3},{8,12},{9,13},{10,... | collective-permute-start | bytes 294920 | tf_op jit(solution)/shard_map/ppermute | solution.py:383
  73.0 11.8 %collective-permute-start.8 = (bf16[96,512]{1,0:T(8,128)(2,1)}, bf16[96,512]{1,0:T(8,128)(2,1)}, u32[]{:S(2)}, u32[]{:S(2)}) collective-permute-start(bf16[96,512]{1,0:T(8,128)(2,1)} %get-tuple-element.50), channel_id=1, source_target_pairs={{0,8},{1,9},{2,10},{3,11},{4,12},{5,13},{6,14},{7,15},{8,0},{9,1},... | collective-permute-start | bytes 294920 | tf_op jit(solution)/shard_map/ppermute | solution.py:383
  75.6 9.2 %collective-permute-start.9 = (bf16[96,512]{1,0:T(8,128)(2,1)S(1)}, bf16[96,512]{1,0:T(8,128)(2,1)}, u32[]{:S(2)}, u32[]{:S(2)}) collective-permute-start(bf16[96,512]{1,0:T(8,128)(2,1)S(1)} %get-tuple-element.51.dep_ref), channel_id=1, source_target_pairs={{0,12},{1,13},{2,14},{3,15},{4,8},{5,9},{6,10},{7,11},{8,4},{9,5},... | collective-permute-start | bytes 294920 | tf_op jit(solution)/shard_map/ppermute | solution.py:383
  75.6 14.1 %collective-permute-start.15 = (f32[1,128]{1,0:T(1,128)S(1)}, f32[1,128]{1,0:T(1,128)S(1)}, u32[]{:S(2)}, u32[]{:S(2)}) collective-permute-start(f32[1,128]{1,0:T(1,128)S(1)} %bitcast.18), channel_id=1, source_target_pairs={{0,3},{1,2},{2,1},{3,0},{4,7},{5,6},{6,5},{7,4},{8,11},{9,10},{10,... | collective-permute-start | bytes 1544 | tf_op jit(solution)/shard_map/ppermute | solution.py:383
  75.6 23.0 %collective-permute-start.14 = (f32[1,128]{1,0:T(1,128)S(1)}, f32[1,128]{1,0:T(1,128)S(1)}, u32[]{:S(2)}, u32[]{:S(2)}) collective-permute-start(f32[1,128]{1,0:T(1,128)S(1)} %bitcast.19), channel_id=1, source_target_pairs={{0,2},{1,3},{2,0},{3,1},{4,6},{5,7},{6,4},{7,5},{8,10},{9,11},{10,... | collective-permute-start | bytes 1544 | tf_op jit(solution)/shard_map/ppermute | solution.py:383
  83.6 15.0 %collective-permute-start.13 = (f32[1,128]{1,0:T(1,128)S(1)}, f32[1,128]{1,0:T(1,128)S(1)}, u32[]{:S(2)}, u32[]{:S(2)}) collective-permute-start(f32[1,128]{1,0:T(1,128)S(1)} %bitcast.20), channel_id=1, source_target_pairs={{0,1},{1,0},{2,3},{3,2},{4,5},{5,4},{6,7},{7,6},{8,9},{9,8},{10,11... | collective-permute-start | bytes 1544 | tf_op jit(solution)/shard_map/ppermute | solution.py:383
  85.8 12.7 %collective-permute-start.12 = (bf16[96,512]{1,0:T(8,128)(2,1)S(1)}, bf16[96,512]{1,0:T(8,128)(2,1)}, u32[]{:S(2)}, u32[]{:S(2)}) collective-permute-start(bf16[96,512]{1,0:T(8,128)(2,1)S(1)} %first_activation.1.dep_ref.refs_2_.refs_5_.refs_3_), channel_id=1, source_target_pairs={{0,12},{1,13},{2,14},{3,15},{4,8},{5,9},{6,10},{7,11},{8,4},{9,5},... | collective-permute-start | bytes 294920 | tf_op jit(solution)/shard_map/ppermute | solution.py:383
  89.7 8.8 %collective-permute-start.11 = (bf16[96,512]{1,0:T(8,128)(2,1)S(1)}, bf16[96,512]{1,0:T(8,128)(2,1)}, u32[]{:S(2)}, u32[]{:S(2)}) collective-permute-start(bf16[96,512]{1,0:T(8,128)(2,1)S(1)} %first_activation.1.dep_ref.refs_2_.refs_5_.refs_3_), channel_id=1, source_target_pairs={{0,8},{1,9},{2,10},{3,11},{4,12},{5,13},{6,14},{7,15},{8,0},{9,1},... | collective-permute-start | bytes 294920 | tf_op jit(solution)/shard_map/ppermute | solution.py:383
  89.7 8.8 %collective-permute-start.10 = (bf16[96,512]{1,0:T(8,128)(2,1)S(1)}, bf16[96,512]{1,0:T(8,128)(2,1)}, u32[]{:S(2)}, u32[]{:S(2)}) collective-permute-start(bf16[96,512]{1,0:T(8,128)(2,1)S(1)} %first_activation.1.dep_ref.refs_2_.refs_5_.refs_3_), channel_id=1, source_target_pairs={{0,4},{1,5},{2,6},{3,7},{4,0},{5,1},{6,2},{7,3},{8,12},{9,13},{10,... | collective-permute-start | bytes 294920 | tf_op jit(solution)/shard_map/ppermute | solution.py:383
  101.2 4.9 %collective-permute-start.16 = (bf16[112,512]{1,0:T(8,128)(2,1)S(1)}, bf16[112,512]{1,0:T(8,128)(2,1)S(1)}, u32[]{:S(2)}, u32[]{:S(2)}) collective-permute-start(bf16[112,512]{1,0:T(8,128)(2,1)S(1)} %get-tuple-element.52), channel_id=1, source_target_pairs={{0,4},{1,5},{2,6},{3,7},{4,0},{5,1},{6,2},{7,3},{8,12},{9,13},{10,... | collective-permute-start | bytes 344072 | tf_op jit(solution)/shard_map/ppermute | solution.py:383
  115.1 7.7 %collective-permute-start.22 = (bf16[2,2064,128]{2,1,0:T(8,128)(2,1)S(1)}, bf16[2,2064,128]{2,1,0:T(8,128)(2,1)S(1)}, u32[]{:S(2)}, u32[]{:S(2)}) collective-permute-start(bf16[2,2064,128]{2,1,0:T(8,128)(2,1)S(1)} %get-tuple-element.62), channel_id=1, source_target_pairs={{0,1},{1,0},{2,3},{3,2},{4,5},{5,4},{6,7},{7,6},{8,9},{9,8},{10,11... | collective-permute-start | bytes 3170312 | tf_op jit(solution)/shard_map/ppermute | solution.py:383
  115.2 7.7 %collective-permute-start.18 = (bf16[112,512]{1,0:T(8,128)(2,1)S(1)}, bf16[112,512]{1,0:T(8,128)(2,1)S(1)}, u32[]{:S(2)}, u32[]{:S(2)}) collective-permute-start(bf16[112,512]{1,0:T(8,128)(2,1)S(1)} %get-tuple-element.56), channel_id=1, source_target_pairs={{0,12},{1,13},{2,14},{3,15},{4,8},{5,9},{6,10},{7,11},{8,4},{9,5},... | collective-permute-start | bytes 344072 | tf_op jit(solution)/shard_map/ppermute | solution.py:383
  123.1 13.7 %collective-permute-start.23 = (bf16[2064,128]{1,0:T(8,128)(2,1)S(1)}, bf16[2064,128]{1,0:T(8,128)(2,1)S(1)}, u32[]{:S(2)}, u32[]{:S(2)}) collective-permute-start(bf16[2064,128]{1,0:T(8,128)(2,1)S(1)} %get-tuple-element.64), channel_id=1, source_target_pairs={{0,2},{1,3},{2,0},{3,1},{4,6},{5,7},{6,4},{7,5},{8,10},{9,11},{10,... | collective-permute-start | bytes 1585160 | tf_op jit(solution)/shard_map/ppermute | solution.py:383
  123.5 7.9 %collective-permute-start.17 = (bf16[112,512]{1,0:T(8,128)(2,1)S(1)}, bf16[112,512]{1,0:T(8,128)(2,1)S(1)}, u32[]{:S(2)}, u32[]{:S(2)}) collective-permute-start(bf16[112,512]{1,0:T(8,128)(2,1)S(1)} %get-tuple-element.55), channel_id=1, source_target_pairs={{0,8},{1,9},{2,10},{3,11},{4,12},{5,13},{6,14},{7,15},{8,0},{9,1},... | collective-permute-start | bytes 344072 | tf_op jit(solution)/shard_map/ppermute | solution.py:383
  131.5 6.5 %collective-permute-start.21 = (bf16[96,512]{1,0:T(8,128)(2,1)S(1)}, bf16[96,512]{1,0:T(8,128)(2,1)S(1)}, u32[]{:S(2)}, u32[]{:S(2)}) collective-permute-start(bf16[96,512]{1,0:T(8,128)(2,1)S(1)} %get-tuple-element.57.refs_0_), channel_id=1, source_target_pairs={{0,12},{1,13},{2,14},{3,15},{4,8},{5,9},{6,10},{7,11},{8,4},{9,5},... | collective-permute-start | bytes 294920 | tf_op jit(solution)/shard_map/ppermute | solution.py:383
  135.2 5.6 %collective-permute-start.20 = (bf16[96,512]{1,0:T(8,128)(2,1)S(1)}, bf16[96,512]{1,0:T(8,128)(2,1)S(1)}, u32[]{:S(2)}, u32[]{:S(2)}) collective-permute-start(bf16[96,512]{1,0:T(8,128)(2,1)S(1)} %get-tuple-element.57.refs_0_), channel_id=1, source_target_pairs={{0,8},{1,9},{2,10},{3,11},{4,12},{5,13},{6,14},{7,15},{8,0},{9,1},... | collective-permute-start | bytes 294920 | tf_op jit(solution)/shard_map/ppermute | solution.py:383
  135.2 5.7 %collective-permute-start.19 = (bf16[96,512]{1,0:T(8,128)(2,1)S(1)}, bf16[96,512]{1,0:T(8,128)(2,1)S(1)}, u32[]{:S(2)}, u32[]{:S(2)}) collective-permute-start(bf16[96,512]{1,0:T(8,128)(2,1)S(1)} %get-tuple-element.57.refs_0_), channel_id=1, source_target_pairs={{0,4},{1,5},{2,6},{3,7},{4,0},{5,1},{6,2},{7,3},{8,12},{9,13},{10,... | collective-permute-start | bytes 294920 | tf_op jit(solution)/shard_map/ppermute | solution.py:383
  142.0 8.0 %collective-permute-start.25 = (bf16[400,512]{1,0:T(8,128)(2,1)S(1)}, bf16[400,512]{1,0:T(8,128)(2,1)S(1)}, u32[]{:S(2)}, u32[]{:S(2)}) collective-permute-start(bf16[400,512]{1,0:T(8,128)(2,1)S(1)} %stack_parts.1.refs_4_), channel_id=1, source_target_pairs={{0,2},{1,3},{2,0},{3,1},{4,6},{5,7},{6,4},{7,5},{8,10},{9,11},{10,... | collective-permute-start | bytes 1228808 | tf_op jit(solution)/shard_map/ppermute | solution.py:383
  143.8 6.2 %collective-permute-start.24 = (bf16[400,512]{1,0:T(8,128)(2,1)S(1)}, bf16[400,512]{1,0:T(8,128)(2,1)S(1)}, u32[]{:S(2)}, u32[]{:S(2)}) collective-permute-start(bf16[400,512]{1,0:T(8,128)(2,1)S(1)} %stack_parts.1.refs_4_), channel_id=1, source_target_pairs={{0,1},{1,0},{2,3},{3,2},{4,5},{5,4},{6,7},{7,6},{8,9},{9,8},{10,11... | collective-permute-start | bytes 1228808 | tf_op jit(solution)/shard_map/ppermute | solution.py:383
  (22 other events, 266.2 us)

commit v3 on v2

--- a/solution.py
+++ b/solution.py
@@ -1,6 +1,7 @@
 import functools
 import jax
 import jax.numpy as jnp
+import numpy as np
 from jax import lax
 from jax.experimental import pallas as pl
 from jax.experimental.pallas import tpu as pltpu
@@ -80,60 +81,79 @@
     return jnp.concatenate([high, low, ones, zeros], axis=0)
 
 
-def half_shifts(levels, table_ref):
-    results = []
-    for t in range(levels.shape[1]):
-        level = jnp.broadcast_to(levels[:, t : t + 1], (levels.shape[0], LANES))
+def band_matrix(columns):
+    beside = np.eye(columns, k=1) + np.eye(columns, k=-1)
+    flux = np.eye(columns, k=1) - np.eye(columns, k=-1)
+    centre = (1.0 - 4.0 * diffusion_rate) * np.eye(columns) + diffusion_rate * beside
+    return jnp.asarray(np.concatenate([centre, flux], axis=0), dtype=bf16)
+
+
+def half_shifts(levels_ref, table_ref, shift_ref):
+    scenarios = levels_ref.shape[1]
+    for t in range(levels_ref.shape[0]):
+        level = jnp.broadcast_to(levels_ref[t : t + 1, :].astype(f32), (LANES, scenarios)).T
         for c in range(2):
             shift = jnp.zeros(level.shape, f32)
-            for n in range(table_ref.shape[0]):
-                shift = jnp.where(level == n, 0.5 * table_ref[n, c], shift)
-            results.append(shift)
-    return results
-
-
-def sweep_rows(read, coefficient, first, last, shift_x, shift_y, columns):
-    lane_tiles = columns // LANES
-    wide_x = jnp.concatenate([shift_x] * lane_tiles, axis=1)
-    wide_y = jnp.concatenate([shift_y] * lane_tiles, axis=1)
-    column = lax.broadcasted_iota(jnp.int32, wide_x.shape, 1)
-    twice = 2.0 * diffusion_rate
-    before = now = None
-    for row in range(first, last + 1):
+            for n in range(table_ref.shape[1]):
+                shift = jnp.where(level == n, 0.5 * table_ref[c, n], shift)
+            shift_ref[2 * t + c] = shift
+
+
+def wide(values, columns):
+    return jnp.concatenate([values] * (columns // LANES), axis=1)
+
+
+def one_step(segments, read, half_drift, band, shift_x, shift_y, pairs, terms, write):
+    size, columns = shift_x.shape
+    places = [row for first, last in segments for row in range(first + 1, last)]
+    for k, row in enumerate(places):
         density = read(row)
-        up = density * (coefficient(0, row) + wide_x)
-        coming = (density, up, twice * density - up)
-        if before is not None:
-            middle = now[0]
-            rising = middle * (coefficient(1, row - 1) + wide_y)
-            falling = twice * middle - rising
-            from_left = jnp.where(column > 0, pltpu.roll(rising, 1, 1), 0.0)
-            from_right = jnp.where(column < columns - 1, pltpu.roll(falling, columns - 1, 1), 0.0)
-            result = (1.0 - 2.0 * twice) * middle + (before[1] + coming[2]) + (from_left + from_right)
-            yield row - 1, result
-        before, now = now, coming
-
-
-def two_steps(read, coefficient, edge, first, last, shifts, columns, write):
-    middle = sweep_rows(read, coefficient, first - 2, last + 2, shifts[0], shifts[1], columns)
+        pairs[pl.ds(k * size, size), pl.ds(0, columns)] = density.astype(bf16)
+        flux = (half_drift(1, row) + shift_y) * density
+        pairs[pl.ds(k * size, size), pl.ds(columns, columns)] = flux.astype(bf16)
+    count = len(places) * size
+    terms[pl.ds(0, count), :] = jnp.dot(pairs[pl.ds(0, count), :], band, preferred_element_type=f32)
+    for k, row in enumerate(places):
+        low = read(row - 1) * ((diffusion_rate + half_drift(0, row - 1)) + shift_x)
+        high = read(row + 1) * ((diffusion_rate - half_drift(0, row + 1)) - shift_x)
+        write(row, terms[pl.ds(k * size, size), :] + low + high)
+
+
+def two_steps(segments, read, half_drift, edge, band, shifts, scratch, write):
+    pairs, terms, middle = scratch
+    size, columns = shifts[0].shape
+    before = [(first - 2, last + 2) for first, last in segments]
+    between = [(first - 1, last + 1) for first, last in segments]
+    places = [row for first, last in between for row in range(first, last + 1)]
+
+    def write_middle(row, density):
+        middle[pl.ds(places.index(row) * size, size), :] = edge(row, density).astype(bf16)
 
     def read_middle(row):
-        at, density = next(middle)
-        assert at == row
-        return edge(row, density)
-
-    for row, density in sweep_rows(read_middle, coefficient, first - 1, last + 1, shifts[2], shifts[3], columns):
-        write(row, density)
+        return middle[pl.ds(places.index(row) * size, size), :].astype(f32)
+
+    one_step(before, read, half_drift, band, shifts[0], shifts[1], pairs, terms, write_middle)
+    one_step(between, read_middle, half_drift, band, shifts[2], shifts[3], pairs, terms, write)
+
+
+def step_scratch(rows, size, columns):
+    return [
+        pltpu.VMEM((rows * size, 2 * columns), bf16),
+        pltpu.VMEM((rows * size, columns), f32),
+        pltpu.VMEM((rows * size, columns), bf16),
+    ]
 
 
 def inner_kernel(
-    rows, size, hist_ref, drift_ref, levels_ref, table_ref, first_ref, next_ref, prev_ref, last_ref, inner_ref, work
+    rows, size, hist_ref, drift_ref, levels_ref, table_ref, band_ref,
+    first_ref, next_ref, prev_ref, last_ref, shift_ref, inner_ref, *scratch,
 ):
     step = pl.program_id(0)
     columns = drift_ref.shape[2]
 
     @pl.when(step == 0)
     def _():
+        half_shifts(levels_ref, table_ref, shift_ref)
         for out, start in ((first_ref, 0), (last_ref, rows - 2)):
             out[pl.ds(out.shape[0] - EXTRA, EXTRA), :] = drift_tail(drift_ref, start)
 
@@ -144,89 +164,68 @@
     if rows <= 4:
         return
 
-    def coefficient(c, row):
-        return diffusion_rate + 0.5 * drift_ref[c, row : row + 1, :]
-
-    def group(g, carry):
-        base = pl.multiple_of(g * GROUP, GROUP)
-        for half in range(GROUP // SUBLANES):
-            at = base + half * SUBLANES
-            shifts = half_shifts(levels_ref[pl.ds(pl.multiple_of(at, SUBLANES), SUBLANES), :], table_ref)
-
-            def write(row, density):
-                work[pl.ds(half * SUBLANES, SUBLANES), pl.ds((row - 2) * columns, columns)] = density
-
-            two_steps(
-                lambda row: read_row(hist_ref, at, SUBLANES, row, rows, columns),
-                coefficient,
-                lambda row, density: density,
-                2,
-                rows - 3,
-                shifts,
-                columns,
-                write,
-            )
-        inner_ref[pl.ds(base, GROUP), :] = work[...].astype(bf16)
-        return carry
-
-    lax.fori_loop(0, size // GROUP, group, 0)
-
-
-def inner_steps(tiles, drift, shocks, table):
-    scenarios = shocks.shape[0]
+    def write(row, density):
+        inner_ref[:, pl.ds((row - 2) * columns, columns)] = density.astype(bf16)
+
+    two_steps(
+        [(2, rows - 3)],
+        lambda row: read_row(hist_ref, 0, size, row, rows, columns),
+        lambda c, row: 0.5 * drift_ref[c, row : row + 1, :],
+        lambda row, density: density,
+        band_ref[...],
+        [wide(shift_ref[n, where, :], columns) for n in range(4)],
+        scratch,
+        write,
+    )
+
+
+def inner_steps(tiles, drift, levels, table, band):
+    scenarios = levels.shape[1]
     rows, columns = drift.shape[1:]
     per = tiles.shape[0] // scenarios
     size = scenario_block(scenarios)
     inner = max(rows - 4, 1) * columns
     edge = jax.ShapeDtypeStruct((scenarios, 2 * columns), bf16)
     sent = jax.ShapeDtypeStruct((scenarios + EXTRA, 2 * columns), bf16)
-    whole = [pl.BlockSpec(shape.shape, lambda i: (0, 0)) for shape in (sent, edge, edge, sent)]
+    shifts = jax.ShapeDtypeStruct((4, scenarios, LANES), f32)
     return pl.pallas_call(
         functools.partial(inner_kernel, rows, size),
         grid=(scenarios // size,),
         in_specs=[
             pl.BlockSpec((size * per, LANES), lambda i: (i, 0)),
             pl.BlockSpec(drift.shape, lambda i: (0, 0, 0)),
-            pl.BlockSpec((size, shocks.shape[1]), lambda i: (i, 0)),
+            pl.BlockSpec(levels.shape, lambda i: (0, 0)),
             smem(),
+            pl.BlockSpec(band.shape, lambda i: (0, 0)),
         ],
-        out_specs=whole + [pl.BlockSpec((size, inner), lambda i: (i, 0))],
-        out_shape=[sent, edge, edge, sent, jax.ShapeDtypeStruct((scenarios, inner), bf16)],
-        scratch_shapes=[pltpu.VMEM((GROUP, inner), f32)],
+        out_specs=[pl.BlockSpec(shape.shape, lambda i: (0, 0)) for shape in (sent, edge, edge, sent)]
+        + [pl.BlockSpec(shifts.shape, lambda i: (0, 0, 0)), pl.BlockSpec((size, inner), lambda i: (i, 0))],
+        out_shape=[sent, edge, edge, sent, shifts, jax.ShapeDtypeStruct((scenarios, inner), bf16)],
+        scratch_shapes=step_scratch(max(rows - 2, 1), size, columns),
         compiler_params=params(),
         cost_estimate=pl.CostEstimate(flops=1, bytes_accessed=1, transcendentals=0),
         name="inner_density_steps",
-    )(tiles, drift, shocks, table)
+    )(tiles, drift, levels, table, band)
 
 
 def halo_drift(ref, columns):
     tail = ref[pl.ds(ref.shape[0] - EXTRA, EXTRA), :].astype(f32)
-    rows = [[tail[c : c + 1, k * columns : (k + 1) * columns] + tail[2 + c : 3 + c, k * columns : (k + 1) * columns] for k in range(2)] for c in range(2)]
+    both = 0.5 * (tail[0:2] + tail[2:4])
+    rows = [[both[c : c + 1, k * columns : (k + 1) * columns] for k in range(2)] for c in range(2)]
     return rows, tail[4:5, :columns]
 
 
-def coefficients(drift_ref, below, above, rows):
-    def coefficient(c, row):
-        if row < 0:
-            drift = below[c][row + 2]
-        elif row >= rows:
-            drift = above[c][row - rows]
-        else:
-            drift = drift_ref[c, row : row + 1, :]
-        return diffusion_rate + 0.5 * drift
-
-    return coefficient
-
-
-def edge_kernel(
-    size, drift_ref, levels_ref, table_ref, first_ref, next_ref, prev_ref, last_ref, below_ref, above_ref, *refs
-):
-    low_ref, high_ref, work = refs[-3:]
-    step = pl.program_id(0)
+def with_halo(drift_ref, below_ref, above_ref):
     rows, columns = drift_ref.shape[1:]
     below, below_valid = halo_drift(below_ref, columns)
     above, above_valid = halo_drift(above_ref, columns)
-    coefficient = coefficients(drift_ref, below, above, rows)
+
+    def half_drift(c, row):
+        if row < 0:
+            return below[c][row + 2]
+        if row >= rows:
+            return above[c][row - rows]
+        return 0.5 * drift_ref[c, row : row + 1, :]
 
     def edge(row, density):
         if row < 0:
@@ -235,38 +234,34 @@
             return density * above_valid
         return density
 
-    start = pl.multiple_of(step * size, size)
-
-    def group(g, carry):
-        base = pl.multiple_of(g * GROUP, GROUP)
-        every = pl.ds(pl.multiple_of(start + base, GROUP), GROUP)
-        for out, refs, first in (
-            (low_ref, (below_ref, first_ref, next_ref), 0),
-            (high_ref, (prev_ref, last_ref, above_ref), rows - 2),
-        ):
-            wide = [ref[every, :].astype(f32) for ref in refs]
-            for half in range(GROUP // SUBLANES):
-                part = slice(half * SUBLANES, (half + 1) * SUBLANES)
-                levels = levels_ref[pl.ds(pl.multiple_of(base + half * SUBLANES, SUBLANES), SUBLANES), :]
-
-                def read(row):
-                    at = row - (first - 2)
-                    return wide[at // 2][part, at % 2 * columns : (at % 2 + 1) * columns]
-
-                def write(row, density):
-                    work[part, pl.ds((row - first) * columns, columns)] = density
-
-                two_steps(
-                    read, coefficient, edge, first, first + 1, half_shifts(levels, table_ref), columns, write
-                )
-            out[pl.ds(base, GROUP), :] = work[...].astype(bf16)
-        return carry
-
-    lax.fori_loop(0, size // GROUP, group, 0)
-
-
-def edge_steps(drift, shocks, table, own, below, above, deps):
-    scenarios = shocks.shape[0]
+    return half_drift, edge
+
+
+def edge_kernel(
+    size, drift_ref, shift_ref, band_ref, first_ref, next_ref, prev_ref, last_ref, below_ref, above_ref, *refs
+):
+    low_ref, high_ref, *scratch = refs[-5:]
+    rows, columns = drift_ref.shape[1:]
+    half_drift, edge = with_halo(drift_ref, below_ref, above_ref)
+    where = pl.ds(pl.multiple_of(pl.program_id(0) * size, size), size)
+    shifts = [wide(shift_ref[n, where, :], columns) for n in range(4)]
+    for out, refs, first in (
+        (low_ref, (below_ref, first_ref, next_ref), 0),
+        (high_ref, (prev_ref, last_ref, above_ref), rows - 2),
+    ):
+
+        def read(row):
+            at = row - (first - 2)
+            return refs[at // 2][where, pl.ds(at % 2 * columns, columns)].astype(f32)
+
+        def write(row, density):
+            out[:, pl.ds((row - first) * columns, columns)] = density.astype(bf16)
+
+        two_steps([(first, first + 1)], read, half_drift, edge, band_ref[...], shifts, scratch, write)
+
+
+def edge_steps(drift, shifts, band, own, below, above, deps):
+    scenarios = shifts.shape[1]
     columns = drift.shape[2]
     size = scenario_block(scenarios)
     edge = jax.ShapeDtypeStruct((scenarios, 2 * columns), bf16)
@@ -276,83 +271,62 @@
         grid=(scenarios // size,),
         in_specs=[
             pl.BlockSpec(drift.shape, lambda i: (0, 0, 0)),
-            pl.BlockSpec((size, shocks.shape[1]), lambda i: (i, 0)),
-            smem(),
+            pl.BlockSpec(shifts.shape, lambda i: (0, 0, 0)),
+            pl.BlockSpec(band.shape, lambda i: (0, 0)),
         ]
         + [pl.BlockSpec(ref.shape, lambda i: (0, 0)) for ref in (*own, below, above)]
         + any_specs(deps),
         out_specs=[spec, spec],
         out_shape=[edge, edge],
-        scratch_shapes=[pltpu.VMEM((GROUP, 2 * columns), f32)],
+        scratch_shapes=step_scratch(4, size, columns),
         compiler_params=params(),
         cost_estimate=pl.CostEstimate(flops=1, bytes_accessed=1, transcendentals=0),
         name="edge_density_steps",
-    )(drift, shocks, table, *own, below, above, *deps)
+    )(drift, shifts, band, *own, below, above, *deps)
 
 
 def density_kernel(
-    rows, size, first_step, hist_ref, drift_ref, levels_ref, table_ref, below_ref, above_ref, dep_ref, *refs
+    rows, size, first_step, hist_ref, drift_ref, shift_ref, band_ref, below_ref, above_ref, dep_ref, *refs
 ):
-    next_ref = refs[-1]
+    next_ref, *scratch = refs[-4:]
     columns = drift_ref.shape[2]
-    below, below_valid = halo_drift(below_ref, columns)
-    above, above_valid = halo_drift(above_ref, columns)
-    coefficient = coefficients(drift_ref, below, above, rows)
-    start = (first_step + pl.program_id(0)) * size
-
-    def edge(row, density):
+    half_drift, edge = with_halo(drift_ref, below_ref, above_ref)
+    where = pl.ds(pl.multiple_of((first_step + pl.program_id(0)) * size, size), size)
+
+    def read(row):
         if row < 0:
-            return density * below_valid
+            return below_ref[where, pl.ds((row + 2) * columns, columns)].astype(f32)
         if row >= rows:
-            return density * above_valid
-        return density
-
-    def group(g, carry):
-        base = pl.multiple_of(g * GROUP, GROUP)
-        every = pl.ds(pl.multiple_of(start + base, GROUP), GROUP)
-        wide = [ref[every, :].astype(f32) for ref in (below_ref, above_ref)]
-        for half in range(GROUP // SUBLANES):
-            part = slice(half * SUBLANES, (half + 1) * SUBLANES)
-            at = pl.multiple_of(base + half * SUBLANES, SUBLANES)
-
-            def read(row):
-                if row < 0:
-                    return wide[0][part, (row + 2) * columns : (row + 3) * columns]
-                if row >= rows:
-                    return wide[1][part, (row - rows) * columns : (row - rows + 1) * columns]
-                return read_row(hist_ref, at, SUBLANES, row, rows, columns)
-
-            shifts = half_shifts(levels_ref[pl.ds(at, SUBLANES), :], table_ref)
-            two_steps(
-                read,
-                coefficient,
-                edge,
-                0,
-                rows - 1,
-                shifts,
-                columns,
-                lambda row, density: write_row(next_ref, at, SUBLANES, row, rows, columns, density),
-            )
-        return carry
-
-    lax.fori_loop(0, size // GROUP, group, 0)
-
-
-def density_steps(tiles, drift, shocks, table, below, above, dep, so_far, turn, turns):
-    scenarios = shocks.shape[0]
+            return above_ref[where, pl.ds((row - rows) * columns, columns)].astype(f32)
+        return read_row(hist_ref, 0, size, row, rows, columns)
+
+    two_steps(
+        [(0, rows - 1)],
+        read,
+        half_drift,
+        edge,
+        band_ref[...],
+        [wide(shift_ref[n, where, :], columns) for n in range(4)],
+        scratch,
+        lambda row, density: write_row(next_ref, 0, size, row, rows, columns, density),
+    )
+
+
+def density_steps(tiles, drift, shifts, band, below, above, dep, so_far, turn, turns):
+    scenarios = shifts.shape[1]
     rows, columns = drift.shape[1:]
     per = tiles.shape[0] // scenarios
-    size = GROUP * 2 if scenarios % (turns * GROUP * 2) == 0 else GROUP
+    size = 3 * GROUP if scenarios % (turns * GROUP * 3) == 0 else GROUP
     steps = scenarios // size // turns
     first = turn * steps
     block = pl.BlockSpec((size * per, LANES), lambda i: (first + i, 0))
     hidden = pl.BlockSpec(memory_space=pl.ANY)
-    args = [tiles, drift, shocks, table, below, above, dep]
+    args = [tiles, drift, shifts, band, below, above, dep]
     in_specs = [
         block,
         pl.BlockSpec(drift.shape, lambda i: (0, 0, 0)),
-        pl.BlockSpec((size, shocks.shape[1]), lambda i: (first + i, 0)),
-        smem(),
+        pl.BlockSpec(shifts.shape, lambda i: (0, 0, 0)),
+        pl.BlockSpec(band.shape, lambda i: (0, 0)),
         pl.BlockSpec(below.shape, lambda i: (0, 0)),
         pl.BlockSpec(above.shape, lambda i: (0, 0)),
         hidden,
@@ -369,6 +343,7 @@
         out_specs=block,
         out_shape=jax.ShapeDtypeStruct(tiles.shape, f32),
         input_output_aliases=aliases,
+        scratch_shapes=step_scratch(rows + 2, size, columns),
         compiler_params=params(),
         cost_estimate=pl.CostEstimate(flops=1, bytes_accessed=1, transcendentals=0),
         name="density_steps",
@@ -540,7 +515,7 @@
     mid_refs = refs[2 + pieces : 6 + pieces]
     weight_refs = refs[6 + pieces : 10 + pieces]
     outs = refs[-(3 + parts) :]
-    back_ref, own_ref, value_ref, head_ref = outs[:4]
+    own_ref, value_ref, mid_keep_ref, mid_send_ref = outs[:4]
     send_refs = outs[4:]
     part = place_ref[2]
     block = cot_ref.shape[0]
@@ -566,9 +541,9 @@
         value = jnp.concatenate([value, jnp.zeros((1, width - block), f32)], axis=1)
     value_ref[...] = value
     cot = cot_ref[...]
-    head_ref[...] = jnp.sum(cot * second, axis=0, keepdims=True)
+    head_part = jnp.sum(cot * second, axis=0, keepdims=True)
     back = (cot * head * (1.0 - second * second)).astype(bf16)
-    back_ref[...] = back
+    units = mid_refs[0].shape[1]
     for k in range(parts):
         for c in range(chunks):
             piece = lax.dot_general(
@@ -580,64 +555,38 @@
                 send_refs[k - 1][pl.ds(c * block, block), :] = piece.astype(bf16)
         if k > 0:
             send_refs[k - 1][pl.ds(chunks * block, EXTRA), :] = tail_rows(value)
+    for c in range(chunks):
+        for k in range(parts):
+            product = lax.dot_general(
+                first_refs[c * parts + k][...], back, (((0,), (0,)), ((), ())), preferred_element_type=f32
+            ).astype(bf16)
+            for p in range(4):
+                out = (mid_keep_ref, mid_send_ref)[p % 2]
+                out[p // 2, pl.ds(start_of(c, k), width), :] = product[:, p * units : (p + 1) * units]
+    for p in range(4):
+        out = (mid_keep_ref, mid_send_ref)[p % 2]
+        out[p // 2, pl.ds(pieces * width, EXTRA), :] = tail_rows(head_part[:, p * units : (p + 1) * units])
 
 
 def middle(place, cot, firsts, mids, heads, chunks, parts, width, deps=()):
     block = cot.shape[0]
-    units = 4 * mids[0].shape[1]
+    hidden, units = mids[0].shape
+    partial = jax.ShapeDtypeStruct((2, hidden + EXTRA, units), bf16)
     vmem = pl.BlockSpec(memory_space=pltpu.VMEM)
     return pl.pallas_call(
         functools.partial(middle_kernel, chunks, parts, width),
         in_specs=[smem()] + [vmem] * (1 + len(firsts) + 8) + any_specs(deps),
         out_shape=[
-            jax.ShapeDtypeStruct((block, units), bf16),
             jax.ShapeDtypeStruct((chunks * block, width), f32),
             jax.ShapeDtypeStruct((1, width), f32),
-            jax.ShapeDtypeStruct((1, units), f32),
+            partial,
+            partial,
         ]
         + [jax.ShapeDtypeStruct((chunks * block + EXTRA, width), bf16)] * (parts - 1),
         compiler_params=params(),
         cost_estimate=pl.CostEstimate(flops=1, bytes_accessed=1, transcendentals=0),
         name="value_layers",
     )(place, cot, *firsts, *mids, *heads, *deps)
-
-
-def mid_grad_kernel(chunks, parts, width, *refs):
-    pieces = chunks * parts
-    place_ref, back_ref, head_ref = refs[:3]
-    first_refs = refs[3 : 3 + pieces]
-    keep_ref, send_ref = refs[-2:]
-    part = place_ref[2]
-    units = back_ref.shape[1] // 4
-    for c in range(chunks):
-        for k in range(parts):
-            start = pl.multiple_of((c * parts + (part ^ k)) * width, width)
-            product = lax.dot_general(
-                first_refs[c * parts + k][...],
-                back_ref[...],
-                (((0,), (0,)), ((), ())),
-                preferred_element_type=f32,
-            ).astype(bf16)
-            for p in range(4):
-                out = (keep_ref, send_ref)[p % 2]
-                out[p // 2, pl.ds(start, width), :] = product[:, p * units : (p + 1) * units]
-    for p in range(4):
-        out = (keep_ref, send_ref)[p % 2]
-        out[p // 2, pl.ds(pieces * width, EXTRA), :] = tail_rows(head_ref[:, p * units : (p + 1) * units])
-
-
-def mid_grad(place, back, head, firsts, chunks, parts, width, deps=()):
-    units = back.shape[1] // 4
-    vmem = pl.BlockSpec(memory_space=pltpu.VMEM)
-    shape = jax.ShapeDtypeStruct((2, chunks * parts * width + EXTRA, units), bf16)
-    return pl.pallas_call(
-        functools.partial(mid_grad_kernel, chunks, parts, width),
-        in_specs=[smem()] + [vmem] * (2 + len(firsts)) + any_specs(deps),
-        out_shape=[shape, shape],
-        compiler_params=params(),
-        cost_estimate=pl.CostEstimate(flops=1, bytes_accessed=1, transcendentals=0),
-        name="mid_gradient",
-    )(place, back, head, *firsts, *deps)
 
 
 def add_tail(left, right, hidden):
@@ -740,78 +689,85 @@
     )(*pieces, *deps)
 
 
-def first_grad_kernel(parts, block, with_inner, with_value, with_output, *refs):
-    place_ref, low_ref, high_ref = refs[:3]
-    stacks = refs[3 + with_inner : 7 + with_inner]
-    out_ref = refs[7 + with_inner + with_output]
+def turn_kernel(count, *refs):
+    for ref, out in zip(refs[:count], refs[-count:]):
+        out[...] = ref[...].T
+
+
+def transposed(arrays, deps):
+    vmem = pl.BlockSpec(memory_space=pltpu.VMEM)
+    return pl.pallas_call(
+        functools.partial(turn_kernel, len(arrays)),
+        in_specs=[vmem] * len(arrays) + any_specs(deps),
+        out_shape=[jax.ShapeDtypeStruct(array.shape[::-1], array.dtype) for array in arrays],
+        compiler_params=params(),
+        cost_estimate=pl.CostEstimate(flops=1, bytes_accessed=1, transcendentals=0),
+        name="transposed_inputs",
+    )(*arrays, *deps)
+
+
+def first_grad_kernel(parts, block, count, tile, with_value, with_output, *refs):
+    place_ref = refs[0]
+    lefts = refs[1 : 1 + count]
+    stacks = refs[1 + count : 5 + count]
+    out_ref = refs[5 + count + with_output]
     whole = refs[-1]
     width = stacks[0].shape[1]
     step = pl.program_id(0)
-
-    @pl.when(step == 0)
-    def _():
-        part, mine = place_ref[2], place_ref[3]
-        for t, ref in enumerate(stacks):
-            at = mine ^ (2 * (t % 2) + t // 2)
-            for k in range(parts):
-                column = pl.multiple_of((part ^ k) * width, width)
-                whole[pl.ds(pl.multiple_of(at * block, block), block), pl.ds(column, width)] = ref[
-                    pl.ds(k * block, block), :
-                ]
-            if with_value:
+    part, mine = place_ref[2], place_ref[3]
+
+    if with_value:
+
+        @pl.when(step == 0)
+        def _():
+            for t, ref in enumerate(stacks):
+                at = mine ^ (2 * (t % 2) + t // 2)
                 tail = ref[pl.ds(parts * block, EXTRA), :].astype(f32)
-                refs[8 + with_inner + with_output][pl.ds(at, 1), :] = tail[0:1] + tail[1:2]
-
-    def product(ref):
-        out_ref[...] = jnp.dot(ref[...].T, whole[...], preferred_element_type=f32).astype(bf16)
-
-    @pl.when(step == 0)
-    def _():
-        product(low_ref)
-
-    if with_inner:
-
-        @pl.when((step > 0) & (step < pl.num_programs(0) - 1))
-        def _():
-            product(refs[3])
-
-    @pl.when(step == pl.num_programs(0) - 1)
-    def _():
-        product(high_ref)
-
-
-def first_grad(place, low, inner, high, stacks, so_far, hidden, parts, block, chunk):
-    scenarios, size = low.shape
-    inner_steps = 0 if inner is None else inner.shape[1] // size
-    cells = (inner_steps + 2) * size
+                refs[6 + count + with_output][pl.ds(at, 1), :] = tail[0:1] + tail[1:2]
+
+    tiles = width // tile
+    piece = step // tiles ^ part
+    column = pl.ds(pl.multiple_of(step % tiles * tile, tile), tile)
+    for t, ref in enumerate(stacks):
+        at = mine ^ (2 * (t % 2) + t // 2)
+        whole[pl.ds(pl.multiple_of(at * block, block), block), :] = ref[
+            pl.ds(pl.multiple_of(piece * block, block), block), column
+        ]
+    start = 0
+    for ref in lefts:
+        cells = ref.shape[0]
+        out_ref[pl.ds(start, cells), :] = jnp.dot(ref[...], whole[...], preferred_element_type=f32).astype(bf16)
+        start += cells
+
+
+def first_grad(place, lefts, stacks, so_far, hidden, parts, block, chunk):
+    scenarios = lefts[0].shape[1]
+    cells = sum(left.shape[0] for left in lefts)
     width = stacks[0].shape[1]
+    tile = min(width, 256)
+    steps = parts * width // tile
     with_value = chunk == 0
     with_output = so_far is not None
-    in_specs = [smem()] + [pl.BlockSpec(low.shape, lambda i: (0, 0))] * 2
-    args = [place, low, high]
-    if inner is not None:
-        in_specs.append(pl.BlockSpec((scenarios, size), lambda i: (0, jnp.clip(i - 1, 0, inner_steps - 1))))
-        args.append(inner)
-    in_specs += [pl.BlockSpec(ref.shape, lambda i: (0, 0)) for ref in stacks]
-    args += stacks
+    in_specs = [smem()] + [pl.BlockSpec(ref.shape, lambda i: (0, 0)) for ref in (*lefts, *stacks)]
+    args = [place, *lefts, *stacks]
     aliases = {}
     if with_output:
         aliases = {len(args): 0}
         in_specs.append(pl.BlockSpec(memory_space=pl.ANY))
         args.append(so_far)
-    out_specs = [pl.BlockSpec((size, parts * width), lambda i: (i, chunk))]
+    out_specs = [pl.BlockSpec((cells, tile), lambda i: (0, chunk * steps + i))]
     out_shape = [jax.ShapeDtypeStruct((cells, hidden), bf16)]
     if with_value:
         out_specs.append(pl.BlockSpec((4, width), lambda i: (0, 0)))
         out_shape.append(jax.ShapeDtypeStruct((4, width), f32))
     return pl.pallas_call(
-        functools.partial(first_grad_kernel, parts, block, inner is not None, with_value, with_output),
-        grid=(inner_steps + 2,),
+        functools.partial(first_grad_kernel, parts, block, len(lefts), tile, with_value, with_output),
+        grid=(steps,),
         in_specs=in_specs,
         out_specs=out_specs,
         out_shape=out_shape,
         input_output_aliases=aliases,
-        scratch_shapes=[pltpu.VMEM((scenarios, parts * width), bf16)],
+        scratch_shapes=[pltpu.VMEM((scenarios, tile), bf16)],
         compiler_params=params(),
         cost_estimate=pl.CostEstimate(flops=1, bytes_accessed=1, transcendentals=0),
         name="first_gradient",
@@ -837,7 +793,8 @@
     heads = [head_weight[None, :]]
     mids = [mid_weight]
 
-    *own_rows, inner = inner_steps(tiles, drift, shocks, shock_table)
+    band = band_matrix(columns)
+    *own_rows, shifts, inner = inner_steps(tiles, drift, shocks.T, shock_table.T, band)
     inner = inner if rows > 4 else None
     forward = [(i, i + 1) for i in range(count - 1)]
     backward = [(i + 1, i) for i in range(count - 1)]
@@ -847,10 +804,10 @@
     mids.append(swap(mids[0], count, 2))
     product = None if inner is None else inner_product(inner, first_weight, width, mids[1:])
     mids.append(swap(mids[2], count, 1))
-    low, high = edge_steps(drift, shocks, shock_table, own_rows, below, above, [] if product is None else [product])
+    low, high = edge_steps(drift, shifts, band, own_rows, below, above, [] if product is None else [product])
 
     def density_turn(turn, dep, so_far):
-        return density_steps(tiles, drift, shocks, shock_table, below, above, dep, so_far, turn, 4)
+        return density_steps(tiles, drift, shifts, band, below, above, dep, so_far, turn, 4)
 
     owned, firsts, density = [], [], None
     products = [edge_product(place, low, high, first_weight, product, parts, width, c) for c in range(chunks)]
@@ -870,22 +827,22 @@
         firsts += [swap(first, count, 4 * k) for k in range(1, parts)]
     heads += [swap(heads[0], count, k) for k in range(1, 4)]
     density = density_turn(2, owned[-1], density)
-    back_second, own, value, head_part, *sends = middle(
+    own, value, mid_keep, mid_send, *sends = middle(
         place, cot, firsts, mids, heads, chunks, parts, width, [density]
     )
     received = [swap(piece, count, 4 * (k + 1)) for k, piece in enumerate(sends)]
-    density = density_turn(3, received[0], density)
-    keep, send = mid_grad(place, back_second, head_part, firsts, chunks, parts, width, [density])
-    *backs, tail = back_first(own, value, received, owned, [density])
-    keep, send = mid_add(keep, swap(send, count, 1), [received[-1]])
-    grad_mid, grad_head = mid_final(keep, swap(send, count, 2))
+    *backs, tail = back_first(own, value, received, owned)
+    mid_keep, mid_send = mid_add(mid_keep, swap(mid_send, count, 1), [backs[-1]])
+    density = density_turn(3, backs[-1], density)
+    lefts = transposed([low, high] if inner is None else [low, inner, high], [density])
+    grad_mid, grad_head = mid_final(mid_keep, swap(mid_send, count, 2))
     grad_first = None
     for c in range(chunks):
         pieces = [backs[c]] + [swap(backs[c], count, 4 * k) for k in range(1, parts)]
-        mine_stack = stack(pieces + [tail] if c == 0 else pieces, [grad_mid])
+        mine_stack = stack(pieces + [tail] if c == 0 else pieces, [grad_mid, lefts[0]])
         stacks = [mine_stack, swap(mine_stack, count, 1), swap(mine_stack, count, 2)]
         stacks.append(swap(stacks[2], count, 1))
-        results = first_grad(place, low, inner, high, stacks, grad_first, hidden, parts, block, c)
+        results = first_grad(place, lefts, stacks, grad_first, hidden, parts, block, c)
         grad_first = results[0]
         if c == 0:
             value = results[1][:, :block].reshape(scenarios)

time: 166 us -> 158 us (0.952)
  local copies, waits for them, and re-layouts: 7.08 us -> 12.8 us
  waiting for transfers between devices: 29.6 us -> 24.3 us
  Pallas kernels: 90.6 us -> 85.3 us
  starting transfers between devices: 36.9 us -> 33.5 us
    ppermute x25, waiting for transfers between devices: 29.6 us -> 24.3 us  [swap(): return lax.ppermute(values, 'grid', [(i, i ^ flip) for i in range(count)])]
    unnamed x40 -> x50, local copies, waits for them, and re-layouts: 5.63 us -> 10.2 us
    ppermute x25, starting transfers between devices: 33.6 us -> 29.9 us  [swap(): return lax.ppermute(values, 'grid', [(i, i ^ flip) for i in range(count)])]
    pallas_call x1, Pallas kernels: 8.86 us -> 5.36 us  [edge_steps(): pl.pallas_call(functools.partial(edge_kernel, size), grid=(scenarios // s...]
    pallas_call x4, Pallas kernels: 29.2 us -> 26.6 us  [density_steps(): pl.pallas_call(functools.partial(density_kernel, rows, size, first), grid...]
  transfers between devices with their start and end apart: 27 -> 27, of which waited for: 10 -> 6; matrix products, arithmetic and copies ran while one was open for 1% -> 1% of each run, Pallas kernels for 30% -> 36%
where the time goes in v3:
time: 158 us; the launch traced here: 157 us
  Pallas kernels  85.3 us (54%)
  starting transfers between devices  33.5 us (21%)
  waiting for transfers between devices  24.3 us (15%)
  local copies, waits for them, and re-layouts  12.8 us (8%)
    ppermute x25, starting transfers between devices, swap(): return lax.ppermute(values, 'grid', [(i, i ^ flip) for i in range(count)])  29.9 us
    pallas_call x4, Pallas kernels, density_steps(): pl.pallas_call(functools.partial(density_kernel, rows, size, first), grid...  26.6 us
    ppermute x25, waiting for transfers between devices, swap(): return lax.ppermute(values, 'grid', [(i, i ^ flip) for i in range(count)])  24.3 us
    pallas_call x1, Pallas kernels, inner_steps(): pl.pallas_call(functools.partial(inner_kernel, rows, size), grid=(scenari...  16.4 us
    pallas_call x1, Pallas kernels, first_grad(): pl.pallas_call(functools.partial(first_grad_kernel, parts, block, len(lef...  12.5 us
    unnamed x50, local copies, waits for them, and re-layouts  10.2 us
    pallas_call x1, Pallas kernels, inner_product(): pl.pallas_call(functools.partial(inner_product_kernel, count, len(deps)),...  9.33 us
    pallas_call x1, Pallas kernels, edge_product(): pl.pallas_call(functools.partial(edge_product_kernel, block, inner is not...  5.39 us
  transfers between devices with their start and end apart: 27, of which 6 were waited for; matrix products, arithmetic and copies ran while one was open for 1% of the time, Pallas kernels for 36%

profile of v3, /device:TPU:0, one launch (start us, length us, event | category | flops | bytes accessed | tf_op | source)
XLA Modules:
  0.0 157.0 jit_solution(7337848455560235510)
XLA Ops:
  1.2 2.6 %collective-permute-start.3 = (bf16[2048,128]{1,0:T(8,128)(2,1)}, bf16[2048,128]{1,0:T(8,128)(2,1)S(1)}, u32[]{:S(2)}, u32[]{:S(2)}) collective-permute-start(bf16[2048,128]{1,0:T(8,128)(2,1)} %refs_6_.3), channel_id=1, source_target_pairs={{0,2},{1,3},{2,0},{3,1},{4,6},{5,7},{6,4},{7,5},{8,10},{9,11},{10,... | collective-permute-start | bytes 1572872 | tf_op jit(solution)/shard_map/ppermute | solution.py:358
  6.8 16.4 %inner_density_steps.1 = (bf16[400,512]{1,0:T(8,128)(2,1)S(1)}, bf16[384,512]{1,0:T(8,128)(2,1)S(1)}, bf16[384,512]{1,0:T(8,128)(2,1)S(1)}, bf16[400,512]{1,0:T(...) custom-call(f32[12288,128]{1,0:T(8,128)} %bitcast.27, f32[2,16,256]{2,1,0:T(8,128)S(1)} %copy-done.9, ...), custom_call_target="tpu_custom_call" | custom-call | flops 1 | bytes 1 | tf_op jit(solution)/shard_map/inner_density_steps/pallas_call | solution.py:191
  26.2 2.1 %collective-permute-start = (bf16[400,512]{1,0:T(8,128)(2,1)}, bf16[400,512]{1,0:T(8,128)(2,1)S(1)}, u32[]{:S(2)}, u32[]{:S(2)}) collective-permute-start(bf16[400,512]{1,0:T(8,128)(2,1)} %get-tuple-element.40.last_ref), channel_id=1, source_target_pairs={{0,1},{1,2},{2,3},{3,4},{4,5},{5,6},{6,7},{7,8},{8,9},{9,10},{10,1... | collective-permute-start | bytes 1228808 | tf_op jit(solution)/shard_map/ppermute | solution.py:801
  31.5 9.3 %inner_product.1.refs_0_ = f32[4,384,512]{2,1,0:T(8,128)} custom-call(bf16[384,3072]{1,0:T(8,128)(2,1)S(1)} %copy-done.4, bf16[4096,2048]{1,0:T(8,128)(2,1)} %bottom_ref.1, bf16[4096,2048]{1,0:T(8,128)(2,1)} %bottom_ref.1, bf16[4096,2048]{1,0:T(8,128)(2,1)} %bottom_ref.1, bf16[4096,2048]{1,0:T(8,128)(2,1)} %bottom_ref.1, bf16[4096,2048]{1,0:T(8,128)(2,1)} %bottom_ref.1, ...), custom_call_target="tpu_custom_call" | custom-call | flops 1 | bytes 1 | tf_op jit(solution)/shard_map/inner_product/pallas_call | solution.py:378
  40.9 5.4 %edge_density_steps.1 = (bf16[384,512]{1,0:T(8,128)(2,1)S(1)}, bf16[384,512]{1,0:T(8,128)(2,1)S(1)}) custom-call(f32[2,16,256]{2,1,0:T(8,128)S(1)} %copy-done.10, f32[4,384,128]{2,1,0:T(8,128)S(1)} %get-tuple-element.39.shift_ref, bf16[512,256]{1,0:T(8,128)(2,1)S(1)} %copy-done.2, bf16[400,512]{1,0:T(8,128)(2,1)S(1)} %get-tuple-element.41.first_ref, ...), custom_call_target="tpu_custom_call" | custom-call | flops 1 | bytes 1 | tf_op jit(solution)/shard_map/edge_density_steps/pallas_call | solution.py:269
  46.3 5.4 %edge_product.1 = (f32[2,4,96,512]{3,2,1,0:T(8,128)S(1)}, bf16[2,4,96,512]{3,2,1,0:T(8,128)(2,1)S(1)}) custom-call(s32[4]{0:T(128)S(1)} %pad_add_fusion.place_ref.refs_0_, bf16[384,512]{1,0:T(8,128)(2,1)S(1)} %get-tuple-element.45.low_ref.refs_0_, bf16[384,512]{1,0:T(8,128)(2,1)S(1)} %get-tuple-element.46.high_ref.refs_2_, bf16[4096,2048]{1,0:T(8,128)(2,1)} %bottom_ref.1, ...), custom_call_target="tpu_custom_call" | custom-call | flops 1 | bytes 1 | tf_op jit(solution)/shard_map/edge_product/pallas_call | solution.py:422
  53.0 2.6 %collective-permute-done.5.refs_0_.refs_9_ = bf16[2048,128]{1,0:T(8,128)(2,1)S(1)} collective-permute-done((bf16[2048,128]{1,0:T(8,128)(2,1)S(1)}, bf16[2048,128]{1,0:T(8,128)(2,1)S(1)}, u32[]{:S(2)}, u32[]{:S(2)}) %collective-permute-start.5) | collective-permute-done | bytes 524320 | tf_op jit(solution)/shard_map/ppermute | solution.py:358
  56.3 2.5 %collective-permute-start.6 = (bf16[4,96,512]{2,1,0:T(8,128)(2,1)S(1)}, bf16[4,96,512]{2,1,0:T(8,128)(2,1)S(1)}, u32[]{:S(2)}, u32[]{:S(2)}) collective-permute-start(bf16[4,96,512]{2,1,0:T(8,128)(2,1)S(1)} %get-tuple-element.50.dep_ref), channel_id=1, source_target_pairs={{0,2},{1,3},{2,0},{3,1},{4,6},{5,7},{6,4},{7,5},{8,10},{9,11},{10,... | collective-permute-start | bytes 1179656 | tf_op jit(solution)/shard_map/ppermute | solution.py:358
  58.8 6.6 %density_steps.4.refs_0_ = f32[12288,128]{1,0:T(8,128)} custom-call(f32[12288,128]{1,0:T(8,128)} %bitcast.28, f32[2,16,256]{2,1,0:T(8,128)S(1)} %copy-done.10, f32[4,384,128]{2,1,0:T(8,128)S(1)} %get-tuple-element.39.shift_ref, bf16[512,256]{1,0:T(8,128)(2,1)S(1)} %copy-done.2, bf16[400,512]{1,0:T(8,128)(2,1)S(1)} %collective-permute-done.below_ref, ...), custom_call_target="tpu_custom_call" | custom-call | flops 1 | bytes 1 | tf_op jit(solution)/shard_map/density_steps/pallas_call | solution.py:339
  65.5 3.0 %collective-permute-done.6.other_ref = bf16[4,96,512]{2,1,0:T(8,128)(2,1)S(1)} collective-permute-done((bf16[4,96,512]{2,1,0:T(8,128)(2,1)S(1)}, bf16[4,96,512]{2,1,0:T(8,128)(2,1)S(1)}, u32[]{:S(2)}, u32[]{:S(2)}) %collective-permute-start.6) | collective-permute-done | bytes 393248 | tf_op jit(solution)/shard_map/ppermute | solution.py:358
  70.5 2.9 %collective-permute-start.7 = (bf16[96,512]{1,0:T(8,128)(2,1)}, bf16[96,512]{1,0:T(8,128)(2,1)}, u32[]{:S(2)}, u32[]{:S(2)}) collective-permute-start(bf16[96,512]{1,0:T(8,128)(2,1)} %get-tuple-element.52), channel_id=1, source_target_pairs={{0,4},{1,5},{2,6},{3,7},{4,0},{5,1},{6,2},{7,3},{8,12},{9,13},{10,... | collective-permute-start | bytes 294920 | tf_op jit(solution)/shard_map/ppermute | solution.py:358
  73.4 2.6 %collective-permute-start.8 = (bf16[96,512]{1,0:T(8,128)(2,1)}, bf16[96,512]{1,0:T(8,128)(2,1)}, u32[]{:S(2)}, u32[]{:S(2)}) collective-permute-start(bf16[96,512]{1,0:T(8,128)(2,1)} %get-tuple-element.53), channel_id=1, source_target_pairs={{0,8},{1,9},{2,10},{3,11},{4,12},{5,13},{6,14},{7,15},{8,0},{9,1},... | collective-permute-start | bytes 294920 | tf_op jit(solution)/shard_map/ppermute | solution.py:358
  76.6 6.7 %density_steps.5.refs_4_.refs_0_ = f32[12288,128]{1,0:T(8,128)} custom-call(f32[12288,128]{1,0:T(8,128)} %bitcast.29, f32[2,16,256]{2,1,0:T(8,128)S(1)} %copy-done.10, f32[4,384,128]{2,1,0:T(8,128)S(1)} %get-tuple-element.39.shift_ref, bf16[512,256]{1,0:T(8,128)(2,1)S(1)} %copy-done.2, ...), custom_call_target="tpu_custom_call", output_to_operand_aliasing={{}: (7, {})} | custom-call | flops 1 | bytes 1 | tf_op jit(solution)/shard_map/density_steps/pallas_call | solution.py:339
  85.6 3.9 %collective-permute-start.12 = (bf16[96,512]{1,0:T(8,128)(2,1)S(1)}, bf16[96,512]{1,0:T(8,128)(2,1)}, u32[]{:S(2)}, u32[]{:S(2)}) collective-permute-start(bf16[96,512]{1,0:T(8,128)(2,1)S(1)} %first_activation.1.dep_ref.refs_2_.refs_5_), channel_id=1, source_target_pairs={{0,12},{1,13},{2,14},{3,15},{4,8},{5,9},{6,10},{7,11},{8,4},{9,5},... | collective-permute-start | bytes 294920 | tf_op jit(solution)/shard_map/ppermute | solution.py:358
  92.9 6.7 %density_steps.6.refs_14_.refs_0_ = f32[12288,128]{1,0:T(8,128)} custom-call(f32[12288,128]{1,0:T(8,128)} %bitcast.30, f32[2,16,256]{2,1,0:T(8,128)S(1)} %copy-done.11, f32[4,384,128]{2,1,0:T(8,128)S(1)} %get-tuple-element.39.shift_ref, bf16[512,256]{1,0:T(8,128)(2,1)S(1)} %copy-done.2, ...), custom_call_target="tpu_custom_call", output_to_operand_aliasing={{}: (7, {})} | custom-call | flops 1 | bytes 1 | tf_op jit(solution)/shard_map/density_steps/pallas_call | solution.py:339
  99.6 2.9 %value_layers.1 = (f32[96,512]{1,0:T(8,128)S(1)}, f32[1,512]{1,0:T(1,128)S(1)}, bf16[2,2064,128]{2,1,0:T(8,128)(2,1)S(1)}, bf16[2,2064,128]{2,1,0:T(8,128)(2,1)S...) custom-call(s32[4]{0:T(128)S(1)} %pad_add_fusion.place_ref.refs_0_, ...), custom_call_target="tpu_custom_call" | custom-call | flops 1 | bytes 1 | tf_op jit(solution)/shard_map/value_layers/pallas_call | solution.py:576
  104.0 2.9 %collective-permute-start.17 = (bf16[112,512]{1,0:T(8,128)(2,1)S(1)}, bf16[112,512]{1,0:T(8,128)(2,1)S(1)}, u32[]{:S(2)}, u32[]{:S(2)}) collective-permute-start(bf16[112,512]{1,0:T(8,128)(2,1)S(1)} %get-tuple-element.58), channel_id=1, source_target_pairs={{0,8},{1,9},{2,10},{3,11},{4,12},{5,13},{6,14},{7,15},{8,0},{9,1},... | collective-permute-start | bytes 344072 | tf_op jit(solution)/shard_map/ppermute | solution.py:358
  107.0 3.1 %collective-permute-done.16.refs_2_ = bf16[112,512]{1,0:T(8,128)(2,1)S(1)} collective-permute-done((bf16[112,512]{1,0:T(8,128)(2,1)S(1)}, bf16[112,512]{1,0:T(8,128)(2,1)S(1)}, u32[]{:S(2)}, u32[]{:S(2)}) %collective-permute-start.16) | collective-permute-done | bytes 114720 | tf_op jit(solution)/shard_map/ppermute | solution.py:358
  110.1 5.7 %collective-permute-done.17.refs_3_ = bf16[112,512]{1,0:T(8,128)(2,1)S(1)} collective-permute-done((bf16[112,512]{1,0:T(8,128)(2,1)S(1)}, bf16[112,512]{1,0:T(8,128)(2,1)S(1)}, u32[]{:S(2)}, u32[]{:S(2)}) %collective-permute-start.17) | collective-permute-done | bytes 114720 | tf_op jit(solution)/shard_map/ppermute | solution.py:358
  116.6 2.5 %collective-permute-start.21 = (bf16[96,512]{1,0:T(8,128)(2,1)S(1)}, bf16[96,512]{1,0:T(8,128)(2,1)S(1)}, u32[]{:S(2)}, u32[]{:S(2)}) collective-permute-start(bf16[96,512]{1,0:T(8,128)(2,1)S(1)} %get-tuple-element.60.dep_ref.refs_0_), channel_id=1, source_target_pairs={{0,12},{1,13},{2,14},{3,15},{4,8},{5,9},{6,10},{7,11},{8,4},{9,5},... | collective-permute-start | bytes 294920 | tf_op jit(solution)/shard_map/ppermute | solution.py:358
  121.0 6.7 %density_steps.7.refs_3_ = f32[12288,128]{1,0:T(8,128)} custom-call(f32[12288,128]{1,0:T(8,128)} %bitcast.31, f32[2,16,256]{2,1,0:T(8,128)S(1)} %copy-done.12, f32[4,384,128]{2,1,0:T(8,128)S(1)} %get-tuple-element.39.shift_ref, bf16[512,256]{1,0:T(8,128)(2,1)S(1)} %copy-done.2, ...), custom_call_target="tpu_custom_call", output_to_operand_aliasing={{}: (7, {})} | custom-call | flops 1 | bytes 1 | tf_op jit(solution)/shard_map/density_steps/pallas_call | solution.py:339
  127.7 2.5 %transposed_inputs.1 = (bf16[512,384]{1,0:T(8,128)(2,1)S(1)}, bf16[3072,384]{1,0:T(8,128)(2,1)S(1)}, bf16[512,384]{1,0:T(8,128)(2,1)S(1)}) custom-call(bf16[384,512]{1,0:T(8,128)(2,1)S(1)} %copy-done.6, bf16[384,3072]{1,0:T(8,128)(2,1)} %copy-done.3, bf16[384,512]{1,0:T(8,128)(2,1)S(1)} %copy-done.8, f32[12288,128]{1,0:T(8,128)} %density_steps.7.refs_3_), custom_call_target="tpu_custom_call" | custom-call | flops 1 | bytes 1 | tf_op jit(solution)/shard_map/transposed_inputs/pallas_call | solution.py:699
  134.0 8.1 %collective-permute-done.25.refs_6_ = bf16[400,512]{1,0:T(8,128)(2,1)S(1)} collective-permute-done((bf16[400,512]{1,0:T(8,128)(2,1)S(1)}, bf16[400,512]{1,0:T(8,128)(2,1)S(1)}, u32[]{:S(2)}, u32[]{:S(2)}) %collective-permute-start.25) | collective-permute-done | bytes 409632 | tf_op jit(solution)/shard_map/ppermute | solution.py:358
  143.9 12.5 %first_gradient.1 = (bf16[4096,2048]{1,0:T(8,128)(2,1)}, f32[4,512]{1,0:T(4,128)S(1)}) custom-call(s32[4]{0:T(128)S(1)} %pad_add_fusion.place_ref.refs_0_, bf16[512,384]{1,0:T(8,128)(2,1)S(1)} %get-tuple-element.61.refs_6_.refs_1_, bf16[3072,384]{1,0:T(8,128)(2,1)S(1)} %get-tuple-element.62.refs_2_, bf16[512,384]{1,0:T(8,128)(2,1)S(1)} %get-tuple-element.63.refs_3_, ...), custom_call_target="tpu_custom_call" | custom-call | flops 1 | bytes 1 | tf_op jit(solution)/shard_map/first_gradient/pallas_call | solution.py:763
  (103 shorter events, 30.5 us)
Async XLA Ops:
  0.6 29.2 %collective-permute-start.2 = (bf16[2048,128]{1,0:T(8,128)(2,1)}, bf16[2048,128]{1,0:T(8,128)(2,1)S(1)}, u32[]{:S(2)}, u32[]{:S(2)}) collective-permute-start(bf16[2048,128]{1,0:T(8,128)(2,1)} %refs_6_.3), channel_id=1, source_target_pairs={{0,1},{1,0},{2,3},{3,2},{4,5},{5,4},{6,7},{7,6},{8,9},{9,8},{10,11... | collective-permute-start | bytes 1572872 | tf_op jit(solution)/shard_map/ppermute | solution.py:358
  1.2 28.7 %collective-permute-start.3 = (bf16[2048,128]{1,0:T(8,128)(2,1)}, bf16[2048,128]{1,0:T(8,128)(2,1)S(1)}, u32[]{:S(2)}, u32[]{:S(2)}) collective-permute-start(bf16[2048,128]{1,0:T(8,128)(2,1)} %refs_6_.3), channel_id=1, source_target_pairs={{0,2},{1,3},{2,0},{3,1},{4,6},{5,7},{6,4},{7,5},{8,10},{9,11},{10,... | collective-permute-start | bytes 1572872 | tf_op jit(solution)/shard_map/ppermute | solution.py:358
  26.2 14.7 %collective-permute-start = (bf16[400,512]{1,0:T(8,128)(2,1)}, bf16[400,512]{1,0:T(8,128)(2,1)S(1)}, u32[]{:S(2)}, u32[]{:S(2)}) collective-permute-start(bf16[400,512]{1,0:T(8,128)(2,1)} %get-tuple-element.40.last_ref), channel_id=1, source_target_pairs={{0,1},{1,2},{2,3},{3,4},{4,5},{5,6},{6,7},{7,8},{8,9},{9,10},{10,1... | collective-permute-start | bytes 1228808 | tf_op jit(solution)/shard_map/ppermute | solution.py:801
  28.3 12.6 %collective-permute-start.1 = (bf16[400,512]{1,0:T(8,128)(2,1)S(1)}, bf16[400,512]{1,0:T(8,128)(2,1)S(1)}, u32[]{:S(2)}, u32[]{:S(2)}) collective-permute-start(bf16[400,512]{1,0:T(8,128)(2,1)S(1)} %get-tuple-element.41.first_ref), channel_id=1, source_target_pairs={{1,0},{2,1},{3,2},{4,3},{5,4},{6,5},{7,6},{8,7},{9,8},{10,9},{11,1... | collective-permute-start | bytes 1228808 | tf_op jit(solution)/shard_map/ppermute | solution.py:802
  56.3 12.2 %collective-permute-start.6 = (bf16[4,96,512]{2,1,0:T(8,128)(2,1)S(1)}, bf16[4,96,512]{2,1,0:T(8,128)(2,1)S(1)}, u32[]{:S(2)}, u32[]{:S(2)}) collective-permute-start(bf16[4,96,512]{2,1,0:T(8,128)(2,1)S(1)} %get-tuple-element.50.dep_ref), channel_id=1, source_target_pairs={{0,2},{1,3},{2,0},{3,1},{4,6},{5,7},{6,4},{7,5},{8,10},{9,11},{10,... | collective-permute-start | bytes 1179656 | tf_op jit(solution)/shard_map/ppermute | solution.py:358
  70.5 12.8 %collective-permute-start.7 = (bf16[96,512]{1,0:T(8,128)(2,1)}, bf16[96,512]{1,0:T(8,128)(2,1)}, u32[]{:S(2)}, u32[]{:S(2)}) collective-permute-start(bf16[96,512]{1,0:T(8,128)(2,1)} %get-tuple-element.52), channel_id=1, source_target_pairs={{0,4},{1,5},{2,6},{3,7},{4,0},{5,1},{6,2},{7,3},{8,12},{9,13},{10,... | collective-permute-start | bytes 294920 | tf_op jit(solution)/shard_map/ppermute | solution.py:358
  73.4 11.1 %collective-permute-start.8 = (bf16[96,512]{1,0:T(8,128)(2,1)}, bf16[96,512]{1,0:T(8,128)(2,1)}, u32[]{:S(2)}, u32[]{:S(2)}) collective-permute-start(bf16[96,512]{1,0:T(8,128)(2,1)} %get-tuple-element.53), channel_id=1, source_target_pairs={{0,8},{1,9},{2,10},{3,11},{4,12},{5,13},{6,14},{7,15},{8,0},{9,1},... | collective-permute-start | bytes 294920 | tf_op jit(solution)/shard_map/ppermute | solution.py:358
  76.0 8.6 %collective-permute-start.9 = (bf16[96,512]{1,0:T(8,128)(2,1)}, bf16[96,512]{1,0:T(8,128)(2,1)}, u32[]{:S(2)}, u32[]{:S(2)}) collective-permute-start(bf16[96,512]{1,0:T(8,128)(2,1)} %get-tuple-element.54.dep_ref), channel_id=1, source_target_pairs={{0,12},{1,13},{2,14},{3,15},{4,8},{5,9},{6,10},{7,11},{8,4},{9,5},... | collective-permute-start | bytes 294920 | tf_op jit(solution)/shard_map/ppermute | solution.py:358
  76.0 13.5 %collective-permute-start.15 = (f32[1,128]{1,0:T(1,128)S(1)}, f32[1,128]{1,0:T(1,128)S(1)}, u32[]{:S(2)}, u32[]{:S(2)}) collective-permute-start(f32[1,128]{1,0:T(1,128)S(1)} %bitcast.22), channel_id=1, source_target_pairs={{0,3},{1,2},{2,1},{3,0},{4,7},{5,6},{6,5},{7,4},{8,11},{9,10},{10,... | collective-permute-start | bytes 1544 | tf_op jit(solution)/shard_map/ppermute | solution.py:358
  76.0 23.5 %collective-permute-start.14 = (f32[1,128]{1,0:T(1,128)S(1)}, f32[1,128]{1,0:T(1,128)}, u32[]{:S(2)}, u32[]{:S(2)}) collective-permute-start(f32[1,128]{1,0:T(1,128)S(1)} %bitcast.23), channel_id=1, source_target_pairs={{0,2},{1,3},{2,0},{3,1},{4,6},{5,7},{6,4},{7,5},{8,10},{9,11},{10,... | collective-permute-start | bytes 1544 | tf_op jit(solution)/shard_map/ppermute | solution.py:358
  83.3 16.2 %collective-permute-start.13 = (f32[1,128]{1,0:T(1,128)S(1)}, f32[1,128]{1,0:T(1,128)}, u32[]{:S(2)}, u32[]{:S(2)}) collective-permute-start(f32[1,128]{1,0:T(1,128)S(1)} %bitcast.24), channel_id=1, source_target_pairs={{0,1},{1,0},{2,3},{3,2},{4,5},{5,4},{6,7},{7,6},{8,9},{9,8},{10,11... | collective-permute-start | bytes 1544 | tf_op jit(solution)/shard_map/ppermute | solution.py:358
  85.6 13.9 %collective-permute-start.12 = (bf16[96,512]{1,0:T(8,128)(2,1)S(1)}, bf16[96,512]{1,0:T(8,128)(2,1)}, u32[]{:S(2)}, u32[]{:S(2)}) collective-permute-start(bf16[96,512]{1,0:T(8,128)(2,1)S(1)} %first_activation.1.dep_ref.refs_2_.refs_5_), channel_id=1, source_target_pairs={{0,12},{1,13},{2,14},{3,15},{4,8},{5,9},{6,10},{7,11},{8,4},{9,5},... | collective-permute-start | bytes 294920 | tf_op jit(solution)/shard_map/ppermute | solution.py:358
  89.5 10.1 %collective-permute-start.11 = (bf16[96,512]{1,0:T(8,128)(2,1)S(1)}, bf16[96,512]{1,0:T(8,128)(2,1)}, u32[]{:S(2)}, u32[]{:S(2)}) collective-permute-start(bf16[96,512]{1,0:T(8,128)(2,1)S(1)} %first_activation.1.dep_ref.refs_2_.refs_5_), channel_id=1, source_target_pairs={{0,8},{1,9},{2,10},{3,11},{4,12},{5,13},{6,14},{7,15},{8,0},{9,1},... | collective-permute-start | bytes 294920 | tf_op jit(solution)/shard_map/ppermute | solution.py:358
  89.5 10.1 %collective-permute-start.10 = (bf16[96,512]{1,0:T(8,128)(2,1)S(1)}, bf16[96,512]{1,0:T(8,128)(2,1)}, u32[]{:S(2)}, u32[]{:S(2)}) collective-permute-start(bf16[96,512]{1,0:T(8,128)(2,1)S(1)} %first_activation.1.dep_ref.refs_2_.refs_5_), channel_id=1, source_target_pairs={{0,4},{1,5},{2,6},{3,7},{4,0},{5,1},{6,2},{7,3},{8,12},{9,13},{10,... | collective-permute-start | bytes 294920 | tf_op jit(solution)/shard_map/ppermute | solution.py:358
  102.5 13.5 %collective-permute-start.22 = (bf16[2,2064,128]{2,1,0:T(8,128)(2,1)S(1)}, bf16[2,2064,128]{2,1,0:T(8,128)(2,1)S(1)}, u32[]{:S(2)}, u32[]{:S(2)}) collective-permute-start(bf16[2,2064,128]{2,1,0:T(8,128)(2,1)S(1)} %get-tuple-element.66), channel_id=1, source_target_pairs={{0,1},{1,0},{2,3},{3,2},{4,5},{5,4},{6,7},{7,6},{8,9},{9,8},{10,11... | collective-permute-start | bytes 3170312 | tf_op jit(solution)/shard_map/ppermute | solution.py:358
  102.5 7.5 %collective-permute-start.16 = (bf16[112,512]{1,0:T(8,128)(2,1)S(1)}, bf16[112,512]{1,0:T(8,128)(2,1)S(1)}, u32[]{:S(2)}, u32[]{:S(2)}) collective-permute-start(bf16[112,512]{1,0:T(8,128)(2,1)S(1)} %get-tuple-element.57), channel_id=1, source_target_pairs={{0,4},{1,5},{2,6},{3,7},{4,0},{5,1},{6,2},{7,3},{8,12},{9,13},{10,... | collective-permute-start | bytes 344072 | tf_op jit(solution)/shard_map/ppermute | solution.py:358
  104.0 11.8 %collective-permute-start.17 = (bf16[112,512]{1,0:T(8,128)(2,1)S(1)}, bf16[112,512]{1,0:T(8,128)(2,1)S(1)}, u32[]{:S(2)}, u32[]{:S(2)}) collective-permute-start(bf16[112,512]{1,0:T(8,128)(2,1)S(1)} %get-tuple-element.58), channel_id=1, source_target_pairs={{0,8},{1,9},{2,10},{3,11},{4,12},{5,13},{6,14},{7,15},{8,0},{9,1},... | collective-permute-start | bytes 344072 | tf_op jit(solution)/shard_map/ppermute | solution.py:358
  106.9 8.9 %collective-permute-start.18 = (bf16[112,512]{1,0:T(8,128)(2,1)S(1)}, bf16[112,512]{1,0:T(8,128)(2,1)S(1)}, u32[]{:S(2)}, u32[]{:S(2)}) collective-permute-start(bf16[112,512]{1,0:T(8,128)(2,1)S(1)} %get-tuple-element.59), channel_id=1, source_target_pairs={{0,12},{1,13},{2,14},{3,15},{4,8},{5,9},{6,10},{7,11},{8,4},{9,5},... | collective-permute-start | bytes 344072 | tf_op jit(solution)/shard_map/ppermute | solution.py:358
  116.2 14.0 %collective-permute-start.23 = (bf16[2064,128]{1,0:T(8,128)(2,1)S(1)}, bf16[2064,128]{1,0:T(8,128)(2,1)S(1)}, u32[]{:S(2)}, u32[]{:S(2)}) collective-permute-start(bf16[2064,128]{1,0:T(8,128)(2,1)S(1)} %get-tuple-element.68), channel_id=1, source_target_pairs={{0,2},{1,3},{2,0},{3,1},{4,6},{5,7},{6,4},{7,5},{8,10},{9,11},{10,... | collective-permute-start | bytes 1585160 | tf_op jit(solution)/shard_map/ppermute | solution.py:358
  116.6 14.5 %collective-permute-start.21 = (bf16[96,512]{1,0:T(8,128)(2,1)S(1)}, bf16[96,512]{1,0:T(8,128)(2,1)S(1)}, u32[]{:S(2)}, u32[]{:S(2)}) collective-permute-start(bf16[96,512]{1,0:T(8,128)(2,1)S(1)} %get-tuple-element.60.dep_ref.refs_0_), channel_id=1, source_target_pairs={{0,12},{1,13},{2,14},{3,15},{4,8},{5,9},{6,10},{7,11},{8,4},{9,5},... | collective-permute-start | bytes 294920 | tf_op jit(solution)/shard_map/ppermute | solution.py:358
  119.1 12.1 %collective-permute-start.20 = (bf16[96,512]{1,0:T(8,128)(2,1)S(1)}, bf16[96,512]{1,0:T(8,128)(2,1)S(1)}, u32[]{:S(2)}, u32[]{:S(2)}) collective-permute-start(bf16[96,512]{1,0:T(8,128)(2,1)S(1)} %get-tuple-element.60.dep_ref.refs_0_), channel_id=1, source_target_pairs={{0,8},{1,9},{2,10},{3,11},{4,12},{5,13},{6,14},{7,15},{8,0},{9,1},... | collective-permute-start | bytes 294920 | tf_op jit(solution)/shard_map/ppermute | solution.py:358
  120.6 10.5 %collective-permute-start.19 = (bf16[96,512]{1,0:T(8,128)(2,1)S(1)}, bf16[96,512]{1,0:T(8,128)(2,1)S(1)}, u32[]{:S(2)}, u32[]{:S(2)}) collective-permute-start(bf16[96,512]{1,0:T(8,128)(2,1)S(1)} %get-tuple-element.60.dep_ref.refs_0_), channel_id=1, source_target_pairs={{0,4},{1,5},{2,6},{3,7},{4,0},{5,1},{6,2},{7,3},{8,12},{9,13},{10,... | collective-permute-start | bytes 294920 | tf_op jit(solution)/shard_map/ppermute | solution.py:358
  132.2 9.9 %collective-permute-start.25 = (bf16[400,512]{1,0:T(8,128)(2,1)S(1)}, bf16[400,512]{1,0:T(8,128)(2,1)S(1)}, u32[]{:S(2)}, u32[]{:S(2)}) collective-permute-start(bf16[400,512]{1,0:T(8,128)(2,1)S(1)} %stack_parts.1.refs_4_), channel_id=1, source_target_pairs={{0,2},{1,3},{2,0},{3,1},{4,6},{5,7},{6,4},{7,5},{8,10},{9,11},{10,... | collective-permute-start | bytes 1228808 | tf_op jit(solution)/shard_map/ppermute | solution.py:358
  134.0 8.2 %collective-permute-start.24 = (bf16[400,512]{1,0:T(8,128)(2,1)S(1)}, bf16[400,512]{1,0:T(8,128)(2,1)S(1)}, u32[]{:S(2)}, u32[]{:S(2)}) collective-permute-start(bf16[400,512]{1,0:T(8,128)(2,1)S(1)} %stack_parts.1.refs_4_), channel_id=1, source_target_pairs={{0,1},{1,0},{2,3},{3,2},{4,5},{5,4},{6,7},{7,6},{8,9},{9,8},{10,11... | collective-permute-start | bytes 1228808 | tf_op jit(solution)/shard_map/ppermute | solution.py:358
  (28 other events, 232.6 us)

commit v4 on v3

--- a/solution.py
+++ b/solution.py
@@ -1,14 +1,13 @@
 import functools
 import jax
 import jax.numpy as jnp
-import numpy as np
 from jax import lax
 from jax.experimental import pallas as pl
 from jax.experimental.pallas import tpu as pltpu
 from jax.sharding import PartitionSpec as P
 
 diffusion_rate = 0.24
-VMEM_BYTES = 48 * 1024 * 1024
+VMEM_BYTES = 40 * 1024 * 1024
 EXTRA = 16
 bf16 = jnp.bfloat16
 f32 = jnp.float32
@@ -28,7 +27,7 @@
 LANES = 128
 SUBLANES = 8
 GROUP = 16
-CHUNKS = 1
+CHUNKS = 2
 
 
 def to_tiles(hist):
@@ -82,10 +81,12 @@
 
 
 def band_matrix(columns):
-    beside = np.eye(columns, k=1) + np.eye(columns, k=-1)
-    flux = np.eye(columns, k=1) - np.eye(columns, k=-1)
-    centre = (1.0 - 4.0 * diffusion_rate) * np.eye(columns) + diffusion_rate * beside
-    return jnp.asarray(np.concatenate([centre, flux], axis=0), dtype=bf16)
+    row = lax.broadcasted_iota(jnp.int32, (columns, columns), 0)
+    column = lax.broadcasted_iota(jnp.int32, (columns, columns), 1)
+    right = jnp.where(column == row + 1, 1.0, 0.0)
+    left = jnp.where(column == row - 1, 1.0, 0.0)
+    centre = jnp.where(column == row, 1.0 - 4.0 * diffusion_rate, diffusion_rate * (right + left))
+    return centre.astype(bf16), (right - left).astype(bf16)
 
 
 def half_shifts(levels_ref, table_ref, shift_ref):
@@ -95,7 +96,7 @@
         for c in range(2):
             shift = jnp.zeros(level.shape, f32)
             for n in range(table_ref.shape[1]):
-                shift = jnp.where(level == n, 0.5 * table_ref[c, n], shift)
+                shift = jnp.where(level == n, 0.5 * table_ref[c : c + 1, n : n + 1], shift)
             shift_ref[2 * t + c] = shift
 
 
@@ -103,73 +104,100 @@
     return jnp.concatenate([values] * (columns // LANES), axis=1)
 
 
-def one_step(segments, read, half_drift, band, shift_x, shift_y, pairs, terms, write):
+def one_step(rows_of, places, half_drift, band, shift_x, shift_y, pairs, terms, write):
     size, columns = shift_x.shape
-    places = [row for first, last in segments for row in range(first + 1, last)]
-    for k, row in enumerate(places):
-        density = read(row)
-        pairs[pl.ds(k * size, size), pl.ds(0, columns)] = density.astype(bf16)
-        flux = (half_drift(1, row) + shift_y) * density
-        pairs[pl.ds(k * size, size), pl.ds(columns, columns)] = flux.astype(bf16)
-    count = len(places) * size
-    terms[pl.ds(0, count), :] = jnp.dot(pairs[pl.ds(0, count), :], band, preferred_element_type=f32)
-    for k, row in enumerate(places):
-        low = read(row - 1) * ((diffusion_rate + half_drift(0, row - 1)) + shift_x)
-        high = read(row + 1) * ((diffusion_rate - half_drift(0, row + 1)) - shift_x)
-        write(row, terms[pl.ds(k * size, size), :] + low + high)
-
-
-def two_steps(segments, read, half_drift, edge, band, shifts, scratch, write):
-    pairs, terms, middle = scratch
+    whole = pl.ds(0, columns)
+
+    def density(row):
+        return pairs[pl.ds(rows_of[row] * size, size), whole].astype(f32)
+
+    for row in places:
+        flux = (half_drift(1, row) + shift_y) * density(row)
+        pairs[pl.ds(rows_of[row] * size, size), pl.ds(columns, columns)] = flux.astype(bf16)
+    runs = []
+    for row in places:
+        at = rows_of[row]
+        if runs and runs[-1][0] + runs[-1][1] == at:
+            runs[-1][1] += 1
+        else:
+            runs.append([at, 1])
+    for at, count in runs:
+        where = pl.ds(at * size, count * size)
+        terms[where, :] = jnp.dot(pairs[where, :], band, preferred_element_type=f32)
+    for row in places:
+        low = density(row - 1) * ((diffusion_rate + half_drift(0, row - 1)) + shift_x)
+        high = density(row + 1) * ((diffusion_rate - half_drift(0, row + 1)) - shift_x)
+        write(row, terms[pl.ds(rows_of[row] * size, size), :] + low + high)
+
+
+def two_steps(first, last, read, half_drift, edge, band, shifts, scratch, write):
+    pairs, later, terms = scratch
     size, columns = shifts[0].shape
-    before = [(first - 2, last + 2) for first, last in segments]
-    between = [(first - 1, last + 1) for first, last in segments]
-    places = [row for first, last in between for row in range(first, last + 1)]
-
-    def write_middle(row, density):
-        middle[pl.ds(places.index(row) * size, size), :] = edge(row, density).astype(bf16)
-
-    def read_middle(row):
-        return middle[pl.ds(places.index(row) * size, size), :].astype(f32)
-
-    one_step(before, read, half_drift, band, shifts[0], shifts[1], pairs, terms, write_middle)
-    one_step(between, read_middle, half_drift, band, shifts[2], shifts[3], pairs, terms, write)
+    rows_of = {row: k for k, row in enumerate(range(first - 2, last + 3))}
+    for row, k in rows_of.items():
+        pairs[pl.ds(k * size, size), pl.ds(0, columns)] = read(row).astype(bf16)
+
+    def write_later(row, density):
+        later[pl.ds(rows_of[row] * size, size), pl.ds(0, columns)] = edge(row, density).astype(bf16)
+
+    one_step(
+        rows_of, range(first - 1, last + 2), half_drift, band, shifts[0], shifts[1], pairs, terms, write_later
+    )
+    one_step(rows_of, range(first, last + 1), half_drift, band, shifts[2], shifts[3], later, terms, write)
 
 
 def step_scratch(rows, size, columns):
-    return [
-        pltpu.VMEM((rows * size, 2 * columns), bf16),
-        pltpu.VMEM((rows * size, columns), f32),
-        pltpu.VMEM((rows * size, columns), bf16),
-    ]
+    pairs = pltpu.VMEM(((rows + 4) * size, 2 * columns), bf16)
+    return [pairs, pairs, pltpu.VMEM(((rows + 4) * size, columns), f32)]
 
 
 def inner_kernel(
-    rows, size, hist_ref, drift_ref, levels_ref, table_ref, band_ref,
-    first_ref, next_ref, prev_ref, last_ref, shift_ref, inner_ref, *scratch,
+    rows, size, hist_ref, drift_hbm, levels_hbm, table_hbm,
+    first_ref, next_ref, prev_ref, last_ref, shift_ref, band_ref, inner_ref,
+    drift_ref, levels_ref, table_ref, arrived, *scratch,
 ):
     step = pl.program_id(0)
     columns = drift_ref.shape[2]
 
     @pl.when(step == 0)
     def _():
+        sources = ((drift_hbm, drift_ref), (levels_hbm, levels_ref), (table_hbm, table_ref))
+        copies = [pltpu.make_async_copy(*pair, arrived.at[n]) for n, pair in enumerate(sources)]
+        for copy in copies:
+            copy.start()
+        centre, flux = band_matrix(columns)
+        band_ref[pl.ds(0, columns), :] = centre
+        band_ref[pl.ds(columns, columns), :] = flux
+        for copy in copies:
+            copy.wait()
         half_shifts(levels_ref, table_ref, shift_ref)
         for out, start in ((first_ref, 0), (last_ref, rows - 2)):
             out[pl.ds(out.shape[0] - EXTRA, EXTRA), :] = drift_tail(drift_ref, start)
 
     where = pl.ds(pl.multiple_of(step * size, size), size)
+    edges = {}
     for out, start in ((first_ref, 0), (next_ref, 2), (prev_ref, rows - 4), (last_ref, rows - 2)):
         for k in range(2):
-            out[where, pl.ds(k * columns, columns)] = read_row(hist_ref, 0, size, start + k, rows, columns).astype(bf16)
+            edges.setdefault(start + k, []).append((out, k))
+
+    def read(row):
+        density = read_row(hist_ref, 0, size, row, rows, columns)
+        for out, k in edges.get(row, []):
+            out[where, pl.ds(k * columns, columns)] = density.astype(bf16)
+        return density
+
     if rows <= 4:
+        for row in range(rows):
+            read(row)
         return
 
     def write(row, density):
         inner_ref[:, pl.ds((row - 2) * columns, columns)] = density.astype(bf16)
 
     two_steps(
-        [(2, rows - 3)],
-        lambda row: read_row(hist_ref, 0, size, row, rows, columns),
+        2,
+        rows - 3,
+        read,
         lambda c, row: 0.5 * drift_ref[c, row : row + 1, :],
         lambda row, density: density,
         band_ref[...],
@@ -179,7 +207,7 @@
     )
 
 
-def inner_steps(tiles, drift, levels, table, band):
+def inner_steps(tiles, drift, levels, table):
     scenarios = levels.shape[1]
     rows, columns = drift.shape[1:]
     per = tiles.shape[0] // scenarios
@@ -188,24 +216,29 @@
     edge = jax.ShapeDtypeStruct((scenarios, 2 * columns), bf16)
     sent = jax.ShapeDtypeStruct((scenarios + EXTRA, 2 * columns), bf16)
     shifts = jax.ShapeDtypeStruct((4, scenarios, LANES), f32)
+    band = jax.ShapeDtypeStruct((2 * columns, columns), bf16)
     return pl.pallas_call(
         functools.partial(inner_kernel, rows, size),
         grid=(scenarios // size,),
-        in_specs=[
-            pl.BlockSpec((size * per, LANES), lambda i: (i, 0)),
-            pl.BlockSpec(drift.shape, lambda i: (0, 0, 0)),
-            pl.BlockSpec(levels.shape, lambda i: (0, 0)),
-            smem(),
+        in_specs=[pl.BlockSpec((size * per, LANES), lambda i: (i, 0))] + [pl.BlockSpec(memory_space=pltpu.HBM)] * 3,
+        out_specs=[pl.BlockSpec(shape.shape, lambda i: (0, 0)) for shape in (sent, edge, edge, sent)]
+        + [
+            pl.BlockSpec(shifts.shape, lambda i: (0, 0, 0)),
             pl.BlockSpec(band.shape, lambda i: (0, 0)),
+            pl.BlockSpec((size, inner), lambda i: (i, 0)),
         ],
-        out_specs=[pl.BlockSpec(shape.shape, lambda i: (0, 0)) for shape in (sent, edge, edge, sent)]
-        + [pl.BlockSpec(shifts.shape, lambda i: (0, 0, 0)), pl.BlockSpec((size, inner), lambda i: (i, 0))],
-        out_shape=[sent, edge, edge, sent, shifts, jax.ShapeDtypeStruct((scenarios, inner), bf16)],
-        scratch_shapes=step_scratch(max(rows - 2, 1), size, columns),
+        out_shape=[sent, edge, edge, sent, shifts, band, jax.ShapeDtypeStruct((scenarios, inner), bf16)],
+        scratch_shapes=[
+            pltpu.VMEM(drift.shape, f32),
+            pltpu.VMEM(levels.shape, levels.dtype),
+            pltpu.VMEM(table.shape, f32),
+            pltpu.SemaphoreType.DMA((3,)),
+        ]
+        + step_scratch(max(rows - 4, 1), size, columns),
         compiler_params=params(),
         cost_estimate=pl.CostEstimate(flops=1, bytes_accessed=1, transcendentals=0),
         name="inner_density_steps",
-    )(tiles, drift, levels, table, band)
+    )(tiles, drift, levels, table)
 
 
 def halo_drift(ref, columns):
@@ -257,7 +290,7 @@
         def write(row, density):
             out[:, pl.ds((row - first) * columns, columns)] = density.astype(bf16)
 
-        two_steps([(first, first + 1)], read, half_drift, edge, band_ref[...], shifts, scratch, write)
+        two_steps(first, first + 1, read, half_drift, edge, band_ref[...], shifts, scratch, write)
 
 
 def edge_steps(drift, shifts, band, own, below, above, deps):
@@ -278,7 +311,7 @@
         + any_specs(deps),
         out_specs=[spec, spec],
         out_shape=[edge, edge],
-        scratch_shapes=step_scratch(4, size, columns),
+        scratch_shapes=step_scratch(2, size, columns),
         compiler_params=params(),
         cost_estimate=pl.CostEstimate(flops=1, bytes_accessed=1, transcendentals=0),
         name="edge_density_steps",
@@ -288,7 +321,8 @@
 def density_kernel(
     rows, size, first_step, hist_ref, drift_ref, shift_ref, band_ref, below_ref, above_ref, dep_ref, *refs
 ):
-    next_ref, *scratch = refs[-4:]
+    next_ref, token_ref, *scratch = refs[-5:]
+    token_ref[...] = jnp.zeros(token_ref.shape, f32)
     columns = drift_ref.shape[2]
     half_drift, edge = with_halo(drift_ref, below_ref, above_ref)
     where = pl.ds(pl.multiple_of((first_step + pl.program_id(0)) * size, size), size)
@@ -301,7 +335,8 @@
         return read_row(hist_ref, 0, size, row, rows, columns)
 
     two_steps(
-        [(0, rows - 1)],
+        0,
+        rows - 1,
         read,
         half_drift,
         edge,
@@ -320,7 +355,7 @@
     steps = scenarios // size // turns
     first = turn * steps
     block = pl.BlockSpec((size * per, LANES), lambda i: (first + i, 0))
-    hidden = pl.BlockSpec(memory_space=pl.ANY)
+    hidden = pl.BlockSpec(memory_space=pltpu.HBM)
     args = [tiles, drift, shifts, band, below, above, dep]
     in_specs = [
         block,
@@ -340,10 +375,10 @@
         functools.partial(density_kernel, rows, size, first),
         grid=(steps,),
         in_specs=in_specs,
-        out_specs=block,
-        out_shape=jax.ShapeDtypeStruct(tiles.shape, f32),
+        out_specs=[block, pl.BlockSpec((SUBLANES, LANES), lambda i: (0, 0))],
+        out_shape=[pltpu.HBM(tiles.shape, f32), jax.ShapeDtypeStruct((SUBLANES, LANES), f32)],
         input_output_aliases=aliases,
-        scratch_shapes=step_scratch(rows + 2, size, columns),
+        scratch_shapes=step_scratch(rows, size, columns),
         compiler_params=params(),
         cost_estimate=pl.CostEstimate(flops=1, bytes_accessed=1, transcendentals=0),
         name="density_steps",
@@ -786,24 +821,20 @@
     index = lax.axis_index("grid")
     core, side, part = index % 2, index // 2 % 2, index // 4
     mine = 2 * core + side
-    tiles = to_tiles(hist)
+    tiles = pltpu.with_memory_space_constraint(to_tiles(hist), pltpu.HBM)
 
     place = jnp.stack([core, side, part, mine])
     cot = lax.dynamic_slice_in_dim(cotangent, mine * block, block)[:, None]
     heads = [head_weight[None, :]]
     mids = [mid_weight]
 
-    band = band_matrix(columns)
-    *own_rows, shifts, inner = inner_steps(tiles, drift, shocks.T, shock_table.T, band)
+    *own_rows, shifts, band, inner = inner_steps(tiles, drift, shocks.T, shock_table.T)
     inner = inner if rows > 4 else None
     forward = [(i, i + 1) for i in range(count - 1)]
     backward = [(i + 1, i) for i in range(count - 1)]
     below = lax.ppermute(own_rows[3], "grid", forward)
     above = lax.ppermute(own_rows[0], "grid", backward)
-    mids.append(swap(mids[0], count, 1))
-    mids.append(swap(mids[0], count, 2))
-    product = None if inner is None else inner_product(inner, first_weight, width, mids[1:])
-    mids.append(swap(mids[2], count, 1))
+    product = None if inner is None else inner_product(inner, first_weight, width, [])
     low, high = edge_steps(drift, shifts, band, own_rows, below, above, [] if product is None else [product])
 
     def density_turn(turn, dep, so_far):
@@ -813,28 +844,31 @@
     products = [edge_product(place, low, high, first_weight, product, parts, width, c) for c in range(chunks)]
     sums = []
     for c, (keep, send) in enumerate(products):
-        keep, send = add_side(place, keep, swap(send, count, 1), [mids[3]])
+        keep, send = add_side(place, keep, swap(send, count, 1))
         sums.append((keep, send, swap(send, count, 2)))
-    density = density_turn(0, sums[-1][1], density)
+    density, token = density_turn(0, sums[-1][1], density)
+    mids.append(swap(mids[0], count, 1))
+    mids.append(swap(mids[0], count, 2))
+    mids.append(swap(mids[2], count, 1))
     for c, (keep, send, other) in enumerate(sums):
-        own, *sends = add_parts(place, keep, other, [density])
+        own, *sends = add_parts(place, keep, other, [token])
         received = [swap(piece, count, 4 * (k + 1)) for k, piece in enumerate(sends)]
         if c == chunks - 1:
-            density = density_turn(1, sends[-1], density)
-        owned.append(activate(own, received, [density]))
+            density, token = density_turn(1, sends[-1], density)
+        owned.append(activate(own, received, [token, mids[2]] if c == chunks - 1 else []))
     for first in owned:
         firsts.append(first)
         firsts += [swap(first, count, 4 * k) for k in range(1, parts)]
     heads += [swap(heads[0], count, k) for k in range(1, 4)]
-    density = density_turn(2, owned[-1], density)
+    density, token = density_turn(2, owned[-1], density)
     own, value, mid_keep, mid_send, *sends = middle(
-        place, cot, firsts, mids, heads, chunks, parts, width, [density]
+        place, cot, firsts, mids, heads, chunks, parts, width, [token]
     )
     received = [swap(piece, count, 4 * (k + 1)) for k, piece in enumerate(sends)]
     *backs, tail = back_first(own, value, received, owned)
     mid_keep, mid_send = mid_add(mid_keep, swap(mid_send, count, 1), [backs[-1]])
-    density = density_turn(3, backs[-1], density)
-    lefts = transposed([low, high] if inner is None else [low, inner, high], [density])
+    density, token = density_turn(3, backs[-1], density)
+    lefts = transposed([low, high] if inner is None else [low, inner, high], [token])
     grad_mid, grad_head = mid_final(mid_keep, swap(mid_send, count, 2))
     grad_first = None
     for c in range(chunks):

time: 158 us -> 167 us (1.057)
  starting transfers between devices: 33.5 us -> 50.2 us
  Pallas kernels: 85.3 us -> 77.3 us
    ppermute x25 -> x39, starting transfers between devices: 29.9 us -> 45.8 us  [swap(): return lax.ppermute(values, 'grid', [(i, i ^ flip) for i in range(count)])]
    pallas_call x1, Pallas kernels: 16.4 us -> 10 us  [inner_steps(): pl.pallas_call(functools.partial(inner_kernel, rows, size), grid=(scenari...]
    pallas_call x4, Pallas kernels: 26.6 us -> 22.2 us  [density_steps(): pl.pallas_call(functools.partial(density_kernel, rows, size, first), grid...]
    pallas_call x1 -> x2, Pallas kernels: 12.5 us -> 14.7 us  [first_grad(): pl.pallas_call(functools.partial(first_grad_kernel, parts, block, len(lef...]
    pallas_call x1 -> x2, Pallas kernels: 5.39 us -> 7.19 us  [edge_product(): pl.pallas_call(functools.partial(edge_product_kernel, block, inner is not...]
    broadcast_in_dim x2, local copies, waits for them, and re-layouts: 1.95 us -> 0.18 us  [local(): cot = lax.dynamic_slice_in_dim(cotangent, mine * block, block)[:, None]]
    ppermute x25 -> x39, waiting for transfers between devices: 24.3 us -> 25.4 us  [swap(): return lax.ppermute(values, 'grid', [(i, i ^ flip) for i in range(count)])]
    unnamed x50 -> x54, local copies, waits for them, and re-layouts: 10.2 us -> 10.7 us
  transfers between devices with their start and end apart: 27 -> 41, of which waited for: 6 -> 10; matrix products, arithmetic and copies ran while one was open for 1% -> 1% of each run, Pallas kernels for 36% -> 34%
where the time goes in v4:
time: 167 us; the launch traced here: 166 us
  Pallas kernels  77.3 us (46%)
  starting transfers between devices  50.2 us (30%)
  waiting for transfers between devices  25.4 us (15%)
  local copies, waits for them, and re-layouts  11.6 us (7%)
    ppermute x39, starting transfers between devices, swap(): return lax.ppermute(values, 'grid', [(i, i ^ flip) for i in range(count)])  45.8 us
    ppermute x39, waiting for transfers between devices, swap(): return lax.ppermute(values, 'grid', [(i, i ^ flip) for i in range(count)])  25.4 us
    pallas_call x4, Pallas kernels, density_steps(): pl.pallas_call(functools.partial(density_kernel, rows, size, first), grid...  22.2 us
    pallas_call x2, Pallas kernels, first_grad(): pl.pallas_call(functools.partial(first_grad_kernel, parts, block, len(lef...  14.7 us
    unnamed x54, local copies, waits for them, and re-layouts  10.7 us
    pallas_call x1, Pallas kernels, inner_steps(): pl.pallas_call(functools.partial(inner_kernel, rows, size), grid=(scenari...  10 us
    pallas_call x1, Pallas kernels, inner_product(): pl.pallas_call(functools.partial(inner_product_kernel, count, len(deps)),...  9.79 us
    pallas_call x2, Pallas kernels, edge_product(): pl.pallas_call(functools.partial(edge_product_kernel, block, inner is not...  7.19 us
  transfers between devices with their start and end apart: 41, of which 10 were waited for; matrix products, arithmetic and copies ran while one was open for 1% of the time, Pallas kernels for 34%

profile of v4, /device:TPU:0, one launch (start us, length us, event | category | flops | bytes accessed | tf_op | source)
XLA Modules:
  0.0 165.6 jit_solution(1210046566953063247)
XLA Ops:
  2.8 10.0 %inner_density_steps.1 = (bf16[400,512]{1,0:T(8,128)(2,1)}, bf16[384,512]{1,0:T(8,128)(2,1)S(1)}, bf16[384,512]{1,0:T(8,128)(2,1)S(1)}, bf16[400,512]{1,0:T(8,12...) custom-call(f32[12288,128]{1,0:T(8,128)} %bitcast.26, ...), custom_call_target="tpu_custom_call" | custom-call | flops 1 | bytes 1 | tf_op jit(solution)/shard_map/inner_density_steps/pallas_call | solution.py:220
  13.7 3.1 %collective-permute-start = (bf16[400,512]{1,0:T(8,128)(2,1)}, bf16[400,512]{1,0:T(8,128)(2,1)}, u32[]{:S(2)}, u32[]{:S(2)}) collective-permute-start(bf16[400,512]{1,0:T(8,128)(2,1)} %get-tuple-element.59.last_ref), channel_id=1, source_target_pairs={{0,1},{1,2},{2,3},{3,4},{4,5},{5,6},{6,7},{7,8},{8,9},{9,10},{10,1... | collective-permute-start | bytes 1228808 | tf_op jit(solution)/shard_map/ppermute | solution.py:835
  18.1 4.2 %collective-permute-start.15 = (bf16[2048,128]{1,0:T(8,128)(2,1)}, bf16[2048,128]{1,0:T(8,128)(2,1)}, u32[]{:S(2)}, u32[]{:S(2)}) collective-permute-start(bf16[2048,128]{1,0:T(8,128)(2,1)} %refs_10_.1), channel_id=1, source_target_pairs={{0,2},{1,3},{2,0},{3,1},{4,6},{5,7},{6,4},{7,5},{8,10},{9,11},{10,... | collective-permute-start | bytes 1572872 | tf_op jit(solution)/shard_map/ppermute | solution.py:393
  22.3 9.8 %inner_product.1.refs_0_ = f32[8,384,256]{2,1,0:T(8,128)S(1)} custom-call(bf16[384,3072]{1,0:T(8,128)(2,1)S(1)} %get-tuple-element.63.refs_0_.refs_1_, bf16[4096,2048]{1,0:T(8,128)(2,1)} %bottom_ref.3, bf16[4096,2048]{1,0:T(8,128)(2,1)} %bottom_ref.3, bf16[4096,2048]{1,0:T(8,128)(2,1)} %bottom_ref.3, bf16[4096,2048]{1,0:T(8,128)(2,1)} %bottom_ref.3, ...), custom_call_target="tpu_custom_call" | custom-call | flops 1 | bytes 1 | tf_op jit(solution)/shard_map/inner_product/pallas_call | solution.py:413
  35.4 5.7 %edge_density_steps.1 = (bf16[384,512]{1,0:T(8,128)(2,1)S(1)}, bf16[384,512]{1,0:T(8,128)(2,1)S(1)}) custom-call(f32[2,16,256]{2,1,0:T(8,128)S(1)} %copy-done.13, f32[4,384,128]{2,1,0:T(8,128)S(1)} %copy-done.2, bf16[512,256]{1,0:T(8,128)(2,1)S(1)} %get-tuple-element.58.band_ref, bf16[400,512]{1,0:T(8,128)(2,1)} %get-tuple-element.60.first_ref, ...), custom_call_target="tpu_custom_call" | custom-call | flops 1 | bytes 1 | tf_op jit(solution)/shard_map/edge_density_steps/pallas_call | solution.py:302
  41.2 3.7 %edge_product.2 = (f32[2,4,96,256]{3,2,1,0:T(8,128)S(1)}, bf16[2,4,96,256]{3,2,1,0:T(8,128)(2,1)S(1)}) custom-call(s32[4]{0:T(128)S(1)} %pad_add_fusion.place_ref.refs_0_, bf16[384,512]{1,0:T(8,128)(2,1)S(1)} %get-tuple-element.64.low_ref.refs_0_, bf16[384,512]{1,0:T(8,128)(2,1)S(1)} %get-tuple-element.65.high_ref.refs_2_, bf16[4096,2048]{1,0:T(8,128)(2,1)} %bottom_ref.3, ...), custom_call_target="tpu_custom_call" | custom-call | flops 1 | bytes 1 | tf_op jit(solution)/shard_map/edge_product/pallas_call | solution.py:457
  45.3 3.5 %edge_product.3 = (f32[2,4,96,256]{3,2,1,0:T(8,128)S(1)}, bf16[2,4,96,256]{3,2,1,0:T(8,128)(2,1)S(1)}) custom-call(s32[4]{0:T(128)S(1)} %pad_add_fusion.place_ref.refs_0_, bf16[384,512]{1,0:T(8,128)(2,1)S(1)} %get-tuple-element.64.low_ref.refs_0_, bf16[384,512]{1,0:T(8,128)(2,1)S(1)} %get-tuple-element.65.high_ref.refs_2_, bf16[4096,2048]{1,0:T(8,128)(2,1)} %bottom_ref.3, ...), custom_call_target="tpu_custom_call" | custom-call | flops 1 | bytes 1 | tf_op jit(solution)/shard_map/edge_product/pallas_call | solution.py:457
  53.0 5.5 %density_steps.4 = (f32[12288,128]{1,0:T(8,128)}, f32[8,128]{1,0:T(8,128)S(1)}) custom-call(f32[12288,128]{1,0:T(8,128)} %bitcast.27, f32[2,16,256]{2,1,0:T(8,128)S(1)} %copy-done.13, f32[4,384,128]{2,1,0:T(8,128)S(1)} %copy-done.3, bf16[512,256]{1,0:T(8,128)(2,1)S(1)} %get-tuple-element.58.band_ref, bf16[400,512]{1,0:T(8,128)(2,1)} %collective-permute-done.below_ref, ...), custom_call_target="tpu_custom_call" | custom-call | flops 1 | bytes 1 | tf_op jit(solution)/shard_map/density_steps/pallas_call | solution.py:374
  59.1 3.2 %collective-permute-start.5 = (bf16[96,256]{1,0:T(8,128)(2,1)S(1)}, bf16[96,256]{1,0:T(8,128)(2,1)S(1)}, u32[]{:S(2)}, u32[]{:S(2)}) collective-permute-start(bf16[96,256]{1,0:T(8,128)(2,1)S(1)} %get-tuple-element.75), channel_id=1, source_target_pairs={{0,4},{1,5},{2,6},{3,7},{4,0},{5,1},{6,2},{7,3},{8,12},{9,13},{10,... | collective-permute-start | bytes 147464 | tf_op jit(solution)/shard_map/ppermute | solution.py:393
  62.3 3.0 %collective-permute-done.23.refs_17_ = f32[1,128]{1,0:T(1,128)S(1)} collective-permute-done((f32[1,128]{1,0:T(1,128)S(1)}, f32[1,128]{1,0:T(1,128)S(1)}, u32[]{:S(2)}, u32[]{:S(2)}) %collective-permute-start.23) | collective-permute-done | bytes 544 | tf_op jit(solution)/shard_map/ppermute | solution.py:393
  74.7 3.3 %collective-permute-start.10 = (bf16[96,256]{1,0:T(8,128)(2,1)S(1)}, bf16[96,256]{1,0:T(8,128)(2,1)S(1)}, u32[]{:S(2)}, u32[]{:S(2)}) collective-permute-start(bf16[96,256]{1,0:T(8,128)(2,1)S(1)} %first_activation.2.refs_2_.refs_5_), channel_id=1, source_target_pairs={{0,12},{1,13},{2,14},{3,15},{4,8},{5,9},{6,10},{7,11},{8,4},{9,5},... | collective-permute-start | bytes 147464 | tf_op jit(solution)/shard_map/ppermute | solution.py:393
  79.9 5.5 %density_steps.5 = (f32[12288,128]{1,0:T(8,128)}, f32[8,128]{1,0:T(8,128)S(1)}) custom-call(f32[12288,128]{1,0:T(8,128)} %bitcast.28, f32[2,16,256]{2,1,0:T(8,128)S(1)} %copy-done.13, f32[4,384,128]{2,1,0:T(8,128)S(1)} %copy-done.4, bf16[512,256]{1,0:T(8,128)(2,1)S(1)} %get-tuple-element.58.band_ref, ...), custom_call_target="tpu_custom_call", output_to_operand_aliasing={{0}: (7, {})} | custom-call | flops 1 | bytes 1 | tf_op jit(solution)/shard_map/density_steps/pallas_call | solution.py:374
  87.1 2.8 %collective-permute-start.18 = (bf16[96,256]{1,0:T(8,128)(2,1)S(1)}, bf16[96,256]{1,0:T(8,128)(2,1)S(1)}, u32[]{:S(2)}, u32[]{:S(2)}) collective-permute-start(bf16[96,256]{1,0:T(8,128)(2,1)S(1)} %first_activation.3.dep_ref.refs_6_), channel_id=1, source_target_pairs={{0,12},{1,13},{2,14},{3,15},{4,8},{5,9},{6,10},{7,11},{8,4},{9,5},... | collective-permute-start | bytes 147464 | tf_op jit(solution)/shard_map/ppermute | solution.py:393
  91.7 5.5 %density_steps.6 = (f32[12288,128]{1,0:T(8,128)}, f32[8,128]{1,0:T(8,128)S(1)}) custom-call(f32[12288,128]{1,0:T(8,128)} %bitcast.29, f32[2,16,256]{2,1,0:T(8,128)S(1)} %copy-done.13, f32[4,384,128]{2,1,0:T(8,128)S(1)} %copy-done.4, bf16[512,256]{1,0:T(8,128)(2,1)S(1)} %get-tuple-element.58.band_ref, ...), custom_call_target="tpu_custom_call", output_to_operand_aliasing={{0}: (7, {})} | custom-call | flops 1 | bytes 1 | tf_op jit(solution)/shard_map/density_steps/pallas_call | solution.py:374
  100.7 3.1 %value_layers.1 = (f32[192,256]{1,0:T(8,128)S(1)}, f32[1,256]{1,0:T(1,128)S(1)}, bf16[2,2064,128]{2,1,0:T(8,128)(2,1)S(1)}, bf16[2,2064,128]{2,1,0:T(8,128)(2,1)...) custom-call(s32[4]{0:T(128)S(1)} %pad_add_fusion.place_ref.refs_0_, ...), custom_call_target="tpu_custom_call" | custom-call | flops 1 | bytes 1 | tf_op jit(solution)/shard_map/value_layers/pallas_call | solution.py:611
  104.4 2.9 %collective-permute-start.25 = (bf16[208,256]{1,0:T(8,128)(2,1)S(1)}, bf16[208,256]{1,0:T(8,128)(2,1)S(1)}, u32[]{:S(2)}, u32[]{:S(2)}) collective-permute-start(bf16[208,256]{1,0:T(8,128)(2,1)S(1)} %get-tuple-element.90), channel_id=1, source_target_pairs={{0,8},{1,9},{2,10},{3,11},{4,12},{5,13},{6,14},{7,15},{8,0},{9,1},... | collective-permute-start | bytes 319496 | tf_op jit(solution)/shard_map/ppermute | solution.py:393
  108.3 2.8 %collective-permute-done.24.refs_2_ = bf16[208,256]{1,0:T(8,128)(2,1)S(1)} collective-permute-done((bf16[208,256]{1,0:T(8,128)(2,1)S(1)}, bf16[208,256]{1,0:T(8,128)(2,1)S(1)}, u32[]{:S(2)}, u32[]{:S(2)}) %collective-permute-start.24) | collective-permute-done | bytes 106528 | tf_op jit(solution)/shard_map/ppermute | solution.py:393
  111.1 4.5 %collective-permute-done.25.refs_3_ = bf16[208,256]{1,0:T(8,128)(2,1)S(1)} collective-permute-done((bf16[208,256]{1,0:T(8,128)(2,1)S(1)}, bf16[208,256]{1,0:T(8,128)(2,1)S(1)}, u32[]{:S(2)}, u32[]{:S(2)}) %collective-permute-start.25) | collective-permute-done | bytes 106528 | tf_op jit(solution)/shard_map/ppermute | solution.py:393
  124.9 4.2 %collective-permute-done.31.other_ref = bf16[2064,128]{1,0:T(8,128)(2,1)S(1)} collective-permute-done((bf16[2064,128]{1,0:T(8,128)(2,1)S(1)}, bf16[2064,128]{1,0:T(8,128)(2,1)S(1)}, u32[]{:S(2)}, u32[]{:S(2)}) %collective-permute-start.31) | collective-permute-done | bytes 528416 | tf_op jit(solution)/shard_map/ppermute | solution.py:393
  129.0 2.9 %collective-permute-start.35 = (bf16[96,256]{1,0:T(8,128)(2,1)S(1)}, bf16[96,256]{1,0:T(8,128)(2,1)S(1)}, u32[]{:S(2)}, u32[]{:S(2)}) collective-permute-start(bf16[96,256]{1,0:T(8,128)(2,1)S(1)} %get-tuple-element.92.dep_ref.refs_0_), channel_id=1, source_target_pairs={{0,4},{1,5},{2,6},{3,7},{4,0},{5,1},{6,2},{7,3},{8,12},{9,13},{10,... | collective-permute-start | bytes 147464 | tf_op jit(solution)/shard_map/ppermute | solution.py:393
  131.9 5.8 %density_steps.7 = (f32[12288,128]{1,0:T(8,128)}, f32[8,128]{1,0:T(8,128)S(1)}) custom-call(f32[12288,128]{1,0:T(8,128)} %bitcast.30, f32[2,16,256]{2,1,0:T(8,128)S(1)} %copy-done.13, f32[4,384,128]{2,1,0:T(8,128)S(1)} %copy-done.4, bf16[512,256]{1,0:T(8,128)(2,1)S(1)} %get-tuple-element.58.band_ref, ...), custom_call_target="tpu_custom_call", output_to_operand_aliasing={{0}: (7, {})} | custom-call | flops 1 | bytes 1 | tf_op jit(solution)/shard_map/density_steps/pallas_call | solution.py:374
  142.8 5.4 %collective-permute-done.33.refs_6_ = bf16[400,256]{1,0:T(8,128)(2,1)S(1)} collective-permute-done((bf16[400,256]{1,0:T(8,128)(2,1)S(1)}, bf16[400,256]{1,0:T(8,128)(2,1)S(1)}, u32[]{:S(2)}, u32[]{:S(2)}) %collective-permute-start.33) | collective-permute-done | bytes 204832 | tf_op jit(solution)/shard_map/ppermute | solution.py:393
  150.3 7.1 %first_gradient.2 = (bf16[4096,2048]{1,0:T(8,128)(2,1)}, f32[4,256]{1,0:T(4,128)S(1)}) custom-call(s32[4]{0:T(128)S(1)} %pad_add_fusion.place_ref.refs_0_, bf16[512,384]{1,0:T(8,128)(2,1)S(1)} %get-tuple-element.96.refs_6_.refs_1_.refs_5_, bf16[3072,384]{1,0:T(8,128)(2,1)S(1)} %get-tuple-element.97.refs_2_, bf16[512,384]{1,0:T(8,128)(2,1)S(1)} %get-tuple-element.98.refs_3_, ...), custom_call_target="tpu_custom_call" | custom-call | flops 1 | bytes 1 | tf_op jit(solution)/shard_map/first_gradient/pallas_call | solution.py:798
  158.1 7.6 %first_gradient.3 = bf16[4096,2048]{1,0:T(8,128)(2,1)} custom-call(s32[4]{0:T(128)S(1)} %pad_add_fusion.place_ref.refs_0_, bf16[512,384]{1,0:T(8,128)(2,1)S(1)} %get-tuple-element.96.refs_6_.refs_1_.refs_5_, bf16[3072,384]{1,0:T(8,128)(2,1)S(1)} %get-tuple-element.97.refs_2_, ...), custom_call_target="tpu_custom_call", output_to_operand_aliasing={{}: (8, {})} | custom-call | flops 1 | bytes 1 | tf_op jit(solution)/shard_map/first_gradient/pallas_call | solution.py:798
  (141 shorter events, 49.7 us)
Async XLA Ops:
  13.7 18.6 %collective-permute-start = (bf16[400,512]{1,0:T(8,128)(2,1)}, bf16[400,512]{1,0:T(8,128)(2,1)}, u32[]{:S(2)}, u32[]{:S(2)}) collective-permute-start(bf16[400,512]{1,0:T(8,128)(2,1)} %get-tuple-element.59.last_ref), channel_id=1, source_target_pairs={{0,1},{1,2},{2,3},{3,4},{4,5},{5,6},{6,7},{7,8},{8,9},{9,10},{10,1... | collective-permute-start | bytes 1228808 | tf_op jit(solution)/shard_map/ppermute | solution.py:835
  16.9 15.4 %collective-permute-start.1 = (bf16[400,512]{1,0:T(8,128)(2,1)}, bf16[400,512]{1,0:T(8,128)(2,1)}, u32[]{:S(2)}, u32[]{:S(2)}) collective-permute-start(bf16[400,512]{1,0:T(8,128)(2,1)} %get-tuple-element.60.first_ref), channel_id=1, source_target_pairs={{1,0},{2,1},{3,2},{4,3},{5,4},{6,5},{7,6},{8,7},{9,8},{10,9},{11,1... | collective-permute-start | bytes 1228808 | tf_op jit(solution)/shard_map/ppermute | solution.py:836
  18.1 31.3 %collective-permute-start.15 = (bf16[2048,128]{1,0:T(8,128)(2,1)}, bf16[2048,128]{1,0:T(8,128)(2,1)}, u32[]{:S(2)}, u32[]{:S(2)}) collective-permute-start(bf16[2048,128]{1,0:T(8,128)(2,1)} %refs_10_.1), channel_id=1, source_target_pairs={{0,2},{1,3},{2,0},{3,1},{4,6},{5,7},{6,4},{7,5},{8,10},{9,11},{10,... | collective-permute-start | bytes 1572872 | tf_op jit(solution)/shard_map/ppermute | solution.py:393
  49.1 38.0 %collective-permute-start.19 = (bf16[2048,128]{1,0:T(8,128)(2,1)}, bf16[2048,128]{1,0:T(8,128)(2,1)S(1)}, u32[]{:S(2)}, u32[]{:S(2)}) collective-permute-start(bf16[2048,128]{1,0:T(8,128)(2,1)} %refs_10_.1), channel_id=1, source_target_pairs={{0,1},{1,0},{2,3},{3,2},{4,5},{5,4},{6,7},{7,6},{8,9},{9,8},{10,11... | collective-permute-start | bytes 1572872 | tf_op jit(solution)/shard_map/ppermute | solution.py:393
  49.4 40.5 %collective-permute-start.20 = (bf16[2048,128]{1,0:T(8,128)(2,1)}, bf16[2048,128]{1,0:T(8,128)(2,1)S(1)}, u32[]{:S(2)}, u32[]{:S(2)}) collective-permute-start(bf16[2048,128]{1,0:T(8,128)(2,1)} %collective-permute-done.15.refs_5_.refs_12_), channel_id=1, source_target_pairs={{0,1},{1,0},{2,3},{3,2},{4,5},{5,4},{6,7},{7,6},{8,9},{9,8},{10,11... | collective-permute-start | bytes 1572872 | tf_op jit(solution)/shard_map/ppermute | solution.py:393
  50.2 8.2 %collective-permute-start.3 = (bf16[4,96,256]{2,1,0:T(8,128)(2,1)S(1)}, bf16[4,96,256]{2,1,0:T(8,128)(2,1)S(1)}, u32[]{:S(2)}, u32[]{:S(2)}) collective-permute-start(bf16[4,96,256]{2,1,0:T(8,128)(2,1)S(1)} %get-tuple-element.69), channel_id=1, source_target_pairs={{0,2},{1,3},{2,0},{3,1},{4,6},{5,7},{6,4},{7,5},{8,10},{9,11},{10,... | collective-permute-start | bytes 589832 | tf_op jit(solution)/shard_map/ppermute | solution.py:393
  51.2 16.6 %collective-permute-start.11 = (bf16[4,96,256]{2,1,0:T(8,128)(2,1)S(1)}, bf16[4,96,256]{2,1,0:T(8,128)(2,1)S(1)}, u32[]{:S(2)}, u32[]{:S(2)}) collective-permute-start(bf16[4,96,256]{2,1,0:T(8,128)(2,1)S(1)} %get-tuple-element.72.dep_ref), channel_id=1, source_target_pairs={{0,2},{1,3},{2,0},{3,1},{4,6},{5,7},{6,4},{7,5},{8,10},{9,11},{10,... | collective-permute-start | bytes 589832 | tf_op jit(solution)/shard_map/ppermute | solution.py:393
  59.1 9.4 %collective-permute-start.5 = (bf16[96,256]{1,0:T(8,128)(2,1)S(1)}, bf16[96,256]{1,0:T(8,128)(2,1)S(1)}, u32[]{:S(2)}, u32[]{:S(2)}) collective-permute-start(bf16[96,256]{1,0:T(8,128)(2,1)S(1)} %get-tuple-element.75), channel_id=1, source_target_pairs={{0,4},{1,5},{2,6},{3,7},{4,0},{5,1},{6,2},{7,3},{8,12},{9,13},{10,... | collective-permute-start | bytes 147464 | tf_op jit(solution)/shard_map/ppermute | solution.py:393
  74.7 15.2 %collective-permute-start.10 = (bf16[96,256]{1,0:T(8,128)(2,1)S(1)}, bf16[96,256]{1,0:T(8,128)(2,1)S(1)}, u32[]{:S(2)}, u32[]{:S(2)}) collective-permute-start(bf16[96,256]{1,0:T(8,128)(2,1)S(1)} %first_activation.2.refs_2_.refs_5_), channel_id=1, source_target_pairs={{0,12},{1,13},{2,14},{3,15},{4,8},{5,9},{6,10},{7,11},{8,4},{9,5},... | collective-permute-start | bytes 147464 | tf_op jit(solution)/shard_map/ppermute | solution.py:393
  85.4 11.8 %collective-permute-start.9 = (bf16[96,256]{1,0:T(8,128)(2,1)S(1)}, bf16[96,256]{1,0:T(8,128)(2,1)S(1)}, u32[]{:S(2)}, u32[]{:S(2)}) collective-permute-start(bf16[96,256]{1,0:T(8,128)(2,1)S(1)} %first_activation.2.refs_2_.refs_5_), channel_id=1, source_target_pairs={{0,8},{1,9},{2,10},{3,11},{4,12},{5,13},{6,14},{7,15},{8,0},{9,1},... | collective-permute-start | bytes 147464 | tf_op jit(solution)/shard_map/ppermute | solution.py:393
  85.5 11.7 %collective-permute-start.8 = (bf16[96,256]{1,0:T(8,128)(2,1)S(1)}, bf16[96,256]{1,0:T(8,128)(2,1)S(1)}, u32[]{:S(2)}, u32[]{:S(2)}) collective-permute-start(bf16[96,256]{1,0:T(8,128)(2,1)S(1)} %first_activation.2.refs_2_.refs_5_), channel_id=1, source_target_pairs={{0,4},{1,5},{2,6},{3,7},{4,0},{5,1},{6,2},{7,3},{8,12},{9,13},{10,... | collective-permute-start | bytes 147464 | tf_op jit(solution)/shard_map/ppermute | solution.py:393
  87.1 10.1 %collective-permute-start.18 = (bf16[96,256]{1,0:T(8,128)(2,1)S(1)}, bf16[96,256]{1,0:T(8,128)(2,1)S(1)}, u32[]{:S(2)}, u32[]{:S(2)}) collective-permute-start(bf16[96,256]{1,0:T(8,128)(2,1)S(1)} %first_activation.3.dep_ref.refs_6_), channel_id=1, source_target_pairs={{0,12},{1,13},{2,14},{3,15},{4,8},{5,9},{6,10},{7,11},{8,4},{9,5},... | collective-permute-start | bytes 147464 | tf_op jit(solution)/shard_map/ppermute | solution.py:393
  89.9 7.9 %collective-permute-start.16 = (bf16[96,256]{1,0:T(8,128)(2,1)S(1)}, bf16[96,256]{1,0:T(8,128)(2,1)S(1)}, u32[]{:S(2)}, u32[]{:S(2)}) collective-permute-start(bf16[96,256]{1,0:T(8,128)(2,1)S(1)} %first_activation.3.dep_ref.refs_6_), channel_id=1, source_target_pairs={{0,4},{1,5},{2,6},{3,7},{4,0},{5,1},{6,2},{7,3},{8,12},{9,13},{10,... | collective-permute-start | bytes 147464 | tf_op jit(solution)/shard_map/ppermute | solution.py:393
  103.8 12.0 %collective-permute-start.30 = (bf16[2,2064,128]{2,1,0:T(8,128)(2,1)S(1)}, bf16[2,2064,128]{2,1,0:T(8,128)(2,1)S(1)}, u32[]{:S(2)}, u32[]{:S(2)}) collective-permute-start(bf16[2,2064,128]{2,1,0:T(8,128)(2,1)S(1)} %get-tuple-element.102), channel_id=1, source_target_pairs={{0,1},{1,0},{2,3},{3,2},{4,5},{5,4},{6,7},{7,6},{8,9},{9,8},{10,11... | collective-permute-start | bytes 3170312 | tf_op jit(solution)/shard_map/ppermute | solution.py:393
  104.4 11.3 %collective-permute-start.25 = (bf16[208,256]{1,0:T(8,128)(2,1)S(1)}, bf16[208,256]{1,0:T(8,128)(2,1)S(1)}, u32[]{:S(2)}, u32[]{:S(2)}) collective-permute-start(bf16[208,256]{1,0:T(8,128)(2,1)S(1)} %get-tuple-element.90), channel_id=1, source_target_pairs={{0,8},{1,9},{2,10},{3,11},{4,12},{5,13},{6,14},{7,15},{8,0},{9,1},... | collective-permute-start | bytes 319496 | tf_op jit(solution)/shard_map/ppermute | solution.py:393
  107.2 8.4 %collective-permute-start.26 = (bf16[208,256]{1,0:T(8,128)(2,1)S(1)}, bf16[208,256]{1,0:T(8,128)(2,1)S(1)}, u32[]{:S(2)}, u32[]{:S(2)}) collective-permute-start(bf16[208,256]{1,0:T(8,128)(2,1)S(1)} %get-tuple-element.91), channel_id=1, source_target_pairs={{0,12},{1,13},{2,14},{3,15},{4,8},{5,9},{6,10},{7,11},{8,4},{9,5},... | collective-permute-start | bytes 319496 | tf_op jit(solution)/shard_map/ppermute | solution.py:393
  116.0 13.0 %collective-permute-start.31 = (bf16[2064,128]{1,0:T(8,128)(2,1)S(1)}, bf16[2064,128]{1,0:T(8,128)(2,1)S(1)}, u32[]{:S(2)}, u32[]{:S(2)}) collective-permute-start(bf16[2064,128]{1,0:T(8,128)(2,1)S(1)} %get-tuple-element.104), channel_id=1, source_target_pairs={{0,2},{1,3},{2,0},{3,1},{4,6},{5,7},{6,4},{7,5},{8,10},{9,11},{10,... | collective-permute-start | bytes 1585160 | tf_op jit(solution)/shard_map/ppermute | solution.py:393
  119.3 20.3 %collective-permute-start.28 = (bf16[96,256]{1,0:T(8,128)(2,1)S(1)}, bf16[96,256]{1,0:T(8,128)(2,1)S(1)}, u32[]{:S(2)}, u32[]{:S(2)}) collective-permute-start(bf16[96,256]{1,0:T(8,128)(2,1)S(1)} %get-tuple-element.99.refs_0_), channel_id=1, source_target_pairs={{0,8},{1,9},{2,10},{3,11},{4,12},{5,13},{6,14},{7,15},{8,0},{9,1},... | collective-permute-start | bytes 147464 | tf_op jit(solution)/shard_map/ppermute | solution.py:393
  120.7 18.9 %collective-permute-start.27 = (bf16[96,256]{1,0:T(8,128)(2,1)S(1)}, bf16[96,256]{1,0:T(8,128)(2,1)S(1)}, u32[]{:S(2)}, u32[]{:S(2)}) collective-permute-start(bf16[96,256]{1,0:T(8,128)(2,1)S(1)} %get-tuple-element.99.refs_0_), channel_id=1, source_target_pairs={{0,4},{1,5},{2,6},{3,7},{4,0},{5,1},{6,2},{7,3},{8,12},{9,13},{10,... | collective-permute-start | bytes 147464 | tf_op jit(solution)/shard_map/ppermute | solution.py:393
  121.3 20.2 %collective-permute-start.37 = (bf16[96,256]{1,0:T(8,128)(2,1)S(1)}, bf16[96,256]{1,0:T(8,128)(2,1)S(1)}, u32[]{:S(2)}, u32[]{:S(2)}) collective-permute-start(bf16[96,256]{1,0:T(8,128)(2,1)S(1)} %get-tuple-element.92.dep_ref.refs_0_), channel_id=1, source_target_pairs={{0,12},{1,13},{2,14},{3,15},{4,8},{5,9},{6,10},{7,11},{8,4},{9,5},... | collective-permute-start | bytes 147464 | tf_op jit(solution)/shard_map/ppermute | solution.py:393
  123.7 17.8 %collective-permute-start.36 = (bf16[96,256]{1,0:T(8,128)(2,1)S(1)}, bf16[96,256]{1,0:T(8,128)(2,1)S(1)}, u32[]{:S(2)}, u32[]{:S(2)}) collective-permute-start(bf16[96,256]{1,0:T(8,128)(2,1)S(1)} %get-tuple-element.92.dep_ref.refs_0_), channel_id=1, source_target_pairs={{0,8},{1,9},{2,10},{3,11},{4,12},{5,13},{6,14},{7,15},{8,0},{9,1},... | collective-permute-start | bytes 147464 | tf_op jit(solution)/shard_map/ppermute | solution.py:393
  129.0 12.4 %collective-permute-start.35 = (bf16[96,256]{1,0:T(8,128)(2,1)S(1)}, bf16[96,256]{1,0:T(8,128)(2,1)S(1)}, u32[]{:S(2)}, u32[]{:S(2)}) collective-permute-start(bf16[96,256]{1,0:T(8,128)(2,1)S(1)} %get-tuple-element.92.dep_ref.refs_0_), channel_id=1, source_target_pairs={{0,4},{1,5},{2,6},{3,7},{4,0},{5,1},{6,2},{7,3},{8,12},{9,13},{10,... | collective-permute-start | bytes 147464 | tf_op jit(solution)/shard_map/ppermute | solution.py:393
  141.5 8.8 %collective-permute-start.39 = (bf16[384,256]{1,0:T(8,128)(2,1)S(1)}, bf16[384,256]{1,0:T(8,128)(2,1)S(1)}, u32[]{:S(2)}, u32[]{:S(2)}) collective-permute-start(bf16[384,256]{1,0:T(8,128)(2,1)S(1)} %stack_parts.3.refs_4_), channel_id=1, source_target_pairs={{0,2},{1,3},{2,0},{3,1},{4,6},{5,7},{6,4},{7,5},{8,10},{9,11},{10,... | collective-permute-start | bytes 589832 | tf_op jit(solution)/shard_map/ppermute | solution.py:393
  148.2 9.9 %collective-permute-start.38 = (bf16[384,256]{1,0:T(8,128)(2,1)S(1)}, bf16[384,256]{1,0:T(8,128)(2,1)}, u32[]{:S(2)}, u32[]{:S(2)}) collective-permute-start(bf16[384,256]{1,0:T(8,128)(2,1)S(1)} %stack_parts.3.refs_4_), channel_id=1, source_target_pairs={{0,1},{1,0},{2,3},{3,2},{4,5},{5,4},{6,7},{7,6},{8,9},{9,8},{10,11... | collective-permute-start | bytes 589832 | tf_op jit(solution)/shard_map/ppermute | solution.py:393
  (44 other events, 356.4 us)

commit v5 on v4

v5 whole, which is shorter than its diff:
```python
import functools
import jax
import jax.numpy as jnp
from jax import lax
from jax.experimental import pallas as pl
from jax.experimental.pallas import tpu as pltpu
from jax.sharding import PartitionSpec as P

diffusion_rate = 0.24
VMEM_BYTES = 40 * 1024 * 1024
EXTRA = 16
bf16 = jnp.bfloat16
f32 = jnp.float32


def params():
    return pltpu.CompilerParams(vmem_limit_bytes=VMEM_BYTES)


def scenario_block(scenarios):
    for size in (64, 32, 16):
        if scenarios % size == 0:
            return size
    return scenarios


LANES = 128
SUBLANES = 8
GROUP = 16


def to_tiles(hist):
    scenarios, rows, columns = hist.shape
    high = min(rows, SUBLANES)
    tiles = hist.reshape(scenarios, rows // high, high, columns // LANES, LANES)
    return tiles.transpose(0, 1, 3, 2, 4).reshape(scenarios * rows * (columns // LANES), LANES)


def from_tiles(tiles, shape):
    scenarios, rows, columns = shape
    high = min(rows, SUBLANES)
    parts = tiles.reshape(scenarios, rows // high, columns // LANES, high, LANES)
    return parts.transpose(0, 1, 3, 2, 4).reshape(shape)


def tile_offset(row, lane_tile, rows, lane_tiles):
    high = min(rows, SUBLANES)
    return (row // high * lane_tiles + lane_tile) * high + row % high


def read_row(ref, first_scenario, count, row, rows, columns):
    lane_tiles = columns // LANES
    per = rows * lane_tiles
    return jnp.concatenate(
        [
            ref[pl.ds(first_scenario * per + tile_offset(row, t, rows, lane_tiles), count, stride=per), :]
            for t in range(lane_tiles)
        ],
        axis=1,
    )


def write_row(ref, first_scenario, count, row, rows, columns, values):
    lane_tiles = columns // LANES
    per = rows * lane_tiles
    for t in range(lane_tiles):
        place = pl.ds(first_scenario * per + tile_offset(row, t, rows, lane_tiles), count, stride=per)
        ref[place, :] = values[:, t * LANES : (t + 1) * LANES]


def drift_tail(drift_ref, start):
    pieces = [
        jnp.concatenate([drift_ref[c, start : start + 1], drift_ref[c, start + 1 : start + 2]], axis=1)
        for c in range(2)
    ]
    high, low = two_halves(jnp.concatenate(pieces, axis=0))
    ones = jnp.ones((1, high.shape[1]), bf16)
    zeros = jnp.zeros((EXTRA - 5, high.shape[1]), bf16)
    return jnp.concatenate([high, low, ones, zeros], axis=0)


def band_matrix(columns):
    row = lax.broadcasted_iota(jnp.int32, (columns, columns), 0)
    column = lax.broadcasted_iota(jnp.int32, (columns, columns), 1)
    right = jnp.where(column == row + 1, 1.0, 0.0)
    left = jnp.where(column == row - 1, 1.0, 0.0)
    centre = jnp.where(column == row, 1.0 - 4.0 * diffusion_rate, diffusion_rate * (right + left))
    return centre.astype(bf16), (right - left).astype(bf16)


def half_shifts(levels_ref, table_ref, shift_ref):
    scenarios = levels_ref.shape[1]
    for t in range(levels_ref.shape[0]):
        level = jnp.broadcast_to(levels_ref[t : t + 1, :].astype(f32), (LANES, scenarios)).T
        for c in range(2):
            shift = jnp.zeros(level.shape, f32)
            for n in range(table_ref.shape[1]):
                shift = jnp.where(level == n, 0.5 * table_ref[c : c + 1, n : n + 1], shift)
            shift_ref[2 * t + c] = shift


def wide(values, columns):
    return jnp.concatenate([values] * (columns // LANES), axis=1)


def one_step(rows_of, places, half_drift, band, shift_x, shift_y, pairs, terms, write):
    size, columns = shift_x.shape
    whole = pl.ds(0, columns)

    def density(row):
        return pairs[pl.ds(rows_of[row] * size, size), whole].astype(f32)

    for row in places:
        flux = (half_drift(1, row) + shift_y) * density(row)
        pairs[pl.ds(rows_of[row] * size, size), pl.ds(columns, columns)] = flux.astype(bf16)
    start = rows_of[places[0]] * size
    count = (rows_of[places[-1]] + 1) * size - start
    terms[pl.ds(start, count), :] = jnp.dot(pairs[pl.ds(start, count), :], band, preferred_element_type=f32)
    for row in places:
        low = density(row - 1) * ((diffusion_rate + half_drift(0, row - 1)) + shift_x)
        high = density(row + 1) * ((diffusion_rate - half_drift(0, row + 1)) - shift_x)
        write(row, terms[pl.ds(rows_of[row] * size, size), :] + low + high)


def two_steps(segments, read, half_drift, edge, band, shifts, scratch, write):
    pairs, later, terms = scratch
    size, columns = shifts[0].shape
    before, between, after = [
        [row for first, last in segments for row in range(first - more, last + more + 1)] for more in (2, 1, 0)
    ]
    rows_of = {row: k for k, row in enumerate(before)}
    for row, k in rows_of.items():
        pairs[pl.ds(k * size, size), pl.ds(0, columns)] = read(row)

    def write_later(row, density):
        later[pl.ds(rows_of[row] * size, size), pl.ds(0, columns)] = edge(row, density).astype(bf16)

    one_step(rows_of, between, half_drift, band, shifts[0], shifts[1], pairs, terms, write_later)
    one_step(rows_of, after, half_drift, band, shifts[2], shifts[3], later, terms, write)


def step_scratch(segments, size, columns):
    rows = sum(last - first + 5 for first, last in segments)
    pairs = pltpu.VMEM((rows * size, 2 * columns), bf16)
    return [pairs, pairs, pltpu.VMEM((rows * size, columns), f32)]


def edge_segments(rows):
    return [(0, 1), (rows - 2, rows - 1)] if rows >= 8 else [(0, rows - 1)]


def inner_kernel(
    rows, size, hist_ref, drift_hbm, levels_hbm, table_hbm,
    first_ref, last_ref, shift_ref, band_ref, rows_ref, inner_ref,
    drift_ref, levels_ref, table_ref, arrived, all_shifts, *scratch,
):
    step = pl.program_id(0)
    columns = drift_ref.shape[2]

    @pl.when(step == 0)
    def _():
        sources = ((drift_hbm, drift_ref), (levels_hbm, levels_ref), (table_hbm, table_ref))
        copies = [pltpu.make_async_copy(*pair, arrived.at[n]) for n, pair in enumerate(sources)]
        for copy in copies:
            copy.start()
        centre, flux = band_matrix(columns)
        band_ref[pl.ds(0, columns), :] = centre
        band_ref[pl.ds(columns, columns), :] = flux
        for copy in copies:
            copy.wait()
        half_shifts(levels_ref, table_ref, all_shifts)
        for out, start in ((first_ref, 0), (last_ref, rows - 2)):
            out[pl.ds(out.shape[0] - EXTRA, EXTRA), :] = drift_tail(drift_ref, start)

    where = pl.ds(pl.multiple_of(step * size, size), size)
    for n in range(4):
        shift_ref[n] = all_shifts[n, where, :]
    for row in range(rows):
        density = read_row(hist_ref, 0, size, row, rows, columns).astype(bf16)
        rows_ref[:, pl.ds(row * columns, columns)] = density
        if row < 2:
            first_ref[where, pl.ds(row * columns, columns)] = density
        if row >= rows - 2:
            last_ref[where, pl.ds((row - rows + 2) * columns, columns)] = density
    if rows <= 4:
        return

    def write(row, density):
        inner_ref[:, pl.ds((row - 2) * columns, columns)] = density.astype(bf16)

    two_steps(
        [(2, rows - 3)],
        lambda row: rows_ref[:, pl.ds(row * columns, columns)],
        lambda c, row: 0.5 * drift_ref[c, row : row + 1, :],
        lambda row, density: density,
        band_ref[...],
        [wide(shift_ref[n], columns) for n in range(4)],
        scratch,
        write,
    )


def inner_steps(tiles, drift, levels, table):
    scenarios = levels.shape[1]
    rows, columns = drift.shape[1:]
    per = tiles.shape[0] // scenarios
    size = scenario_block(scenarios)
    inner = max(rows - 4, 1) * columns
    sent = jax.ShapeDtypeStruct((scenarios + EXTRA, 2 * columns), bf16)
    shifts = jax.ShapeDtypeStruct((4, scenarios, LANES), f32)
    band = jax.ShapeDtypeStruct((2 * columns, columns), bf16)
    return pl.pallas_call(
        functools.partial(inner_kernel, rows, size),
        grid=(scenarios // size,),
        in_specs=[pl.BlockSpec((size * per, LANES), lambda i: (i, 0))] + [pl.BlockSpec(memory_space=pltpu.HBM)] * 3,
        out_specs=[pl.BlockSpec(sent.shape, lambda i: (0, 0))] * 2
        + [
            pl.BlockSpec((4, size, LANES), lambda i: (0, i, 0)),
            pl.BlockSpec(band.shape, lambda i: (0, 0)),
            pl.BlockSpec((size, rows * columns), lambda i: (i, 0)),
            pl.BlockSpec((size, inner), lambda i: (i, 0)),
        ],
        out_shape=[
            sent,
            sent,
            shifts,
            band,
            jax.ShapeDtypeStruct((scenarios, rows * columns), bf16),
            jax.ShapeDtypeStruct((scenarios, inner), bf16),
        ],
        scratch_shapes=[
            pltpu.VMEM(drift.shape, f32),
            pltpu.VMEM(levels.shape, levels.dtype),
            pltpu.VMEM(table.shape, f32),
            pltpu.SemaphoreType.DMA((3,)),
            pltpu.VMEM(shifts.shape, f32),
        ]
        + step_scratch([(2, max(rows - 3, 2))], size, columns),
        compiler_params=params(),
        cost_estimate=pl.CostEstimate(flops=1, bytes_accessed=1, transcendentals=0),
        name="inner_density_steps",
    )(tiles, drift, levels, table)


def halo_drift(ref, columns):
    tail = ref[...].astype(f32)
    both = 0.5 * (tail[0:2] + tail[2:4])
    rows = [[both[c : c + 1, k * columns : (k + 1) * columns] for k in range(2)] for c in range(2)]
    return rows, tail[4:5, :columns]


def with_halo(drift_ref, below_tail, above_tail):
    rows, columns = drift_ref.shape[1:]
    below, below_valid = halo_drift(below_tail, columns)
    above, above_valid = halo_drift(above_tail, columns)

    def half_drift(c, row):
        if row < 0:
            return below[c][row + 2]
        if row >= rows:
            return above[c][row - rows]
        return 0.5 * drift_ref[c, row : row + 1, :]

    def edge(row, density):
        if row < 0:
            return density * below_valid
        if row >= rows:
            return density * above_valid
        return density

    return half_drift, edge


def density_kernel(segments, drift_ref, shift_ref, band_ref, rows_ref, below_ref, above_ref, below_tail, above_tail, dep_ref, *refs):
    scratch = refs[-3:]
    rows, columns = drift_ref.shape[1:]
    size = shift_ref.shape[1]
    half_drift, edge = with_halo(drift_ref, below_tail, above_tail)

    def read(row):
        if row < 0:
            return below_ref[:, pl.ds((row + 2) * columns, columns)]
        if row >= rows:
            return above_ref[:, pl.ds((row - rows) * columns, columns)]
        return rows_ref[:, pl.ds(row * columns, columns)]

    if segments is None:
        next_ref, token_ref = refs[-5:-3]
        token_ref[...] = jnp.zeros(token_ref.shape, f32)

        def write(row, density):
            write_row(next_ref, 0, size, row, rows, columns, density)

    else:
        low_ref, high_ref = refs[-5:-3]

        def write(row, density):
            if row < 2:
                low_ref[:, pl.ds(row * columns, columns)] = density.astype(bf16)
            else:
                high_ref[:, pl.ds((row - rows + 2) * columns, columns)] = density.astype(bf16)

    shifts = [wide(shift_ref[n], columns) for n in range(4)]
    two_steps(segments or [(0, rows - 1)], read, half_drift, edge, band_ref[...], shifts, scratch, write)


def density_specs(drift, shifts, band, own, below, size, first):
    columns = drift.shape[2]
    scenarios = shifts.shape[1]
    halo = pl.BlockSpec((size, 2 * columns), lambda i: (first + i, 0))
    tail = pl.BlockSpec((EXTRA, 2 * columns), lambda i: (scenarios // EXTRA, 0))
    return [
        pl.BlockSpec(drift.shape, lambda i: (0, 0, 0)),
        pl.BlockSpec((4, size, LANES), lambda i: (0, first + i, 0)),
        pl.BlockSpec(band.shape, lambda i: (0, 0)),
        pl.BlockSpec((size, own.shape[1]), lambda i: (first + i, 0)),
        halo,
        halo,
        tail,
        tail,
        pl.BlockSpec(memory_space=pl.ANY),
    ]


def edge_steps(drift, shifts, band, own, below, above, dep):
    scenarios = shifts.shape[1]
    rows, columns = drift.shape[1:]
    size = 2 * scenario_block(scenarios)
    size = size if scenarios % size == 0 else size // 2
    edge = jax.ShapeDtypeStruct((scenarios, 2 * columns), bf16)
    spec = pl.BlockSpec((size, 2 * columns), lambda i: (i, 0))
    segments = edge_segments(rows)
    return pl.pallas_call(
        functools.partial(density_kernel, segments),
        grid=(scenarios // size,),
        in_specs=density_specs(drift, shifts, band, own, below, size, 0),
        out_specs=[spec, spec],
        out_shape=[edge, edge],
        scratch_shapes=step_scratch(segments, size, columns),
        compiler_params=params(),
        cost_estimate=pl.CostEstimate(flops=1, bytes_accessed=1, transcendentals=0),
        name="edge_density_steps",
    )(drift, shifts, band, own, below, above, below, above, dep)


def density_steps(drift, shifts, band, own, below, above, dep, so_far, turn, turns):
    scenarios = shifts.shape[1]
    rows, columns = drift.shape[1:]
    per = rows * (columns // LANES)
    size = 3 * GROUP if scenarios % (turns * GROUP * 3) == 0 else GROUP
    steps = scenarios // size // turns
    first = turn * steps
    args = [drift, shifts, band, own, below, above, below, above, dep]
    in_specs = density_specs(drift, shifts, band, own, below, size, first)
    aliases = {}
    if so_far is not None:
        aliases = {len(args): 0}
        args.append(so_far)
        in_specs.append(pl.BlockSpec(memory_space=pltpu.HBM))
    return pl.pallas_call(
        functools.partial(density_kernel, None),
        grid=(steps,),
        in_specs=in_specs,
        out_specs=[
            pl.BlockSpec((size * per, LANES), lambda i: (first + i, 0)),
            pl.BlockSpec((SUBLANES, LANES), lambda i: (0, 0)),
        ],
        out_shape=[pltpu.HBM((scenarios * per, LANES), f32), jax.ShapeDtypeStruct((SUBLANES, LANES), f32)],
        input_output_aliases=aliases,
        scratch_shapes=step_scratch([(0, rows - 1)], size, columns),
        compiler_params=params(),
        cost_estimate=pl.CostEstimate(flops=1, bytes_accessed=1, transcendentals=0),
        name="density_steps",
    )(*args)


def smem():
    return pl.BlockSpec(memory_space=pltpu.SMEM)


def vmem():
    return pl.BlockSpec(memory_space=pltpu.VMEM)


def swap(values, count, flip):
    return lax.ppermute(values, "grid", [(i, i ^ flip) for i in range(count)])


def inner_product_kernel(count, inputs_ref, *refs):
    weight = jnp.concatenate([ref[...] for ref in refs[:count]], axis=0)
    refs[-1][pl.program_id(0)] = jnp.dot(inputs_ref[...], weight, preferred_element_type=f32)


def inner_product(inner, weight, width):
    scenarios, cells = inner.shape
    total, hidden = weight.shape
    size = (total - cells) // 2
    count = cells // size

    def spec(k):
        return pl.BlockSpec((size, width), lambda n: (1 + k, n))

    return pl.pallas_call(
        functools.partial(inner_product_kernel, count),
        grid=(hidden // width,),
        in_specs=[vmem()] + [spec(k) for k in range(count)],
        out_specs=vmem(),
        out_shape=jax.ShapeDtypeStruct((hidden // width, scenarios, width), f32),
        compiler_params=params(),
        cost_estimate=pl.CostEstimate(flops=1, bytes_accessed=1, transcendentals=0),
        name="inner_product",
    )(inner, *([weight] * count))


def edge_product_kernel(block, with_inner, place_ref, low_ref, high_ref, top_ref, bottom_ref, *refs):
    keep_ref, send_ref, total = refs[-3:]
    step = pl.program_id(0)
    left = jnp.concatenate([low_ref[...], high_ref[...]], axis=1)
    weight = jnp.concatenate([top_ref[...], bottom_ref[...]], axis=0)
    product = jnp.dot(left, weight, preferred_element_type=f32)
    total[...] = product + refs[0][step] if with_inner else product
    core = place_ref[0]
    for out, half in ((keep_ref, core), (send_ref, 1 - core)):
        for side in range(2):
            start = pl.multiple_of((2 * half + side) * block, block)
            out[side, step] = total[pl.ds(start, block), :].astype(out.dtype)


def edge_product(place, low, high, weight, inner, parts, width):
    scenarios, size = low.shape
    block = scenarios // 4
    last = weight.shape[0] // size - 1
    shape = (2, parts, block, width)
    in_specs = [
        smem(),
        vmem(),
        vmem(),
        pl.BlockSpec((size, width), lambda n: (0, n)),
        pl.BlockSpec((size, width), lambda n: (last, n)),
    ]
    args = [place, low, high, weight, weight]
    if inner is not None:
        in_specs.append(vmem())
        args.append(inner)
    return pl.pallas_call(
        functools.partial(edge_product_kernel, block, inner is not None),
        grid=(parts,),
        in_specs=in_specs,
        out_specs=[vmem(), vmem()],
        out_shape=[jax.ShapeDtypeStruct(shape, f32), jax.ShapeDtypeStruct(shape, bf16)],
        scratch_shapes=[pltpu.VMEM((scenarios, width), f32)],
        compiler_params=params(),
        cost_estimate=pl.CostEstimate(flops=1, bytes_accessed=1, transcendentals=0),
        name="edge_product",
    )(*args)


def add_side_kernel(place_ref, mine_ref, other_ref, *refs):
    keep_ref, send_ref = refs[-2:]
    side = place_ref[1]
    keep_ref[...] = mine_ref[side] + other_ref[side].astype(f32)
    send_ref[...] = (mine_ref[1 - side] + other_ref[1 - side].astype(f32)).astype(bf16)


def any_specs(deps):
    return [pl.BlockSpec(memory_space=pl.ANY)] * len(deps)


def add_side(place, mine, other, deps=()):
    shape = mine.shape[1:]
    return pl.pallas_call(
        add_side_kernel,
        in_specs=[smem()] + [vmem()] * 2 + any_specs(deps),
        out_shape=[jax.ShapeDtypeStruct(shape, f32), jax.ShapeDtypeStruct(shape, bf16)],
        compiler_params=params(),
        cost_estimate=pl.CostEstimate(flops=1, bytes_accessed=1, transcendentals=0),
        name="add_side",
    )(place, mine, other, *deps)


def add_parts_kernel(dep_count, place_ref, mine_ref, other_ref, *refs):
    own_ref, *send_refs = refs[dep_count:]
    part = place_ref[2]
    own_ref[...] = mine_ref[part] + other_ref[part].astype(f32)
    for k, out in enumerate(send_refs):
        at = part ^ (k + 1)
        out[...] = (mine_ref[at] + other_ref[at].astype(f32)).astype(bf16)


def add_parts(place, mine, other, deps=()):
    parts = mine.shape[0]
    return pl.pallas_call(
        functools.partial(add_parts_kernel, len(deps)),
        in_specs=[smem(), vmem(), vmem()] + any_specs(deps),
        out_shape=[jax.ShapeDtypeStruct(mine.shape[1:], f32)]
        + [jax.ShapeDtypeStruct(mine.shape[1:], bf16)] * (parts - 1),
        compiler_params=params(),
        cost_estimate=pl.CostEstimate(flops=1, bytes_accessed=1, transcendentals=0),
        name="add_parts",
    )(place, mine, other, *deps)


def activate_kernel(count, *refs):
    total = refs[0][...]
    for ref in refs[1 : 1 + count]:
        total = total + ref[...].astype(f32)
    refs[-1][...] = jnp.tanh(total).astype(bf16)


def activate(own, received, deps=()):
    return pl.pallas_call(
        functools.partial(activate_kernel, len(received)),
        in_specs=[vmem()] * (1 + len(received)) + any_specs(deps),
        out_shape=jax.ShapeDtypeStruct(own.shape, bf16),
        compiler_params=params(),
        cost_estimate=pl.CostEstimate(flops=1, bytes_accessed=1, transcendentals=0),
        name="first_activation",
    )(own, *received, *deps)


def pack_kernel(mid_ref, head_ref, *refs):
    out_ref = refs[-1]
    hidden = mid_ref.shape[0]
    out_ref[pl.ds(0, hidden), :] = mid_ref[...]
    out_ref[pl.ds(hidden, EXTRA), :] = tail_rows(head_ref[...])


def pack(mid_weight, head, deps):
    hidden, units = mid_weight.shape
    return pl.pallas_call(
        pack_kernel,
        in_specs=[vmem()] * 2 + any_specs(deps),
        out_shape=jax.ShapeDtypeStruct((hidden + EXTRA, units), bf16),
        compiler_params=params(),
        cost_estimate=pl.CostEstimate(flops=1, bytes_accessed=1, transcendentals=0),
        name="mid_with_head",
    )(mid_weight, head, *deps)


def two_halves(exact):
    high = exact.astype(bf16)
    low = (exact - high.astype(f32)).astype(bf16)
    return high, low


def tail_rows(exact):
    high, low = two_halves(exact)
    zeros = jnp.zeros((EXTRA - 2, exact.shape[1]), bf16)
    return jnp.concatenate([high, low, zeros], axis=0)


def middle_kernel(chunks, parts, width, *refs):
    pieces = chunks * parts
    place_ref, cot_ref = refs[0], refs[1]
    first_refs = refs[2 : 2 + pieces]
    mid_refs = refs[2 + pieces : 6 + pieces]
    outs = refs[-(3 + parts) :]
    own_ref, value_ref, mid_keep_ref, mid_send_ref = outs[:4]
    send_refs = outs[4:]
    part = place_ref[2]
    block = cot_ref.shape[0]

    def mid_rows(start):
        return jnp.concatenate([ref[pl.ds(start, width), :] for ref in mid_refs], axis=1)

    def start_of(c, k):
        return pl.multiple_of((c * parts + (part ^ k)) * width, width)

    total = None
    for c in range(chunks):
        for k in range(parts):
            term = jnp.dot(first_refs[c * parts + k][...], mid_rows(start_of(c, k)), preferred_element_type=f32)
            total = term if total is None else total + term
    second_low = jnp.tanh(total).astype(bf16)
    second = second_low.astype(f32)
    heads = jnp.concatenate([ref[pl.ds(pieces * width, EXTRA), :] for ref in mid_refs], axis=1)
    head = heads[0:1].astype(f32) + heads[1:2].astype(f32)
    rows = lax.dot_general(heads, second_low, (((1,), (1,)), ((), ())), preferred_element_type=f32)
    value = rows[0:1] + rows[1:2]
    if width > block:
        value = jnp.concatenate([value, jnp.zeros((1, width - block), f32)], axis=1)
    value_ref[...] = value
    cot = cot_ref[...]
    head_part = jnp.sum(cot * second, axis=0, keepdims=True)
    back = (cot * head * (1.0 - second * second)).astype(bf16)
    units = mid_refs[0].shape[1]
    for k in range(parts):
        for c in range(chunks):
            piece = lax.dot_general(
                back, mid_rows(start_of(c, k)), (((1,), (1,)), ((), ())), preferred_element_type=f32
            )
            if k == 0:
                own_ref[pl.ds(c * block, block), :] = piece
            else:
                send_refs[k - 1][pl.ds(c * block, block), :] = piece.astype(bf16)
        if k > 0:
            send_refs[k - 1][pl.ds(chunks * block, EXTRA), :] = tail_rows(value)
    for c in range(chunks):
        for k in range(parts):
            product = lax.dot_general(
                first_refs[c * parts + k][...], back, (((0,), (0,)), ((), ())), preferred_element_type=f32
            ).astype(bf16)
            for p in range(4):
                out = (mid_keep_ref, mid_send_ref)[p % 2]
                out[p // 2, pl.ds(start_of(c, k), width), :] = product[:, p * units : (p + 1) * units]
    for p in range(4):
        out = (mid_keep_ref, mid_send_ref)[p % 2]
        out[p // 2, pl.ds(pieces * width, EXTRA), :] = tail_rows(head_part[:, p * units : (p + 1) * units])


def middle(place, cot, firsts, mids, chunks, parts, width, deps=()):
    block = cot.shape[0]
    partial = jax.ShapeDtypeStruct((2, *mids[0].shape), bf16)
    return pl.pallas_call(
        functools.partial(middle_kernel, chunks, parts, width),
        in_specs=[smem()] + [vmem()] * (1 + len(firsts) + 4) + any_specs(deps),
        out_shape=[
            jax.ShapeDtypeStruct((chunks * block, width), f32),
            jax.ShapeDtypeStruct((1, width), f32),
            partial,
            partial,
        ]
        + [jax.ShapeDtypeStruct((chunks * block + EXTRA, width), bf16)] * (parts - 1),
        compiler_params=params(),
        cost_estimate=pl.CostEstimate(flops=1, bytes_accessed=1, transcendentals=0),
        name="value_layers",
    )(place, cot, *firsts, *mids, *deps)


def add_tail(left, right, hidden):
    body = left[:hidden].astype(f32) + right[:hidden].astype(f32)
    tails = left[hidden:].astype(f32) + right[hidden:].astype(f32)
    return body.astype(bf16), tails[0:1] + tails[1:2]


def mid_add_kernel(keep_ref, other_ref, *refs):
    own_ref, send_ref = refs[-2:]
    hidden = own_ref.shape[0] - EXTRA
    for at, out in enumerate((own_ref, send_ref)):
        body, tail = add_tail(keep_ref[at], other_ref[at], hidden)
        out[pl.ds(0, hidden), :] = body
        out[pl.ds(hidden, EXTRA), :] = tail_rows(tail)


def mid_add(keep, other, deps=()):
    shape = jax.ShapeDtypeStruct(keep.shape[1:], bf16)
    return pl.pallas_call(
        mid_add_kernel,
        in_specs=[vmem()] * 2 + any_specs(deps),
        out_shape=[shape, shape],
        compiler_params=params(),
        cost_estimate=pl.CostEstimate(flops=1, bytes_accessed=1, transcendentals=0),
        name="mid_gradient_add",
    )(keep, other, *deps)


def mid_final_kernel(own_ref, other_ref, *refs):
    out_ref, head_ref = refs[-2:]
    body, tail = add_tail(own_ref[...], other_ref[...], out_ref.shape[0])
    out_ref[...] = body
    head_ref[...] = tail


def mid_final(own, other, deps=()):
    hidden = own.shape[0] - EXTRA
    return pl.pallas_call(
        mid_final_kernel,
        in_specs=[vmem()] * 2 + any_specs(deps),
        out_shape=[
            jax.ShapeDtypeStruct((hidden, own.shape[1]), bf16),
            jax.ShapeDtypeStruct((1, own.shape[1]), f32),
        ],
        compiler_params=params(),
        cost_estimate=pl.CostEstimate(flops=1, bytes_accessed=1, transcendentals=0),
        name="mid_gradient_final",
    )(own, other, *deps)


def back_first_kernel(chunks, count, *refs):
    own_ref, value_ref = refs[:2]
    received = refs[2 : 2 + count]
    first_refs = refs[2 + count : 2 + count + chunks]
    out_refs = refs[-1 - chunks : -1]
    tail_ref = refs[-1]
    block = first_refs[0].shape[0]
    value = value_ref[...]
    for ref in received:
        tail = ref[pl.ds(chunks * block, EXTRA), :].astype(f32)
        value = value + (tail[0:1] + tail[1:2])
    tail_ref[...] = tail_rows(value)
    for c in range(chunks):
        total = own_ref[pl.ds(c * block, block), :]
        for ref in received:
            total = total + ref[pl.ds(c * block, block), :].astype(f32)
        first = first_refs[c][...].astype(f32)
        out_refs[c][...] = (total * (1.0 - first * first)).astype(bf16)


def back_first(own, value, received, firsts, deps=()):
    chunks = len(firsts)
    shape = firsts[0].shape
    return pl.pallas_call(
        functools.partial(back_first_kernel, chunks, len(received)),
        in_specs=[vmem()] * (2 + len(received) + chunks) + any_specs(deps),
        out_shape=[jax.ShapeDtypeStruct(shape, bf16)] * chunks
        + [jax.ShapeDtypeStruct((EXTRA, shape[1]), bf16)],
        compiler_params=params(),
        cost_estimate=pl.CostEstimate(flops=1, bytes_accessed=1, transcendentals=0),
        name="back_first",
    )(own, value, *received, *firsts, *deps)


def stack_kernel(count, halves, *refs):
    outs = refs[-halves:]
    width = outs[0].shape[1]
    at = 0
    for ref in refs[:count]:
        for n, out in enumerate(outs):
            out[pl.ds(at, ref.shape[0]), :] = ref[:, pl.ds(n * width, width)]
        at += ref.shape[0]


def stack(pieces, halves, deps=()):
    rows = sum(piece.shape[0] for piece in pieces)
    shape = jax.ShapeDtypeStruct((rows, pieces[0].shape[1] // halves), bf16)
    return pl.pallas_call(
        functools.partial(stack_kernel, len(pieces), halves),
        in_specs=[vmem()] * len(pieces) + any_specs(deps),
        out_shape=[shape] * halves,
        compiler_params=params(),
        cost_estimate=pl.CostEstimate(flops=1, bytes_accessed=1, transcendentals=0),
        name="stack_parts",
    )(*pieces, *deps)


def turn_kernel(count, *refs):
    for ref, out in zip(refs[:count], refs[-count:]):
        out[...] = ref[...].T


def transposed(arrays, deps):
    return pl.pallas_call(
        functools.partial(turn_kernel, len(arrays)),
        in_specs=[vmem()] * len(arrays) + any_specs(deps),
        out_shape=[jax.ShapeDtypeStruct(array.shape[::-1], array.dtype) for array in arrays],
        compiler_params=params(),
        cost_estimate=pl.CostEstimate(flops=1, bytes_accessed=1, transcendentals=0),
        name="transposed_inputs",
    )(*arrays, *deps)


def first_grad_kernel(parts, block, count, with_value, *refs):
    place_ref = refs[0]
    lefts = refs[1 : 1 + count]
    stacks = refs[1 + count : 5 + count]
    outs = refs[-3:-1] if with_value else refs[-2:-1]
    whole = refs[-1]
    step = pl.program_id(0)
    mine = place_ref[3]
    for t, ref in enumerate(stacks):
        at = mine ^ (2 * (t % 2) + t // 2)
        piece = step ^ place_ref[2]
        whole[pl.ds(pl.multiple_of(at * block, block), block), :] = ref[
            pl.ds(pl.multiple_of(piece * block, block), block), :
        ]
        if with_value:
            tail = ref[pl.ds(parts * block, EXTRA), :].astype(f32)
            outs[1][pl.ds(at, 1), :] = tail[0:1] + tail[1:2]
    start = 0
    for ref in lefts:
        cells = ref.shape[0]
        outs[0][pl.ds(start, cells), :] = jnp.dot(ref[...], whole[...], preferred_element_type=f32).astype(bf16)
        start += cells


def first_grad(place, lefts, stacks, so_far, hidden, parts, block, half, halves, deps):
    scenarios = lefts[0].shape[1]
    cells = sum(left.shape[0] for left in lefts)
    width = stacks[0].shape[1]
    with_value = half == 0
    in_specs = [smem()] + [vmem()] * (len(lefts) + 4) + any_specs(deps)
    args = [place, *lefts, *stacks, *deps]
    aliases = {}
    if so_far is not None:
        aliases = {len(args): 0}
        in_specs.append(pl.BlockSpec(memory_space=pltpu.HBM))
        args.append(so_far)
    out_specs = [pl.BlockSpec((cells, width), lambda i: (0, i * halves + half))]
    out_shape = [pltpu.HBM((cells, hidden), bf16)]
    if with_value:
        out_specs.append(pl.BlockSpec((4, width), lambda i: (0, 0)))
        out_shape.append(jax.ShapeDtypeStruct((4, width), f32))
    return pl.pallas_call(
        functools.partial(first_grad_kernel, parts, block, len(lefts), with_value),
        grid=(parts,),
        in_specs=in_specs,
        out_specs=out_specs,
        out_shape=out_shape,
        input_output_aliases=aliases,
        scratch_shapes=[pltpu.VMEM((scenarios, width), bf16)],
        compiler_params=params(),
        cost_estimate=pl.CostEstimate(flops=1, bytes_accessed=1, transcendentals=0),
        name="first_gradient",
    )(*args)


def local(hist, drift, shocks, shock_table, first_weight, mid_weight, head_weight, cotangent):
    scenarios, rows, columns = hist.shape
    count = lax.axis_size("grid")
    hidden = first_weight.shape[1]
    units = mid_weight.shape[1]
    parts = count // 4
    width = hidden // parts
    block = scenarios // 4
    index = lax.axis_index("grid")
    core, side, part = index % 2, index // 2 % 2, index // 4
    mine = 2 * core + side
    tiles = pltpu.with_memory_space_constraint(to_tiles(hist), pltpu.HBM)

    place = jnp.stack([core, side, part, mine])
    cot = lax.dynamic_slice_in_dim(cotangent, mine * block, block)[:, None]
    halves = 2 if width % 256 == 0 else 1

    small = [pltpu.with_memory_space_constraint(array, pltpu.HBM) for array in (drift, shocks.T, shock_table.T)]
    first_rows, last_rows, shifts, band, own_rows, inner = inner_steps(tiles, *small)
    inner = inner if rows > 4 else None
    forward = [(i, i + 1) for i in range(count - 1)]
    backward = [(i + 1, i) for i in range(count - 1)]
    below = lax.ppermute(last_rows, "grid", forward)
    above = lax.ppermute(first_rows, "grid", backward)
    product = None if inner is None else inner_product(inner, first_weight, width)
    low, high = edge_steps(drift, shifts, band, own_rows, below, above, own_rows if product is None else product)

    def density_turn(turn, dep, so_far):
        return density_steps(drift, shifts, band, own_rows, below, above, dep, so_far, turn, 2)

    keep, send = edge_product(place, low, high, first_weight, product, parts, width)
    mids = [pack(mid_weight, head_weight[None, :], [send])]
    keep, send = add_side(place, keep, swap(send, count, 1), mids)
    other = swap(send, count, 2)
    density, token = density_turn(0, send, None)
    own, *sends = add_parts(place, keep, other, [token])
    received = [swap(piece, count, 4 * (k + 1)) for k, piece in enumerate(sends)]
    mids.append(swap(mids[0], count, 1))
    mids.append(swap(mids[0], count, 2))
    mids.append(swap(mids[2], count, 1))
    first = activate(own, received, [mids[2]])
    firsts = [first] + [swap(first, count, 4 * k) for k in range(1, parts)]
    density, token = density_turn(1, first, density)
    own, value, mid_keep, mid_send, *sends = middle(place, cot, firsts, mids, 1, parts, width, [token])
    received = [swap(piece, count, 4 * (k + 1)) for k, piece in enumerate(sends)]
    back, tail = back_first(own, value, received, [first])
    mid_keep, mid_send = mid_add(mid_keep, swap(mid_send, count, 1), [back])
    lefts = transposed([low, high] if inner is None else [low, inner, high], [back])
    pieces = [back] + [swap(back, count, 4 * k) for k in range(1, parts)]
    stacks = stack(pieces + [tail], halves, [lefts[0]])
    grad_mid, grad_head = mid_final(mid_keep, swap(mid_send, count, 2), stacks[:1])
    grad_first = None
    for half, own_stack in enumerate(stacks):
        gathered = [own_stack, swap(own_stack, count, 1), swap(own_stack, count, 2)]
        gathered.append(swap(gathered[2], count, 1))
        results = first_grad(
            place, lefts, gathered, grad_first, hidden, parts, block, half, halves, [grad_head]
        )
        grad_first = results[0]
        if half == 0:
            value = results[1][:, :block].reshape(scenarios)
    return from_tiles(density, hist.shape), value, grad_first, grad_mid, grad_head[0]


def solution(mesh):
    in_specs = (
        P("groups", "grid", None),
        P(None, "grid", None),
        P("groups", None),
        P("groups", None),
        P(("groups", "grid"), None),
        P("groups", "grid"),
        P(("groups", "grid")),
        P("groups"),
    )
    out_specs = (
        P("groups", "grid", None),
        P("groups"),
        P(("groups", "grid"), None),
        P("groups", "grid"),
        P(("groups", "grid")),
    )
    return jax.shard_map(local, mesh=mesh, in_specs=in_specs, out_specs=out_specs, check_vma=False)
```

time: 167 us -> 154 us (0.922)
  starting transfers between devices: 50.2 us -> 32.2 us
  waiting for transfers between devices: 25.4 us -> 40.9 us
  Pallas kernels: 77.3 us -> 67.3 us
    ppermute x39 -> x25, starting transfers between devices: 45.8 us -> 27.9 us  [swap(): return lax.ppermute(values, 'grid', [(i, i ^ flip) for i in range(count)])]
    ppermute x39 -> x25, waiting for transfers between devices: 25.4 us -> 40.9 us  [swap(): return lax.ppermute(values, 'grid', [(i, i ^ flip) for i in range(count)])]
    pallas_call x12 -> x9, Pallas kernels: 40.1 us -> 30.2 us  [the longest x2 14.7 us: density_steps(): pl.pallas_call(functools.partial(density_kernel, None), grid=(steps,), in...]
    pallas_call x2 -> x1, Pallas kernels: 7.19 us -> 4.73 us  [edge_product(): pl.pallas_call(functools.partial(edge_product_kernel, block, inner is not...]
    unnamed x54 -> x48, local copies, waits for them, and re-layouts: 10.7 us -> 9.75 us
  transfers between devices with their start and end apart: 41 -> 27, of which waited for: 10 -> 10; matrix products, arithmetic and copies ran while one was open for 1% -> 1% of each run, Pallas kernels for 34% -> 23%
where the time goes in v5:
time: 154 us; the launch traced here: 153 us
  Pallas kernels  67.3 us (44%)
  waiting for transfers between devices  40.9 us (27%)
  starting transfers between devices  32.2 us (21%)
  local copies, waits for them, and re-layouts  11.2 us (7%)
    ppermute x25, waiting for transfers between devices, swap(): return lax.ppermute(values, 'grid', [(i, i ^ flip) for i in range(count)])  40.9 us
    ppermute x25, starting transfers between devices, swap(): return lax.ppermute(values, 'grid', [(i, i ^ flip) for i in range(count)])  27.9 us
    pallas_call x2, Pallas kernels, first_grad(): pl.pallas_call(functools.partial(first_grad_kernel, parts, block, len(lef...  14.7 us
    pallas_call x2, Pallas kernels, density_steps(): pl.pallas_call(functools.partial(density_kernel, None), grid=(steps,), in...  14.7 us
    pallas_call x1, Pallas kernels, inner_steps(): pl.pallas_call(functools.partial(inner_kernel, rows, size), grid=(scenari...  10.8 us
    unnamed x48, local copies, waits for them, and re-layouts  9.75 us
    pallas_call x1, Pallas kernels, inner_product(): pl.pallas_call(functools.partial(inner_product_kernel, count), grid=(hidd...  8.02 us
    pallas_call x1, Pallas kernels, edge_product(): pl.pallas_call(functools.partial(edge_product_kernel, block, inner is not...  4.73 us
  transfers between devices with their start and end apart: 27, of which 10 were waited for; matrix products, arithmetic and copies ran while one was open for 1% of the time, Pallas kernels for 23%

profile of v5, /device:TPU:0, one launch (start us, length us, event | category | flops | bytes accessed | tf_op | source)
XLA Modules:
  0.0 152.8 jit_solution(8424856613157527561)
XLA Ops:
  0.6 10.8 %inner_density_steps.1 = (bf16[400,512]{1,0:T(8,128)(2,1)}, bf16[400,512]{1,0:T(8,128)(2,1)}, f32[4,384,128]{2,1,0:T(8,128)S(1)}, bf16[512,256]{1,0:T(8,128)(2,1...) custom-call(f32[12288,128]{1,0:T(8,128)} %bitcast.23, f32[2,16,256]{2,1,0:T(8,128)} %drift_ref.5, ...), custom_call_target="tpu_custom_call" | custom-call | flops 1 | bytes 1 | tf_op jit(solution)/shard_map/inner_density_steps/pallas_call | solution.py:212
  13.1 3.1 %collective-permute-start = (bf16[400,512]{1,0:T(8,128)(2,1)}, bf16[400,512]{1,0:T(8,128)(2,1)}, u32[]{:S(2)}, u32[]{:S(2)}) collective-permute-start(bf16[400,512]{1,0:T(8,128)(2,1)} %get-tuple-element.48), channel_id=1, source_target_pairs={{0,1},{1,2},{2,3},{3,4},{4,5},{5,6},{6,7},{7,8},{8,9},{9,10},{10,1... | collective-permute-start | bytes 1228808 | tf_op jit(solution)/shard_map/ppermute | solution.py:829
  17.5 8.0 %inner_product.1.dep_ref.refs_0_ = f32[4,384,512]{2,1,0:T(8,128)S(1)} custom-call(bf16[384,3072]{1,0:T(8,128)(2,1)S(1)} %get-tuple-element.50.inputs_ref.refs_1_, bf16[4096,2048]{1,0:T(8,128)(2,1)} %bottom_ref.1, bf16[4096,2048]{1,0:T(8,128)(2,1)} %bottom_ref.1, bf16[4096,2048]{1,0:T(8,128)(2,1)} %bottom_ref.1, bf16[4096,2048]{1,0:T(8,128)(2,1)} %bottom_ref.1, ...), custom_call_target="tpu_custom_call" | custom-call | flops 1 | bytes 1 | tf_op jit(solution)/shard_map/inner_product/pallas_call | solution.py:403
  28.7 4.6 %edge_density_steps.1 = (bf16[384,512]{1,0:T(8,128)(2,1)S(1)}, bf16[384,512]{1,0:T(8,128)(2,1)S(1)}) custom-call(f32[2,16,256]{2,1,0:T(8,128)S(1)} %copy-done.14, f32[4,384,128]{2,1,0:T(8,128)S(1)} %copy-done.7, bf16[512,256]{1,0:T(8,128)(2,1)S(1)} %get-tuple-element.46.band_ref, bf16[384,4096]{1,0:T(8,128)(2,1)S(1)} %copy-done.2, ...), custom_call_target="tpu_custom_call" | custom-call | flops 1 | bytes 1 | tf_op jit(solution)/shard_map/edge_density_steps/pallas_call | solution.py:333
  33.4 4.7 %edge_product.1 = (f32[2,4,96,512]{3,2,1,0:T(8,128)S(1)}, bf16[2,4,96,512]{3,2,1,0:T(8,128)(2,1)S(1)}) custom-call(s32[4]{0:T(128)S(1)} %pad_add_fusion.place_ref.refs_0_, bf16[384,512]{1,0:T(8,128)(2,1)S(1)} %get-tuple-element.51.low_ref.refs_0_, bf16[384,512]{1,0:T(8,128)(2,1)S(1)} %get-tuple-element.52.high_ref.refs_2_, bf16[4096,2048]{1,0:T(8,128)(2,1)} %bottom_ref.1, ...), custom_call_target="tpu_custom_call" | custom-call | flops 1 | bytes 1 | tf_op jit(solution)/shard_map/edge_product/pallas_call | solution.py:445
  38.2 2.6 %collective-permute-start.2 = (bf16[2,4,96,512]{3,2,1,0:T(8,128)(2,1)S(1)}, bf16[2,4,96,512]{3,2,1,0:T(8,128)(2,1)S(1)}, u32[]{:S(2)}, u32[]{:S(2)}) collective-permute-start(bf16[2,4,96,512]{3,2,1,0:T(8,128)(2,1)S(1)} %get-tuple-element.54.refs_0_), channel_id=1, source_target_pairs={{0,1},{1,0},{2,3},{3,2},{4,5},{5,4},{6,7},{7,6},{8,9},{9,8},{10,11... | collective-permute-start | bytes 2359304 | tf_op jit(solution)/shard_map/ppermute | solution.py:386
  41.7 1.9 %collective-permute-start.7 = (bf16[2064,128]{1,0:T(8,128)(2,1)}, bf16[2064,128]{1,0:T(8,128)(2,1)}, u32[]{:S(2)}, u32[]{:S(2)}) collective-permute-start(bf16[2064,128]{1,0:T(8,128)(2,1)} %mid_with_head.1.refs_0_.refs_6_), channel_id=1, source_target_pairs={{0,2},{1,3},{2,0},{3,1},{4,6},{5,7},{6,4},{7,5},{8,10},{9,11},{10,... | collective-permute-start | bytes 1585160 | tf_op jit(solution)/shard_map/ppermute | solution.py:386
  45.5 11.3 %collective-permute-done.7.refs_4_.refs_8_ = bf16[2064,128]{1,0:T(8,128)(2,1)} collective-permute-done((bf16[2064,128]{1,0:T(8,128)(2,1)}, bf16[2064,128]{1,0:T(8,128)(2,1)}, u32[]{:S(2)}, u32[]{:S(2)}) %collective-permute-start.7) | collective-permute-done | bytes 528416 | tf_op jit(solution)/shard_map/ppermute | solution.py:386
  56.8 7.4 %density_steps.2 = (f32[12288,128]{1,0:T(8,128)}, f32[8,128]{1,0:T(8,128)S(1)}) custom-call(f32[2,16,256]{2,1,0:T(8,128)S(1)} %copy-done.14, f32[4,384,128]{2,1,0:T(8,128)S(1)} %copy-done.8, bf16[512,256]{1,0:T(8,128)(2,1)S(1)} %get-tuple-element.46.band_ref, bf16[384,4096]{1,0:T(8,128)(2,1)S(1)} %copy-done.3, ...), custom_call_target="tpu_custom_call" | custom-call | flops 1 | bytes 1 | tf_op jit(solution)/shard_map/density_steps/pallas_call | solution.py:360
  66.6 2.7 %collective-permute-start.4 = (bf16[96,512]{1,0:T(8,128)(2,1)}, bf16[96,512]{1,0:T(8,128)(2,1)S(1)}, u32[]{:S(2)}, u32[]{:S(2)}) collective-permute-start(bf16[96,512]{1,0:T(8,128)(2,1)} %get-tuple-element.59), channel_id=1, source_target_pairs={{0,4},{1,5},{2,6},{3,7},{4,0},{5,1},{6,2},{7,3},{8,12},{9,13},{10,... | collective-permute-start | bytes 294920 | tf_op jit(solution)/shard_map/ppermute | solution.py:386
  69.3 2.6 %collective-permute-start.5 = (bf16[96,512]{1,0:T(8,128)(2,1)}, bf16[96,512]{1,0:T(8,128)(2,1)}, u32[]{:S(2)}, u32[]{:S(2)}) collective-permute-start(bf16[96,512]{1,0:T(8,128)(2,1)} %get-tuple-element.60), channel_id=1, source_target_pairs={{0,8},{1,9},{2,10},{3,11},{4,12},{5,13},{6,14},{7,15},{8,0},{9,1},... | collective-permute-start | bytes 294920 | tf_op jit(solution)/shard_map/ppermute | solution.py:386
  73.1 7.1 %collective-permute-done.5.refs_2_ = bf16[96,512]{1,0:T(8,128)(2,1)} collective-permute-done((bf16[96,512]{1,0:T(8,128)(2,1)}, bf16[96,512]{1,0:T(8,128)(2,1)}, u32[]{:S(2)}, u32[]{:S(2)}) %collective-permute-start.5) | collective-permute-done | bytes 98336 | tf_op jit(solution)/shard_map/ppermute | solution.py:386
  83.0 2.5 %collective-permute-start.10 = (bf16[96,512]{1,0:T(8,128)(2,1)S(1)}, bf16[96,512]{1,0:T(8,128)(2,1)}, u32[]{:S(2)}, u32[]{:S(2)}) collective-permute-start(bf16[96,512]{1,0:T(8,128)(2,1)S(1)} %first_activation.1.dep_ref.refs_2_.refs_5_), channel_id=1, source_target_pairs={{0,12},{1,13},{2,14},{3,15},{4,8},{5,9},{6,10},{7,11},{8,4},{9,5},... | collective-permute-start | bytes 294920 | tf_op jit(solution)/shard_map/ppermute | solution.py:386
  89.4 7.3 %density_steps.3 = (f32[12288,128]{1,0:T(8,128)}, f32[8,128]{1,0:T(8,128)S(1)}) custom-call(f32[2,16,256]{2,1,0:T(8,128)S(1)} %copy-done.14, f32[4,384,128]{2,1,0:T(8,128)S(1)} %copy-done.9, bf16[512,256]{1,0:T(8,128)(2,1)S(1)} %get-tuple-element.46.band_ref, bf16[384,4096]{1,0:T(8,128)(2,1)S(1)} %copy-done.3, ...), custom_call_target="tpu_custom_call", output_to_operand_aliasing={{0}: (9, {})} | custom-call | flops 1 | bytes 1 | tf_op jit(solution)/shard_map/density_steps/pallas_call | solution.py:360
  96.9 3.6 %value_layers.1 = (f32[96,512]{1,0:T(8,128)S(1)}, f32[1,512]{1,0:T(1,128)S(1)}, bf16[2,2064,128]{2,1,0:T(8,128)(2,1)S(1)}, bf16[2,2064,128]{2,1,0:T(8,128)(2,1)S...) custom-call(s32[4]{0:T(128)S(1)} %pad_add_fusion.place_ref.refs_0_, ...), custom_call_target="tpu_custom_call" | custom-call | flops 1 | bytes 1 | tf_op jit(solution)/shard_map/value_layers/pallas_call | solution.py:614
  101.4 2.3 %collective-permute-start.14 = (bf16[112,512]{1,0:T(8,128)(2,1)S(1)}, bf16[112,512]{1,0:T(8,128)(2,1)S(1)}, u32[]{:S(2)}, u32[]{:S(2)}) collective-permute-start(bf16[112,512]{1,0:T(8,128)(2,1)S(1)} %get-tuple-element.68), channel_id=1, source_target_pairs={{0,8},{1,9},{2,10},{3,11},{4,12},{5,13},{6,14},{7,15},{8,0},{9,1},... | collective-permute-start | bytes 344072 | tf_op jit(solution)/shard_map/ppermute | solution.py:386
  105.0 3.1 %collective-permute-done.13.refs_2_ = bf16[112,512]{1,0:T(8,128)(2,1)S(1)} collective-permute-done((bf16[112,512]{1,0:T(8,128)(2,1)S(1)}, bf16[112,512]{1,0:T(8,128)(2,1)S(1)}, u32[]{:S(2)}, u32[]{:S(2)}) %collective-permute-start.13) | collective-permute-done | bytes 114720 | tf_op jit(solution)/shard_map/ppermute | solution.py:386
  108.2 5.1 %collective-permute-done.14.refs_3_ = bf16[112,512]{1,0:T(8,128)(2,1)S(1)} collective-permute-done((bf16[112,512]{1,0:T(8,128)(2,1)S(1)}, bf16[112,512]{1,0:T(8,128)(2,1)S(1)}, u32[]{:S(2)}, u32[]{:S(2)}) %collective-permute-start.14) | collective-permute-done | bytes 114720 | tf_op jit(solution)/shard_map/ppermute | solution.py:386
  114.5 2.4 %collective-permute-start.18 = (bf16[96,512]{1,0:T(8,128)(2,1)S(1)}, bf16[96,512]{1,0:T(8,128)(2,1)S(1)}, u32[]{:S(2)}, u32[]{:S(2)}) collective-permute-start(bf16[96,512]{1,0:T(8,128)(2,1)S(1)} %get-tuple-element.70.refs_3_.refs_0_), channel_id=1, source_target_pairs={{0,12},{1,13},{2,14},{3,15},{4,8},{5,9},{6,10},{7,11},{8,4},{9,5},... | collective-permute-start | bytes 294920 | tf_op jit(solution)/shard_map/ppermute | solution.py:386
  119.8 2.1 %collective-permute-done.18.refs_3_ = bf16[96,512]{1,0:T(8,128)(2,1)S(1)} collective-permute-done((bf16[96,512]{1,0:T(8,128)(2,1)S(1)}, bf16[96,512]{1,0:T(8,128)(2,1)S(1)}, u32[]{:S(2)}, u32[]{:S(2)}) %collective-permute-start.18) | collective-permute-done | bytes 98336 | tf_op jit(solution)/shard_map/ppermute | solution.py:386
  121.9 3.8 %collective-permute-done.17.refs_2_ = bf16[96,512]{1,0:T(8,128)(2,1)S(1)} collective-permute-done((bf16[96,512]{1,0:T(8,128)(2,1)S(1)}, bf16[96,512]{1,0:T(8,128)(2,1)S(1)}, u32[]{:S(2)}, u32[]{:S(2)}) %collective-permute-start.17) | collective-permute-done | bytes 98336 | tf_op jit(solution)/shard_map/ppermute | solution.py:386
  127.9 5.5 %collective-permute-done.20.refs_6_ = bf16[400,256]{1,0:T(8,128)(2,1)S(1)} collective-permute-done((bf16[400,256]{1,0:T(8,128)(2,1)S(1)}, bf16[400,256]{1,0:T(8,128)(2,1)S(1)}, u32[]{:S(2)}, u32[]{:S(2)}) %collective-permute-start.20) | collective-permute-done | bytes 204832 | tf_op jit(solution)/shard_map/ppermute | solution.py:386
  137.4 7.0 %first_gradient.2 = (bf16[4096,2048]{1,0:T(8,128)(2,1)}, f32[4,256]{1,0:T(4,128)S(1)}) custom-call(s32[4]{0:T(128)S(1)} %pad_add_fusion.place_ref.refs_0_, bf16[512,384]{1,0:T(8,128)(2,1)S(1)} %get-tuple-element.71.refs_5_.refs_1_, bf16[3072,384]{1,0:T(8,128)(2,1)S(1)} %get-tuple-element.72.refs_2_, bf16[512,384]{1,0:T(8,128)(2,1)S(1)} %get-tuple-element.73.refs_3_, ...), custom_call_target="tpu_custom_call" | custom-call | flops 1 | bytes 1 | tf_op jit(solution)/shard_map/first_gradient/pallas_call | solution.py:793
  145.1 7.7 %first_gradient.3 = bf16[4096,2048]{1,0:T(8,128)(2,1)} custom-call(s32[4]{0:T(128)S(1)} %pad_add_fusion.place_ref.refs_0_, bf16[512,384]{1,0:T(8,128)(2,1)S(1)} %get-tuple-element.71.refs_5_.refs_1_, bf16[3072,384]{1,0:T(8,128)(2,1)S(1)} %get-tuple-element.72.refs_2_, ...), custom_call_target="tpu_custom_call", output_to_operand_aliasing={{}: (9, {})} | custom-call | flops 1 | bytes 1 | tf_op jit(solution)/shard_map/first_gradient/pallas_call | solution.py:793
  (101 shorter events, 32.3 us)
Async XLA Ops:
  13.1 12.6 %collective-permute-start = (bf16[400,512]{1,0:T(8,128)(2,1)}, bf16[400,512]{1,0:T(8,128)(2,1)}, u32[]{:S(2)}, u32[]{:S(2)}) collective-permute-start(bf16[400,512]{1,0:T(8,128)(2,1)} %get-tuple-element.48), channel_id=1, source_target_pairs={{0,1},{1,2},{2,3},{3,4},{4,5},{5,6},{6,7},{7,8},{8,9},{9,10},{10,1... | collective-permute-start | bytes 1228808 | tf_op jit(solution)/shard_map/ppermute | solution.py:829
  16.2 9.5 %collective-permute-start.1 = (bf16[400,512]{1,0:T(8,128)(2,1)}, bf16[400,512]{1,0:T(8,128)(2,1)}, u32[]{:S(2)}, u32[]{:S(2)}) collective-permute-start(bf16[400,512]{1,0:T(8,128)(2,1)} %get-tuple-element.49), channel_id=1, source_target_pairs={{1,0},{2,1},{3,2},{4,3},{5,4},{6,5},{7,6},{8,7},{9,8},{10,9},{11,1... | collective-permute-start | bytes 1228808 | tf_op jit(solution)/shard_map/ppermute | solution.py:830
  41.7 15.1 %collective-permute-start.7 = (bf16[2064,128]{1,0:T(8,128)(2,1)}, bf16[2064,128]{1,0:T(8,128)(2,1)}, u32[]{:S(2)}, u32[]{:S(2)}) collective-permute-start(bf16[2064,128]{1,0:T(8,128)(2,1)} %mid_with_head.1.refs_0_.refs_6_), channel_id=1, source_target_pairs={{0,2},{1,3},{2,0},{3,1},{4,6},{5,7},{6,4},{7,5},{8,10},{9,11},{10,... | collective-permute-start | bytes 1585160 | tf_op jit(solution)/shard_map/ppermute | solution.py:386
  44.3 20.3 %collective-permute-start.3 = (bf16[4,96,512]{2,1,0:T(8,128)(2,1)S(1)}, bf16[4,96,512]{2,1,0:T(8,128)(2,1)S(1)}, u32[]{:S(2)}, u32[]{:S(2)}) collective-permute-start(bf16[4,96,512]{2,1,0:T(8,128)(2,1)S(1)} %get-tuple-element.56.dep_ref), channel_id=1, source_target_pairs={{0,2},{1,3},{2,0},{3,1},{4,6},{5,7},{6,4},{7,5},{8,10},{9,11},{10,... | collective-permute-start | bytes 1179656 | tf_op jit(solution)/shard_map/ppermute | solution.py:386
  45.5 51.3 %collective-permute-start.11 = (bf16[2064,128]{1,0:T(8,128)(2,1)}, bf16[2064,128]{1,0:T(8,128)(2,1)}, u32[]{:S(2)}, u32[]{:S(2)}) collective-permute-start(bf16[2064,128]{1,0:T(8,128)(2,1)} %mid_with_head.1.refs_0_.refs_6_), channel_id=1, source_target_pairs={{0,1},{1,0},{2,3},{3,2},{4,5},{5,4},{6,7},{7,6},{8,9},{9,8},{10,11... | collective-permute-start | bytes 1585160 | tf_op jit(solution)/shard_map/ppermute | solution.py:386
  56.8 40.0 %collective-permute-start.12 = (bf16[2064,128]{1,0:T(8,128)(2,1)}, bf16[2064,128]{1,0:T(8,128)(2,1)}, u32[]{:S(2)}, u32[]{:S(2)}) collective-permute-start(bf16[2064,128]{1,0:T(8,128)(2,1)} %collective-permute-done.7.refs_4_.refs_8_), channel_id=1, source_target_pairs={{0,1},{1,0},{2,3},{3,2},{4,5},{5,4},{6,7},{7,6},{8,9},{9,8},{10,11... | collective-permute-start | bytes 1585160 | tf_op jit(solution)/shard_map/ppermute | solution.py:386
  69.3 10.9 %collective-permute-start.5 = (bf16[96,512]{1,0:T(8,128)(2,1)}, bf16[96,512]{1,0:T(8,128)(2,1)}, u32[]{:S(2)}, u32[]{:S(2)}) collective-permute-start(bf16[96,512]{1,0:T(8,128)(2,1)} %get-tuple-element.60), channel_id=1, source_target_pairs={{0,8},{1,9},{2,10},{3,11},{4,12},{5,13},{6,14},{7,15},{8,0},{9,1},... | collective-permute-start | bytes 294920 | tf_op jit(solution)/shard_map/ppermute | solution.py:386
  71.9 8.3 %collective-permute-start.6 = (bf16[96,512]{1,0:T(8,128)(2,1)}, bf16[96,512]{1,0:T(8,128)(2,1)}, u32[]{:S(2)}, u32[]{:S(2)}) collective-permute-start(bf16[96,512]{1,0:T(8,128)(2,1)} %get-tuple-element.61), channel_id=1, source_target_pairs={{0,12},{1,13},{2,14},{3,15},{4,8},{5,9},{6,10},{7,11},{8,4},{9,5},... | collective-permute-start | bytes 294920 | tf_op jit(solution)/shard_map/ppermute | solution.py:386
  83.0 13.8 %collective-permute-start.10 = (bf16[96,512]{1,0:T(8,128)(2,1)S(1)}, bf16[96,512]{1,0:T(8,128)(2,1)}, u32[]{:S(2)}, u32[]{:S(2)}) collective-permute-start(bf16[96,512]{1,0:T(8,128)(2,1)S(1)} %first_activation.1.dep_ref.refs_2_.refs_5_), channel_id=1, source_target_pairs={{0,12},{1,13},{2,14},{3,15},{4,8},{5,9},{6,10},{7,11},{8,4},{9,5},... | collective-permute-start | bytes 294920 | tf_op jit(solution)/shard_map/ppermute | solution.py:386
  85.6 11.3 %collective-permute-start.9 = (bf16[96,512]{1,0:T(8,128)(2,1)S(1)}, bf16[96,512]{1,0:T(8,128)(2,1)}, u32[]{:S(2)}, u32[]{:S(2)}) collective-permute-start(bf16[96,512]{1,0:T(8,128)(2,1)S(1)} %first_activation.1.dep_ref.refs_2_.refs_5_), channel_id=1, source_target_pairs={{0,8},{1,9},{2,10},{3,11},{4,12},{5,13},{6,14},{7,15},{8,0},{9,1},... | collective-permute-start | bytes 294920 | tf_op jit(solution)/shard_map/ppermute | solution.py:386
  86.2 10.7 %collective-permute-start.8 = (bf16[96,512]{1,0:T(8,128)(2,1)S(1)}, bf16[96,512]{1,0:T(8,128)(2,1)}, u32[]{:S(2)}, u32[]{:S(2)}) collective-permute-start(bf16[96,512]{1,0:T(8,128)(2,1)S(1)} %first_activation.1.dep_ref.refs_2_.refs_5_), channel_id=1, source_target_pairs={{0,4},{1,5},{2,6},{3,7},{4,0},{5,1},{6,2},{7,3},{8,12},{9,13},{10,... | collective-permute-start | bytes 294920 | tf_op jit(solution)/shard_map/ppermute | solution.py:386
  100.5 12.8 %collective-permute-start.22 = (bf16[2,2064,128]{2,1,0:T(8,128)(2,1)S(1)}, bf16[2,2064,128]{2,1,0:T(8,128)(2,1)S(1)}, u32[]{:S(2)}, u32[]{:S(2)}) collective-permute-start(bf16[2,2064,128]{2,1,0:T(8,128)(2,1)S(1)} %get-tuple-element.77), channel_id=1, source_target_pairs={{0,1},{1,0},{2,3},{3,2},{4,5},{5,4},{6,7},{7,6},{8,9},{9,8},{10,11... | collective-permute-start | bytes 3170312 | tf_op jit(solution)/shard_map/ppermute | solution.py:386
  100.6 7.6 %collective-permute-start.13 = (bf16[112,512]{1,0:T(8,128)(2,1)S(1)}, bf16[112,512]{1,0:T(8,128)(2,1)S(1)}, u32[]{:S(2)}, u32[]{:S(2)}) collective-permute-start(bf16[112,512]{1,0:T(8,128)(2,1)S(1)} %get-tuple-element.67), channel_id=1, source_target_pairs={{0,4},{1,5},{2,6},{3,7},{4,0},{5,1},{6,2},{7,3},{8,12},{9,13},{10,... | collective-permute-start | bytes 344072 | tf_op jit(solution)/shard_map/ppermute | solution.py:386
  101.4 11.8 %collective-permute-start.14 = (bf16[112,512]{1,0:T(8,128)(2,1)S(1)}, bf16[112,512]{1,0:T(8,128)(2,1)S(1)}, u32[]{:S(2)}, u32[]{:S(2)}) collective-permute-start(bf16[112,512]{1,0:T(8,128)(2,1)S(1)} %get-tuple-element.68), channel_id=1, source_target_pairs={{0,8},{1,9},{2,10},{3,11},{4,12},{5,13},{6,14},{7,15},{8,0},{9,1},... | collective-permute-start | bytes 344072 | tf_op jit(solution)/shard_map/ppermute | solution.py:386
  103.7 9.5 %collective-permute-start.15 = (bf16[112,512]{1,0:T(8,128)(2,1)S(1)}, bf16[112,512]{1,0:T(8,128)(2,1)S(1)}, u32[]{:S(2)}, u32[]{:S(2)}) collective-permute-start(bf16[112,512]{1,0:T(8,128)(2,1)S(1)} %get-tuple-element.69), channel_id=1, source_target_pairs={{0,12},{1,13},{2,14},{3,15},{4,8},{5,9},{6,10},{7,11},{8,4},{9,5},... | collective-permute-start | bytes 344072 | tf_op jit(solution)/shard_map/ppermute | solution.py:386
  113.6 22.1 %collective-permute-start.23 = (bf16[2064,128]{1,0:T(8,128)(2,1)S(1)}, bf16[2064,128]{1,0:T(8,128)(2,1)S(1)}, u32[]{:S(2)}, u32[]{:S(2)}) collective-permute-start(bf16[2064,128]{1,0:T(8,128)(2,1)S(1)} %get-tuple-element.79), channel_id=1, source_target_pairs={{0,2},{1,3},{2,0},{3,1},{4,6},{5,7},{6,4},{7,5},{8,10},{9,11},{10,... | collective-permute-start | bytes 1585160 | tf_op jit(solution)/shard_map/ppermute | solution.py:386
  114.5 7.4 %collective-permute-start.18 = (bf16[96,512]{1,0:T(8,128)(2,1)S(1)}, bf16[96,512]{1,0:T(8,128)(2,1)S(1)}, u32[]{:S(2)}, u32[]{:S(2)}) collective-permute-start(bf16[96,512]{1,0:T(8,128)(2,1)S(1)} %get-tuple-element.70.refs_3_.refs_0_), channel_id=1, source_target_pairs={{0,12},{1,13},{2,14},{3,15},{4,8},{5,9},{6,10},{7,11},{8,4},{9,5},... | collective-permute-start | bytes 294920 | tf_op jit(solution)/shard_map/ppermute | solution.py:386
  116.9 8.9 %collective-permute-start.17 = (bf16[96,512]{1,0:T(8,128)(2,1)S(1)}, bf16[96,512]{1,0:T(8,128)(2,1)S(1)}, u32[]{:S(2)}, u32[]{:S(2)}) collective-permute-start(bf16[96,512]{1,0:T(8,128)(2,1)S(1)} %get-tuple-element.70.refs_3_.refs_0_), channel_id=1, source_target_pairs={{0,8},{1,9},{2,10},{3,11},{4,12},{5,13},{6,14},{7,15},{8,0},{9,1},... | collective-permute-start | bytes 294920 | tf_op jit(solution)/shard_map/ppermute | solution.py:386
  118.2 7.5 %collective-permute-start.16 = (bf16[96,512]{1,0:T(8,128)(2,1)S(1)}, bf16[96,512]{1,0:T(8,128)(2,1)S(1)}, u32[]{:S(2)}, u32[]{:S(2)}) collective-permute-start(bf16[96,512]{1,0:T(8,128)(2,1)S(1)} %get-tuple-element.70.refs_3_.refs_0_), channel_id=1, source_target_pairs={{0,4},{1,5},{2,6},{3,7},{4,0},{5,1},{6,2},{7,3},{8,12},{9,13},{10,... | collective-permute-start | bytes 294920 | tf_op jit(solution)/shard_map/ppermute | solution.py:386
  125.8 7.6 %collective-permute-start.20 = (bf16[400,256]{1,0:T(8,128)(2,1)S(1)}, bf16[400,256]{1,0:T(8,128)(2,1)S(1)}, u32[]{:S(2)}, u32[]{:S(2)}) collective-permute-start(bf16[400,256]{1,0:T(8,128)(2,1)S(1)} %get-tuple-element.75.refs_0_.refs_4_), channel_id=1, source_target_pairs={{0,2},{1,3},{2,0},{3,1},{4,6},{5,7},{6,4},{7,5},{8,10},{9,11},{10,... | collective-permute-start | bytes 614408 | tf_op jit(solution)/shard_map/ppermute | solution.py:386
  127.0 8.7 %collective-permute-start.25 = (bf16[400,256]{1,0:T(8,128)(2,1)S(1)}, bf16[400,256]{1,0:T(8,128)(2,1)}, u32[]{:S(2)}, u32[]{:S(2)}) collective-permute-start(bf16[400,256]{1,0:T(8,128)(2,1)S(1)} %get-tuple-element.82.refs_4_), channel_id=1, source_target_pairs={{0,2},{1,3},{2,0},{3,1},{4,6},{5,7},{6,4},{7,5},{8,10},{9,11},{10,... | collective-permute-start | bytes 614408 | tf_op jit(solution)/shard_map/ppermute | solution.py:386
  127.9 8.8 %collective-permute-start.19 = (bf16[400,256]{1,0:T(8,128)(2,1)S(1)}, bf16[400,256]{1,0:T(8,128)(2,1)S(1)}, u32[]{:S(2)}, u32[]{:S(2)}) collective-permute-start(bf16[400,256]{1,0:T(8,128)(2,1)S(1)} %get-tuple-element.75.refs_0_.refs_4_), channel_id=1, source_target_pairs={{0,1},{1,0},{2,3},{3,2},{4,5},{5,4},{6,7},{7,6},{8,9},{9,8},{10,11... | collective-permute-start | bytes 614408 | tf_op jit(solution)/shard_map/ppermute | solution.py:386
  133.4 11.7 %collective-permute-start.24 = (bf16[400,256]{1,0:T(8,128)(2,1)S(1)}, bf16[400,256]{1,0:T(8,128)(2,1)}, u32[]{:S(2)}, u32[]{:S(2)}) collective-permute-start(bf16[400,256]{1,0:T(8,128)(2,1)S(1)} %get-tuple-element.82.refs_4_), channel_id=1, source_target_pairs={{0,1},{1,0},{2,3},{3,2},{4,5},{5,4},{6,7},{7,6},{8,9},{9,8},{10,11... | collective-permute-start | bytes 614408 | tf_op jit(solution)/shard_map/ppermute | solution.py:386
  135.7 9.4 %collective-permute-start.26 = (bf16[400,256]{1,0:T(8,128)(2,1)}, bf16[400,256]{1,0:T(8,128)(2,1)}, u32[]{:S(2)}, u32[]{:S(2)}) collective-permute-start(bf16[400,256]{1,0:T(8,128)(2,1)} %collective-permute-done.25.refs_6_), channel_id=1, source_target_pairs={{0,1},{1,0},{2,3},{3,2},{4,5},{5,4},{6,7},{7,6},{8,9},{9,8},{10,11... | collective-permute-start | bytes 614408 | tf_op jit(solution)/shard_map/ppermute | solution.py:386
  (27 other events, 287.8 us)

commit v6 on v5

--- a/solution.py
+++ b/solution.py
@@ -7,7 +7,7 @@
 from jax.sharding import PartitionSpec as P
 
 diffusion_rate = 0.24
-VMEM_BYTES = 40 * 1024 * 1024
+VMEM_BYTES = 24 * 1024 * 1024
 EXTRA = 16
 bf16 = jnp.bfloat16
 f32 = jnp.float32
@@ -223,9 +223,9 @@
         out_shape=[
             sent,
             sent,
-            shifts,
+            pltpu.HBM(shifts.shape, f32),
             band,
-            jax.ShapeDtypeStruct((scenarios, rows * columns), bf16),
+            pltpu.HBM((scenarios, rows * columns), bf16),
             jax.ShapeDtypeStruct((scenarios, inner), bf16),
         ],
         scratch_shapes=[
@@ -391,7 +391,7 @@
     refs[-1][pl.program_id(0)] = jnp.dot(inputs_ref[...], weight, preferred_element_type=f32)
 
 
-def inner_product(inner, weight, width):
+def inner_product(inner, weight, width, deps):
     scenarios, cells = inner.shape
     total, hidden = weight.shape
     size = (total - cells) // 2
@@ -403,13 +403,13 @@
     return pl.pallas_call(
         functools.partial(inner_product_kernel, count),
         grid=(hidden // width,),
-        in_specs=[vmem()] + [spec(k) for k in range(count)],
+        in_specs=[vmem()] + [spec(k) for k in range(count)] + any_specs(deps),
         out_specs=vmem(),
         out_shape=jax.ShapeDtypeStruct((hidden // width, scenarios, width), f32),
         compiler_params=params(),
         cost_estimate=pl.CostEstimate(flops=1, bytes_accessed=1, transcendentals=0),
         name="inner_product",
-    )(inner, *([weight] * count))
+    )(inner, *([weight] * count), *deps)
 
 
 def edge_product_kernel(block, with_inner, place_ref, low_ref, high_ref, top_ref, bottom_ref, *refs):
@@ -518,23 +518,31 @@
     )(own, *received, *deps)
 
 
-def pack_kernel(mid_ref, head_ref, *refs):
-    out_ref = refs[-1]
+def pack_kernel(mid_ref, head_ref, out_ref, head_row, arrived):
     hidden = mid_ref.shape[0]
-    out_ref[pl.ds(0, hidden), :] = mid_ref[...]
-    out_ref[pl.ds(hidden, EXTRA), :] = tail_rows(head_ref[...])
-
-
-def pack(mid_weight, head, deps):
+    copies = [
+        pltpu.make_async_copy(mid_ref, out_ref.at[pl.ds(0, hidden), :], arrived.at[0]),
+        pltpu.make_async_copy(head_ref, head_row, arrived.at[1]),
+    ]
+    for copy in copies:
+        copy.start()
+    copies[1].wait()
+    out_ref[pl.ds(hidden, EXTRA), :] = tail_rows(head_row[...])
+    copies[0].wait()
+
+
+def pack(mid_weight, head):
     hidden, units = mid_weight.shape
     return pl.pallas_call(
         pack_kernel,
-        in_specs=[vmem()] * 2 + any_specs(deps),
+        in_specs=[pl.BlockSpec(memory_space=pltpu.HBM)] * 2,
+        out_specs=vmem(),
         out_shape=jax.ShapeDtypeStruct((hidden + EXTRA, units), bf16),
+        scratch_shapes=[pltpu.VMEM(head.shape, f32), pltpu.SemaphoreType.DMA((2,))],
         compiler_params=params(),
         cost_estimate=pl.CostEstimate(flops=1, bytes_accessed=1, transcendentals=0),
         name="mid_with_head",
-    )(mid_weight, head, *deps)
+    )(*[pltpu.with_memory_space_constraint(array, pltpu.HBM) for array in (mid_weight, head)])
 
 
 def two_halves(exact):
@@ -819,8 +827,10 @@
 
     place = jnp.stack([core, side, part, mine])
     cot = lax.dynamic_slice_in_dim(cotangent, mine * block, block)[:, None]
-    halves = 2 if width % 256 == 0 else 1
-
+    halves = 1
+
+    mids = [pack(mid_weight, head_weight[None, :])]
+    mids += [swap(mids[0], count, 1), swap(mids[0], count, 2)]
     small = [pltpu.with_memory_space_constraint(array, pltpu.HBM) for array in (drift, shocks.T, shock_table.T)]
     first_rows, last_rows, shifts, band, own_rows, inner = inner_steps(tiles, *small)
     inner = inner if rows > 4 else None
@@ -828,23 +838,21 @@
     backward = [(i + 1, i) for i in range(count - 1)]
     below = lax.ppermute(last_rows, "grid", forward)
     above = lax.ppermute(first_rows, "grid", backward)
-    product = None if inner is None else inner_product(inner, first_weight, width)
+    first_weight = pltpu.with_memory_space_constraint(first_weight, pltpu.HBM)
+    product = None if inner is None else inner_product(inner, first_weight, width, mids[1:])
     low, high = edge_steps(drift, shifts, band, own_rows, below, above, own_rows if product is None else product)
+    mids.append(swap(mids[2], count, 1))
 
     def density_turn(turn, dep, so_far):
         return density_steps(drift, shifts, band, own_rows, below, above, dep, so_far, turn, 2)
 
     keep, send = edge_product(place, low, high, first_weight, product, parts, width)
-    mids = [pack(mid_weight, head_weight[None, :], [send])]
-    keep, send = add_side(place, keep, swap(send, count, 1), mids)
+    keep, send = add_side(place, keep, swap(send, count, 1))
     other = swap(send, count, 2)
     density, token = density_turn(0, send, None)
-    own, *sends = add_parts(place, keep, other, [token])
+    own, *sends = add_parts(place, keep, other, [token, mids[3]])
     received = [swap(piece, count, 4 * (k + 1)) for k, piece in enumerate(sends)]
-    mids.append(swap(mids[0], count, 1))
-    mids.append(swap(mids[0], count, 2))
-    mids.append(swap(mids[2], count, 1))
-    first = activate(own, received, [mids[2]])
+    first = activate(own, received)
     firsts = [first] + [swap(first, count, 4 * k) for k in range(1, parts)]
     density, token = density_turn(1, first, density)
     own, value, mid_keep, mid_send, *sends = middle(place, cot, firsts, mids, 1, parts, width, [token])
@@ -853,8 +861,8 @@
     mid_keep, mid_send = mid_add(mid_keep, swap(mid_send, count, 1), [back])
     lefts = transposed([low, high] if inner is None else [low, inner, high], [back])
     pieces = [back] + [swap(back, count, 4 * k) for k in range(1, parts)]
-    stacks = stack(pieces + [tail], halves, [lefts[0]])
-    grad_mid, grad_head = mid_final(mid_keep, swap(mid_send, count, 2), stacks[:1])
+    grad_mid, grad_head = mid_final(mid_keep, swap(mid_send, count, 2))
+    stacks = stack(pieces + [tail], halves, [lefts[0], grad_head])
     grad_first = None
     for half, own_stack in enumerate(stacks):
         gathered = [own_stack, swap(own_stack, count, 1), swap(own_stack, count, 2)]

time: 154 us -> 150 us (0.974)
  waiting for transfers between devices: 40.9 us -> 36.6 us
  local copies, waits for them, and re-layouts: 11.2 us -> 14.7 us
  starting transfers between devices: 32.2 us -> 30.2 us
  Pallas kernels: 67.3 us -> 65.3 us
    ppermute x25 -> x22, waiting for transfers between devices: 40.9 us -> 36.6 us  [swap(): return lax.ppermute(values, 'grid', [(i, i ^ flip) for i in range(count)])]
    unnamed x48 -> x60, local copies, waits for them, and re-layouts: 9.75 us -> 13.2 us
    pallas_call x2 -> x1, Pallas kernels: 14.7 us -> 12.1 us  [first_grad(): pl.pallas_call(functools.partial(first_grad_kernel, parts, block, len(lef...]
    ppermute x25 -> x22, starting transfers between devices: 27.9 us -> 25.8 us  [swap(): return lax.ppermute(values, 'grid', [(i, i ^ flip) for i in range(count)])]
  transfers between devices with their start and end apart: 27 -> 24, of which waited for: 10 -> 9; matrix products, arithmetic and copies ran while one was open for 1% -> 1% of each run, Pallas kernels for 23% -> 25%
where the time goes in v6:
time: 150 us; the launch traced here: 148 us
  Pallas kernels  65.3 us (44%)
  waiting for transfers between devices  36.6 us (24%)
  starting transfers between devices  30.2 us (20%)
  local copies, waits for them, and re-layouts  14.7 us (10%)
    ppermute x22, waiting for transfers between devices, swap(): return lax.ppermute(values, 'grid', [(i, i ^ flip) for i in range(count)])  36.6 us
    ppermute x22, starting transfers between devices, swap(): return lax.ppermute(values, 'grid', [(i, i ^ flip) for i in range(count)])  25.8 us
    pallas_call x2, Pallas kernels, density_steps(): pl.pallas_call(functools.partial(density_kernel, None), grid=(steps,), in...  14.8 us
    unnamed x60, local copies, waits for them, and re-layouts  13.2 us
    pallas_call x1, Pallas kernels, first_grad(): pl.pallas_call(functools.partial(first_grad_kernel, parts, block, len(lef...  12.1 us
    pallas_call x1, Pallas kernels, inner_steps(): pl.pallas_call(functools.partial(inner_kernel, rows, size), grid=(scenari...  11.5 us
    pallas_call x1, Pallas kernels, inner_product(): pl.pallas_call(functools.partial(inner_product_kernel, count), grid=(hidd...  8.15 us
    pallas_call x1, Pallas kernels, edge_product(): pl.pallas_call(functools.partial(edge_product_kernel, block, inner is not...  4.73 us
  transfers between devices with their start and end apart: 24, of which 9 were waited for; matrix products, arithmetic and copies ran while one was open for 1% of the time, Pallas kernels for 25%

profile of v6, /device:TPU:0, one launch (start us, length us, event | category | flops | bytes accessed | tf_op | source)
XLA Modules:
  0.0 147.9 jit_solution(8249109755376161936)
XLA Ops:
  1.7 3.0 %collective-permute-start.3 = (bf16[2064,128]{1,0:T(8,128)(2,1)S(1)}, bf16[2064,128]{1,0:T(8,128)(2,1)S(1)}, u32[]{:S(2)}, u32[]{:S(2)}) collective-permute-start(bf16[2064,128]{1,0:T(8,128)(2,1)S(1)} %mid_with_head.1.refs_6_), channel_id=1, source_target_pairs={{0,2},{1,3},{2,0},{3,1},{4,6},{5,7},{6,4},{7,5},{8,10},{9,11},{10,... | collective-permute-start | bytes 1585160 | tf_op jit(solution)/shard_map/ppermute | solution.py:386
  4.8 11.5 %inner_density_steps.1 = (bf16[400,512]{1,0:T(8,128)(2,1)}, bf16[400,512]{1,0:T(8,128)(2,1)}, f32[4,384,128]{2,1,0:T(8,128)}, bf16[512,256]{1,0:T(8,128)(2,1)S(1...) custom-call(f32[12288,128]{1,0:T(8,128)} %bitcast.22, f32[2,16,256]{2,1,0:T(8,128)} %drift_ref.5, ...), custom_call_target="tpu_custom_call" | custom-call | flops 1 | bytes 1 | tf_op jit(solution)/shard_map/inner_density_steps/pallas_call | solution.py:212
  17.7 3.1 %collective-permute-start = (bf16[400,512]{1,0:T(8,128)(2,1)}, bf16[400,512]{1,0:T(8,128)(2,1)}, u32[]{:S(2)}, u32[]{:S(2)}) collective-permute-start(bf16[400,512]{1,0:T(8,128)(2,1)} %get-tuple-element.46), channel_id=1, source_target_pairs={{0,1},{1,2},{2,3},{3,4},{4,5},{5,6},{6,7},{7,8},{8,9},{9,10},{10,1... | collective-permute-start | bytes 1228808 | tf_op jit(solution)/shard_map/ppermute | solution.py:839
  23.9 1.7 %copy-done.3 = bf16[384,3072]{1,0:T(8,128)(2,1)S(1)} copy-done((bf16[384,3072]{1,0:T(8,128)(2,1)S(1)}, bf16[384,3072]{1,0:T(8,128)(2,1)}, u32[]{:S(2)}) %copy-start.3) | copy-done | bytes 2359320
  27.6 8.2 %inner_product.1.dep_ref.refs_0_ = f32[4,384,512]{2,1,0:T(8,128)S(1)} custom-call(bf16[384,3072]{1,0:T(8,128)(2,1)S(1)} %copy-done.3, bf16[4096,2048]{1,0:T(8,128)(2,1)} %bottom_ref.1, bf16[4096,2048]{1,0:T(8,128)(2,1)} %bottom_ref.1, bf16[4096,2048]{1,0:T(8,128)(2,1)} %bottom_ref.1, bf16[4096,2048]{1,0:T(8,128)(2,1)} %bottom_ref.1, ...), custom_call_target="tpu_custom_call" | custom-call | flops 1 | bytes 1 | tf_op jit(solution)/shard_map/inner_product/pallas_call | solution.py:403
  35.8 4.6 %edge_density_steps.1 = (bf16[384,512]{1,0:T(8,128)(2,1)S(1)}, bf16[384,512]{1,0:T(8,128)(2,1)S(1)}) custom-call(f32[2,16,256]{2,1,0:T(8,128)S(1)} %copy-done.22, f32[4,384,128]{2,1,0:T(8,128)S(1)} %copy-done.5, bf16[512,256]{1,0:T(8,128)(2,1)S(1)} %get-tuple-element.44.band_ref, bf16[384,4096]{1,0:T(8,128)(2,1)S(1)} %copy-done.1, ...), custom_call_target="tpu_custom_call" | custom-call | flops 1 | bytes 1 | tf_op jit(solution)/shard_map/edge_density_steps/pallas_call | solution.py:333
  40.5 4.7 %edge_product.1 = (f32[2,4,96,512]{3,2,1,0:T(8,128)S(1)}, bf16[2,4,96,512]{3,2,1,0:T(8,128)(2,1)S(1)}) custom-call(s32[4]{0:T(128)S(1)} %pad_add_fusion.place_ref.refs_0_, bf16[384,512]{1,0:T(8,128)(2,1)S(1)} %get-tuple-element.49.low_ref.refs_0_, bf16[384,512]{1,0:T(8,128)(2,1)S(1)} %get-tuple-element.50.high_ref.refs_2_, bf16[4096,2048]{1,0:T(8,128)(2,1)} %bottom_ref.1, ...), custom_call_target="tpu_custom_call" | custom-call | flops 1 | bytes 1 | tf_op jit(solution)/shard_map/edge_product/pallas_call | solution.py:445
  46.6 1.8 %collective-permute-done.4.other_ref = bf16[2,4,96,512]{3,2,1,0:T(8,128)(2,1)S(1)} collective-permute-done((bf16[2,4,96,512]{3,2,1,0:T(8,128)(2,1)S(1)}, bf16[2,4,96,512]{3,2,1,0:T(8,128)(2,1)S(1)}, u32[]{:S(2)}, u32[]{:S(2)}) %collective-permute-start.4) | collective-permute-done | bytes 786464 | tf_op jit(solution)/shard_map/ppermute | solution.py:386
  50.6 7.3 %density_steps.2 = (f32[12288,128]{1,0:T(8,128)}, f32[8,128]{1,0:T(8,128)S(1)}) custom-call(f32[2,16,256]{2,1,0:T(8,128)S(1)} %copy-done.22, f32[4,384,128]{2,1,0:T(8,128)S(1)} %copy-done.5, bf16[512,256]{1,0:T(8,128)(2,1)S(1)} %get-tuple-element.44.band_ref, bf16[384,4096]{1,0:T(8,128)(2,1)S(1)} %copy-done.1, ...), custom_call_target="tpu_custom_call" | custom-call | flops 1 | bytes 1 | tf_op jit(solution)/shard_map/density_steps/pallas_call | solution.py:360
  57.9 2.6 %collective-permute-done.5.other_ref = bf16[4,96,512]{2,1,0:T(8,128)(2,1)S(1)} collective-permute-done((bf16[4,96,512]{2,1,0:T(8,128)(2,1)S(1)}, bf16[4,96,512]{2,1,0:T(8,128)(2,1)S(1)}, u32[]{:S(2)}, u32[]{:S(2)}) %collective-permute-start.5) | collective-permute-done | bytes 393248 | tf_op jit(solution)/shard_map/ppermute | solution.py:386
  63.4 2.6 %collective-permute-start.7 = (bf16[96,512]{1,0:T(8,128)(2,1)}, bf16[96,512]{1,0:T(8,128)(2,1)S(1)}, u32[]{:S(2)}, u32[]{:S(2)}) collective-permute-start(bf16[96,512]{1,0:T(8,128)(2,1)} %get-tuple-element.57), channel_id=1, source_target_pairs={{0,4},{1,5},{2,6},{3,7},{4,0},{5,1},{6,2},{7,3},{8,12},{9,13},{10,... | collective-permute-start | bytes 294920 | tf_op jit(solution)/shard_map/ppermute | solution.py:386
  66.0 2.6 %collective-permute-start.8 = (bf16[96,512]{1,0:T(8,128)(2,1)}, bf16[96,512]{1,0:T(8,128)(2,1)}, u32[]{:S(2)}, u32[]{:S(2)}) collective-permute-start(bf16[96,512]{1,0:T(8,128)(2,1)} %get-tuple-element.58), channel_id=1, source_target_pairs={{0,8},{1,9},{2,10},{3,11},{4,12},{5,13},{6,14},{7,15},{8,0},{9,1},... | collective-permute-start | bytes 294920 | tf_op jit(solution)/shard_map/ppermute | solution.py:386
  69.6 6.7 %collective-permute-done.8.refs_2_ = bf16[96,512]{1,0:T(8,128)(2,1)} collective-permute-done((bf16[96,512]{1,0:T(8,128)(2,1)}, bf16[96,512]{1,0:T(8,128)(2,1)}, u32[]{:S(2)}, u32[]{:S(2)}) %collective-permute-start.8) | collective-permute-done | bytes 98336 | tf_op jit(solution)/shard_map/ppermute | solution.py:386
  79.0 2.5 %collective-permute-start.12 = (bf16[96,512]{1,0:T(8,128)(2,1)S(1)}, bf16[96,512]{1,0:T(8,128)(2,1)}, u32[]{:S(2)}, u32[]{:S(2)}) collective-permute-start(bf16[96,512]{1,0:T(8,128)(2,1)S(1)} %first_activation.1.dep_ref.refs_2_.refs_5_), channel_id=1, source_target_pairs={{0,12},{1,13},{2,14},{3,15},{4,8},{5,9},{6,10},{7,11},{8,4},{9,5},... | collective-permute-start | bytes 294920 | tf_op jit(solution)/shard_map/ppermute | solution.py:386
  85.5 7.5 %density_steps.3 = (f32[12288,128]{1,0:T(8,128)}, f32[8,128]{1,0:T(8,128)S(1)}) custom-call(f32[2,16,256]{2,1,0:T(8,128)S(1)} %copy-done.22, f32[4,384,128]{2,1,0:T(8,128)S(1)} %copy-done.6, bf16[512,256]{1,0:T(8,128)(2,1)S(1)} %get-tuple-element.44.band_ref, bf16[384,4096]{1,0:T(8,128)(2,1)S(1)} %copy-done.1, ...), custom_call_target="tpu_custom_call", output_to_operand_aliasing={{0}: (9, {})} | custom-call | flops 1 | bytes 1 | tf_op jit(solution)/shard_map/density_steps/pallas_call | solution.py:360
  93.1 3.0 %value_layers.1 = (f32[96,512]{1,0:T(8,128)S(1)}, f32[1,512]{1,0:T(1,128)S(1)}, bf16[2,2064,128]{2,1,0:T(8,128)(2,1)S(1)}, bf16[2,2064,128]{2,1,0:T(8,128)(2,1)S...) custom-call(s32[4]{0:T(128)S(1)} %pad_add_fusion.place_ref.refs_0_, ...), custom_call_target="tpu_custom_call" | custom-call | flops 1 | bytes 1 | tf_op jit(solution)/shard_map/value_layers/pallas_call | solution.py:622
  96.9 2.3 %collective-permute-start.14 = (bf16[112,512]{1,0:T(8,128)(2,1)S(1)}, bf16[112,512]{1,0:T(8,128)(2,1)S(1)}, u32[]{:S(2)}, u32[]{:S(2)}) collective-permute-start(bf16[112,512]{1,0:T(8,128)(2,1)S(1)} %get-tuple-element.66), channel_id=1, source_target_pairs={{0,8},{1,9},{2,10},{3,11},{4,12},{5,13},{6,14},{7,15},{8,0},{9,1},... | collective-permute-start | bytes 344072 | tf_op jit(solution)/shard_map/ppermute | solution.py:386
  100.6 3.1 %collective-permute-done.13.refs_2_ = bf16[112,512]{1,0:T(8,128)(2,1)S(1)} collective-permute-done((bf16[112,512]{1,0:T(8,128)(2,1)S(1)}, bf16[112,512]{1,0:T(8,128)(2,1)S(1)}, u32[]{:S(2)}, u32[]{:S(2)}) %collective-permute-start.13) | collective-permute-done | bytes 114720 | tf_op jit(solution)/shard_map/ppermute | solution.py:386
  103.7 5.1 %collective-permute-done.14.refs_3_ = bf16[112,512]{1,0:T(8,128)(2,1)S(1)} collective-permute-done((bf16[112,512]{1,0:T(8,128)(2,1)S(1)}, bf16[112,512]{1,0:T(8,128)(2,1)S(1)}, u32[]{:S(2)}, u32[]{:S(2)}) %collective-permute-start.14) | collective-permute-done | bytes 114720 | tf_op jit(solution)/shard_map/ppermute | solution.py:386
  109.8 2.4 %collective-permute-start.18 = (bf16[96,512]{1,0:T(8,128)(2,1)S(1)}, bf16[96,512]{1,0:T(8,128)(2,1)S(1)}, u32[]{:S(2)}, u32[]{:S(2)}) collective-permute-start(bf16[96,512]{1,0:T(8,128)(2,1)S(1)} %get-tuple-element.68.refs_3_.refs_0_), channel_id=1, source_target_pairs={{0,12},{1,13},{2,14},{3,15},{4,8},{5,9},{6,10},{7,11},{8,4},{9,5},... | collective-permute-start | bytes 294920 | tf_op jit(solution)/shard_map/ppermute | solution.py:386
  115.1 6.7 %collective-permute-done.20.other_ref = bf16[2064,128]{1,0:T(8,128)(2,1)S(1)} collective-permute-done((bf16[2064,128]{1,0:T(8,128)(2,1)S(1)}, bf16[2064,128]{1,0:T(8,128)(2,1)S(1)}, u32[]{:S(2)}, u32[]{:S(2)}) %collective-permute-start.20) | collective-permute-done | bytes 528416 | tf_op jit(solution)/shard_map/ppermute | solution.py:386
  124.2 8.5 %collective-permute-done.22.refs_6_ = bf16[400,512]{1,0:T(8,128)(2,1)S(1)} collective-permute-done((bf16[400,512]{1,0:T(8,128)(2,1)S(1)}, bf16[400,512]{1,0:T(8,128)(2,1)S(1)}, u32[]{:S(2)}, u32[]{:S(2)}) %collective-permute-start.22) | collective-permute-done | bytes 409632 | tf_op jit(solution)/shard_map/ppermute | solution.py:386
  132.7 1.7 %collective-permute-done.23.refs_7_ = bf16[400,512]{1,0:T(8,128)(2,1)S(1)} collective-permute-done((bf16[400,512]{1,0:T(8,128)(2,1)S(1)}, bf16[400,512]{1,0:T(8,128)(2,1)S(1)}, u32[]{:S(2)}, u32[]{:S(2)}) %collective-permute-start.23) | collective-permute-done | bytes 409632 | tf_op jit(solution)/shard_map/ppermute | solution.py:386
  135.1 12.1 %first_gradient.1 = (bf16[4096,2048]{1,0:T(8,128)(2,1)}, f32[4,512]{1,0:T(4,128)S(1)}) custom-call(s32[4]{0:T(128)S(1)} %pad_add_fusion.place_ref.refs_0_, bf16[512,384]{1,0:T(8,128)(2,1)S(1)} %get-tuple-element.69.refs_5_.refs_1_, bf16[3072,384]{1,0:T(8,128)(2,1)S(1)} %get-tuple-element.70.refs_2_, bf16[512,384]{1,0:T(8,128)(2,1)S(1)} %get-tuple-element.71.refs_3_, ...), custom_call_target="tpu_custom_call" | custom-call | flops 1 | bytes 1 | tf_op jit(solution)/shard_map/first_gradient/pallas_call | solution.py:801
  (106 shorter events, 31.3 us)
Async XLA Ops:
  1.7 20.5 %collective-permute-start.3 = (bf16[2064,128]{1,0:T(8,128)(2,1)S(1)}, bf16[2064,128]{1,0:T(8,128)(2,1)S(1)}, u32[]{:S(2)}, u32[]{:S(2)}) collective-permute-start(bf16[2064,128]{1,0:T(8,128)(2,1)S(1)} %mid_with_head.1.refs_6_), channel_id=1, source_target_pairs={{0,2},{1,3},{2,0},{3,1},{4,6},{5,7},{6,4},{7,5},{8,10},{9,11},{10,... | collective-permute-start | bytes 1585160 | tf_op jit(solution)/shard_map/ppermute | solution.py:386
  4.8 18.3 %collective-permute-start.2 = (bf16[2064,128]{1,0:T(8,128)(2,1)S(1)}, bf16[2064,128]{1,0:T(8,128)(2,1)S(1)}, u32[]{:S(2)}, u32[]{:S(2)}) collective-permute-start(bf16[2064,128]{1,0:T(8,128)(2,1)S(1)} %mid_with_head.1.refs_6_), channel_id=1, source_target_pairs={{0,1},{1,0},{2,3},{3,2},{4,5},{5,4},{6,7},{7,6},{8,9},{9,8},{10,11... | collective-permute-start | bytes 1585160 | tf_op jit(solution)/shard_map/ppermute | solution.py:386
  17.7 18.1 %collective-permute-start = (bf16[400,512]{1,0:T(8,128)(2,1)}, bf16[400,512]{1,0:T(8,128)(2,1)}, u32[]{:S(2)}, u32[]{:S(2)}) collective-permute-start(bf16[400,512]{1,0:T(8,128)(2,1)} %get-tuple-element.46), channel_id=1, source_target_pairs={{0,1},{1,2},{2,3},{3,4},{4,5},{5,6},{6,7},{7,8},{8,9},{9,10},{10,1... | collective-permute-start | bytes 1228808 | tf_op jit(solution)/shard_map/ppermute | solution.py:839
  20.8 14.9 %collective-permute-start.1 = (bf16[400,512]{1,0:T(8,128)(2,1)}, bf16[400,512]{1,0:T(8,128)(2,1)}, u32[]{:S(2)}, u32[]{:S(2)}) collective-permute-start(bf16[400,512]{1,0:T(8,128)(2,1)} %get-tuple-element.47), channel_id=1, source_target_pairs={{1,0},{2,1},{3,2},{4,3},{5,4},{6,5},{7,6},{8,7},{9,8},{10,9},{11,1... | collective-permute-start | bytes 1228808 | tf_op jit(solution)/shard_map/ppermute | solution.py:840
  45.3 3.1 %collective-permute-start.4 = (bf16[2,4,96,512]{3,2,1,0:T(8,128)(2,1)S(1)}, bf16[2,4,96,512]{3,2,1,0:T(8,128)(2,1)S(1)}, u32[]{:S(2)}, u32[]{:S(2)}) collective-permute-start(bf16[2,4,96,512]{3,2,1,0:T(8,128)(2,1)S(1)} %get-tuple-element.52), channel_id=1, source_target_pairs={{0,1},{1,0},{2,3},{3,2},{4,5},{5,4},{6,7},{7,6},{8,9},{9,8},{10,11... | collective-permute-start | bytes 2359304 | tf_op jit(solution)/shard_map/ppermute | solution.py:386
  46.5 11.5 %collective-permute-start.6 = (bf16[2064,128]{1,0:T(8,128)(2,1)S(1)}, bf16[2064,128]{1,0:T(8,128)(2,1)S(1)}, u32[]{:S(2)}, u32[]{:S(2)}) collective-permute-start(bf16[2064,128]{1,0:T(8,128)(2,1)S(1)} %copy-done.9), channel_id=1, source_target_pairs={{0,1},{1,0},{2,3},{3,2},{4,5},{5,4},{6,7},{7,6},{8,9},{9,8},{10,11... | collective-permute-start | bytes 1585160 | tf_op jit(solution)/shard_map/ppermute | solution.py:386
  49.1 11.5 %collective-permute-start.5 = (bf16[4,96,512]{2,1,0:T(8,128)(2,1)S(1)}, bf16[4,96,512]{2,1,0:T(8,128)(2,1)S(1)}, u32[]{:S(2)}, u32[]{:S(2)}) collective-permute-start(bf16[4,96,512]{2,1,0:T(8,128)(2,1)S(1)} %get-tuple-element.54.dep_ref), channel_id=1, source_target_pairs={{0,2},{1,3},{2,0},{3,1},{4,6},{5,7},{6,4},{7,5},{8,10},{9,11},{10,... | collective-permute-start | bytes 1179656 | tf_op jit(solution)/shard_map/ppermute | solution.py:386
  63.4 5.5 %collective-permute-start.7 = (bf16[96,512]{1,0:T(8,128)(2,1)}, bf16[96,512]{1,0:T(8,128)(2,1)S(1)}, u32[]{:S(2)}, u32[]{:S(2)}) collective-permute-start(bf16[96,512]{1,0:T(8,128)(2,1)} %get-tuple-element.57), channel_id=1, source_target_pairs={{0,4},{1,5},{2,6},{3,7},{4,0},{5,1},{6,2},{7,3},{8,12},{9,13},{10,... | collective-permute-start | bytes 294920 | tf_op jit(solution)/shard_map/ppermute | solution.py:386
  66.0 10.2 %collective-permute-start.8 = (bf16[96,512]{1,0:T(8,128)(2,1)}, bf16[96,512]{1,0:T(8,128)(2,1)}, u32[]{:S(2)}, u32[]{:S(2)}) collective-permute-start(bf16[96,512]{1,0:T(8,128)(2,1)} %get-tuple-element.58), channel_id=1, source_target_pairs={{0,8},{1,9},{2,10},{3,11},{4,12},{5,13},{6,14},{7,15},{8,0},{9,1},... | collective-permute-start | bytes 294920 | tf_op jit(solution)/shard_map/ppermute | solution.py:386
  68.6 7.6 %collective-permute-start.9 = (bf16[96,512]{1,0:T(8,128)(2,1)}, bf16[96,512]{1,0:T(8,128)(2,1)}, u32[]{:S(2)}, u32[]{:S(2)}) collective-permute-start(bf16[96,512]{1,0:T(8,128)(2,1)} %get-tuple-element.59), channel_id=1, source_target_pairs={{0,12},{1,13},{2,14},{3,15},{4,8},{5,9},{6,10},{7,11},{8,4},{9,5},... | collective-permute-start | bytes 294920 | tf_op jit(solution)/shard_map/ppermute | solution.py:386
  79.0 13.9 %collective-permute-start.12 = (bf16[96,512]{1,0:T(8,128)(2,1)S(1)}, bf16[96,512]{1,0:T(8,128)(2,1)}, u32[]{:S(2)}, u32[]{:S(2)}) collective-permute-start(bf16[96,512]{1,0:T(8,128)(2,1)S(1)} %first_activation.1.dep_ref.refs_2_.refs_5_), channel_id=1, source_target_pairs={{0,12},{1,13},{2,14},{3,15},{4,8},{5,9},{6,10},{7,11},{8,4},{9,5},... | collective-permute-start | bytes 294920 | tf_op jit(solution)/shard_map/ppermute | solution.py:386
  81.6 11.4 %collective-permute-start.11 = (bf16[96,512]{1,0:T(8,128)(2,1)S(1)}, bf16[96,512]{1,0:T(8,128)(2,1)}, u32[]{:S(2)}, u32[]{:S(2)}) collective-permute-start(bf16[96,512]{1,0:T(8,128)(2,1)S(1)} %first_activation.1.dep_ref.refs_2_.refs_5_), channel_id=1, source_target_pairs={{0,8},{1,9},{2,10},{3,11},{4,12},{5,13},{6,14},{7,15},{8,0},{9,1},... | collective-permute-start | bytes 294920 | tf_op jit(solution)/shard_map/ppermute | solution.py:386
  82.2 10.8 %collective-permute-start.10 = (bf16[96,512]{1,0:T(8,128)(2,1)S(1)}, bf16[96,512]{1,0:T(8,128)(2,1)}, u32[]{:S(2)}, u32[]{:S(2)}) collective-permute-start(bf16[96,512]{1,0:T(8,128)(2,1)S(1)} %first_activation.1.dep_ref.refs_2_.refs_5_), channel_id=1, source_target_pairs={{0,4},{1,5},{2,6},{3,7},{4,0},{5,1},{6,2},{7,3},{8,12},{9,13},{10,... | collective-permute-start | bytes 294920 | tf_op jit(solution)/shard_map/ppermute | solution.py:386
  96.1 12.8 %collective-permute-start.19 = (bf16[2,2064,128]{2,1,0:T(8,128)(2,1)S(1)}, bf16[2,2064,128]{2,1,0:T(8,128)(2,1)S(1)}, u32[]{:S(2)}, u32[]{:S(2)}) collective-permute-start(bf16[2,2064,128]{2,1,0:T(8,128)(2,1)S(1)} %get-tuple-element.74), channel_id=1, source_target_pairs={{0,1},{1,0},{2,3},{3,2},{4,5},{5,4},{6,7},{7,6},{8,9},{9,8},{10,11... | collective-permute-start | bytes 3170312 | tf_op jit(solution)/shard_map/ppermute | solution.py:386
  96.1 7.6 %collective-permute-start.13 = (bf16[112,512]{1,0:T(8,128)(2,1)S(1)}, bf16[112,512]{1,0:T(8,128)(2,1)S(1)}, u32[]{:S(2)}, u32[]{:S(2)}) collective-permute-start(bf16[112,512]{1,0:T(8,128)(2,1)S(1)} %get-tuple-element.65), channel_id=1, source_target_pairs={{0,4},{1,5},{2,6},{3,7},{4,0},{5,1},{6,2},{7,3},{8,12},{9,13},{10,... | collective-permute-start | bytes 344072 | tf_op jit(solution)/shard_map/ppermute | solution.py:386
  96.9 11.8 %collective-permute-start.14 = (bf16[112,512]{1,0:T(8,128)(2,1)S(1)}, bf16[112,512]{1,0:T(8,128)(2,1)S(1)}, u32[]{:S(2)}, u32[]{:S(2)}) collective-permute-start(bf16[112,512]{1,0:T(8,128)(2,1)S(1)} %get-tuple-element.66), channel_id=1, source_target_pairs={{0,8},{1,9},{2,10},{3,11},{4,12},{5,13},{6,14},{7,15},{8,0},{9,1},... | collective-permute-start | bytes 344072 | tf_op jit(solution)/shard_map/ppermute | solution.py:386
  99.3 9.5 %collective-permute-start.15 = (bf16[112,512]{1,0:T(8,128)(2,1)S(1)}, bf16[112,512]{1,0:T(8,128)(2,1)S(1)}, u32[]{:S(2)}, u32[]{:S(2)}) collective-permute-start(bf16[112,512]{1,0:T(8,128)(2,1)S(1)} %get-tuple-element.67), channel_id=1, source_target_pairs={{0,12},{1,13},{2,14},{3,15},{4,8},{5,9},{6,10},{7,11},{8,4},{9,5},... | collective-permute-start | bytes 344072 | tf_op jit(solution)/shard_map/ppermute | solution.py:386
  109.1 12.7 %collective-permute-start.20 = (bf16[2064,128]{1,0:T(8,128)(2,1)S(1)}, bf16[2064,128]{1,0:T(8,128)(2,1)S(1)}, u32[]{:S(2)}, u32[]{:S(2)}) collective-permute-start(bf16[2064,128]{1,0:T(8,128)(2,1)S(1)} %get-tuple-element.76), channel_id=1, source_target_pairs={{0,2},{1,3},{2,0},{3,1},{4,6},{5,7},{6,4},{7,5},{8,10},{9,11},{10,... | collective-permute-start | bytes 1585160 | tf_op jit(solution)/shard_map/ppermute | solution.py:386
  109.8 12.9 %collective-permute-start.18 = (bf16[96,512]{1,0:T(8,128)(2,1)S(1)}, bf16[96,512]{1,0:T(8,128)(2,1)S(1)}, u32[]{:S(2)}, u32[]{:S(2)}) collective-permute-start(bf16[96,512]{1,0:T(8,128)(2,1)S(1)} %get-tuple-element.68.refs_3_.refs_0_), channel_id=1, source_target_pairs={{0,12},{1,13},{2,14},{3,15},{4,8},{5,9},{6,10},{7,11},{8,4},{9,5},... | collective-permute-start | bytes 294920 | tf_op jit(solution)/shard_map/ppermute | solution.py:386
  112.3 10.5 %collective-permute-start.17 = (bf16[96,512]{1,0:T(8,128)(2,1)S(1)}, bf16[96,512]{1,0:T(8,128)(2,1)S(1)}, u32[]{:S(2)}, u32[]{:S(2)}) collective-permute-start(bf16[96,512]{1,0:T(8,128)(2,1)S(1)} %get-tuple-element.68.refs_3_.refs_0_), channel_id=1, source_target_pairs={{0,8},{1,9},{2,10},{3,11},{4,12},{5,13},{6,14},{7,15},{8,0},{9,1},... | collective-permute-start | bytes 294920 | tf_op jit(solution)/shard_map/ppermute | solution.py:386
  113.6 9.2 %collective-permute-start.16 = (bf16[96,512]{1,0:T(8,128)(2,1)S(1)}, bf16[96,512]{1,0:T(8,128)(2,1)S(1)}, u32[]{:S(2)}, u32[]{:S(2)}) collective-permute-start(bf16[96,512]{1,0:T(8,128)(2,1)S(1)} %get-tuple-element.68.refs_3_.refs_0_), channel_id=1, source_target_pairs={{0,4},{1,5},{2,6},{3,7},{4,0},{5,1},{6,2},{7,3},{8,12},{9,13},{10,... | collective-permute-start | bytes 294920 | tf_op jit(solution)/shard_map/ppermute | solution.py:386
  123.5 9.2 %collective-permute-start.22 = (bf16[400,512]{1,0:T(8,128)(2,1)S(1)}, bf16[400,512]{1,0:T(8,128)(2,1)S(1)}, u32[]{:S(2)}, u32[]{:S(2)}) collective-permute-start(bf16[400,512]{1,0:T(8,128)(2,1)S(1)} %stack_parts.1.refs_4_), channel_id=1, source_target_pairs={{0,2},{1,3},{2,0},{3,1},{4,6},{5,7},{6,4},{7,5},{8,10},{9,11},{10,... | collective-permute-start | bytes 1228808 | tf_op jit(solution)/shard_map/ppermute | solution.py:386
  124.2 8.5 %collective-permute-start.21 = (bf16[400,512]{1,0:T(8,128)(2,1)S(1)}, bf16[400,512]{1,0:T(8,128)(2,1)S(1)}, u32[]{:S(2)}, u32[]{:S(2)}) collective-permute-start(bf16[400,512]{1,0:T(8,128)(2,1)S(1)} %stack_parts.1.refs_4_), channel_id=1, source_target_pairs={{0,1},{1,0},{2,3},{3,2},{4,5},{5,4},{6,7},{7,6},{8,9},{9,8},{10,11... | collective-permute-start | bytes 1228808 | tf_op jit(solution)/shard_map/ppermute | solution.py:386
  132.7 1.7 %collective-permute-start.23 = (bf16[400,512]{1,0:T(8,128)(2,1)S(1)}, bf16[400,512]{1,0:T(8,128)(2,1)S(1)}, u32[]{:S(2)}, u32[]{:S(2)}) collective-permute-start(bf16[400,512]{1,0:T(8,128)(2,1)S(1)} %collective-permute-done.22.refs_6_), channel_id=1, source_target_pairs={{0,1},{1,0},{2,3},{3,2},{4,5},{5,4},{6,7},{7,6},{8,9},{9,8},{10,11... | collective-permute-start | bytes 1228808 | tf_op jit(solution)/shard_map/ppermute | solution.py:386
  (30 other events, 252.4 us)

commit v7 on v6

--- a/solution.py
+++ b/solution.py
@@ -150,16 +150,16 @@
 
 
 def inner_kernel(
-    rows, size, hist_ref, drift_hbm, levels_hbm, table_hbm,
-    first_ref, last_ref, shift_ref, band_ref, rows_ref, inner_ref,
-    drift_ref, levels_ref, table_ref, arrived, all_shifts, *scratch,
+    rows, size, hist_ref, drift_hbm, levels_hbm, table_hbm, cot_hbm,
+    first_ref, last_ref, shift_ref, band_ref, cot_ref, rows_ref, inner_ref,
+    drift_ref, levels_ref, table_ref, cot_row, arrived, all_shifts, *scratch,
 ):
     step = pl.program_id(0)
     columns = drift_ref.shape[2]
 
     @pl.when(step == 0)
     def _():
-        sources = ((drift_hbm, drift_ref), (levels_hbm, levels_ref), (table_hbm, table_ref))
+        sources = ((drift_hbm, drift_ref), (levels_hbm, levels_ref), (table_hbm, table_ref), (cot_hbm, cot_row))
         copies = [pltpu.make_async_copy(*pair, arrived.at[n]) for n, pair in enumerate(sources)]
         for copy in copies:
             copy.start()
@@ -169,6 +169,7 @@
         for copy in copies:
             copy.wait()
         half_shifts(levels_ref, table_ref, all_shifts)
+        cot_ref[...] = jnp.broadcast_to(cot_row[...], (LANES, cot_row.shape[1])).T
         for out, start in ((first_ref, 0), (last_ref, rows - 2)):
             out[pl.ds(out.shape[0] - EXTRA, EXTRA), :] = drift_tail(drift_ref, start)
 
@@ -200,7 +201,7 @@
     )
 
 
-def inner_steps(tiles, drift, levels, table):
+def inner_steps(tiles, drift, levels, table, cot):
     scenarios = levels.shape[1]
     rows, columns = drift.shape[1:]
     per = tiles.shape[0] // scenarios
@@ -212,11 +213,12 @@
     return pl.pallas_call(
         functools.partial(inner_kernel, rows, size),
         grid=(scenarios // size,),
-        in_specs=[pl.BlockSpec((size * per, LANES), lambda i: (i, 0))] + [pl.BlockSpec(memory_space=pltpu.HBM)] * 3,
+        in_specs=[pl.BlockSpec((size * per, LANES), lambda i: (i, 0))] + [pl.BlockSpec(memory_space=pltpu.HBM)] * 4,
         out_specs=[pl.BlockSpec(sent.shape, lambda i: (0, 0))] * 2
         + [
             pl.BlockSpec((4, size, LANES), lambda i: (0, i, 0)),
             pl.BlockSpec(band.shape, lambda i: (0, 0)),
+            pl.BlockSpec((scenarios, LANES), lambda i: (0, 0)),
             pl.BlockSpec((size, rows * columns), lambda i: (i, 0)),
             pl.BlockSpec((size, inner), lambda i: (i, 0)),
         ],
@@ -225,6 +227,7 @@
             sent,
             pltpu.HBM(shifts.shape, f32),
             band,
+            jax.ShapeDtypeStruct((scenarios, LANES), f32),
             pltpu.HBM((scenarios, rows * columns), bf16),
             jax.ShapeDtypeStruct((scenarios, inner), bf16),
         ],
@@ -232,14 +235,15 @@
             pltpu.VMEM(drift.shape, f32),
             pltpu.VMEM(levels.shape, levels.dtype),
             pltpu.VMEM(table.shape, f32),
-            pltpu.SemaphoreType.DMA((3,)),
+            pltpu.VMEM(cot.shape, f32),
+            pltpu.SemaphoreType.DMA((4,)),
             pltpu.VMEM(shifts.shape, f32),
         ]
         + step_scratch([(2, max(rows - 3, 2))], size, columns),
         compiler_params=params(),
         cost_estimate=pl.CostEstimate(flops=1, bytes_accessed=1, transcendentals=0),
         name="inner_density_steps",
-    )(tiles, drift, levels, table)
+    )(tiles, drift, levels, table, cot)
 
 
 def halo_drift(ref, columns):
@@ -518,7 +522,9 @@
     )(own, *received, *deps)
 
 
-def pack_kernel(mid_ref, head_ref, out_ref, head_row, arrived):
+def pack_kernel(place_ref, mid_ref, head_ref, first_ref, out_ref, place_out_ref, head_row, arrived):
+    for n in range(4):
+        place_out_ref[n] = place_ref[n]
     hidden = mid_ref.shape[0]
     copies = [
         pltpu.make_async_copy(mid_ref, out_ref.at[pl.ds(0, hidden), :], arrived.at[0]),
@@ -531,18 +537,18 @@
     copies[0].wait()
 
 
-def pack(mid_weight, head):
+def pack(place, mid_weight, head, first):
     hidden, units = mid_weight.shape
     return pl.pallas_call(
         pack_kernel,
-        in_specs=[pl.BlockSpec(memory_space=pltpu.HBM)] * 2,
-        out_specs=vmem(),
-        out_shape=jax.ShapeDtypeStruct((hidden + EXTRA, units), bf16),
+        in_specs=[smem()] + [pl.BlockSpec(memory_space=pltpu.HBM)] * 3,
+        out_specs=[vmem(), smem()],
+        out_shape=[jax.ShapeDtypeStruct((hidden + EXTRA, units), bf16), jax.ShapeDtypeStruct(place.shape, place.dtype)],
         scratch_shapes=[pltpu.VMEM(head.shape, f32), pltpu.SemaphoreType.DMA((2,))],
         compiler_params=params(),
         cost_estimate=pl.CostEstimate(flops=1, bytes_accessed=1, transcendentals=0),
         name="mid_with_head",
-    )(*[pltpu.with_memory_space_constraint(array, pltpu.HBM) for array in (mid_weight, head)])
+    )(place, *[pltpu.with_memory_space_constraint(array, pltpu.HBM) for array in (mid_weight, head)], first)
 
 
 def two_halves(exact):
@@ -566,7 +572,7 @@
     own_ref, value_ref, mid_keep_ref, mid_send_ref = outs[:4]
     send_refs = outs[4:]
     part = place_ref[2]
-    block = cot_ref.shape[0]
+    block = first_refs[0].shape[0]
 
     def mid_rows(start):
         return jnp.concatenate([ref[pl.ds(start, width), :] for ref in mid_refs], axis=1)
@@ -588,7 +594,7 @@
     if width > block:
         value = jnp.concatenate([value, jnp.zeros((1, width - block), f32)], axis=1)
     value_ref[...] = value
-    cot = cot_ref[...]
+    cot = cot_ref[pl.ds(pl.multiple_of(place_ref[3] * block, SUBLANES), block), :1]
     head_part = jnp.sum(cot * second, axis=0, keepdims=True)
     back = (cot * head * (1.0 - second * second)).astype(bf16)
     units = mid_refs[0].shape[1]
@@ -617,7 +623,7 @@
 
 
 def middle(place, cot, firsts, mids, chunks, parts, width, deps=()):
-    block = cot.shape[0]
+    block = firsts[0].shape[0]
     partial = jax.ShapeDtypeStruct((2, *mids[0].shape), bf16)
     return pl.pallas_call(
         functools.partial(middle_kernel, chunks, parts, width),
@@ -663,7 +669,8 @@
 
 
 def mid_final_kernel(own_ref, other_ref, *refs):
-    out_ref, head_ref = refs[-2:]
+    out_ref, head_ref, token_ref = refs[-3:]
+    token_ref[...] = jnp.zeros(token_ref.shape, f32)
     body, tail = add_tail(own_ref[...], other_ref[...], out_ref.shape[0])
     out_ref[...] = body
     head_ref[...] = tail
@@ -677,6 +684,7 @@
         out_shape=[
             jax.ShapeDtypeStruct((hidden, own.shape[1]), bf16),
             jax.ShapeDtypeStruct((1, own.shape[1]), f32),
+            jax.ShapeDtypeStruct((SUBLANES, LANES), f32),
         ],
         compiler_params=params(),
         cost_estimate=pl.CostEstimate(flops=1, bytes_accessed=1, transcendentals=0),
@@ -765,6 +773,7 @@
     whole = refs[-1]
     step = pl.program_id(0)
     mine = place_ref[3]
+    values = [jnp.zeros((1, block), f32)] * 4
     for t, ref in enumerate(stacks):
         at = mine ^ (2 * (t % 2) + t // 2)
         piece = step ^ place_ref[2]
@@ -772,8 +781,12 @@
             pl.ds(pl.multiple_of(piece * block, block), block), :
         ]
         if with_value:
-            tail = ref[pl.ds(parts * block, EXTRA), :].astype(f32)
-            outs[1][pl.ds(at, 1), :] = tail[0:1] + tail[1:2]
+            tail = ref[pl.ds(parts * block, EXTRA), :block].astype(f32)
+            value = tail[0:1] + tail[1:2]
+            for q in range(4):
+                values[q] = jnp.where(at == q, value, values[q])
+    if with_value:
+        outs[1][...] = jnp.concatenate(values, axis=1)
     start = 0
     for ref in lefts:
         cells = ref.shape[0]
@@ -796,8 +809,8 @@
     out_specs = [pl.BlockSpec((cells, width), lambda i: (0, i * halves + half))]
     out_shape = [pltpu.HBM((cells, hidden), bf16)]
     if with_value:
-        out_specs.append(pl.BlockSpec((4, width), lambda i: (0, 0)))
-        out_shape.append(jax.ShapeDtypeStruct((4, width), f32))
+        out_specs.append(pl.BlockSpec((1, scenarios), lambda i: (0, 0)))
+        out_shape.append(jax.ShapeDtypeStruct((1, scenarios), f32))
     return pl.pallas_call(
         functools.partial(first_grad_kernel, parts, block, len(lefts), with_value),
         grid=(parts,),
@@ -821,18 +834,18 @@
     width = hidden // parts
     block = scenarios // 4
     index = lax.axis_index("grid")
-    core, side, part = index % 2, index // 2 % 2, index // 4
+    core, side, part = index & 1, (index >> 1) & 1, index >> 2
     mine = 2 * core + side
     tiles = pltpu.with_memory_space_constraint(to_tiles(hist), pltpu.HBM)
 
     place = jnp.stack([core, side, part, mine])
-    cot = lax.dynamic_slice_in_dim(cotangent, mine * block, block)[:, None]
     halves = 1
 
-    mids = [pack(mid_weight, head_weight[None, :])]
+    small = [pltpu.with_memory_space_constraint(array, pltpu.HBM) for array in (drift, shocks.T, shock_table.T, cotangent[None, :])]
+    packed, place = pack(place, mid_weight, head_weight[None, :], small[-1])
+    mids = [packed]
     mids += [swap(mids[0], count, 1), swap(mids[0], count, 2)]
-    small = [pltpu.with_memory_space_constraint(array, pltpu.HBM) for array in (drift, shocks.T, shock_table.T)]
-    first_rows, last_rows, shifts, band, own_rows, inner = inner_steps(tiles, *small)
+    first_rows, last_rows, shifts, band, cot, own_rows, inner = inner_steps(tiles, *small)
     inner = inner if rows > 4 else None
     forward = [(i, i + 1) for i in range(count - 1)]
     backward = [(i + 1, i) for i in range(count - 1)]
@@ -861,18 +874,18 @@
     mid_keep, mid_send = mid_add(mid_keep, swap(mid_send, count, 1), [back])
     lefts = transposed([low, high] if inner is None else [low, inner, high], [back])
     pieces = [back] + [swap(back, count, 4 * k) for k in range(1, parts)]
-    grad_mid, grad_head = mid_final(mid_keep, swap(mid_send, count, 2))
-    stacks = stack(pieces + [tail], halves, [lefts[0], grad_head])
+    grad_mid, grad_head, token = mid_final(mid_keep, swap(mid_send, count, 2))
+    stacks = stack(pieces + [tail], halves, [lefts[0], token])
     grad_first = None
     for half, own_stack in enumerate(stacks):
         gathered = [own_stack, swap(own_stack, count, 1), swap(own_stack, count, 2)]
         gathered.append(swap(gathered[2], count, 1))
         results = first_grad(
-            place, lefts, gathered, grad_first, hidden, parts, block, half, halves, [grad_head]
+            place, lefts, gathered, grad_first, hidden, parts, block, half, halves, []
         )
         grad_first = results[0]
         if half == 0:
-            value = results[1][:, :block].reshape(scenarios)
+            value = results[1].reshape(scenarios)
     return from_tiles(density, hist.shape), value, grad_first, grad_mid, grad_head[0]
 
 

time: 150 us -> 134 us (0.89)
  local copies, waits for them, and re-layouts: 14.7 us -> 1.26 us
  Pallas kernels: 65.3 us -> 60.9 us
  starting transfers between devices: 30.2 us -> 32.5 us
    unnamed x60 -> x6, local copies, waits for them, and re-layouts: 13.2 us -> 0.02 us
    ppermute x22, starting transfers between devices: 25.8 us -> 28.6 us  [swap(): return lax.ppermute(values, 'grid', [(i, i ^ flip) for i in range(count)])]
    pallas_call x2, Pallas kernels: 14.8 us -> 12.9 us  [density_steps(): pl.pallas_call(functools.partial(density_kernel, None), grid=(steps,), in...]
  transfers between devices with their start and end apart: 24 -> 24, of which waited for: 9 -> 8; matrix products, arithmetic and copies ran while one was open for 1% -> 0% of each run, Pallas kernels for 25% -> 27%
where the time goes in v7:
time: 134 us; the launch traced here: 132 us
  Pallas kernels  60.9 us (45%)
  waiting for transfers between devices  36.2 us (27%)
  starting transfers between devices  32.5 us (24%)
    ppermute x22, waiting for transfers between devices, swap(): return lax.ppermute(values, 'grid', [(i, i ^ flip) for i in range(count)])  36.2 us
    ppermute x22, starting transfers between devices, swap(): return lax.ppermute(values, 'grid', [(i, i ^ flip) for i in range(count)])  28.6 us
    pallas_call x2, Pallas kernels, density_steps(): pl.pallas_call(functools.partial(density_kernel, None), grid=(steps,), in...  12.9 us
    pallas_call x1, Pallas kernels, first_grad(): pl.pallas_call(functools.partial(first_grad_kernel, parts, block, len(lef...  12.1 us
    pallas_call x1, Pallas kernels, inner_steps(): pl.pallas_call(functools.partial(inner_kernel, rows, size), grid=(scenari...  11.5 us
    pallas_call x1, Pallas kernels, inner_product(): pl.pallas_call(functools.partial(inner_product_kernel, count), grid=(hidd...  8.17 us
    pallas_call x1, Pallas kernels, edge_product(): pl.pallas_call(functools.partial(edge_product_kernel, block, inner is not...  4.43 us
    pallas_call x1, Pallas kernels, edge_steps(): pl.pallas_call(functools.partial(density_kernel, segments), grid=(scenari...  3.65 us
  transfers between devices with their start and end apart: 24, of which 8 were waited for; matrix products, arithmetic and copies ran while one was open for 0% of the time, Pallas kernels for 27%

profile of v7, /device:TPU:0, one launch (start us, length us, event | category | flops | bytes accessed | tf_op | source)
XLA Modules:
  0.0 132.4 jit_solution(1220526959590109532)
XLA Ops:
  2.0 2.2 %mid_with_head.1 = (bf16[2064,128]{1,0:T(8,128)(2,1)S(1)}, s32[4]{0:T(128)S(1)}) custom-call(s32[4]{0:T(128)S(1)} %pad_add_fusion.place_ref, bf16[2048,128]{1,0:T(8,128)(2,1)} %mid_ref.1, f32[1,128]{1,0:T(1,128)} %bitcast.22, f32[1,384]{1,0:T(1,128)} %broadcast_in_dim.6.cot_hbm.first_ref), custom_call_target="tpu_custom_call" | custom-call | flops 1 | bytes 1 | tf_op jit(solution)/shard_map/mid_with_head/pallas_call | solution.py:542
  4.2 3.0 %collective-permute-start.3 = (bf16[2064,128]{1,0:T(8,128)(2,1)S(1)}, bf16[2064,128]{1,0:T(8,128)(2,1)S(1)}, u32[]{:S(2)}, u32[]{:S(2)}) collective-permute-start(bf16[2064,128]{1,0:T(8,128)(2,1)S(1)} %get-tuple-element.54.refs_6_), channel_id=1, source_target_pairs={{0,2},{1,3},{2,0},{3,1},{4,6},{5,7},{6,4},{7,5},{8,10},{9,11},{10,... | collective-permute-start | bytes 1585160 | tf_op jit(solution)/shard_map/ppermute | solution.py:390
  7.2 11.5 %inner_density_steps.1 = (bf16[400,512]{1,0:T(8,128)(2,1)S(1)}, bf16[400,512]{1,0:T(8,128)(2,1)S(1)}, f32[4,384,128]{2,1,0:T(8,128)}, bf16[512,256]{1,0:T(8,128)...) custom-call(f32[12288,128]{1,0:T(8,128)} %bitcast.18, ...), custom_call_target="tpu_custom_call" | custom-call | flops 1 | bytes 1 | tf_op jit(solution)/shard_map/inner_density_steps/pallas_call | solution.py:213
  18.7 2.4 %collective-permute-start = (bf16[400,512]{1,0:T(8,128)(2,1)S(1)}, bf16[400,512]{1,0:T(8,128)(2,1)S(1)}, u32[]{:S(2)}, u32[]{:S(2)}) collective-permute-start(bf16[400,512]{1,0:T(8,128)(2,1)S(1)} %get-tuple-element.50), channel_id=1, source_target_pairs={{0,1},{1,2},{2,3},{3,4},{4,5},{5,6},{6,7},{7,8},{8,9},{9,10},{10,1... | collective-permute-start | bytes 1228808 | tf_op jit(solution)/shard_map/ppermute | solution.py:852
  22.7 8.2 %inner_product.1.dep_ref.refs_0_ = f32[4,384,512]{2,1,0:T(8,128)S(1)} custom-call(bf16[384,3072]{1,0:T(8,128)(2,1)S(1)} %get-tuple-element.53.inputs_ref.refs_1_, bf16[4096,2048]{1,0:T(8,128)(2,1)} %bottom_ref.1, bf16[4096,2048]{1,0:T(8,128)(2,1)} %bottom_ref.1, bf16[4096,2048]{1,0:T(8,128)(2,1)} %bottom_ref.1, bf16[4096,2048]{1,0:T(8,128)(2,1)} %bottom_ref.1, ...), custom_call_target="tpu_custom_call" | custom-call | flops 1 | bytes 1 | tf_op jit(solution)/shard_map/inner_product/pallas_call | solution.py:407
  30.9 3.7 %edge_density_steps.1 = (bf16[384,512]{1,0:T(8,128)(2,1)S(1)}, bf16[384,512]{1,0:T(8,128)(2,1)S(1)}) custom-call(f32[2,16,256]{2,1,0:T(8,128)S(1)} %copy-done.2, f32[4,384,128]{2,1,0:T(8,128)S(1)} %copy-done.1, bf16[512,256]{1,0:T(8,128)(2,1)S(1)} %get-tuple-element.48.band_ref, bf16[384,4096]{1,0:T(8,128)(2,1)S(1)} %copy-done, ...), custom_call_target="tpu_custom_call" | custom-call | flops 1 | bytes 1 | tf_op jit(solution)/shard_map/edge_density_steps/pallas_call | solution.py:337
  34.6 4.4 %edge_product.1 = (f32[2,4,96,512]{3,2,1,0:T(8,128)S(1)}, bf16[2,4,96,512]{3,2,1,0:T(8,128)(2,1)S(1)}) custom-call(s32[4]{0:T(128)S(1)} %get-tuple-element.52.place_ref.refs_0_, bf16[384,512]{1,0:T(8,128)(2,1)S(1)} %get-tuple-element.55.low_ref.refs_0_, bf16[384,512]{1,0:T(8,128)(2,1)S(1)} %get-tuple-element.56.high_ref.refs_2_, ...), custom_call_target="tpu_custom_call" | custom-call | flops 1 | bytes 1 | tf_op jit(solution)/shard_map/edge_product/pallas_call | solution.py:449
  40.3 1.8 %collective-permute-done.4.other_ref = bf16[2,4,96,512]{3,2,1,0:T(8,128)(2,1)S(1)} collective-permute-done((bf16[2,4,96,512]{3,2,1,0:T(8,128)(2,1)S(1)}, bf16[2,4,96,512]{3,2,1,0:T(8,128)(2,1)S(1)}, u32[]{:S(2)}, u32[]{:S(2)}) %collective-permute-start.4) | collective-permute-done | bytes 786464 | tf_op jit(solution)/shard_map/ppermute | solution.py:390
  42.8 2.2 %collective-permute-start.5 = (bf16[4,96,512]{2,1,0:T(8,128)(2,1)S(1)}, bf16[4,96,512]{2,1,0:T(8,128)(2,1)S(1)}, u32[]{:S(2)}, u32[]{:S(2)}) collective-permute-start(bf16[4,96,512]{2,1,0:T(8,128)(2,1)S(1)} %get-tuple-element.60.dep_ref), channel_id=1, source_target_pairs={{0,2},{1,3},{2,0},{3,1},{4,6},{5,7},{6,4},{7,5},{8,10},{9,11},{10,... | collective-permute-start | bytes 1179656 | tf_op jit(solution)/shard_map/ppermute | solution.py:390
  45.0 6.5 %density_steps.2 = (f32[12288,128]{1,0:T(8,128)}, f32[8,128]{1,0:T(8,128)S(1)}) custom-call(f32[2,16,256]{2,1,0:T(8,128)S(1)} %copy-done.2, f32[4,384,128]{2,1,0:T(8,128)S(1)} %copy-done.1, bf16[512,256]{1,0:T(8,128)(2,1)S(1)} %get-tuple-element.48.band_ref, bf16[384,4096]{1,0:T(8,128)(2,1)S(1)} %copy-done, ...), custom_call_target="tpu_custom_call" | custom-call | flops 1 | bytes 1 | tf_op jit(solution)/shard_map/density_steps/pallas_call | solution.py:364
  51.5 3.2 %collective-permute-done.5.other_ref = bf16[4,96,512]{2,1,0:T(8,128)(2,1)S(1)} collective-permute-done((bf16[4,96,512]{2,1,0:T(8,128)(2,1)S(1)}, bf16[4,96,512]{2,1,0:T(8,128)(2,1)S(1)}, u32[]{:S(2)}, u32[]{:S(2)}) %collective-permute-start.5) | collective-permute-done | bytes 393248 | tf_op jit(solution)/shard_map/ppermute | solution.py:390
  55.3 3.0 %collective-permute-start.7 = (bf16[96,512]{1,0:T(8,128)(2,1)S(1)}, bf16[96,512]{1,0:T(8,128)(2,1)S(1)}, u32[]{:S(2)}, u32[]{:S(2)}) collective-permute-start(bf16[96,512]{1,0:T(8,128)(2,1)S(1)} %get-tuple-element.63), channel_id=1, source_target_pairs={{0,4},{1,5},{2,6},{3,7},{4,0},{5,1},{6,2},{7,3},{8,12},{9,13},{10,... | collective-permute-start | bytes 294920 | tf_op jit(solution)/shard_map/ppermute | solution.py:390
  58.3 2.6 %collective-permute-start.8 = (bf16[96,512]{1,0:T(8,128)(2,1)S(1)}, bf16[96,512]{1,0:T(8,128)(2,1)S(1)}, u32[]{:S(2)}, u32[]{:S(2)}) collective-permute-start(bf16[96,512]{1,0:T(8,128)(2,1)S(1)} %get-tuple-element.64), channel_id=1, source_target_pairs={{0,8},{1,9},{2,10},{3,11},{4,12},{5,13},{6,14},{7,15},{8,0},{9,1},... | collective-permute-start | bytes 294920 | tf_op jit(solution)/shard_map/ppermute | solution.py:390
  60.9 7.3 %collective-permute-done.8.refs_2_ = bf16[96,512]{1,0:T(8,128)(2,1)S(1)} collective-permute-done((bf16[96,512]{1,0:T(8,128)(2,1)S(1)}, bf16[96,512]{1,0:T(8,128)(2,1)S(1)}, u32[]{:S(2)}, u32[]{:S(2)}) %collective-permute-start.8) | collective-permute-done | bytes 98336 | tf_op jit(solution)/shard_map/ppermute | solution.py:390
  68.2 2.5 %collective-permute-start.12 = (bf16[96,512]{1,0:T(8,128)(2,1)S(1)}, bf16[96,512]{1,0:T(8,128)(2,1)S(1)}, u32[]{:S(2)}, u32[]{:S(2)}) collective-permute-start(bf16[96,512]{1,0:T(8,128)(2,1)S(1)} %first_activation.1.dep_ref.refs_2_.refs_5_), channel_id=1, source_target_pairs={{0,12},{1,13},{2,14},{3,15},{4,8},{5,9},{6,10},{7,11},{8,4},{9,5},... | collective-permute-start | bytes 294920 | tf_op jit(solution)/shard_map/ppermute | solution.py:390
  72.7 6.5 %density_steps.3 = (f32[12288,128]{1,0:T(8,128)}, f32[8,128]{1,0:T(8,128)S(1)}) custom-call(f32[2,16,256]{2,1,0:T(8,128)S(1)} %copy-done.2, f32[4,384,128]{2,1,0:T(8,128)S(1)} %copy-done.1, bf16[512,256]{1,0:T(8,128)(2,1)S(1)} %get-tuple-element.48.band_ref, bf16[384,4096]{1,0:T(8,128)(2,1)S(1)} %copy-done, ...), custom_call_target="tpu_custom_call", output_to_operand_aliasing={{0}: (9, {})} | custom-call | flops 1 | bytes 1 | tf_op jit(solution)/shard_map/density_steps/pallas_call | solution.py:364
  79.2 2.4 %value_layers.1 = (f32[96,512]{1,0:T(8,128)S(1)}, f32[1,512]{1,0:T(1,128)S(1)}, bf16[2,2064,128]{2,1,0:T(8,128)(2,1)S(1)}, bf16[2,2064,128]{2,1,0:T(8,128)(2,1)S...) custom-call(s32[4]{0:T(128)S(1)} %get-tuple-element.52.place_ref.refs_0_, ...), custom_call_target="tpu_custom_call" | custom-call | flops 1 | bytes 1 | tf_op jit(solution)/shard_map/value_layers/pallas_call | solution.py:628
  82.4 2.3 %collective-permute-start.14 = (bf16[112,512]{1,0:T(8,128)(2,1)S(1)}, bf16[112,512]{1,0:T(8,128)(2,1)S(1)}, u32[]{:S(2)}, u32[]{:S(2)}) collective-permute-start(bf16[112,512]{1,0:T(8,128)(2,1)S(1)} %get-tuple-element.73), channel_id=1, source_target_pairs={{0,8},{1,9},{2,10},{3,11},{4,12},{5,13},{6,14},{7,15},{8,0},{9,1},... | collective-permute-start | bytes 344072 | tf_op jit(solution)/shard_map/ppermute | solution.py:390
  86.1 3.1 %collective-permute-done.13.refs_2_ = bf16[112,512]{1,0:T(8,128)(2,1)S(1)} collective-permute-done((bf16[112,512]{1,0:T(8,128)(2,1)S(1)}, bf16[112,512]{1,0:T(8,128)(2,1)S(1)}, u32[]{:S(2)}, u32[]{:S(2)}) %collective-permute-start.13) | collective-permute-done | bytes 114720 | tf_op jit(solution)/shard_map/ppermute | solution.py:390
  89.2 5.1 %collective-permute-done.14.refs_3_ = bf16[112,512]{1,0:T(8,128)(2,1)S(1)} collective-permute-done((bf16[112,512]{1,0:T(8,128)(2,1)S(1)}, bf16[112,512]{1,0:T(8,128)(2,1)S(1)}, u32[]{:S(2)}, u32[]{:S(2)}) %collective-permute-start.14) | collective-permute-done | bytes 114720 | tf_op jit(solution)/shard_map/ppermute | solution.py:390
  96.0 2.6 %collective-permute-start.18 = (bf16[96,512]{1,0:T(8,128)(2,1)S(1)}, bf16[96,512]{1,0:T(8,128)(2,1)S(1)}, u32[]{:S(2)}, u32[]{:S(2)}) collective-permute-start(bf16[96,512]{1,0:T(8,128)(2,1)S(1)} %get-tuple-element.75.refs_3_.refs_0_), channel_id=1, source_target_pairs={{0,12},{1,13},{2,14},{3,15},{4,8},{5,9},{6,10},{7,11},{8,4},{9,5},... | collective-permute-start | bytes 294920 | tf_op jit(solution)/shard_map/ppermute | solution.py:390
  101.3 6.1 %collective-permute-done.20.other_ref = bf16[2064,128]{1,0:T(8,128)(2,1)S(1)} collective-permute-done((bf16[2064,128]{1,0:T(8,128)(2,1)S(1)}, bf16[2064,128]{1,0:T(8,128)(2,1)S(1)}, u32[]{:S(2)}, u32[]{:S(2)}) %collective-permute-start.20) | collective-permute-done | bytes 528416 | tf_op jit(solution)/shard_map/ppermute | solution.py:390
  110.1 7.8 %collective-permute-done.22.refs_6_ = bf16[400,512]{1,0:T(8,128)(2,1)S(1)} collective-permute-done((bf16[400,512]{1,0:T(8,128)(2,1)S(1)}, bf16[400,512]{1,0:T(8,128)(2,1)S(1)}, u32[]{:S(2)}, u32[]{:S(2)}) %collective-permute-start.22) | collective-permute-done | bytes 409632 | tf_op jit(solution)/shard_map/ppermute | solution.py:390
  119.6 12.1 %first_gradient.1 = (bf16[4096,2048]{1,0:T(8,128)(2,1)}, f32[1,384]{1,0:T(1,128)S(1)}) custom-call(s32[4]{0:T(128)S(1)} %get-tuple-element.52.place_ref.refs_0_, bf16[512,384]{1,0:T(8,128)(2,1)S(1)} %get-tuple-element.76.refs_5_.refs_1_, bf16[3072,384]{1,0:T(8,128)(2,1)S(1)} %get-tuple-element.77.refs_2_, bf16[512,384]{1,0:T(8,128)(2,1)S(1)} %get-tuple-element.78.refs_3_, ...), custom_call_target="tpu_custom_call" | custom-call | flops 1 | bytes 1 | tf_op jit(solution)/shard_map/first_gradient/pallas_call | solution.py:814
  (50 shorter events, 19.1 us)
Async XLA Ops:
  4.2 18.5 %collective-permute-start.3 = (bf16[2064,128]{1,0:T(8,128)(2,1)S(1)}, bf16[2064,128]{1,0:T(8,128)(2,1)S(1)}, u32[]{:S(2)}, u32[]{:S(2)}) collective-permute-start(bf16[2064,128]{1,0:T(8,128)(2,1)S(1)} %get-tuple-element.54.refs_6_), channel_id=1, source_target_pairs={{0,2},{1,3},{2,0},{3,1},{4,6},{5,7},{6,4},{7,5},{8,10},{9,11},{10,... | collective-permute-start | bytes 1585160 | tf_op jit(solution)/shard_map/ppermute | solution.py:390
  7.2 15.5 %collective-permute-start.2 = (bf16[2064,128]{1,0:T(8,128)(2,1)S(1)}, bf16[2064,128]{1,0:T(8,128)(2,1)S(1)}, u32[]{:S(2)}, u32[]{:S(2)}) collective-permute-start(bf16[2064,128]{1,0:T(8,128)(2,1)S(1)} %get-tuple-element.54.refs_6_), channel_id=1, source_target_pairs={{0,1},{1,0},{2,3},{3,2},{4,5},{5,4},{6,7},{7,6},{8,9},{9,8},{10,11... | collective-permute-start | bytes 1585160 | tf_op jit(solution)/shard_map/ppermute | solution.py:390
  18.7 12.2 %collective-permute-start = (bf16[400,512]{1,0:T(8,128)(2,1)S(1)}, bf16[400,512]{1,0:T(8,128)(2,1)S(1)}, u32[]{:S(2)}, u32[]{:S(2)}) collective-permute-start(bf16[400,512]{1,0:T(8,128)(2,1)S(1)} %get-tuple-element.50), channel_id=1, source_target_pairs={{0,1},{1,2},{2,3},{3,4},{4,5},{5,6},{6,7},{7,8},{8,9},{9,10},{10,1... | collective-permute-start | bytes 1228808 | tf_op jit(solution)/shard_map/ppermute | solution.py:852
  21.2 9.7 %collective-permute-start.1 = (bf16[400,512]{1,0:T(8,128)(2,1)S(1)}, bf16[400,512]{1,0:T(8,128)(2,1)S(1)}, u32[]{:S(2)}, u32[]{:S(2)}) collective-permute-start(bf16[400,512]{1,0:T(8,128)(2,1)S(1)} %get-tuple-element.51), channel_id=1, source_target_pairs={{1,0},{2,1},{3,2},{4,3},{5,4},{6,5},{7,6},{8,7},{9,8},{10,9},{11,1... | collective-permute-start | bytes 1228808 | tf_op jit(solution)/shard_map/ppermute | solution.py:853
  39.0 3.1 %collective-permute-start.4 = (bf16[2,4,96,512]{3,2,1,0:T(8,128)(2,1)S(1)}, bf16[2,4,96,512]{3,2,1,0:T(8,128)(2,1)S(1)}, u32[]{:S(2)}, u32[]{:S(2)}) collective-permute-start(bf16[2,4,96,512]{3,2,1,0:T(8,128)(2,1)S(1)} %get-tuple-element.58), channel_id=1, source_target_pairs={{0,1},{1,0},{2,3},{3,2},{4,5},{5,4},{6,7},{7,6},{8,9},{9,8},{10,11... | collective-permute-start | bytes 2359304 | tf_op jit(solution)/shard_map/ppermute | solution.py:390
  40.2 11.3 %collective-permute-start.6 = (bf16[2064,128]{1,0:T(8,128)(2,1)S(1)}, bf16[2064,128]{1,0:T(8,128)(2,1)S(1)}, u32[]{:S(2)}, u32[]{:S(2)}) collective-permute-start(bf16[2064,128]{1,0:T(8,128)(2,1)S(1)} %collective-permute-done.3.refs_7_.refs_8_), channel_id=1, source_target_pairs={{0,1},{1,0},{2,3},{3,2},{4,5},{5,4},{6,7},{7,6},{8,9},{9,8},{10,11... | collective-permute-start | bytes 1585160 | tf_op jit(solution)/shard_map/ppermute | solution.py:390
  42.8 11.9 %collective-permute-start.5 = (bf16[4,96,512]{2,1,0:T(8,128)(2,1)S(1)}, bf16[4,96,512]{2,1,0:T(8,128)(2,1)S(1)}, u32[]{:S(2)}, u32[]{:S(2)}) collective-permute-start(bf16[4,96,512]{2,1,0:T(8,128)(2,1)S(1)} %get-tuple-element.60.dep_ref), channel_id=1, source_target_pairs={{0,2},{1,3},{2,0},{3,1},{4,6},{5,7},{6,4},{7,5},{8,10},{9,11},{10,... | collective-permute-start | bytes 1179656 | tf_op jit(solution)/shard_map/ppermute | solution.py:390
  55.3 5.6 %collective-permute-start.7 = (bf16[96,512]{1,0:T(8,128)(2,1)S(1)}, bf16[96,512]{1,0:T(8,128)(2,1)S(1)}, u32[]{:S(2)}, u32[]{:S(2)}) collective-permute-start(bf16[96,512]{1,0:T(8,128)(2,1)S(1)} %get-tuple-element.63), channel_id=1, source_target_pairs={{0,4},{1,5},{2,6},{3,7},{4,0},{5,1},{6,2},{7,3},{8,12},{9,13},{10,... | collective-permute-start | bytes 294920 | tf_op jit(solution)/shard_map/ppermute | solution.py:390
  58.3 9.9 %collective-permute-start.8 = (bf16[96,512]{1,0:T(8,128)(2,1)S(1)}, bf16[96,512]{1,0:T(8,128)(2,1)S(1)}, u32[]{:S(2)}, u32[]{:S(2)}) collective-permute-start(bf16[96,512]{1,0:T(8,128)(2,1)S(1)} %get-tuple-element.64), channel_id=1, source_target_pairs={{0,8},{1,9},{2,10},{3,11},{4,12},{5,13},{6,14},{7,15},{8,0},{9,1},... | collective-permute-start | bytes 294920 | tf_op jit(solution)/shard_map/ppermute | solution.py:390
  60.9 7.3 %collective-permute-start.9 = (bf16[96,512]{1,0:T(8,128)(2,1)S(1)}, bf16[96,512]{1,0:T(8,128)(2,1)S(1)}, u32[]{:S(2)}, u32[]{:S(2)}) collective-permute-start(bf16[96,512]{1,0:T(8,128)(2,1)S(1)} %get-tuple-element.65), channel_id=1, source_target_pairs={{0,12},{1,13},{2,14},{3,15},{4,8},{5,9},{6,10},{7,11},{8,4},{9,5},... | collective-permute-start | bytes 294920 | tf_op jit(solution)/shard_map/ppermute | solution.py:390
  68.2 10.9 %collective-permute-start.12 = (bf16[96,512]{1,0:T(8,128)(2,1)S(1)}, bf16[96,512]{1,0:T(8,128)(2,1)S(1)}, u32[]{:S(2)}, u32[]{:S(2)}) collective-permute-start(bf16[96,512]{1,0:T(8,128)(2,1)S(1)} %first_activation.1.dep_ref.refs_2_.refs_5_), channel_id=1, source_target_pairs={{0,12},{1,13},{2,14},{3,15},{4,8},{5,9},{6,10},{7,11},{8,4},{9,5},... | collective-permute-start | bytes 294920 | tf_op jit(solution)/shard_map/ppermute | solution.py:390
  70.8 8.4 %collective-permute-start.11 = (bf16[96,512]{1,0:T(8,128)(2,1)S(1)}, bf16[96,512]{1,0:T(8,128)(2,1)S(1)}, u32[]{:S(2)}, u32[]{:S(2)}) collective-permute-start(bf16[96,512]{1,0:T(8,128)(2,1)S(1)} %first_activation.1.dep_ref.refs_2_.refs_5_), channel_id=1, source_target_pairs={{0,8},{1,9},{2,10},{3,11},{4,12},{5,13},{6,14},{7,15},{8,0},{9,1},... | collective-permute-start | bytes 294920 | tf_op jit(solution)/shard_map/ppermute | solution.py:390
  71.4 7.8 %collective-permute-start.10 = (bf16[96,512]{1,0:T(8,128)(2,1)S(1)}, bf16[96,512]{1,0:T(8,128)(2,1)S(1)}, u32[]{:S(2)}, u32[]{:S(2)}) collective-permute-start(bf16[96,512]{1,0:T(8,128)(2,1)S(1)} %first_activation.1.dep_ref.refs_2_.refs_5_), channel_id=1, source_target_pairs={{0,4},{1,5},{2,6},{3,7},{4,0},{5,1},{6,2},{7,3},{8,12},{9,13},{10,... | collective-permute-start | bytes 294920 | tf_op jit(solution)/shard_map/ppermute | solution.py:390
  81.6 12.8 %collective-permute-start.19 = (bf16[2,2064,128]{2,1,0:T(8,128)(2,1)S(1)}, bf16[2,2064,128]{2,1,0:T(8,128)(2,1)S(1)}, u32[]{:S(2)}, u32[]{:S(2)}) collective-permute-start(bf16[2,2064,128]{2,1,0:T(8,128)(2,1)S(1)} %get-tuple-element.81), channel_id=1, source_target_pairs={{0,1},{1,0},{2,3},{3,2},{4,5},{5,4},{6,7},{7,6},{8,9},{9,8},{10,11... | collective-permute-start | bytes 3170312 | tf_op jit(solution)/shard_map/ppermute | solution.py:390
  81.6 7.6 %collective-permute-start.13 = (bf16[112,512]{1,0:T(8,128)(2,1)S(1)}, bf16[112,512]{1,0:T(8,128)(2,1)S(1)}, u32[]{:S(2)}, u32[]{:S(2)}) collective-permute-start(bf16[112,512]{1,0:T(8,128)(2,1)S(1)} %get-tuple-element.72), channel_id=1, source_target_pairs={{0,4},{1,5},{2,6},{3,7},{4,0},{5,1},{6,2},{7,3},{8,12},{9,13},{10,... | collective-permute-start | bytes 344072 | tf_op jit(solution)/shard_map/ppermute | solution.py:390
  82.4 11.9 %collective-permute-start.14 = (bf16[112,512]{1,0:T(8,128)(2,1)S(1)}, bf16[112,512]{1,0:T(8,128)(2,1)S(1)}, u32[]{:S(2)}, u32[]{:S(2)}) collective-permute-start(bf16[112,512]{1,0:T(8,128)(2,1)S(1)} %get-tuple-element.73), channel_id=1, source_target_pairs={{0,8},{1,9},{2,10},{3,11},{4,12},{5,13},{6,14},{7,15},{8,0},{9,1},... | collective-permute-start | bytes 344072 | tf_op jit(solution)/shard_map/ppermute | solution.py:390
  84.7 9.5 %collective-permute-start.15 = (bf16[112,512]{1,0:T(8,128)(2,1)S(1)}, bf16[112,512]{1,0:T(8,128)(2,1)S(1)}, u32[]{:S(2)}, u32[]{:S(2)}) collective-permute-start(bf16[112,512]{1,0:T(8,128)(2,1)S(1)} %get-tuple-element.74), channel_id=1, source_target_pairs={{0,12},{1,13},{2,14},{3,15},{4,8},{5,9},{6,10},{7,11},{8,4},{9,5},... | collective-permute-start | bytes 344072 | tf_op jit(solution)/shard_map/ppermute | solution.py:390
  94.7 12.7 %collective-permute-start.20 = (bf16[2064,128]{1,0:T(8,128)(2,1)S(1)}, bf16[2064,128]{1,0:T(8,128)(2,1)S(1)}, u32[]{:S(2)}, u32[]{:S(2)}) collective-permute-start(bf16[2064,128]{1,0:T(8,128)(2,1)S(1)} %get-tuple-element.83), channel_id=1, source_target_pairs={{0,2},{1,3},{2,0},{3,1},{4,6},{5,7},{6,4},{7,5},{8,10},{9,11},{10,... | collective-permute-start | bytes 1585160 | tf_op jit(solution)/shard_map/ppermute | solution.py:390
  96.0 12.2 %collective-permute-start.18 = (bf16[96,512]{1,0:T(8,128)(2,1)S(1)}, bf16[96,512]{1,0:T(8,128)(2,1)S(1)}, u32[]{:S(2)}, u32[]{:S(2)}) collective-permute-start(bf16[96,512]{1,0:T(8,128)(2,1)S(1)} %get-tuple-element.75.refs_3_.refs_0_), channel_id=1, source_target_pairs={{0,12},{1,13},{2,14},{3,15},{4,8},{5,9},{6,10},{7,11},{8,4},{9,5},... | collective-permute-start | bytes 294920 | tf_op jit(solution)/shard_map/ppermute | solution.py:390
  98.6 9.7 %collective-permute-start.17 = (bf16[96,512]{1,0:T(8,128)(2,1)S(1)}, bf16[96,512]{1,0:T(8,128)(2,1)S(1)}, u32[]{:S(2)}, u32[]{:S(2)}) collective-permute-start(bf16[96,512]{1,0:T(8,128)(2,1)S(1)} %get-tuple-element.75.refs_3_.refs_0_), channel_id=1, source_target_pairs={{0,8},{1,9},{2,10},{3,11},{4,12},{5,13},{6,14},{7,15},{8,0},{9,1},... | collective-permute-start | bytes 294920 | tf_op jit(solution)/shard_map/ppermute | solution.py:390
  99.7 8.5 %collective-permute-start.16 = (bf16[96,512]{1,0:T(8,128)(2,1)S(1)}, bf16[96,512]{1,0:T(8,128)(2,1)S(1)}, u32[]{:S(2)}, u32[]{:S(2)}) collective-permute-start(bf16[96,512]{1,0:T(8,128)(2,1)S(1)} %get-tuple-element.75.refs_3_.refs_0_), channel_id=1, source_target_pairs={{0,4},{1,5},{2,6},{3,7},{4,0},{5,1},{6,2},{7,3},{8,12},{9,13},{10,... | collective-permute-start | bytes 294920 | tf_op jit(solution)/shard_map/ppermute | solution.py:390
  108.3 9.6 %collective-permute-start.22 = (bf16[400,512]{1,0:T(8,128)(2,1)S(1)}, bf16[400,512]{1,0:T(8,128)(2,1)S(1)}, u32[]{:S(2)}, u32[]{:S(2)}) collective-permute-start(bf16[400,512]{1,0:T(8,128)(2,1)S(1)} %stack_parts.1.refs_4_), channel_id=1, source_target_pairs={{0,2},{1,3},{2,0},{3,1},{4,6},{5,7},{6,4},{7,5},{8,10},{9,11},{10,... | collective-permute-start | bytes 1228808 | tf_op jit(solution)/shard_map/ppermute | solution.py:390
  110.1 7.8 %collective-permute-start.21 = (bf16[400,512]{1,0:T(8,128)(2,1)S(1)}, bf16[400,512]{1,0:T(8,128)(2,1)S(1)}, u32[]{:S(2)}, u32[]{:S(2)}) collective-permute-start(bf16[400,512]{1,0:T(8,128)(2,1)S(1)} %stack_parts.1.refs_4_), channel_id=1, source_target_pairs={{0,1},{1,0},{2,3},{3,2},{4,5},{5,4},{6,7},{7,6},{8,9},{9,8},{10,11... | collective-permute-start | bytes 1228808 | tf_op jit(solution)/shard_map/ppermute | solution.py:390
  117.9 1.7 %collective-permute-start.23 = (bf16[400,512]{1,0:T(8,128)(2,1)S(1)}, bf16[400,512]{1,0:T(8,128)(2,1)S(1)}, u32[]{:S(2)}, u32[]{:S(2)}) collective-permute-start(bf16[400,512]{1,0:T(8,128)(2,1)S(1)} %collective-permute-done.22.refs_6_), channel_id=1, source_target_pairs={{0,1},{1,0},{2,3},{3,2},{4,5},{5,4},{6,7},{7,6},{8,9},{9,8},{10,11... | collective-permute-start | bytes 1228808 | tf_op jit(solution)/shard_map/ppermute | solution.py:390
  (3 other events, 24.7 us)

commit v8 on v7

--- a/solution.py
+++ b/solution.py
@@ -169,7 +169,7 @@
         for copy in copies:
             copy.wait()
         half_shifts(levels_ref, table_ref, all_shifts)
-        cot_ref[...] = jnp.broadcast_to(cot_row[...], (LANES, cot_row.shape[1])).T
+        cot_ref[...] = jnp.broadcast_to(cot_row[...].reshape(1, -1), (LANES, cot_row.shape[0])).T
         for out, start in ((first_ref, 0), (last_ref, rows - 2)):
             out[pl.ds(out.shape[0] - EXTRA, EXTRA), :] = drift_tail(drift_ref, start)
 
@@ -459,49 +459,32 @@
     )(*args)
 
 
-def add_side_kernel(place_ref, mine_ref, other_ref, *refs):
-    keep_ref, send_ref = refs[-2:]
-    side = place_ref[1]
-    keep_ref[...] = mine_ref[side] + other_ref[side].astype(f32)
-    send_ref[...] = (mine_ref[1 - side] + other_ref[1 - side].astype(f32)).astype(bf16)
-
-
 def any_specs(deps):
     return [pl.BlockSpec(memory_space=pl.ANY)] * len(deps)
 
 
-def add_side(place, mine, other, deps=()):
-    shape = mine.shape[1:]
-    return pl.pallas_call(
-        add_side_kernel,
-        in_specs=[smem()] + [vmem()] * 2 + any_specs(deps),
-        out_shape=[jax.ShapeDtypeStruct(shape, f32), jax.ShapeDtypeStruct(shape, bf16)],
-        compiler_params=params(),
-        cost_estimate=pl.CostEstimate(flops=1, bytes_accessed=1, transcendentals=0),
-        name="add_side",
-    )(place, mine, other, *deps)
-
-
-def add_parts_kernel(dep_count, place_ref, mine_ref, other_ref, *refs):
-    own_ref, *send_refs = refs[dep_count:]
-    part = place_ref[2]
-    own_ref[...] = mine_ref[part] + other_ref[part].astype(f32)
-    for k, out in enumerate(send_refs):
-        at = part ^ (k + 1)
+def other_places(parts):
+    return [(side, part) for side in range(2) for part in range(parts) if side or part]
+
+
+def add_core_kernel(place_ref, mine_ref, other_ref, own_ref, *send_refs):
+    side, part = place_ref[1], place_ref[2]
+    own_ref[...] = mine_ref[side, part] + other_ref[side, part].astype(f32)
+    for (by_side, by_part), out in zip(other_places(mine_ref.shape[1]), send_refs):
+        at = side ^ by_side, part ^ by_part
         out[...] = (mine_ref[at] + other_ref[at].astype(f32)).astype(bf16)
 
 
-def add_parts(place, mine, other, deps=()):
-    parts = mine.shape[0]
-    return pl.pallas_call(
-        functools.partial(add_parts_kernel, len(deps)),
-        in_specs=[smem(), vmem(), vmem()] + any_specs(deps),
-        out_shape=[jax.ShapeDtypeStruct(mine.shape[1:], f32)]
-        + [jax.ShapeDtypeStruct(mine.shape[1:], bf16)] * (parts - 1),
-        compiler_params=params(),
-        cost_estimate=pl.CostEstimate(flops=1, bytes_accessed=1, transcendentals=0),
-        name="add_parts",
-    )(place, mine, other, *deps)
+def add_core(place, mine, other):
+    parts, *piece = mine.shape[1:]
+    return pl.pallas_call(
+        add_core_kernel,
+        in_specs=[smem(), vmem(), vmem()],
+        out_shape=[jax.ShapeDtypeStruct(piece, f32)] + [jax.ShapeDtypeStruct(piece, bf16)] * (2 * parts - 1),
+        compiler_params=params(),
+        cost_estimate=pl.CostEstimate(flops=1, bytes_accessed=1, transcendentals=0),
+        name="add_core",
+    )(place, mine, other)
 
 
 def activate_kernel(count, *refs):
@@ -692,57 +675,55 @@
     )(own, other, *deps)
 
 
-def back_first_kernel(chunks, count, *refs):
-    own_ref, value_ref = refs[:2]
-    received = refs[2 : 2 + count]
-    first_refs = refs[2 + count : 2 + count + chunks]
-    out_refs = refs[-1 - chunks : -1]
-    tail_ref = refs[-1]
-    block = first_refs[0].shape[0]
+def back_first_kernel(count, own_ref, value_ref, *refs):
+    received = refs[:count]
+    first_ref, out_ref, with_tail_ref = refs[count:]
+    block = first_ref.shape[0]
     value = value_ref[...]
+    total = own_ref[...]
     for ref in received:
-        tail = ref[pl.ds(chunks * block, EXTRA), :].astype(f32)
+        tail = ref[pl.ds(block, EXTRA), :].astype(f32)
         value = value + (tail[0:1] + tail[1:2])
-    tail_ref[...] = tail_rows(value)
-    for c in range(chunks):
-        total = own_ref[pl.ds(c * block, block), :]
-        for ref in received:
-            total = total + ref[pl.ds(c * block, block), :].astype(f32)
-        first = first_refs[c][...].astype(f32)
-        out_refs[c][...] = (total * (1.0 - first * first)).astype(bf16)
-
-
-def back_first(own, value, received, firsts, deps=()):
-    chunks = len(firsts)
-    shape = firsts[0].shape
-    return pl.pallas_call(
-        functools.partial(back_first_kernel, chunks, len(received)),
-        in_specs=[vmem()] * (2 + len(received) + chunks) + any_specs(deps),
-        out_shape=[jax.ShapeDtypeStruct(shape, bf16)] * chunks
-        + [jax.ShapeDtypeStruct((EXTRA, shape[1]), bf16)],
+        total = total + ref[pl.ds(0, block), :].astype(f32)
+    first = first_ref[...].astype(f32)
+    back = (total * (1.0 - first * first)).astype(bf16)
+    out_ref[...] = back
+    with_tail_ref[pl.ds(0, block), :] = back
+    with_tail_ref[pl.ds(block, EXTRA), :] = tail_rows(value)
+
+
+def back_first(own, value, received, first):
+    block, width = first.shape
+    return pl.pallas_call(
+        functools.partial(back_first_kernel, len(received)),
+        in_specs=[vmem()] * (3 + len(received)),
+        out_shape=[jax.ShapeDtypeStruct((rows, width), bf16) for rows in (block, block + EXTRA)],
         compiler_params=params(),
         cost_estimate=pl.CostEstimate(flops=1, bytes_accessed=1, transcendentals=0),
         name="back_first",
-    )(own, value, *received, *firsts, *deps)
-
-
-def stack_kernel(count, halves, *refs):
-    outs = refs[-halves:]
-    width = outs[0].shape[1]
+    )(own, value, *received, first)
+
+
+def stack_kernel(count, *refs):
+    out_ref = refs[-1]
+    block = refs[0].shape[0] - EXTRA
+    parts = count // 2
     at = 0
-    for ref in refs[:count]:
-        for n, out in enumerate(outs):
-            out[pl.ds(at, ref.shape[0]), :] = ref[:, pl.ds(n * width, width)]
-        at += ref.shape[0]
-
-
-def stack(pieces, halves, deps=()):
+    for side in range(2):
+        section = refs[side * parts : (side + 1) * parts]
+        for ref in section:
+            out_ref[pl.ds(at, block), :] = ref[pl.ds(0, block), :]
+            at += block
+        out_ref[pl.ds(at, EXTRA), :] = section[0][pl.ds(block, EXTRA), :]
+        at += EXTRA
+
+
+def stack(pieces, deps):
     rows = sum(piece.shape[0] for piece in pieces)
-    shape = jax.ShapeDtypeStruct((rows, pieces[0].shape[1] // halves), bf16)
-    return pl.pallas_call(
-        functools.partial(stack_kernel, len(pieces), halves),
+    return pl.pallas_call(
+        functools.partial(stack_kernel, len(pieces)),
         in_specs=[vmem()] * len(pieces) + any_specs(deps),
-        out_shape=[shape] * halves,
+        out_shape=jax.ShapeDtypeStruct((rows, pieces[0].shape[1]), bf16),
         compiler_params=params(),
         cost_estimate=pl.CostEstimate(flops=1, bytes_accessed=1, transcendentals=0),
         name="stack_parts",
@@ -765,64 +746,49 @@
     )(*arrays, *deps)
 
 
-def first_grad_kernel(parts, block, count, with_value, *refs):
+def first_grad_kernel(parts, block, count, *refs):
     place_ref = refs[0]
     lefts = refs[1 : 1 + count]
-    stacks = refs[1 + count : 5 + count]
-    outs = refs[-3:-1] if with_value else refs[-2:-1]
-    whole = refs[-1]
-    step = pl.program_id(0)
+    stacks = refs[1 + count : 3 + count]
+    out_ref, value_ref, whole = refs[-3:]
+    piece = pl.program_id(0) ^ place_ref[2]
     mine = place_ref[3]
     values = [jnp.zeros((1, block), f32)] * 4
-    for t, ref in enumerate(stacks):
-        at = mine ^ (2 * (t % 2) + t // 2)
-        piece = step ^ place_ref[2]
-        whole[pl.ds(pl.multiple_of(at * block, block), block), :] = ref[
-            pl.ds(pl.multiple_of(piece * block, block), block), :
-        ]
-        if with_value:
-            tail = ref[pl.ds(parts * block, EXTRA), :block].astype(f32)
+    for by_core in range(2):
+        for by_side in range(2):
+            ref = stacks[by_core]
+            start = by_side * (parts * block + EXTRA)
+            at = mine ^ (2 * by_core + by_side)
+            whole[pl.ds(pl.multiple_of(at * block, block), block), :] = ref[
+                pl.ds(pl.multiple_of(start + piece * block, EXTRA), block), :
+            ]
+            tail = ref[pl.ds(start + parts * block, EXTRA), :block].astype(f32)
             value = tail[0:1] + tail[1:2]
             for q in range(4):
                 values[q] = jnp.where(at == q, value, values[q])
-    if with_value:
-        outs[1][...] = jnp.concatenate(values, axis=1)
+    value_ref[...] = jnp.concatenate(values, axis=1)
     start = 0
     for ref in lefts:
         cells = ref.shape[0]
-        outs[0][pl.ds(start, cells), :] = jnp.dot(ref[...], whole[...], preferred_element_type=f32).astype(bf16)
+        out_ref[pl.ds(start, cells), :] = jnp.dot(ref[...], whole[...], preferred_element_type=f32).astype(bf16)
         start += cells
 
 
-def first_grad(place, lefts, stacks, so_far, hidden, parts, block, half, halves, deps):
+def first_grad(place, lefts, stacks, parts, block, deps):
     scenarios = lefts[0].shape[1]
     cells = sum(left.shape[0] for left in lefts)
     width = stacks[0].shape[1]
-    with_value = half == 0
-    in_specs = [smem()] + [vmem()] * (len(lefts) + 4) + any_specs(deps)
-    args = [place, *lefts, *stacks, *deps]
-    aliases = {}
-    if so_far is not None:
-        aliases = {len(args): 0}
-        in_specs.append(pl.BlockSpec(memory_space=pltpu.HBM))
-        args.append(so_far)
-    out_specs = [pl.BlockSpec((cells, width), lambda i: (0, i * halves + half))]
-    out_shape = [pltpu.HBM((cells, hidden), bf16)]
-    if with_value:
-        out_specs.append(pl.BlockSpec((1, scenarios), lambda i: (0, 0)))
-        out_shape.append(jax.ShapeDtypeStruct((1, scenarios), f32))
-    return pl.pallas_call(
-        functools.partial(first_grad_kernel, parts, block, len(lefts), with_value),
+    return pl.pallas_call(
+        functools.partial(first_grad_kernel, parts, block, len(lefts)),
         grid=(parts,),
-        in_specs=in_specs,
-        out_specs=out_specs,
-        out_shape=out_shape,
-        input_output_aliases=aliases,
+        in_specs=[smem()] + [vmem()] * (len(lefts) + 2) + any_specs(deps),
+        out_specs=[pl.BlockSpec((cells, width), lambda i: (0, i)), pl.BlockSpec((1, scenarios), lambda i: (0, 0))],
+        out_shape=[pltpu.HBM((cells, parts * width), bf16), jax.ShapeDtypeStruct((1, scenarios), f32)],
         scratch_shapes=[pltpu.VMEM((scenarios, width), bf16)],
         compiler_params=params(),
         cost_estimate=pl.CostEstimate(flops=1, bytes_accessed=1, transcendentals=0),
         name="first_gradient",
-    )(*args)
+    )(place, *lefts, *stacks, *deps)
 
 
 def local(hist, drift, shocks, shock_table, first_weight, mid_weight, head_weight, cotangent):
@@ -839,9 +805,8 @@
     tiles = pltpu.with_memory_space_constraint(to_tiles(hist), pltpu.HBM)
 
     place = jnp.stack([core, side, part, mine])
-    halves = 1
-
-    small = [pltpu.with_memory_space_constraint(array, pltpu.HBM) for array in (drift, shocks.T, shock_table.T, cotangent[None, :])]
+
+    small = [pltpu.with_memory_space_constraint(array, pltpu.HBM) for array in (drift, shocks.T, shock_table.T, cotangent)]
     packed, place = pack(place, mid_weight, head_weight[None, :], small[-1])
     mids = [packed]
     mids += [swap(mids[0], count, 1), swap(mids[0], count, 2)]
@@ -860,32 +825,23 @@
         return density_steps(drift, shifts, band, own_rows, below, above, dep, so_far, turn, 2)
 
     keep, send = edge_product(place, low, high, first_weight, product, parts, width)
-    keep, send = add_side(place, keep, swap(send, count, 1))
-    other = swap(send, count, 2)
-    density, token = density_turn(0, send, None)
-    own, *sends = add_parts(place, keep, other, [token, mids[3]])
-    received = [swap(piece, count, 4 * (k + 1)) for k, piece in enumerate(sends)]
-    first = activate(own, received)
+    own, *sends = add_core(place, keep, swap(send, count, 1))
+    flips = [2 * by_side + 4 * by_part for by_side, by_part in other_places(parts)]
+    received = [swap(piece, count, flip) for piece, flip in zip(sends, flips)]
+    density, token = density_turn(0, sends[-1], None)
+    first = activate(own, received, [token])
     firsts = [first] + [swap(first, count, 4 * k) for k in range(1, parts)]
     density, token = density_turn(1, first, density)
-    own, value, mid_keep, mid_send, *sends = middle(place, cot, firsts, mids, 1, parts, width, [token])
+    own, value, mid_keep, mid_send, *sends = middle(place, cot, firsts, mids, 1, parts, width, [token, mids[1], mids[3]])
     received = [swap(piece, count, 4 * (k + 1)) for k, piece in enumerate(sends)]
-    back, tail = back_first(own, value, received, [first])
+    back, with_tail = back_first(own, value, received, first)
     mid_keep, mid_send = mid_add(mid_keep, swap(mid_send, count, 1), [back])
     lefts = transposed([low, high] if inner is None else [low, inner, high], [back])
-    pieces = [back] + [swap(back, count, 4 * k) for k in range(1, parts)]
     grad_mid, grad_head, token = mid_final(mid_keep, swap(mid_send, count, 2))
-    stacks = stack(pieces + [tail], halves, [lefts[0], token])
-    grad_first = None
-    for half, own_stack in enumerate(stacks):
-        gathered = [own_stack, swap(own_stack, count, 1), swap(own_stack, count, 2)]
-        gathered.append(swap(gathered[2], count, 1))
-        results = first_grad(
-            place, lefts, gathered, grad_first, hidden, parts, block, half, halves, []
-        )
-        grad_first = results[0]
-        if half == 0:
-            value = results[1].reshape(scenarios)
+    pieces = [with_tail] + [swap(with_tail if flip == 2 else back, count, flip) for flip in flips]
+    own_stack = stack(pieces, [lefts[0]])
+    grad_first, value = first_grad(place, lefts, [own_stack, swap(own_stack, count, 1)], parts, block, [token])
+    value = value.reshape(scenarios)
     return from_tiles(density, hist.shape), value, grad_first, grad_mid, grad_head[0]
 
 

time: 134 us -> 143 us (1.067)
  starting transfers between devices: 32.5 us -> 45.2 us
    ppermute x22 -> x27, starting transfers between devices: 28.6 us -> 41.2 us  [swap(): return lax.ppermute(values, 'grid', [(i, i ^ flip) for i in range(count)])]
    ppermute x22 -> x27, waiting for transfers between devices: 36.2 us -> 35.6 us  [swap(): return lax.ppermute(values, 'grid', [(i, i ^ flip) for i in range(count)])]
  transfers between devices with their start and end apart: 24 -> 29, of which waited for: 8 -> 9; matrix products, arithmetic and copies ran while one was open for 0% -> 0% of each run, Pallas kernels for 27% -> 25%
where the time goes in v8:
time: 143 us
  Pallas kernels  60.4 us (42%)
  starting transfers between devices  45.2 us (32%)
  waiting for transfers between devices  35.6 us (25%)
    ppermute x27, starting transfers between devices, swap(): return lax.ppermute(values, 'grid', [(i, i ^ flip) for i in range(count)])  41.2 us
    ppermute x27, waiting for transfers between devices, swap(): return lax.ppermute(values, 'grid', [(i, i ^ flip) for i in range(count)])  35.6 us
    pallas_call x2, Pallas kernels, density_steps(): pl.pallas_call(functools.partial(density_kernel, None), grid=(steps,), in...  12.9 us
    pallas_call x1, Pallas kernels, first_grad(): pl.pallas_call(functools.partial(first_grad_kernel, parts, block, len(lef...  12.1 us
    pallas_call x1, Pallas kernels, inner_steps(): pl.pallas_call(functools.partial(inner_kernel, rows, size), grid=(scenari...  11.5 us
    pallas_call x1, Pallas kernels, inner_product(): pl.pallas_call(functools.partial(inner_product_kernel, count), grid=(hidd...  8.17 us
    pallas_call x1, Pallas kernels, edge_product(): pl.pallas_call(functools.partial(edge_product_kernel, block, inner is not...  4.43 us
    pallas_call x1, Pallas kernels, edge_steps(): pl.pallas_call(functools.partial(density_kernel, segments), grid=(scenari...  3.65 us
  transfers between devices with their start and end apart: 29, of which 9 were waited for; matrix products, arithmetic and copies ran while one was open for 0% of the time, Pallas kernels for 25%

profile of v8, /device:TPU:0, one launch (start us, length us, event | category | flops | bytes accessed | tf_op | source)
XLA Modules:
  0.0 142.8 jit_solution(16401136261771488961)
XLA Ops:
  0.7 2.2 %mid_with_head.1 = (bf16[2064,128]{1,0:T(8,128)(2,1)S(1)}, s32[4]{0:T(128)S(1)}) custom-call(s32[4]{0:T(128)S(1)} %pad_add_fusion.place_ref, bf16[2048,128]{1,0:T(8,128)(2,1)} %mid_ref.1, f32[1,128]{1,0:T(1,128)} %bitcast.22, f32[384]{0:T(512)} %first_ref.1), custom_call_target="tpu_custom_call" | custom-call | flops 1 | bytes 1 | tf_op jit(solution)/shard_map/mid_with_head/pallas_call | solution.py:525
  2.9 3.0 %collective-permute-start.3 = (bf16[2064,128]{1,0:T(8,128)(2,1)S(1)}, bf16[2064,128]{1,0:T(8,128)(2,1)S(1)}, u32[]{:S(2)}, u32[]{:S(2)}) collective-permute-start(bf16[2064,128]{1,0:T(8,128)(2,1)S(1)} %get-tuple-element.56.refs_6_), channel_id=1, source_target_pairs={{0,2},{1,3},{2,0},{3,1},{4,6},{5,7},{6,4},{7,5},{8,10},{9,11},{10,... | collective-permute-start | bytes 1585160 | tf_op jit(solution)/shard_map/ppermute | solution.py:390
  6.0 11.5 %inner_density_steps.1 = (bf16[400,512]{1,0:T(8,128)(2,1)S(1)}, bf16[400,512]{1,0:T(8,128)(2,1)S(1)}, f32[4,384,128]{2,1,0:T(8,128)}, bf16[512,256]{1,0:T(8,128)...) custom-call(f32[12288,128]{1,0:T(8,128)} %bitcast.18, ...), custom_call_target="tpu_custom_call" | custom-call | flops 1 | bytes 1 | tf_op jit(solution)/shard_map/inner_density_steps/pallas_call | solution.py:213
  17.5 2.4 %collective-permute-start = (bf16[400,512]{1,0:T(8,128)(2,1)S(1)}, bf16[400,512]{1,0:T(8,128)(2,1)S(1)}, u32[]{:S(2)}, u32[]{:S(2)}) collective-permute-start(bf16[400,512]{1,0:T(8,128)(2,1)S(1)} %get-tuple-element.52), channel_id=1, source_target_pairs={{0,1},{1,2},{2,3},{3,4},{4,5},{5,6},{6,7},{7,8},{8,9},{9,10},{10,1... | collective-permute-start | bytes 1228808 | tf_op jit(solution)/shard_map/ppermute | solution.py:817
  21.5 8.2 %inner_product.1.dep_ref.refs_0_ = f32[4,384,512]{2,1,0:T(8,128)S(1)} custom-call(bf16[384,3072]{1,0:T(8,128)(2,1)S(1)} %get-tuple-element.55.inputs_ref.refs_1_, bf16[4096,2048]{1,0:T(8,128)(2,1)} %bottom_ref.1, bf16[4096,2048]{1,0:T(8,128)(2,1)} %bottom_ref.1, bf16[4096,2048]{1,0:T(8,128)(2,1)} %bottom_ref.1, bf16[4096,2048]{1,0:T(8,128)(2,1)} %bottom_ref.1, ...), custom_call_target="tpu_custom_call" | custom-call | flops 1 | bytes 1 | tf_op jit(solution)/shard_map/inner_product/pallas_call | solution.py:407
  29.7 3.7 %edge_density_steps.1 = (bf16[384,512]{1,0:T(8,128)(2,1)S(1)}, bf16[384,512]{1,0:T(8,128)(2,1)S(1)}) custom-call(f32[2,16,256]{2,1,0:T(8,128)S(1)} %copy-done.2, f32[4,384,128]{2,1,0:T(8,128)S(1)} %copy-done.1, bf16[512,256]{1,0:T(8,128)(2,1)S(1)} %get-tuple-element.50.band_ref, bf16[384,4096]{1,0:T(8,128)(2,1)S(1)} %copy-done, ...), custom_call_target="tpu_custom_call" | custom-call | flops 1 | bytes 1 | tf_op jit(solution)/shard_map/edge_density_steps/pallas_call | solution.py:337
  33.3 4.4 %edge_product.1 = (f32[2,4,96,512]{3,2,1,0:T(8,128)S(1)}, bf16[2,4,96,512]{3,2,1,0:T(8,128)(2,1)S(1)}) custom-call(s32[4]{0:T(128)S(1)} %get-tuple-element.54.place_ref.refs_0_, bf16[384,512]{1,0:T(8,128)(2,1)S(1)} %get-tuple-element.57.low_ref.refs_0_, bf16[384,512]{1,0:T(8,128)(2,1)S(1)} %get-tuple-element.58.high_ref.refs_2_, ...), custom_call_target="tpu_custom_call" | custom-call | flops 1 | bytes 1 | tf_op jit(solution)/shard_map/edge_product/pallas_call | solution.py:449
  41.6 3.6 %collective-permute-start.5 = (bf16[96,512]{1,0:T(8,128)(2,1)S(1)}, bf16[96,512]{1,0:T(8,128)(2,1)S(1)}, u32[]{:S(2)}, u32[]{:S(2)}) collective-permute-start(bf16[96,512]{1,0:T(8,128)(2,1)S(1)} %get-tuple-element.62), channel_id=1, source_target_pairs={{0,4},{1,5},{2,6},{3,7},{4,0},{5,1},{6,2},{7,3},{8,12},{9,13},{10,... | collective-permute-start | bytes 294920 | tf_op jit(solution)/shard_map/ppermute | solution.py:390
  45.2 2.6 %collective-permute-start.6 = (bf16[96,512]{1,0:T(8,128)(2,1)S(1)}, bf16[96,512]{1,0:T(8,128)(2,1)S(1)}, u32[]{:S(2)}, u32[]{:S(2)}) collective-permute-start(bf16[96,512]{1,0:T(8,128)(2,1)S(1)} %get-tuple-element.63), channel_id=1, source_target_pairs={{0,8},{1,9},{2,10},{3,11},{4,12},{5,13},{6,14},{7,15},{8,0},{9,1},... | collective-permute-start | bytes 294920 | tf_op jit(solution)/shard_map/ppermute | solution.py:390
  50.4 5.5 %collective-permute-done.6.refs_2_ = bf16[96,512]{1,0:T(8,128)(2,1)S(1)} collective-permute-done((bf16[96,512]{1,0:T(8,128)(2,1)S(1)}, bf16[96,512]{1,0:T(8,128)(2,1)S(1)}, u32[]{:S(2)}, u32[]{:S(2)}) %collective-permute-start.6) | collective-permute-done | bytes 98336 | tf_op jit(solution)/shard_map/ppermute | solution.py:390
  55.9 3.2 %collective-permute-start.11 = (bf16[96,512]{1,0:T(8,128)(2,1)S(1)}, bf16[96,512]{1,0:T(8,128)(2,1)S(1)}, u32[]{:S(2)}, u32[]{:S(2)}) collective-permute-start(bf16[96,512]{1,0:T(8,128)(2,1)S(1)} %get-tuple-element.68.dep_ref), channel_id=1, source_target_pairs={{0,14},{1,15},{2,12},{3,13},{4,10},{5,11},{6,8},{7,9},{8,6},{9,7},... | collective-permute-start | bytes 294920 | tf_op jit(solution)/shard_map/ppermute | solution.py:390
  59.1 6.5 %density_steps.2 = (f32[12288,128]{1,0:T(8,128)}, f32[8,128]{1,0:T(8,128)S(1)}) custom-call(f32[2,16,256]{2,1,0:T(8,128)S(1)} %copy-done.2, f32[4,384,128]{2,1,0:T(8,128)S(1)} %copy-done.1, bf16[512,256]{1,0:T(8,128)(2,1)S(1)} %get-tuple-element.50.band_ref, bf16[384,4096]{1,0:T(8,128)(2,1)S(1)} %copy-done, ...), custom_call_target="tpu_custom_call" | custom-call | flops 1 | bytes 1 | tf_op jit(solution)/shard_map/density_steps/pallas_call | solution.py:364
  70.2 6.5 %density_steps.3 = (f32[12288,128]{1,0:T(8,128)}, f32[8,128]{1,0:T(8,128)S(1)}) custom-call(f32[2,16,256]{2,1,0:T(8,128)S(1)} %copy-done.2, f32[4,384,128]{2,1,0:T(8,128)S(1)} %copy-done.1, bf16[512,256]{1,0:T(8,128)(2,1)S(1)} %get-tuple-element.50.band_ref, bf16[384,4096]{1,0:T(8,128)(2,1)S(1)} %copy-done, ...), custom_call_target="tpu_custom_call", output_to_operand_aliasing={{0}: (9, {})} | custom-call | flops 1 | bytes 1 | tf_op jit(solution)/shard_map/density_steps/pallas_call | solution.py:364
  76.7 2.4 %value_layers.1 = (f32[96,512]{1,0:T(8,128)S(1)}, f32[1,512]{1,0:T(1,128)S(1)}, bf16[2,2064,128]{2,1,0:T(8,128)(2,1)S(1)}, bf16[2,2064,128]{2,1,0:T(8,128)(2,1)S...) custom-call(s32[4]{0:T(128)S(1)} %get-tuple-element.54.place_ref.refs_0_, ...), custom_call_target="tpu_custom_call" | custom-call | flops 1 | bytes 1 | tf_op jit(solution)/shard_map/value_layers/pallas_call | solution.py:611
  81.0 2.6 %collective-permute-start.18 = (bf16[112,512]{1,0:T(8,128)(2,1)S(1)}, bf16[112,512]{1,0:T(8,128)(2,1)S(1)}, u32[]{:S(2)}, u32[]{:S(2)}) collective-permute-start(bf16[112,512]{1,0:T(8,128)(2,1)S(1)} %get-tuple-element.78), channel_id=1, source_target_pairs={{0,12},{1,13},{2,14},{3,15},{4,8},{5,9},{6,10},{7,11},{8,4},{9,5},... | collective-permute-start | bytes 344072 | tf_op jit(solution)/shard_map/ppermute | solution.py:390
  83.6 3.1 %collective-permute-done.16.refs_0_ = bf16[112,512]{1,0:T(8,128)(2,1)S(1)} collective-permute-done((bf16[112,512]{1,0:T(8,128)(2,1)S(1)}, bf16[112,512]{1,0:T(8,128)(2,1)S(1)}, u32[]{:S(2)}, u32[]{:S(2)}) %collective-permute-start.16) | collective-permute-done | bytes 114720 | tf_op jit(solution)/shard_map/ppermute | solution.py:390
  86.8 5.0 %collective-permute-done.17.refs_1_ = bf16[112,512]{1,0:T(8,128)(2,1)S(1)} collective-permute-done((bf16[112,512]{1,0:T(8,128)(2,1)S(1)}, bf16[112,512]{1,0:T(8,128)(2,1)S(1)}, u32[]{:S(2)}, u32[]{:S(2)}) %collective-permute-start.17) | collective-permute-done | bytes 114720 | tf_op jit(solution)/shard_map/ppermute | solution.py:390
  91.8 3.6 %collective-permute-start.25 = (bf16[96,512]{1,0:T(8,128)(2,1)S(1)}, bf16[96,512]{1,0:T(8,128)(2,1)S(1)}, u32[]{:S(2)}, u32[]{:S(2)}) collective-permute-start(bf16[96,512]{1,0:T(8,128)(2,1)S(1)} %get-tuple-element.79.refs_3_.refs_0_), channel_id=1, source_target_pairs={{0,14},{1,15},{2,12},{3,13},{4,10},{5,11},{6,8},{7,9},{8,6},{9,7},... | collective-permute-start | bytes 294920 | tf_op jit(solution)/shard_map/ppermute | solution.py:390
  99.3 3.3 %collective-permute-start.21 = (bf16[96,512]{1,0:T(8,128)(2,1)S(1)}, bf16[96,512]{1,0:T(8,128)(2,1)S(1)}, u32[]{:S(2)}, u32[]{:S(2)}) collective-permute-start(bf16[96,512]{1,0:T(8,128)(2,1)S(1)} %get-tuple-element.79.refs_3_.refs_0_), channel_id=1, source_target_pairs={{0,12},{1,13},{2,14},{3,15},{4,8},{5,9},{6,10},{7,11},{8,4},{9,5},... | collective-permute-start | bytes 294920 | tf_op jit(solution)/shard_map/ppermute | solution.py:390
  102.6 3.0 %collective-permute-done.24.refs_6_ = bf16[96,512]{1,0:T(8,128)(2,1)S(1)} collective-permute-done((bf16[96,512]{1,0:T(8,128)(2,1)S(1)}, bf16[96,512]{1,0:T(8,128)(2,1)S(1)}, u32[]{:S(2)}, u32[]{:S(2)}) %collective-permute-start.24) | collective-permute-done | bytes 98336 | tf_op jit(solution)/shard_map/ppermute | solution.py:390
  109.7 3.7 %collective-permute-done.20.refs_2_ = bf16[96,512]{1,0:T(8,128)(2,1)S(1)} collective-permute-done((bf16[96,512]{1,0:T(8,128)(2,1)S(1)}, bf16[96,512]{1,0:T(8,128)(2,1)S(1)}, u32[]{:S(2)}, u32[]{:S(2)}) %collective-permute-start.20) | collective-permute-done | bytes 98336 | tf_op jit(solution)/shard_map/ppermute | solution.py:390
  113.9 2.6 %collective-permute-start.28 = (bf16[2064,128]{1,0:T(8,128)(2,1)S(1)}, bf16[2064,128]{1,0:T(8,128)(2,1)S(1)}, u32[]{:S(2)}, u32[]{:S(2)}) collective-permute-start(bf16[2064,128]{1,0:T(8,128)(2,1)S(1)} %get-tuple-element.87), channel_id=1, source_target_pairs={{0,2},{1,3},{2,0},{3,1},{4,6},{5,7},{6,4},{7,5},{8,10},{9,11},{10,... | collective-permute-start | bytes 1585160 | tf_op jit(solution)/shard_map/ppermute | solution.py:390
  116.5 12.7 %collective-permute-done.28.other_ref = bf16[2064,128]{1,0:T(8,128)(2,1)S(1)} collective-permute-done((bf16[2064,128]{1,0:T(8,128)(2,1)S(1)}, bf16[2064,128]{1,0:T(8,128)(2,1)S(1)}, u32[]{:S(2)}, u32[]{:S(2)}) %collective-permute-start.28) | collective-permute-done | bytes 528416 | tf_op jit(solution)/shard_map/ppermute | solution.py:390
  130.0 12.1 %first_gradient.1 = (bf16[4096,2048]{1,0:T(8,128)(2,1)}, f32[1,384]{1,0:T(1,128)S(1)}) custom-call(s32[4]{0:T(128)S(1)} %get-tuple-element.54.place_ref.refs_0_, bf16[512,384]{1,0:T(8,128)(2,1)S(1)} %get-tuple-element.80.refs_8_.refs_1_, bf16[3072,384]{1,0:T(8,128)(2,1)S(1)} %get-tuple-element.81.refs_2_, bf16[512,384]{1,0:T(8,128)(2,1)S(1)} %get-tuple-element.82.refs_3_, ...), custom_call_target="tpu_custom_call" | custom-call | flops 1 | bytes 1 | tf_op jit(solution)/shard_map/first_gradient/pallas_call | solution.py:781
  (58 shorter events, 24.6 us)
Async XLA Ops:
  2.9 18.5 %collective-permute-start.3 = (bf16[2064,128]{1,0:T(8,128)(2,1)S(1)}, bf16[2064,128]{1,0:T(8,128)(2,1)S(1)}, u32[]{:S(2)}, u32[]{:S(2)}) collective-permute-start(bf16[2064,128]{1,0:T(8,128)(2,1)S(1)} %get-tuple-element.56.refs_6_), channel_id=1, source_target_pairs={{0,2},{1,3},{2,0},{3,1},{4,6},{5,7},{6,4},{7,5},{8,10},{9,11},{10,... | collective-permute-start | bytes 1585160 | tf_op jit(solution)/shard_map/ppermute | solution.py:390
  6.0 15.5 %collective-permute-start.2 = (bf16[2064,128]{1,0:T(8,128)(2,1)S(1)}, bf16[2064,128]{1,0:T(8,128)(2,1)S(1)}, u32[]{:S(2)}, u32[]{:S(2)}) collective-permute-start(bf16[2064,128]{1,0:T(8,128)(2,1)S(1)} %get-tuple-element.56.refs_6_), channel_id=1, source_target_pairs={{0,1},{1,0},{2,3},{3,2},{4,5},{5,4},{6,7},{7,6},{8,9},{9,8},{10,11... | collective-permute-start | bytes 1585160 | tf_op jit(solution)/shard_map/ppermute | solution.py:390
  17.5 12.2 %collective-permute-start = (bf16[400,512]{1,0:T(8,128)(2,1)S(1)}, bf16[400,512]{1,0:T(8,128)(2,1)S(1)}, u32[]{:S(2)}, u32[]{:S(2)}) collective-permute-start(bf16[400,512]{1,0:T(8,128)(2,1)S(1)} %get-tuple-element.52), channel_id=1, source_target_pairs={{0,1},{1,2},{2,3},{3,4},{4,5},{5,6},{6,7},{7,8},{8,9},{9,10},{10,1... | collective-permute-start | bytes 1228808 | tf_op jit(solution)/shard_map/ppermute | solution.py:817
  19.9 9.7 %collective-permute-start.1 = (bf16[400,512]{1,0:T(8,128)(2,1)S(1)}, bf16[400,512]{1,0:T(8,128)(2,1)S(1)}, u32[]{:S(2)}, u32[]{:S(2)}) collective-permute-start(bf16[400,512]{1,0:T(8,128)(2,1)S(1)} %get-tuple-element.53), channel_id=1, source_target_pairs={{1,0},{2,1},{3,2},{4,3},{5,4},{6,5},{7,6},{8,7},{9,8},{10,9},{11,1... | collective-permute-start | bytes 1228808 | tf_op jit(solution)/shard_map/ppermute | solution.py:818
  39.0 37.7 %collective-permute-start.15 = (bf16[2064,128]{1,0:T(8,128)(2,1)S(1)}, bf16[2064,128]{1,0:T(8,128)(2,1)S(1)}, u32[]{:S(2)}, u32[]{:S(2)}) collective-permute-start(bf16[2064,128]{1,0:T(8,128)(2,1)S(1)} %collective-permute-done.3.refs_7_.refs_8_), channel_id=1, source_target_pairs={{0,1},{1,0},{2,3},{3,2},{4,5},{5,4},{6,7},{7,6},{8,9},{9,8},{10,11... | collective-permute-start | bytes 1585160 | tf_op jit(solution)/shard_map/ppermute | solution.py:390
  45.2 10.7 %collective-permute-start.6 = (bf16[96,512]{1,0:T(8,128)(2,1)S(1)}, bf16[96,512]{1,0:T(8,128)(2,1)S(1)}, u32[]{:S(2)}, u32[]{:S(2)}) collective-permute-start(bf16[96,512]{1,0:T(8,128)(2,1)S(1)} %get-tuple-element.63), channel_id=1, source_target_pairs={{0,8},{1,9},{2,10},{3,11},{4,12},{5,13},{6,14},{7,15},{8,0},{9,1},... | collective-permute-start | bytes 294920 | tf_op jit(solution)/shard_map/ppermute | solution.py:390
  47.8 8.1 %collective-permute-start.7 = (bf16[96,512]{1,0:T(8,128)(2,1)S(1)}, bf16[96,512]{1,0:T(8,128)(2,1)S(1)}, u32[]{:S(2)}, u32[]{:S(2)}) collective-permute-start(bf16[96,512]{1,0:T(8,128)(2,1)S(1)} %get-tuple-element.64), channel_id=1, source_target_pairs={{0,12},{1,13},{2,14},{3,15},{4,8},{5,9},{6,10},{7,11},{8,4},{9,5},... | collective-permute-start | bytes 294920 | tf_op jit(solution)/shard_map/ppermute | solution.py:390
  47.8 17.8 %collective-permute-start.8 = (bf16[96,512]{1,0:T(8,128)(2,1)S(1)}, bf16[96,512]{1,0:T(8,128)(2,1)S(1)}, u32[]{:S(2)}, u32[]{:S(2)}) collective-permute-start(bf16[96,512]{1,0:T(8,128)(2,1)S(1)} %get-tuple-element.65), channel_id=1, source_target_pairs={{0,2},{1,3},{2,0},{3,1},{4,6},{5,7},{6,4},{7,5},{8,10},{9,11},{10,... | collective-permute-start | bytes 294920 | tf_op jit(solution)/shard_map/ppermute | solution.py:390
  48.3 17.3 %collective-permute-start.9 = (bf16[96,512]{1,0:T(8,128)(2,1)S(1)}, bf16[96,512]{1,0:T(8,128)(2,1)S(1)}, u32[]{:S(2)}, u32[]{:S(2)}) collective-permute-start(bf16[96,512]{1,0:T(8,128)(2,1)S(1)} %get-tuple-element.66), channel_id=1, source_target_pairs={{0,6},{1,7},{2,4},{3,5},{4,2},{5,3},{6,0},{7,1},{8,14},{9,15},{10,... | collective-permute-start | bytes 294920 | tf_op jit(solution)/shard_map/ppermute | solution.py:390
  55.9 9.7 %collective-permute-start.10 = (bf16[96,512]{1,0:T(8,128)(2,1)S(1)}, bf16[96,512]{1,0:T(8,128)(2,1)S(1)}, u32[]{:S(2)}, u32[]{:S(2)}) collective-permute-start(bf16[96,512]{1,0:T(8,128)(2,1)S(1)} %get-tuple-element.67), channel_id=1, source_target_pairs={{0,10},{1,11},{2,8},{3,9},{4,14},{5,15},{6,12},{7,13},{8,2},{9,3},... | collective-permute-start | bytes 294920 | tf_op jit(solution)/shard_map/ppermute | solution.py:390
  55.9 9.7 %collective-permute-start.11 = (bf16[96,512]{1,0:T(8,128)(2,1)S(1)}, bf16[96,512]{1,0:T(8,128)(2,1)S(1)}, u32[]{:S(2)}, u32[]{:S(2)}) collective-permute-start(bf16[96,512]{1,0:T(8,128)(2,1)S(1)} %get-tuple-element.68.dep_ref), channel_id=1, source_target_pairs={{0,14},{1,15},{2,12},{3,13},{4,10},{5,11},{6,8},{7,9},{8,6},{9,7},... | collective-permute-start | bytes 294920 | tf_op jit(solution)/shard_map/ppermute | solution.py:390
  65.7 10.9 %collective-permute-start.14 = (bf16[96,512]{1,0:T(8,128)(2,1)S(1)}, bf16[96,512]{1,0:T(8,128)(2,1)S(1)}, u32[]{:S(2)}, u32[]{:S(2)}) collective-permute-start(bf16[96,512]{1,0:T(8,128)(2,1)S(1)} %first_activation.1.dep_ref.refs_2_.refs_3_), channel_id=1, source_target_pairs={{0,12},{1,13},{2,14},{3,15},{4,8},{5,9},{6,10},{7,11},{8,4},{9,5},... | collective-permute-start | bytes 294920 | tf_op jit(solution)/shard_map/ppermute | solution.py:390
  66.8 9.8 %collective-permute-start.13 = (bf16[96,512]{1,0:T(8,128)(2,1)S(1)}, bf16[96,512]{1,0:T(8,128)(2,1)S(1)}, u32[]{:S(2)}, u32[]{:S(2)}) collective-permute-start(bf16[96,512]{1,0:T(8,128)(2,1)S(1)} %first_activation.1.dep_ref.refs_2_.refs_3_), channel_id=1, source_target_pairs={{0,8},{1,9},{2,10},{3,11},{4,12},{5,13},{6,14},{7,15},{8,0},{9,1},... | collective-permute-start | bytes 294920 | tf_op jit(solution)/shard_map/ppermute | solution.py:390
  68.8 7.9 %collective-permute-start.12 = (bf16[96,512]{1,0:T(8,128)(2,1)S(1)}, bf16[96,512]{1,0:T(8,128)(2,1)S(1)}, u32[]{:S(2)}, u32[]{:S(2)}) collective-permute-start(bf16[96,512]{1,0:T(8,128)(2,1)S(1)} %first_activation.1.dep_ref.refs_2_.refs_3_), channel_id=1, source_target_pairs={{0,4},{1,5},{2,6},{3,7},{4,0},{5,1},{6,2},{7,3},{8,12},{9,13},{10,... | collective-permute-start | bytes 294920 | tf_op jit(solution)/shard_map/ppermute | solution.py:390
  79.1 34.5 %collective-permute-start.27 = (bf16[2,2064,128]{2,1,0:T(8,128)(2,1)S(1)}, bf16[2,2064,128]{2,1,0:T(8,128)(2,1)S(1)}, u32[]{:S(2)}, u32[]{:S(2)}) collective-permute-start(bf16[2,2064,128]{2,1,0:T(8,128)(2,1)S(1)} %get-tuple-element.85), channel_id=1, source_target_pairs={{0,1},{1,0},{2,3},{3,2},{4,5},{5,4},{6,7},{7,6},{8,9},{9,8},{10,11... | collective-permute-start | bytes 3170312 | tf_op jit(solution)/shard_map/ppermute | solution.py:390
  79.9 11.9 %collective-permute-start.17 = (bf16[112,512]{1,0:T(8,128)(2,1)S(1)}, bf16[112,512]{1,0:T(8,128)(2,1)S(1)}, u32[]{:S(2)}, u32[]{:S(2)}) collective-permute-start(bf16[112,512]{1,0:T(8,128)(2,1)S(1)} %get-tuple-element.77), channel_id=1, source_target_pairs={{0,8},{1,9},{2,10},{3,11},{4,12},{5,13},{6,14},{7,15},{8,0},{9,1},... | collective-permute-start | bytes 344072 | tf_op jit(solution)/shard_map/ppermute | solution.py:390
  81.0 10.7 %collective-permute-start.18 = (bf16[112,512]{1,0:T(8,128)(2,1)S(1)}, bf16[112,512]{1,0:T(8,128)(2,1)S(1)}, u32[]{:S(2)}, u32[]{:S(2)}) collective-permute-start(bf16[112,512]{1,0:T(8,128)(2,1)S(1)} %get-tuple-element.78), channel_id=1, source_target_pairs={{0,12},{1,13},{2,14},{3,15},{4,8},{5,9},{6,10},{7,11},{8,4},{9,5},... | collective-permute-start | bytes 344072 | tf_op jit(solution)/shard_map/ppermute | solution.py:390
  95.4 10.1 %collective-permute-start.24 = (bf16[96,512]{1,0:T(8,128)(2,1)S(1)}, bf16[96,512]{1,0:T(8,128)(2,1)S(1)}, u32[]{:S(2)}, u32[]{:S(2)}) collective-permute-start(bf16[96,512]{1,0:T(8,128)(2,1)S(1)} %get-tuple-element.79.refs_3_.refs_0_), channel_id=1, source_target_pairs={{0,10},{1,11},{2,8},{3,9},{4,14},{5,15},{6,12},{7,13},{8,2},{9,3},... | collective-permute-start | bytes 294920 | tf_op jit(solution)/shard_map/ppermute | solution.py:390
  96.5 11.0 %collective-permute-start.23 = (bf16[96,512]{1,0:T(8,128)(2,1)S(1)}, bf16[96,512]{1,0:T(8,128)(2,1)S(1)}, u32[]{:S(2)}, u32[]{:S(2)}) collective-permute-start(bf16[96,512]{1,0:T(8,128)(2,1)S(1)} %get-tuple-element.79.refs_3_.refs_0_), channel_id=1, source_target_pairs={{0,6},{1,7},{2,4},{3,5},{4,2},{5,3},{6,0},{7,1},{8,14},{9,15},{10,... | collective-permute-start | bytes 294920 | tf_op jit(solution)/shard_map/ppermute | solution.py:390
  98.1 15.3 %collective-permute-start.22 = (bf16[112,512]{1,0:T(8,128)(2,1)S(1)}, bf16[112,512]{1,0:T(8,128)(2,1)S(1)}, u32[]{:S(2)}, u32[]{:S(2)}) collective-permute-start(bf16[112,512]{1,0:T(8,128)(2,1)S(1)} %get-tuple-element.83.refs_0_), channel_id=1, source_target_pairs={{0,2},{1,3},{2,0},{3,1},{4,6},{5,7},{6,4},{7,5},{8,10},{9,11},{10,... | collective-permute-start | bytes 344072 | tf_op jit(solution)/shard_map/ppermute | solution.py:390
  99.3 10.4 %collective-permute-start.21 = (bf16[96,512]{1,0:T(8,128)(2,1)S(1)}, bf16[96,512]{1,0:T(8,128)(2,1)S(1)}, u32[]{:S(2)}, u32[]{:S(2)}) collective-permute-start(bf16[96,512]{1,0:T(8,128)(2,1)S(1)} %get-tuple-element.79.refs_3_.refs_0_), channel_id=1, source_target_pairs={{0,12},{1,13},{2,14},{3,15},{4,8},{5,9},{6,10},{7,11},{8,4},{9,5},... | collective-permute-start | bytes 294920 | tf_op jit(solution)/shard_map/ppermute | solution.py:390
  105.6 7.9 %collective-permute-start.20 = (bf16[96,512]{1,0:T(8,128)(2,1)S(1)}, bf16[96,512]{1,0:T(8,128)(2,1)S(1)}, u32[]{:S(2)}, u32[]{:S(2)}) collective-permute-start(bf16[96,512]{1,0:T(8,128)(2,1)S(1)} %get-tuple-element.79.refs_3_.refs_0_), channel_id=1, source_target_pairs={{0,8},{1,9},{2,10},{3,11},{4,12},{5,13},{6,14},{7,15},{8,0},{9,1},... | collective-permute-start | bytes 294920 | tf_op jit(solution)/shard_map/ppermute | solution.py:390
  113.5 16.5 %collective-permute-start.26 = (bf16[800,512]{1,0:T(8,128)(2,1)S(1)}, bf16[800,512]{1,0:T(8,128)(2,1)S(1)}, u32[]{:S(2)}, u32[]{:S(2)}) collective-permute-start(bf16[800,512]{1,0:T(8,128)(2,1)S(1)} %stack_parts.1.refs_4_), channel_id=1, source_target_pairs={{0,1},{1,0},{2,3},{3,2},{4,5},{5,4},{6,7},{7,6},{8,9},{9,8},{10,11... | collective-permute-start | bytes 2457608 | tf_op jit(solution)/shard_map/ppermute | solution.py:390
  113.9 15.2 %collective-permute-start.28 = (bf16[2064,128]{1,0:T(8,128)(2,1)S(1)}, bf16[2064,128]{1,0:T(8,128)(2,1)S(1)}, u32[]{:S(2)}, u32[]{:S(2)}) collective-permute-start(bf16[2064,128]{1,0:T(8,128)(2,1)S(1)} %get-tuple-element.87), channel_id=1, source_target_pairs={{0,2},{1,3},{2,0},{3,1},{4,6},{5,7},{6,4},{7,5},{8,10},{9,11},{10,... | collective-permute-start | bytes 1585160 | tf_op jit(solution)/shard_map/ppermute | solution.py:390
  (8 other events, 55.6 us)

commit v9 on v8

--- a/solution.py
+++ b/solution.py
@@ -113,16 +113,18 @@
     for row in places:
         flux = (half_drift(1, row) + shift_y) * density(row)
         pairs[pl.ds(rows_of[row] * size, size), pl.ds(columns, columns)] = flux.astype(bf16)
+    yield
     start = rows_of[places[0]] * size
     count = (rows_of[places[-1]] + 1) * size - start
     terms[pl.ds(start, count), :] = jnp.dot(pairs[pl.ds(start, count), :], band, preferred_element_type=f32)
+    yield
     for row in places:
         low = density(row - 1) * ((diffusion_rate + half_drift(0, row - 1)) + shift_x)
         high = density(row + 1) * ((diffusion_rate - half_drift(0, row + 1)) - shift_x)
         write(row, terms[pl.ds(rows_of[row] * size, size), :] + low + high)
 
 
-def two_steps(segments, read, half_drift, edge, band, shifts, scratch, write):
+def step_stages(segments, read, half_drift, edge, band, shifts, scratch, write):
     pairs, later, terms = scratch
     size, columns = shifts[0].shape
     before, between, after = [
@@ -135,8 +137,22 @@
     def write_later(row, density):
         later[pl.ds(rows_of[row] * size, size), pl.ds(0, columns)] = edge(row, density).astype(bf16)
 
-    one_step(rows_of, between, half_drift, band, shifts[0], shifts[1], pairs, terms, write_later)
-    one_step(rows_of, after, half_drift, band, shifts[2], shifts[3], later, terms, write)
+    yield from one_step(rows_of, between, half_drift, band, shifts[0], shifts[1], pairs, terms, write_later)
+    yield from one_step(rows_of, after, half_drift, band, shifts[2], shifts[3], later, terms, write)
+
+
+def interleave(runs):
+    ahead, live = list(runs), []
+    while ahead or live:
+        if ahead:
+            live.append(ahead.pop(0))
+        for run in list(live):
+            if next(run, live) is live:
+                live.remove(run)
+
+
+def two_steps(*args):
+    interleave([step_stages(*args)])
 
 
 def step_scratch(segments, size, columns):
@@ -185,20 +201,28 @@
             last_ref[where, pl.ds((row - rows + 2) * columns, columns)] = density
     if rows <= 4:
         return
-
-    def write(row, density):
-        inner_ref[:, pl.ds((row - 2) * columns, columns)] = density.astype(bf16)
-
-    two_steps(
-        [(2, rows - 3)],
-        lambda row: rows_ref[:, pl.ds(row * columns, columns)],
-        lambda c, row: 0.5 * drift_ref[c, row : row + 1, :],
-        lambda row, density: density,
-        band_ref[...],
-        [wide(shift_ref[n], columns) for n in range(4)],
-        scratch,
-        write,
-    )
+    band = band_ref[...]
+    count = len(scratch) // 3
+    part = size // count
+
+    def run(n):
+        here = pl.ds(n * part, part)
+
+        def write(row, density):
+            inner_ref[here, pl.ds((row - 2) * columns, columns)] = density.astype(bf16)
+
+        return step_stages(
+            [(2, rows - 3)],
+            lambda row: rows_ref[here, pl.ds(row * columns, columns)],
+            lambda c, row: 0.5 * drift_ref[c, row : row + 1, :],
+            lambda row, density: density,
+            band,
+            [wide(shift_ref[k, here, :], columns) for k in range(4)],
+            scratch[3 * n : 3 * n + 3],
+            write,
+        )
+
+    interleave([run(n) for n in range(count)])
 
 
 def inner_steps(tiles, drift, levels, table, cot):
@@ -239,7 +263,7 @@
             pltpu.SemaphoreType.DMA((4,)),
             pltpu.VMEM(shifts.shape, f32),
         ]
-        + step_scratch([(2, max(rows - 3, 2))], size, columns),
+        + step_scratch([(2, max(rows - 3, 2))], size // 2, columns) * 2,
         compiler_params=params(),
         cost_estimate=pl.CostEstimate(flops=1, bytes_accessed=1, transcendentals=0),
         name="inner_density_steps",
@@ -275,12 +299,7 @@
     return half_drift, edge
 
 
-def density_kernel(segments, drift_ref, shift_ref, band_ref, rows_ref, below_ref, above_ref, below_tail, above_tail, dep_ref, *refs):
-    scratch = refs[-3:]
-    rows, columns = drift_ref.shape[1:]
-    size = shift_ref.shape[1]
-    half_drift, edge = with_halo(drift_ref, below_tail, above_tail)
-
+def density_read(rows_ref, below_ref, above_ref, rows, columns):
     def read(row):
         if row < 0:
             return below_ref[:, pl.ds((row + 2) * columns, columns)]
@@ -288,63 +307,112 @@
             return above_ref[:, pl.ds((row - rows) * columns, columns)]
         return rows_ref[:, pl.ds(row * columns, columns)]
 
-    if segments is None:
-        next_ref, token_ref = refs[-5:-3]
-        token_ref[...] = jnp.zeros(token_ref.shape, f32)
-
-        def write(row, density):
-            write_row(next_ref, 0, size, row, rows, columns, density)
-
-    else:
-        low_ref, high_ref = refs[-5:-3]
-
-        def write(row, density):
-            if row < 2:
-                low_ref[:, pl.ds(row * columns, columns)] = density.astype(bf16)
-            else:
-                high_ref[:, pl.ds((row - rows + 2) * columns, columns)] = density.astype(bf16)
-
+    return read
+
+
+def density_kernel(drift_ref, shift_ref, band_ref, rows_ref, below_ref, above_ref, below_tail, above_tail, dep_ref, *refs):
+    next_ref, token_ref, *scratch = refs[-5:]
+    rows, columns = drift_ref.shape[1:]
+    size = shift_ref.shape[1]
+    half_drift, edge = with_halo(drift_ref, below_tail, above_tail)
+    token_ref[...] = jnp.zeros(token_ref.shape, f32)
+
+    def write(row, density):
+        write_row(next_ref, 0, size, row, rows, columns, density)
+
+    read = density_read(rows_ref, below_ref, above_ref, rows, columns)
     shifts = [wide(shift_ref[n], columns) for n in range(4)]
-    two_steps(segments or [(0, rows - 1)], read, half_drift, edge, band_ref[...], shifts, scratch, write)
-
-
-def density_specs(drift, shifts, band, own, below, size, first):
+    two_steps([(0, rows - 1)], read, half_drift, edge, band_ref[...], shifts, scratch, write)
+
+
+def density_specs(drift, shifts, band, own, below, size, place):
     columns = drift.shape[2]
     scenarios = shifts.shape[1]
-    halo = pl.BlockSpec((size, 2 * columns), lambda i: (first + i, 0))
+    halo = pl.BlockSpec((size, 2 * columns), lambda i: (place(i), 0))
     tail = pl.BlockSpec((EXTRA, 2 * columns), lambda i: (scenarios // EXTRA, 0))
     return [
         pl.BlockSpec(drift.shape, lambda i: (0, 0, 0)),
-        pl.BlockSpec((4, size, LANES), lambda i: (0, first + i, 0)),
+        pl.BlockSpec((4, size, LANES), lambda i: (0, place(i), 0)),
         pl.BlockSpec(band.shape, lambda i: (0, 0)),
-        pl.BlockSpec((size, own.shape[1]), lambda i: (first + i, 0)),
+        pl.BlockSpec((size, own.shape[1]), lambda i: (place(i), 0)),
         halo,
         halo,
         tail,
         tail,
-        pl.BlockSpec(memory_space=pl.ANY),
     ]
 
 
-def edge_steps(drift, shifts, band, own, below, above, dep):
+def edge_kernel(
+    blocks, with_inner, drift_ref, shift_ref, band_ref, rows_ref, below_ref, above_ref, below_tail, above_tail,
+    place_ref, top_ref, bottom_ref, *refs,
+):
+    low_ref, high_ref, keep_ref, send_ref, total, *scratch = refs[-8:]
+    step = pl.program_id(0)
+    rows, columns = drift_ref.shape[1:]
+    size = shift_ref.shape[1]
+    block = keep_ref.shape[2]
+
+    @pl.when(step < blocks)
+    def _():
+        half_drift, edge = with_halo(drift_ref, below_tail, above_tail)
+        where = pl.ds(pl.multiple_of(step * size, size), size)
+
+        def write(row, density):
+            out, at = (low_ref, row) if row < 2 else (high_ref, row - rows + 2)
+            out[where, pl.ds(at * columns, columns)] = density.astype(bf16)
+
+        read = density_read(rows_ref, below_ref, above_ref, rows, columns)
+        shifts = [wide(shift_ref[n], columns) for n in range(4)]
+        two_steps(edge_segments(rows), read, half_drift, edge, band_ref[...], shifts, scratch, write)
+
+    @pl.when(step >= blocks)
+    def _():
+        part = step - blocks
+        left = jnp.concatenate([low_ref[...], high_ref[...]], axis=1)
+        weight = jnp.concatenate([top_ref[...], bottom_ref[...]], axis=0)
+        product = jnp.dot(left, weight, preferred_element_type=f32)
+        total[...] = product + refs[0][part] if with_inner else product
+        core = place_ref[0]
+        for out, half in ((keep_ref, core), (send_ref, 1 - core)):
+            for side in range(2):
+                start = pl.multiple_of((2 * half + side) * block, block)
+                out[side, part] = total[pl.ds(start, block), :].astype(out.dtype)
+
+
+def edge_product(place, drift, shifts, band, own, below, above, weight, inner, parts, width):
     scenarios = shifts.shape[1]
     rows, columns = drift.shape[1:]
     size = 2 * scenario_block(scenarios)
     size = size if scenarios % size == 0 else size // 2
+    blocks = scenarios // size
     edge = jax.ShapeDtypeStruct((scenarios, 2 * columns), bf16)
-    spec = pl.BlockSpec((size, 2 * columns), lambda i: (i, 0))
-    segments = edge_segments(rows)
-    return pl.pallas_call(
-        functools.partial(density_kernel, segments),
-        grid=(scenarios // size,),
-        in_specs=density_specs(drift, shifts, band, own, below, size, 0),
-        out_specs=[spec, spec],
-        out_shape=[edge, edge],
-        scratch_shapes=step_scratch(segments, size, columns),
-        compiler_params=params(),
-        cost_estimate=pl.CostEstimate(flops=1, bytes_accessed=1, transcendentals=0),
-        name="edge_density_steps",
-    )(drift, shifts, band, own, below, above, below, above, dep)
+    last = weight.shape[0] // (2 * columns) - 1
+    shape = (2, parts, scenarios // 4, width)
+
+    def column(i):
+        return jnp.maximum(i - blocks, 0)
+
+    in_specs = density_specs(drift, shifts, band, own, below, size, lambda i: jnp.minimum(i, blocks - 1))
+    in_specs += [
+        smem(),
+        pl.BlockSpec((2 * columns, width), lambda i: (0, column(i))),
+        pl.BlockSpec((2 * columns, width), lambda i: (last, column(i))),
+    ]
+    args = [drift, shifts, band, own, below, above, below, above, place, weight, weight]
+    if inner is not None:
+        in_specs.append(vmem())
+        args.append(inner)
+    return pl.pallas_call(
+        functools.partial(edge_kernel, blocks, inner is not None),
+        grid=(blocks + parts,),
+        in_specs=in_specs,
+        out_specs=[vmem()] * 4,
+        out_shape=[edge, edge, jax.ShapeDtypeStruct(shape, f32), jax.ShapeDtypeStruct(shape, bf16)],
+        scratch_shapes=[pltpu.VMEM((scenarios, width), f32)] + step_scratch(edge_segments(rows), size, columns),
+        compiler_params=params(),
+        cost_estimate=pl.CostEstimate(flops=1, bytes_accessed=1, transcendentals=0),
+        name="edge_steps_and_product",
+    )(*args)
 
 
 def density_steps(drift, shifts, band, own, below, above, dep, so_far, turn, turns):
@@ -355,14 +423,14 @@
     steps = scenarios // size // turns
     first = turn * steps
     args = [drift, shifts, band, own, below, above, below, above, dep]
-    in_specs = density_specs(drift, shifts, band, own, below, size, first)
+    in_specs = density_specs(drift, shifts, band, own, below, size, lambda i: first + i) + any_specs([dep])
     aliases = {}
     if so_far is not None:
         aliases = {len(args): 0}
         args.append(so_far)
         in_specs.append(pl.BlockSpec(memory_space=pltpu.HBM))
     return pl.pallas_call(
-        functools.partial(density_kernel, None),
+        density_kernel,
         grid=(steps,),
         in_specs=in_specs,
         out_specs=[
@@ -414,49 +482,6 @@
         cost_estimate=pl.CostEstimate(flops=1, bytes_accessed=1, transcendentals=0),
         name="inner_product",
     )(inner, *([weight] * count), *deps)
-
-
-def edge_product_kernel(block, with_inner, place_ref, low_ref, high_ref, top_ref, bottom_ref, *refs):
-    keep_ref, send_ref, total = refs[-3:]
-    step = pl.program_id(0)
-    left = jnp.concatenate([low_ref[...], high_ref[...]], axis=1)
-    weight = jnp.concatenate([top_ref[...], bottom_ref[...]], axis=0)
-    product = jnp.dot(left, weight, preferred_element_type=f32)
-    total[...] = product + refs[0][step] if with_inner else product
-    core = place_ref[0]
-    for out, half in ((keep_ref, core), (send_ref, 1 - core)):
-        for side in range(2):
-            start = pl.multiple_of((2 * half + side) * block, block)
-            out[side, step] = total[pl.ds(start, block), :].astype(out.dtype)
-
-
-def edge_product(place, low, high, weight, inner, parts, width):
-    scenarios, size = low.shape
-    block = scenarios // 4
-    last = weight.shape[0] // size - 1
-    shape = (2, parts, block, width)
-    in_specs = [
-        smem(),
-        vmem(),
-        vmem(),
-        pl.BlockSpec((size, width), lambda n: (0, n)),
-        pl.BlockSpec((size, width), lambda n: (last, n)),
-    ]
-    args = [place, low, high, weight, weight]
-    if inner is not None:
-        in_specs.append(vmem())
-        args.append(inner)
-    return pl.pallas_call(
-        functools.partial(edge_product_kernel, block, inner is not None),
-        grid=(parts,),
-        in_specs=in_specs,
-        out_specs=[vmem(), vmem()],
-        out_shape=[jax.ShapeDtypeStruct(shape, f32), jax.ShapeDtypeStruct(shape, bf16)],
-        scratch_shapes=[pltpu.VMEM((scenarios, width), f32)],
-        compiler_params=params(),
-        cost_estimate=pl.CostEstimate(flops=1, bytes_accessed=1, transcendentals=0),
-        name="edge_product",
-    )(*args)
 
 
 def any_specs(deps):
@@ -677,7 +702,7 @@
 
 def back_first_kernel(count, own_ref, value_ref, *refs):
     received = refs[:count]
-    first_ref, out_ref, with_tail_ref = refs[count:]
+    first_ref, out_ref, tail_ref = refs[count:]
     block = first_ref.shape[0]
     value = value_ref[...]
     total = own_ref[...]
@@ -686,10 +711,8 @@
         value = value + (tail[0:1] + tail[1:2])
         total = total + ref[pl.ds(0, block), :].astype(f32)
     first = first_ref[...].astype(f32)
-    back = (total * (1.0 - first * first)).astype(bf16)
-    out_ref[...] = back
-    with_tail_ref[pl.ds(0, block), :] = back
-    with_tail_ref[pl.ds(block, EXTRA), :] = tail_rows(value)
+    out_ref[...] = (total * (1.0 - first * first)).astype(bf16)
+    tail_ref[...] = tail_rows(value)
 
 
 def back_first(own, value, received, first):
@@ -697,7 +720,7 @@
     return pl.pallas_call(
         functools.partial(back_first_kernel, len(received)),
         in_specs=[vmem()] * (3 + len(received)),
-        out_shape=[jax.ShapeDtypeStruct((rows, width), bf16) for rows in (block, block + EXTRA)],
+        out_shape=[jax.ShapeDtypeStruct((rows, width), bf16) for rows in (block, EXTRA)],
         compiler_params=params(),
         cost_estimate=pl.CostEstimate(flops=1, bytes_accessed=1, transcendentals=0),
         name="back_first",
@@ -705,17 +728,10 @@
 
 
 def stack_kernel(count, *refs):
-    out_ref = refs[-1]
-    block = refs[0].shape[0] - EXTRA
-    parts = count // 2
     at = 0
-    for side in range(2):
-        section = refs[side * parts : (side + 1) * parts]
-        for ref in section:
-            out_ref[pl.ds(at, block), :] = ref[pl.ds(0, block), :]
-            at += block
-        out_ref[pl.ds(at, EXTRA), :] = section[0][pl.ds(block, EXTRA), :]
-        at += EXTRA
+    for ref in refs[:count]:
+        refs[-1][pl.ds(at, ref.shape[0]), :] = ref[...]
+        at += ref.shape[0]
 
 
 def stack(pieces, deps):
@@ -746,26 +762,26 @@
     )(*arrays, *deps)
 
 
-def first_grad_kernel(parts, block, count, *refs):
+def first_grad_kernel(parts, block, tiles, count, *refs):
     place_ref = refs[0]
     lefts = refs[1 : 1 + count]
-    stacks = refs[1 + count : 3 + count]
+    stacks = refs[1 + count : 5 + count]
     out_ref, value_ref, whole = refs[-3:]
-    piece = pl.program_id(0) ^ place_ref[2]
+    width = out_ref.shape[1]
+    step = pl.program_id(0)
+    piece = step // tiles ^ place_ref[2]
+    column = pl.ds(pl.multiple_of(step % tiles * width, width), width)
     mine = place_ref[3]
     values = [jnp.zeros((1, block), f32)] * 4
-    for by_core in range(2):
-        for by_side in range(2):
-            ref = stacks[by_core]
-            start = by_side * (parts * block + EXTRA)
-            at = mine ^ (2 * by_core + by_side)
-            whole[pl.ds(pl.multiple_of(at * block, block), block), :] = ref[
-                pl.ds(pl.multiple_of(start + piece * block, EXTRA), block), :
-            ]
-            tail = ref[pl.ds(start + parts * block, EXTRA), :block].astype(f32)
-            value = tail[0:1] + tail[1:2]
-            for q in range(4):
-                values[q] = jnp.where(at == q, value, values[q])
+    for t, ref in enumerate(stacks):
+        at = mine ^ (2 * (t % 2) + t // 2)
+        whole[pl.ds(pl.multiple_of(at * block, block), block), :] = ref[
+            pl.ds(pl.multiple_of(piece * block, block), block), column
+        ]
+        tail = ref[pl.ds(parts * block, EXTRA), :block].astype(f32)
+        value = tail[0:1] + tail[1:2]
+        for q in range(4):
+            values[q] = jnp.where(at == q, value, values[q])
     value_ref[...] = jnp.concatenate(values, axis=1)
     start = 0
     for ref in lefts:
@@ -778,13 +794,15 @@
     scenarios = lefts[0].shape[1]
     cells = sum(left.shape[0] for left in lefts)
     width = stacks[0].shape[1]
-    return pl.pallas_call(
-        functools.partial(first_grad_kernel, parts, block, len(lefts)),
-        grid=(parts,),
-        in_specs=[smem()] + [vmem()] * (len(lefts) + 2) + any_specs(deps),
-        out_specs=[pl.BlockSpec((cells, width), lambda i: (0, i)), pl.BlockSpec((1, scenarios), lambda i: (0, 0))],
+    tile = min(width, 256)
+    tiles = width // tile
+    return pl.pallas_call(
+        functools.partial(first_grad_kernel, parts, block, tiles, len(lefts)),
+        grid=(parts * tiles,),
+        in_specs=[smem()] + [vmem()] * (len(lefts) + 4) + any_specs(deps),
+        out_specs=[pl.BlockSpec((cells, tile), lambda i: (0, i)), pl.BlockSpec((1, scenarios), lambda i: (0, 0))],
         out_shape=[pltpu.HBM((cells, parts * width), bf16), jax.ShapeDtypeStruct((1, scenarios), f32)],
-        scratch_shapes=[pltpu.VMEM((scenarios, width), bf16)],
+        scratch_shapes=[pltpu.VMEM((scenarios, tile), bf16)],
         compiler_params=params(),
         cost_estimate=pl.CostEstimate(flops=1, bytes_accessed=1, transcendentals=0),
         name="first_gradient",
@@ -818,13 +836,14 @@
     above = lax.ppermute(first_rows, "grid", backward)
     first_weight = pltpu.with_memory_space_constraint(first_weight, pltpu.HBM)
     product = None if inner is None else inner_product(inner, first_weight, width, mids[1:])
-    low, high = edge_steps(drift, shifts, band, own_rows, below, above, own_rows if product is None else product)
+    low, high, keep, send = edge_product(
+        place, drift, shifts, band, own_rows, below, above, first_weight, product, parts, width
+    )
     mids.append(swap(mids[2], count, 1))
 
     def density_turn(turn, dep, so_far):
         return density_steps(drift, shifts, band, own_rows, below, above, dep, so_far, turn, 2)
 
-    keep, send = edge_product(place, low, high, first_weight, product, parts, width)
     own, *sends = add_core(place, keep, swap(send, count, 1))
     flips = [2 * by_side + 4 * by_part for by_side, by_part in other_places(parts)]
     received = [swap(piece, count, flip) for piece, flip in zip(sends, flips)]
@@ -834,13 +853,15 @@
     density, token = density_turn(1, first, density)
     own, value, mid_keep, mid_send, *sends = middle(place, cot, firsts, mids, 1, parts, width, [token, mids[1], mids[3]])
     received = [swap(piece, count, 4 * (k + 1)) for k, piece in enumerate(sends)]
-    back, with_tail = back_first(own, value, received, first)
-    mid_keep, mid_send = mid_add(mid_keep, swap(mid_send, count, 1), [back])
+    back, tail = back_first(own, value, received, first)
     lefts = transposed([low, high] if inner is None else [low, inner, high], [back])
-    grad_mid, grad_head, token = mid_final(mid_keep, swap(mid_send, count, 2))
-    pieces = [with_tail] + [swap(with_tail if flip == 2 else back, count, flip) for flip in flips]
-    own_stack = stack(pieces, [lefts[0]])
-    grad_first, value = first_grad(place, lefts, [own_stack, swap(own_stack, count, 1)], parts, block, [token])
+    pieces = [back] + [swap(back, count, 4 * k) for k in range(1, parts)] + [tail]
+    stacks = [stack(pieces, [lefts[0]])]
+    stacks += [swap(stacks[0], count, 1), swap(stacks[0], count, 2)]
+    mid_keep, mid_send = mid_add(mid_keep, swap(mid_send, count, 1), [stacks[2]])
+    stacks.append(swap(stacks[2], count, 1))
+    grad_first, value = first_grad(place, lefts, stacks, parts, block, [mid_send])
+    grad_mid, grad_head, _ = mid_final(mid_keep, swap(mid_send, count, 2), [value])
     value = value.reshape(scenarios)
     return from_tiles(density, hist.shape), value, grad_first, grad_mid, grad_head[0]
 

time: 143 us -> 133 us (0.930)
  starting transfers between devices: 45.2 us -> 37.7 us
  waiting for transfers between devices: 35.6 us -> 32 us
    ppermute x27 -> x25, starting transfers between devices: 41.2 us -> 34.2 us  [swap(): return lax.ppermute(values, 'grid', [(i, i ^ flip) for i in range(count)])]
    ppermute x27 -> x25, waiting for transfers between devices: 35.6 us -> 32 us  [swap(): return lax.ppermute(values, 'grid', [(i, i ^ flip) for i in range(count)])]
    pallas_call x5 -> x4, Pallas kernels: 33.1 us -> 33.9 us  [the longest x2 12.9 us: density_steps(): pl.pallas_call(density_kernel, grid=(steps,), in_specs=in_specs, out_spec...]
  transfers between devices with their start and end apart: 29 -> 27, of which waited for: 9 -> 9; matrix products, arithmetic and copies ran while one was open for 0% -> 0% of each run, Pallas kernels for 25% -> 35%
where the time goes in v9:
time: 133 us
  Pallas kernels  61.3 us (46%)
  starting transfers between devices  37.7 us (28%)
  waiting for transfers between devices  32 us (24%)
    ppermute x25, starting transfers between devices, swap(): return lax.ppermute(values, 'grid', [(i, i ^ flip) for i in range(count)])  34.2 us
    ppermute x25, waiting for transfers between devices, swap(): return lax.ppermute(values, 'grid', [(i, i ^ flip) for i in range(count)])  32 us
    pallas_call x2, Pallas kernels, density_steps(): pl.pallas_call(density_kernel, grid=(steps,), in_specs=in_specs, out_spec...  12.9 us
    pallas_call x1, Pallas kernels, first_grad(): pl.pallas_call(functools.partial(first_grad_kernel, parts, block, tiles,...  12.3 us
    pallas_call x1, Pallas kernels, inner_steps(): pl.pallas_call(functools.partial(inner_kernel, rows, size), grid=(scenari...  11.5 us
    pallas_call x1, Pallas kernels, edge_product(): pl.pallas_call(functools.partial(edge_kernel, blocks, inner is not None),...  8.69 us
    pallas_call x1, Pallas kernels, inner_product(): pl.pallas_call(functools.partial(inner_product_kernel, count), grid=(hidd...  8.29 us
  transfers between devices with their start and end apart: 27, of which 9 were waited for; matrix products, arithmetic and copies ran while one was open for 0% of the time, Pallas kernels for 35%

profile of v9, /device:TPU:0, one launch (start us, length us, event | category | flops | bytes accessed | tf_op | source)
XLA Modules:
  0.0 132.6 jit_solution(12213005902107711813)
XLA Ops:
  0.7 2.2 %mid_with_head.1 = (bf16[2064,128]{1,0:T(8,128)(2,1)S(1)}, s32[4]{0:T(128)S(1)}) custom-call(s32[4]{0:T(128)S(1)} %pad_add_fusion.place_ref, bf16[2048,128]{1,0:T(8,128)(2,1)} %mid_ref.1, f32[1,128]{1,0:T(1,128)} %bitcast.22, f32[384]{0:T(512)} %first_ref.1), custom_call_target="tpu_custom_call" | custom-call | flops 1 | bytes 1 | tf_op jit(solution)/shard_map/mid_with_head/pallas_call | solution.py:550
  3.4 2.6 %collective-permute-start.3 = (bf16[2064,128]{1,0:T(8,128)(2,1)S(1)}, bf16[2064,128]{1,0:T(8,128)(2,1)S(1)}, u32[]{:S(2)}, u32[]{:S(2)}) collective-permute-start(bf16[2064,128]{1,0:T(8,128)(2,1)S(1)} %get-tuple-element.55.refs_6_), channel_id=1, source_target_pairs={{0,2},{1,3},{2,0},{3,1},{4,6},{5,7},{6,4},{7,5},{8,10},{9,11},{10,... | collective-permute-start | bytes 1585160 | tf_op jit(solution)/shard_map/ppermute | solution.py:458
  6.0 11.5 %inner_density_steps.1 = (bf16[400,512]{1,0:T(8,128)(2,1)S(1)}, bf16[400,512]{1,0:T(8,128)(2,1)S(1)}, f32[4,384,128]{2,1,0:T(8,128)}, bf16[512,256]{1,0:T(8,128)...) custom-call(f32[12288,128]{1,0:T(8,128)} %bitcast.18, ...), custom_call_target="tpu_custom_call" | custom-call | flops 1 | bytes 1 | tf_op jit(solution)/shard_map/inner_density_steps/pallas_call | solution.py:237
  17.6 2.1 %collective-permute-start = (bf16[400,512]{1,0:T(8,128)(2,1)S(1)}, bf16[400,512]{1,0:T(8,128)(2,1)S(1)}, u32[]{:S(2)}, u32[]{:S(2)}) collective-permute-start(bf16[400,512]{1,0:T(8,128)(2,1)S(1)} %get-tuple-element.51), channel_id=1, source_target_pairs={{0,1},{1,2},{2,3},{3,4},{4,5},{5,6},{6,7},{7,8},{8,9},{9,10},{10,1... | collective-permute-start | bytes 1228808 | tf_op jit(solution)/shard_map/ppermute | solution.py:835
  21.2 8.3 %inner_product.1.refs_0_ = f32[4,384,512]{2,1,0:T(8,128)S(1)} custom-call(bf16[384,3072]{1,0:T(8,128)(2,1)S(1)} %get-tuple-element.54.inputs_ref.refs_1_, bf16[4096,2048]{1,0:T(8,128)(2,1)} %bottom_ref.1, bf16[4096,2048]{1,0:T(8,128)(2,1)} %bottom_ref.1, bf16[4096,2048]{1,0:T(8,128)(2,1)} %bottom_ref.1, bf16[4096,2048]{1,0:T(8,128)(2,1)} %bottom_ref.1, ...), custom_call_target="tpu_custom_call" | custom-call | flops 1 | bytes 1 | tf_op jit(solution)/shard_map/inner_product/pallas_call | solution.py:475
  29.5 8.7 %edge_steps_and_product.1 = (bf16[384,512]{1,0:T(8,128)(2,1)S(1)}, bf16[384,512]{1,0:T(8,128)(2,1)S(1)}, f32[2,4,96,512]{3,2,1,0:T(8,128)S(1)}, bf16[2,4,96,512]{3,2,1,0:T(8,128)(2,1)S(1)}) custom-call(f32[2,16,256]{2,1,0:T(8,128)S(1)} %copy-done.2, f32[4,384,128]{2,1,0:T(8,128)S(1)} %copy-done.1, bf16[512,256]{1,0:T(8,128)(2,1)S(1)} %get-tuple-element.49.band_ref, ...), custom_call_target="tpu_custom_call" | custom-call | flops 1 | bytes 1 | tf_op jit(solution)/shard_map/edge_steps_and_product/pallas_call | solution.py:405
  39.5 1.8 %collective-permute-done.4.other_ref = bf16[2,4,96,512]{3,2,1,0:T(8,128)(2,1)S(1)} collective-permute-done((bf16[2,4,96,512]{3,2,1,0:T(8,128)(2,1)S(1)}, bf16[2,4,96,512]{3,2,1,0:T(8,128)(2,1)S(1)}, u32[]{:S(2)}, u32[]{:S(2)}) %collective-permute-start.4) | collective-permute-done | bytes 786464 | tf_op jit(solution)/shard_map/ppermute | solution.py:458
  42.0 4.0 %collective-permute-start.5 = (bf16[96,512]{1,0:T(8,128)(2,1)S(1)}, bf16[96,512]{1,0:T(8,128)(2,1)S(1)}, u32[]{:S(2)}, u32[]{:S(2)}) collective-permute-start(bf16[96,512]{1,0:T(8,128)(2,1)S(1)} %get-tuple-element.59), channel_id=1, source_target_pairs={{0,4},{1,5},{2,6},{3,7},{4,0},{5,1},{6,2},{7,3},{8,12},{9,13},{10,... | collective-permute-start | bytes 294920 | tf_op jit(solution)/shard_map/ppermute | solution.py:458
  46.0 2.6 %collective-permute-start.6 = (bf16[96,512]{1,0:T(8,128)(2,1)S(1)}, bf16[96,512]{1,0:T(8,128)(2,1)S(1)}, u32[]{:S(2)}, u32[]{:S(2)}) collective-permute-start(bf16[96,512]{1,0:T(8,128)(2,1)S(1)} %get-tuple-element.60), channel_id=1, source_target_pairs={{0,8},{1,9},{2,10},{3,11},{4,12},{5,13},{6,14},{7,15},{8,0},{9,1},... | collective-permute-start | bytes 294920 | tf_op jit(solution)/shard_map/ppermute | solution.py:458
  49.1 2.1 %collective-permute-start.9 = (bf16[96,512]{1,0:T(8,128)(2,1)S(1)}, bf16[96,512]{1,0:T(8,128)(2,1)S(1)}, u32[]{:S(2)}, u32[]{:S(2)}) collective-permute-start(bf16[96,512]{1,0:T(8,128)(2,1)S(1)} %get-tuple-element.63), channel_id=1, source_target_pairs={{0,6},{1,7},{2,4},{3,5},{4,2},{5,3},{6,0},{7,1},{8,14},{9,15},{10,... | collective-permute-start | bytes 294920 | tf_op jit(solution)/shard_map/ppermute | solution.py:458
  51.2 5.5 %collective-permute-done.6.refs_2_ = bf16[96,512]{1,0:T(8,128)(2,1)S(1)} collective-permute-done((bf16[96,512]{1,0:T(8,128)(2,1)S(1)}, bf16[96,512]{1,0:T(8,128)(2,1)S(1)}, u32[]{:S(2)}, u32[]{:S(2)}) %collective-permute-start.6) | collective-permute-done | bytes 98336 | tf_op jit(solution)/shard_map/ppermute | solution.py:458
  56.7 3.2 %collective-permute-start.11 = (bf16[96,512]{1,0:T(8,128)(2,1)S(1)}, bf16[96,512]{1,0:T(8,128)(2,1)S(1)}, u32[]{:S(2)}, u32[]{:S(2)}) collective-permute-start(bf16[96,512]{1,0:T(8,128)(2,1)S(1)} %get-tuple-element.65.dep_ref), channel_id=1, source_target_pairs={{0,14},{1,15},{2,12},{3,13},{4,10},{5,11},{6,8},{7,9},{8,6},{9,7},... | collective-permute-start | bytes 294920 | tf_op jit(solution)/shard_map/ppermute | solution.py:458
  59.9 6.5 %density_steps.2 = (f32[12288,128]{1,0:T(8,128)}, f32[8,128]{1,0:T(8,128)S(1)}) custom-call(f32[2,16,256]{2,1,0:T(8,128)S(1)} %copy-done.2, f32[4,384,128]{2,1,0:T(8,128)S(1)} %copy-done.1, bf16[512,256]{1,0:T(8,128)(2,1)S(1)} %get-tuple-element.49.band_ref, bf16[384,4096]{1,0:T(8,128)(2,1)S(1)} %copy-done, ...), custom_call_target="tpu_custom_call" | custom-call | flops 1 | bytes 1 | tf_op jit(solution)/shard_map/density_steps/pallas_call | solution.py:432
  69.3 1.7 %collective-permute-start.14 = (bf16[96,512]{1,0:T(8,128)(2,1)S(1)}, bf16[96,512]{1,0:T(8,128)(2,1)S(1)}, u32[]{:S(2)}, u32[]{:S(2)}) collective-permute-start(bf16[96,512]{1,0:T(8,128)(2,1)S(1)} %first_activation.1.dep_ref.refs_2_.refs_3_), channel_id=1, source_target_pairs={{0,12},{1,13},{2,14},{3,15},{4,8},{5,9},{6,10},{7,11},{8,4},{9,5},... | collective-permute-start | bytes 294920 | tf_op jit(solution)/shard_map/ppermute | solution.py:458
  71.0 6.5 %density_steps.3 = (f32[12288,128]{1,0:T(8,128)}, f32[8,128]{1,0:T(8,128)S(1)}) custom-call(f32[2,16,256]{2,1,0:T(8,128)S(1)} %copy-done.2, f32[4,384,128]{2,1,0:T(8,128)S(1)} %copy-done.1, bf16[512,256]{1,0:T(8,128)(2,1)S(1)} %get-tuple-element.49.band_ref, bf16[384,4096]{1,0:T(8,128)(2,1)S(1)} %copy-done, ...), custom_call_target="tpu_custom_call", output_to_operand_aliasing={{0}: (9, {})} | custom-call | flops 1 | bytes 1 | tf_op jit(solution)/shard_map/density_steps/pallas_call | solution.py:432
  77.5 2.4 %value_layers.1 = (f32[96,512]{1,0:T(8,128)S(1)}, f32[1,512]{1,0:T(1,128)S(1)}, bf16[2,2064,128]{2,1,0:T(8,128)(2,1)S(1)}, bf16[2,2064,128]{2,1,0:T(8,128)(2,1)S...) custom-call(s32[4]{0:T(128)S(1)} %get-tuple-element.53.place_ref.refs_0_, ...), custom_call_target="tpu_custom_call" | custom-call | flops 1 | bytes 1 | tf_op jit(solution)/shard_map/value_layers/pallas_call | solution.py:636
  84.4 2.8 %collective-permute-done.16.refs_0_ = bf16[112,512]{1,0:T(8,128)(2,1)S(1)} collective-permute-done((bf16[112,512]{1,0:T(8,128)(2,1)S(1)}, bf16[112,512]{1,0:T(8,128)(2,1)S(1)}, u32[]{:S(2)}, u32[]{:S(2)}) %collective-permute-start.16) | collective-permute-done | bytes 114720 | tf_op jit(solution)/shard_map/ppermute | solution.py:458
  87.2 6.0 %collective-permute-done.17.refs_1_ = bf16[112,512]{1,0:T(8,128)(2,1)S(1)} collective-permute-done((bf16[112,512]{1,0:T(8,128)(2,1)S(1)}, bf16[112,512]{1,0:T(8,128)(2,1)S(1)}, u32[]{:S(2)}, u32[]{:S(2)}) %collective-permute-start.17) | collective-permute-done | bytes 114720 | tf_op jit(solution)/shard_map/ppermute | solution.py:458
  93.3 2.3 %collective-permute-start.19 = (bf16[96,512]{1,0:T(8,128)(2,1)S(1)}, bf16[96,512]{1,0:T(8,128)(2,1)S(1)}, u32[]{:S(2)}, u32[]{:S(2)}) collective-permute-start(bf16[96,512]{1,0:T(8,128)(2,1)S(1)} %get-tuple-element.78.refs_3_.refs_0_), channel_id=1, source_target_pairs={{0,4},{1,5},{2,6},{3,7},{4,0},{5,1},{6,2},{7,3},{8,12},{9,13},{10,... | collective-permute-start | bytes 294920 | tf_op jit(solution)/shard_map/ppermute | solution.py:458
  96.1 2.0 %collective-permute-start.21 = (bf16[96,512]{1,0:T(8,128)(2,1)S(1)}, bf16[96,512]{1,0:T(8,128)(2,1)S(1)}, u32[]{:S(2)}, u32[]{:S(2)}) collective-permute-start(bf16[96,512]{1,0:T(8,128)(2,1)S(1)} %get-tuple-element.78.refs_3_.refs_0_), channel_id=1, source_target_pairs={{0,12},{1,13},{2,14},{3,15},{4,8},{5,9},{6,10},{7,11},{8,4},{9,5},... | collective-permute-start | bytes 294920 | tf_op jit(solution)/shard_map/ppermute | solution.py:458
  98.9 6.4 %collective-permute-done.20.refs_2_ = bf16[96,512]{1,0:T(8,128)(2,1)S(1)} collective-permute-done((bf16[96,512]{1,0:T(8,128)(2,1)S(1)}, bf16[96,512]{1,0:T(8,128)(2,1)S(1)}, u32[]{:S(2)}, u32[]{:S(2)}) %collective-permute-start.20) | collective-permute-done | bytes 98336 | tf_op jit(solution)/shard_map/ppermute | solution.py:458
  106.8 7.6 %collective-permute-done.23.refs_0_.refs_6_ = bf16[400,512]{1,0:T(8,128)(2,1)S(1)} collective-permute-done((bf16[400,512]{1,0:T(8,128)(2,1)S(1)}, bf16[400,512]{1,0:T(8,128)(2,1)S(1)}, u32[]{:S(2)}, u32[]{:S(2)}) %collective-permute-start.23) | collective-permute-done | bytes 409632 | tf_op jit(solution)/shard_map/ppermute | solution.py:458
  114.6 1.8 %collective-permute-start.26 = (bf16[2064,128]{1,0:T(8,128)(2,1)S(1)}, bf16[2064,128]{1,0:T(8,128)(2,1)S(1)}, u32[]{:S(2)}, u32[]{:S(2)}) collective-permute-start(bf16[2064,128]{1,0:T(8,128)(2,1)S(1)} %get-tuple-element.85.refs_8_), channel_id=1, source_target_pairs={{0,2},{1,3},{2,0},{3,1},{4,6},{5,7},{6,4},{7,5},{8,10},{9,11},{10,... | collective-permute-start | bytes 1585160 | tf_op jit(solution)/shard_map/ppermute | solution.py:458
  118.8 12.3 %first_gradient.1 = (bf16[4096,2048]{1,0:T(8,128)(2,1)}, f32[1,384]{1,0:T(1,128)S(1)}) custom-call(s32[4]{0:T(128)S(1)} %get-tuple-element.53.place_ref.refs_0_, bf16[512,384]{1,0:T(8,128)(2,1)S(1)} %get-tuple-element.79.refs_5_.refs_1_, bf16[3072,384]{1,0:T(8,128)(2,1)S(1)} %get-tuple-element.80.refs_2_, bf16[512,384]{1,0:T(8,128)(2,1)S(1)} %get-tuple-element.81.refs_3_, ...), custom_call_target="tpu_custom_call" | custom-call | flops 1 | bytes 1 | tf_op jit(solution)/shard_map/first_gradient/pallas_call | solution.py:799
  (53 shorter events, 19.0 us)
Async XLA Ops:
  2.9 18.2 %collective-permute-start.2 = (bf16[2064,128]{1,0:T(8,128)(2,1)S(1)}, bf16[2064,128]{1,0:T(8,128)(2,1)S(1)}, u32[]{:S(2)}, u32[]{:S(2)}) collective-permute-start(bf16[2064,128]{1,0:T(8,128)(2,1)S(1)} %get-tuple-element.55.refs_6_), channel_id=1, source_target_pairs={{0,1},{1,0},{2,3},{3,2},{4,5},{5,4},{6,7},{7,6},{8,9},{9,8},{10,11... | collective-permute-start | bytes 1585160 | tf_op jit(solution)/shard_map/ppermute | solution.py:458
  3.4 17.7 %collective-permute-start.3 = (bf16[2064,128]{1,0:T(8,128)(2,1)S(1)}, bf16[2064,128]{1,0:T(8,128)(2,1)S(1)}, u32[]{:S(2)}, u32[]{:S(2)}) collective-permute-start(bf16[2064,128]{1,0:T(8,128)(2,1)S(1)} %get-tuple-element.55.refs_6_), channel_id=1, source_target_pairs={{0,2},{1,3},{2,0},{3,1},{4,6},{5,7},{6,4},{7,5},{8,10},{9,11},{10,... | collective-permute-start | bytes 1585160 | tf_op jit(solution)/shard_map/ppermute | solution.py:458
  17.6 11.9 %collective-permute-start = (bf16[400,512]{1,0:T(8,128)(2,1)S(1)}, bf16[400,512]{1,0:T(8,128)(2,1)S(1)}, u32[]{:S(2)}, u32[]{:S(2)}) collective-permute-start(bf16[400,512]{1,0:T(8,128)(2,1)S(1)} %get-tuple-element.51), channel_id=1, source_target_pairs={{0,1},{1,2},{2,3},{3,4},{4,5},{5,6},{6,7},{7,8},{8,9},{9,10},{10,1... | collective-permute-start | bytes 1228808 | tf_op jit(solution)/shard_map/ppermute | solution.py:835
  19.7 9.8 %collective-permute-start.1 = (bf16[400,512]{1,0:T(8,128)(2,1)S(1)}, bf16[400,512]{1,0:T(8,128)(2,1)S(1)}, u32[]{:S(2)}, u32[]{:S(2)}) collective-permute-start(bf16[400,512]{1,0:T(8,128)(2,1)S(1)} %get-tuple-element.52), channel_id=1, source_target_pairs={{1,0},{2,1},{3,2},{4,3},{5,4},{6,5},{7,6},{8,7},{9,8},{10,9},{11,1... | collective-permute-start | bytes 1228808 | tf_op jit(solution)/shard_map/ppermute | solution.py:836
  39.4 38.0 %collective-permute-start.15 = (bf16[2064,128]{1,0:T(8,128)(2,1)S(1)}, bf16[2064,128]{1,0:T(8,128)(2,1)S(1)}, u32[]{:S(2)}, u32[]{:S(2)}) collective-permute-start(bf16[2064,128]{1,0:T(8,128)(2,1)S(1)} %collective-permute-done.3.refs_7_.refs_8_), channel_id=1, source_target_pairs={{0,1},{1,0},{2,3},{3,2},{4,5},{5,4},{6,7},{7,6},{8,9},{9,8},{10,11... | collective-permute-start | bytes 1585160 | tf_op jit(solution)/shard_map/ppermute | solution.py:458
  42.0 7.1 %collective-permute-start.5 = (bf16[96,512]{1,0:T(8,128)(2,1)S(1)}, bf16[96,512]{1,0:T(8,128)(2,1)S(1)}, u32[]{:S(2)}, u32[]{:S(2)}) collective-permute-start(bf16[96,512]{1,0:T(8,128)(2,1)S(1)} %get-tuple-element.59), channel_id=1, source_target_pairs={{0,4},{1,5},{2,6},{3,7},{4,0},{5,1},{6,2},{7,3},{8,12},{9,13},{10,... | collective-permute-start | bytes 294920 | tf_op jit(solution)/shard_map/ppermute | solution.py:458
  46.0 10.7 %collective-permute-start.6 = (bf16[96,512]{1,0:T(8,128)(2,1)S(1)}, bf16[96,512]{1,0:T(8,128)(2,1)S(1)}, u32[]{:S(2)}, u32[]{:S(2)}) collective-permute-start(bf16[96,512]{1,0:T(8,128)(2,1)S(1)} %get-tuple-element.60), channel_id=1, source_target_pairs={{0,8},{1,9},{2,10},{3,11},{4,12},{5,13},{6,14},{7,15},{8,0},{9,1},... | collective-permute-start | bytes 294920 | tf_op jit(solution)/shard_map/ppermute | solution.py:458
  48.6 8.1 %collective-permute-start.7 = (bf16[96,512]{1,0:T(8,128)(2,1)S(1)}, bf16[96,512]{1,0:T(8,128)(2,1)S(1)}, u32[]{:S(2)}, u32[]{:S(2)}) collective-permute-start(bf16[96,512]{1,0:T(8,128)(2,1)S(1)} %get-tuple-element.61), channel_id=1, source_target_pairs={{0,12},{1,13},{2,14},{3,15},{4,8},{5,9},{6,10},{7,11},{8,4},{9,5},... | collective-permute-start | bytes 294920 | tf_op jit(solution)/shard_map/ppermute | solution.py:458
  48.6 17.8 %collective-permute-start.8 = (bf16[96,512]{1,0:T(8,128)(2,1)S(1)}, bf16[96,512]{1,0:T(8,128)(2,1)S(1)}, u32[]{:S(2)}, u32[]{:S(2)}) collective-permute-start(bf16[96,512]{1,0:T(8,128)(2,1)S(1)} %get-tuple-element.62), channel_id=1, source_target_pairs={{0,2},{1,3},{2,0},{3,1},{4,6},{5,7},{6,4},{7,5},{8,10},{9,11},{10,... | collective-permute-start | bytes 294920 | tf_op jit(solution)/shard_map/ppermute | solution.py:458
  49.1 17.3 %collective-permute-start.9 = (bf16[96,512]{1,0:T(8,128)(2,1)S(1)}, bf16[96,512]{1,0:T(8,128)(2,1)S(1)}, u32[]{:S(2)}, u32[]{:S(2)}) collective-permute-start(bf16[96,512]{1,0:T(8,128)(2,1)S(1)} %get-tuple-element.63), channel_id=1, source_target_pairs={{0,6},{1,7},{2,4},{3,5},{4,2},{5,3},{6,0},{7,1},{8,14},{9,15},{10,... | collective-permute-start | bytes 294920 | tf_op jit(solution)/shard_map/ppermute | solution.py:458
  56.7 9.7 %collective-permute-start.10 = (bf16[96,512]{1,0:T(8,128)(2,1)S(1)}, bf16[96,512]{1,0:T(8,128)(2,1)S(1)}, u32[]{:S(2)}, u32[]{:S(2)}) collective-permute-start(bf16[96,512]{1,0:T(8,128)(2,1)S(1)} %get-tuple-element.64), channel_id=1, source_target_pairs={{0,10},{1,11},{2,8},{3,9},{4,14},{5,15},{6,12},{7,13},{8,2},{9,3},... | collective-permute-start | bytes 294920 | tf_op jit(solution)/shard_map/ppermute | solution.py:458
  56.7 9.7 %collective-permute-start.11 = (bf16[96,512]{1,0:T(8,128)(2,1)S(1)}, bf16[96,512]{1,0:T(8,128)(2,1)S(1)}, u32[]{:S(2)}, u32[]{:S(2)}) collective-permute-start(bf16[96,512]{1,0:T(8,128)(2,1)S(1)} %get-tuple-element.65.dep_ref), channel_id=1, source_target_pairs={{0,14},{1,15},{2,12},{3,13},{4,10},{5,11},{6,8},{7,9},{8,6},{9,7},... | collective-permute-start | bytes 294920 | tf_op jit(solution)/shard_map/ppermute | solution.py:458
  66.5 10.9 %collective-permute-start.12 = (bf16[96,512]{1,0:T(8,128)(2,1)S(1)}, bf16[96,512]{1,0:T(8,128)(2,1)S(1)}, u32[]{:S(2)}, u32[]{:S(2)}) collective-permute-start(bf16[96,512]{1,0:T(8,128)(2,1)S(1)} %first_activation.1.dep_ref.refs_2_.refs_3_), channel_id=1, source_target_pairs={{0,4},{1,5},{2,6},{3,7},{4,0},{5,1},{6,2},{7,3},{8,12},{9,13},{10,... | collective-permute-start | bytes 294920 | tf_op jit(solution)/shard_map/ppermute | solution.py:458
  68.1 9.3 %collective-permute-start.13 = (bf16[96,512]{1,0:T(8,128)(2,1)S(1)}, bf16[96,512]{1,0:T(8,128)(2,1)S(1)}, u32[]{:S(2)}, u32[]{:S(2)}) collective-permute-start(bf16[96,512]{1,0:T(8,128)(2,1)S(1)} %first_activation.1.dep_ref.refs_2_.refs_3_), channel_id=1, source_target_pairs={{0,8},{1,9},{2,10},{3,11},{4,12},{5,13},{6,14},{7,15},{8,0},{9,1},... | collective-permute-start | bytes 294920 | tf_op jit(solution)/shard_map/ppermute | solution.py:458
  69.3 8.2 %collective-permute-start.14 = (bf16[96,512]{1,0:T(8,128)(2,1)S(1)}, bf16[96,512]{1,0:T(8,128)(2,1)S(1)}, u32[]{:S(2)}, u32[]{:S(2)}) collective-permute-start(bf16[96,512]{1,0:T(8,128)(2,1)S(1)} %first_activation.1.dep_ref.refs_2_.refs_3_), channel_id=1, source_target_pairs={{0,12},{1,13},{2,14},{3,15},{4,8},{5,9},{6,10},{7,11},{8,4},{9,5},... | collective-permute-start | bytes 294920 | tf_op jit(solution)/shard_map/ppermute | solution.py:458
  79.9 34.5 %collective-permute-start.25 = (bf16[2,2064,128]{2,1,0:T(8,128)(2,1)S(1)}, bf16[2,2064,128]{2,1,0:T(8,128)(2,1)S(1)}, u32[]{:S(2)}, u32[]{:S(2)}) collective-permute-start(bf16[2,2064,128]{2,1,0:T(8,128)(2,1)S(1)} %get-tuple-element.84), channel_id=1, source_target_pairs={{0,1},{1,0},{2,3},{3,2},{4,5},{5,4},{6,7},{7,6},{8,9},{9,8},{10,11... | collective-permute-start | bytes 3170312 | tf_op jit(solution)/shard_map/ppermute | solution.py:458
  80.0 7.3 %collective-permute-start.16 = (bf16[112,512]{1,0:T(8,128)(2,1)S(1)}, bf16[112,512]{1,0:T(8,128)(2,1)S(1)}, u32[]{:S(2)}, u32[]{:S(2)}) collective-permute-start(bf16[112,512]{1,0:T(8,128)(2,1)S(1)} %get-tuple-element.75), channel_id=1, source_target_pairs={{0,4},{1,5},{2,6},{3,7},{4,0},{5,1},{6,2},{7,3},{8,12},{9,13},{10,... | collective-permute-start | bytes 344072 | tf_op jit(solution)/shard_map/ppermute | solution.py:458
  81.3 11.9 %collective-permute-start.17 = (bf16[112,512]{1,0:T(8,128)(2,1)S(1)}, bf16[112,512]{1,0:T(8,128)(2,1)S(1)}, u32[]{:S(2)}, u32[]{:S(2)}) collective-permute-start(bf16[112,512]{1,0:T(8,128)(2,1)S(1)} %get-tuple-element.76), channel_id=1, source_target_pairs={{0,8},{1,9},{2,10},{3,11},{4,12},{5,13},{6,14},{7,15},{8,0},{9,1},... | collective-permute-start | bytes 344072 | tf_op jit(solution)/shard_map/ppermute | solution.py:458
  82.7 10.5 %collective-permute-start.18 = (bf16[112,512]{1,0:T(8,128)(2,1)S(1)}, bf16[112,512]{1,0:T(8,128)(2,1)S(1)}, u32[]{:S(2)}, u32[]{:S(2)}) collective-permute-start(bf16[112,512]{1,0:T(8,128)(2,1)S(1)} %get-tuple-element.77), channel_id=1, source_target_pairs={{0,12},{1,13},{2,14},{3,15},{4,8},{5,9},{6,10},{7,11},{8,4},{9,5},... | collective-permute-start | bytes 344072 | tf_op jit(solution)/shard_map/ppermute | solution.py:458
  93.3 5.6 %collective-permute-start.19 = (bf16[96,512]{1,0:T(8,128)(2,1)S(1)}, bf16[96,512]{1,0:T(8,128)(2,1)S(1)}, u32[]{:S(2)}, u32[]{:S(2)}) collective-permute-start(bf16[96,512]{1,0:T(8,128)(2,1)S(1)} %get-tuple-element.78.refs_3_.refs_0_), channel_id=1, source_target_pairs={{0,4},{1,5},{2,6},{3,7},{4,0},{5,1},{6,2},{7,3},{8,12},{9,13},{10,... | collective-permute-start | bytes 294920 | tf_op jit(solution)/shard_map/ppermute | solution.py:458
  95.6 9.7 %collective-permute-start.20 = (bf16[96,512]{1,0:T(8,128)(2,1)S(1)}, bf16[96,512]{1,0:T(8,128)(2,1)S(1)}, u32[]{:S(2)}, u32[]{:S(2)}) collective-permute-start(bf16[96,512]{1,0:T(8,128)(2,1)S(1)} %get-tuple-element.78.refs_3_.refs_0_), channel_id=1, source_target_pairs={{0,8},{1,9},{2,10},{3,11},{4,12},{5,13},{6,14},{7,15},{8,0},{9,1},... | collective-permute-start | bytes 294920 | tf_op jit(solution)/shard_map/ppermute | solution.py:458
  96.1 9.2 %collective-permute-start.21 = (bf16[96,512]{1,0:T(8,128)(2,1)S(1)}, bf16[96,512]{1,0:T(8,128)(2,1)S(1)}, u32[]{:S(2)}, u32[]{:S(2)}) collective-permute-start(bf16[96,512]{1,0:T(8,128)(2,1)S(1)} %get-tuple-element.78.refs_3_.refs_0_), channel_id=1, source_target_pairs={{0,12},{1,13},{2,14},{3,15},{4,8},{5,9},{6,10},{7,11},{8,4},{9,5},... | collective-permute-start | bytes 294920 | tf_op jit(solution)/shard_map/ppermute | solution.py:458
  105.3 9.0 %collective-permute-start.23 = (bf16[400,512]{1,0:T(8,128)(2,1)S(1)}, bf16[400,512]{1,0:T(8,128)(2,1)S(1)}, u32[]{:S(2)}, u32[]{:S(2)}) collective-permute-start(bf16[400,512]{1,0:T(8,128)(2,1)S(1)} %stack_parts.1.refs_4_), channel_id=1, source_target_pairs={{0,2},{1,3},{2,0},{3,1},{4,6},{5,7},{6,4},{7,5},{8,10},{9,11},{10,... | collective-permute-start | bytes 1228808 | tf_op jit(solution)/shard_map/ppermute | solution.py:458
  114.6 17.0 %collective-permute-start.26 = (bf16[2064,128]{1,0:T(8,128)(2,1)S(1)}, bf16[2064,128]{1,0:T(8,128)(2,1)S(1)}, u32[]{:S(2)}, u32[]{:S(2)}) collective-permute-start(bf16[2064,128]{1,0:T(8,128)(2,1)S(1)} %get-tuple-element.85.refs_8_), channel_id=1, source_target_pairs={{0,2},{1,3},{2,0},{3,1},{4,6},{5,7},{6,4},{7,5},{8,10},{9,11},{10,... | collective-permute-start | bytes 1585160 | tf_op jit(solution)/shard_map/ppermute | solution.py:458
  (6 other events, 32.2 us)

commit v10 on v9

--- a/solution.py
+++ b/solution.py
@@ -342,77 +342,38 @@
     ]
 
 
-def edge_kernel(
-    blocks, with_inner, drift_ref, shift_ref, band_ref, rows_ref, below_ref, above_ref, below_tail, above_tail,
-    place_ref, top_ref, bottom_ref, *refs,
-):
-    low_ref, high_ref, keep_ref, send_ref, total, *scratch = refs[-8:]
-    step = pl.program_id(0)
+def edge_kernel(drift_ref, shift_ref, band_ref, rows_ref, below_ref, above_ref, below_tail, above_tail, dep_ref, *refs):
+    low_ref, high_ref, *scratch = refs
     rows, columns = drift_ref.shape[1:]
-    size = shift_ref.shape[1]
-    block = keep_ref.shape[2]
-
-    @pl.when(step < blocks)
-    def _():
-        half_drift, edge = with_halo(drift_ref, below_tail, above_tail)
-        where = pl.ds(pl.multiple_of(step * size, size), size)
-
-        def write(row, density):
-            out, at = (low_ref, row) if row < 2 else (high_ref, row - rows + 2)
-            out[where, pl.ds(at * columns, columns)] = density.astype(bf16)
-
-        read = density_read(rows_ref, below_ref, above_ref, rows, columns)
-        shifts = [wide(shift_ref[n], columns) for n in range(4)]
-        two_steps(edge_segments(rows), read, half_drift, edge, band_ref[...], shifts, scratch, write)
-
-    @pl.when(step >= blocks)
-    def _():
-        part = step - blocks
-        left = jnp.concatenate([low_ref[...], high_ref[...]], axis=1)
-        weight = jnp.concatenate([top_ref[...], bottom_ref[...]], axis=0)
-        product = jnp.dot(left, weight, preferred_element_type=f32)
-        total[...] = product + refs[0][part] if with_inner else product
-        core = place_ref[0]
-        for out, half in ((keep_ref, core), (send_ref, 1 - core)):
-            for side in range(2):
-                start = pl.multiple_of((2 * half + side) * block, block)
-                out[side, part] = total[pl.ds(start, block), :].astype(out.dtype)
-
-
-def edge_product(place, drift, shifts, band, own, below, above, weight, inner, parts, width):
+    half_drift, edge = with_halo(drift_ref, below_tail, above_tail)
+
+    def write(row, density):
+        out, at = (low_ref, row) if row < 2 else (high_ref, row - rows + 2)
+        out[:, pl.ds(at * columns, columns)] = density.astype(bf16)
+
+    read = density_read(rows_ref, below_ref, above_ref, rows, columns)
+    shifts = [wide(shift_ref[n], columns) for n in range(4)]
+    two_steps(edge_segments(rows), read, half_drift, edge, band_ref[...], shifts, scratch, write)
+
+
+def edge_steps(drift, shifts, band, own, below, above, dep):
     scenarios = shifts.shape[1]
     rows, columns = drift.shape[1:]
     size = 2 * scenario_block(scenarios)
     size = size if scenarios % size == 0 else size // 2
-    blocks = scenarios // size
     edge = jax.ShapeDtypeStruct((scenarios, 2 * columns), bf16)
-    last = weight.shape[0] // (2 * columns) - 1
-    shape = (2, parts, scenarios // 4, width)
-
-    def column(i):
-        return jnp.maximum(i - blocks, 0)
-
-    in_specs = density_specs(drift, shifts, band, own, below, size, lambda i: jnp.minimum(i, blocks - 1))
-    in_specs += [
-        smem(),
-        pl.BlockSpec((2 * columns, width), lambda i: (0, column(i))),
-        pl.BlockSpec((2 * columns, width), lambda i: (last, column(i))),
-    ]
-    args = [drift, shifts, band, own, below, above, below, above, place, weight, weight]
-    if inner is not None:
-        in_specs.append(vmem())
-        args.append(inner)
-    return pl.pallas_call(
-        functools.partial(edge_kernel, blocks, inner is not None),
-        grid=(blocks + parts,),
-        in_specs=in_specs,
-        out_specs=[vmem()] * 4,
-        out_shape=[edge, edge, jax.ShapeDtypeStruct(shape, f32), jax.ShapeDtypeStruct(shape, bf16)],
-        scratch_shapes=[pltpu.VMEM((scenarios, width), f32)] + step_scratch(edge_segments(rows), size, columns),
-        compiler_params=params(),
-        cost_estimate=pl.CostEstimate(flops=1, bytes_accessed=1, transcendentals=0),
-        name="edge_steps_and_product",
-    )(*args)
+    spec = pl.BlockSpec((size, 2 * columns), lambda i: (i, 0))
+    return pl.pallas_call(
+        edge_kernel,
+        grid=(scenarios // size,),
+        in_specs=density_specs(drift, shifts, band, own, below, size, lambda i: i) + any_specs([dep]),
+        out_specs=[spec, spec],
+        out_shape=[edge, edge],
+        scratch_shapes=step_scratch(edge_segments(rows), size, columns),
+        compiler_params=params(),
+        cost_estimate=pl.CostEstimate(flops=1, bytes_accessed=1, transcendentals=0),
+        name="edge_density_steps",
+    )(drift, shifts, band, own, below, above, below, above, dep)
 
 
 def density_steps(drift, shifts, band, own, below, above, dep, so_far, turn, turns):
@@ -482,6 +443,49 @@
         cost_estimate=pl.CostEstimate(flops=1, bytes_accessed=1, transcendentals=0),
         name="inner_product",
     )(inner, *([weight] * count), *deps)
+
+
+def edge_product_kernel(block, with_inner, place_ref, low_ref, high_ref, top_ref, bottom_ref, *refs):
+    keep_ref, send_ref, total = refs[-3:]
+    step = pl.program_id(0)
+    left = jnp.concatenate([low_ref[...], high_ref[...]], axis=1)
+    weight = jnp.concatenate([top_ref[...], bottom_ref[...]], axis=0)
+    product = jnp.dot(left, weight, preferred_element_type=f32)
+    total[...] = product + refs[0][step] if with_inner else product
+    core = place_ref[0]
+    for out, half in ((keep_ref, core), (send_ref, 1 - core)):
+        for side in range(2):
+            start = pl.multiple_of((2 * half + side) * block, block)
+            out[side, step] = total[pl.ds(start, block), :].astype(out.dtype)
+
+
+def edge_product(place, low, high, weight, inner, parts, width):
+    scenarios, size = low.shape
+    block = scenarios // 4
+    last = weight.shape[0] // size - 1
+    shape = (2, parts, block, width)
+    in_specs = [
+        smem(),
+        vmem(),
+        vmem(),
+        pl.BlockSpec((size, width), lambda n: (0, n)),
+        pl.BlockSpec((size, width), lambda n: (last, n)),
+    ]
+    args = [place, low, high, weight, weight]
+    if inner is not None:
+        in_specs.append(vmem())
+        args.append(inner)
+    return pl.pallas_call(
+        functools.partial(edge_product_kernel, block, inner is not None),
+        grid=(parts,),
+        in_specs=in_specs,
+        out_specs=[vmem(), vmem()],
+        out_shape=[jax.ShapeDtypeStruct(shape, f32), jax.ShapeDtypeStruct(shape, bf16)],
+        scratch_shapes=[pltpu.VMEM((scenarios, width), f32)],
+        compiler_params=params(),
+        cost_estimate=pl.CostEstimate(flops=1, bytes_accessed=1, transcendentals=0),
+        name="edge_product",
+    )(*args)
 
 
 def any_specs(deps):
@@ -702,7 +706,7 @@
 
 def back_first_kernel(count, own_ref, value_ref, *refs):
     received = refs[:count]
-    first_ref, out_ref, tail_ref = refs[count:]
+    first_ref, out_ref, tail_ref = refs[count], *refs[-2:]
     block = first_ref.shape[0]
     value = value_ref[...]
     total = own_ref[...]
@@ -715,16 +719,16 @@
     tail_ref[...] = tail_rows(value)
 
 
-def back_first(own, value, received, first):
+def back_first(own, value, received, first, deps):
     block, width = first.shape
     return pl.pallas_call(
         functools.partial(back_first_kernel, len(received)),
-        in_specs=[vmem()] * (3 + len(received)),
+        in_specs=[vmem()] * (3 + len(received)) + any_specs(deps),
         out_shape=[jax.ShapeDtypeStruct((rows, width), bf16) for rows in (block, EXTRA)],
         compiler_params=params(),
         cost_estimate=pl.CostEstimate(flops=1, bytes_accessed=1, transcendentals=0),
         name="back_first",
-    )(own, value, *received, first)
+    )(own, value, *received, first, *deps)
 
 
 def stack_kernel(count, *refs):
@@ -836,9 +840,8 @@
     above = lax.ppermute(first_rows, "grid", backward)
     first_weight = pltpu.with_memory_space_constraint(first_weight, pltpu.HBM)
     product = None if inner is None else inner_product(inner, first_weight, width, mids[1:])
-    low, high, keep, send = edge_product(
-        place, drift, shifts, band, own_rows, below, above, first_weight, product, parts, width
-    )
+    low, high = edge_steps(drift, shifts, band, own_rows, below, above, own_rows if product is None else product)
+    keep, send = edge_product(place, low, high, first_weight, product, parts, width)
     mids.append(swap(mids[2], count, 1))
 
     def density_turn(turn, dep, so_far):
@@ -847,21 +850,22 @@
     own, *sends = add_core(place, keep, swap(send, count, 1))
     flips = [2 * by_side + 4 * by_part for by_side, by_part in other_places(parts)]
     received = [swap(piece, count, flip) for piece, flip in zip(sends, flips)]
-    density, token = density_turn(0, sends[-1], None)
-    first = activate(own, received, [token])
+    first = activate(own, received)
     firsts = [first] + [swap(first, count, 4 * k) for k in range(1, parts)]
-    density, token = density_turn(1, first, density)
+    density, token = density_turn(0, first, None)
     own, value, mid_keep, mid_send, *sends = middle(place, cot, firsts, mids, 1, parts, width, [token, mids[1], mids[3]])
     received = [swap(piece, count, 4 * (k + 1)) for k, piece in enumerate(sends)]
-    back, tail = back_first(own, value, received, first)
+    density, token = density_turn(1, sends[-1], density)
+    mid_keep, mid_send = mid_add(mid_keep, swap(mid_send, count, 1), [token])
+    back, tail = back_first(own, value, received, first, [token, mid_send])
+    mid_other = swap(mid_send, count, 2)
     lefts = transposed([low, high] if inner is None else [low, inner, high], [back])
     pieces = [back] + [swap(back, count, 4 * k) for k in range(1, parts)] + [tail]
-    stacks = [stack(pieces, [lefts[0]])]
+    stacks = [stack(pieces, [lefts[0], mid_other])]
     stacks += [swap(stacks[0], count, 1), swap(stacks[0], count, 2)]
-    mid_keep, mid_send = mid_add(mid_keep, swap(mid_send, count, 1), [stacks[2]])
+    grad_mid, grad_head, token = mid_final(mid_keep, mid_other, [stacks[0]])
     stacks.append(swap(stacks[2], count, 1))
-    grad_first, value = first_grad(place, lefts, stacks, parts, block, [mid_send])
-    grad_mid, grad_head, _ = mid_final(mid_keep, swap(mid_send, count, 2), [value])
+    grad_first, value = first_grad(place, lefts, stacks, parts, block, [token])
     value = value.reshape(scenarios)
     return from_tiles(density, hist.shape), value, grad_first, grad_mid, grad_head[0]
 

time: 133 us -> 137 us (1.030)
  waiting for transfers between devices: 32 us -> 39.2 us
  starting transfers between devices: 37.7 us -> 35.3 us
    ppermute x25, waiting for transfers between devices: 32 us -> 39.2 us  [swap(): return lax.ppermute(values, 'grid', [(i, i ^ flip) for i in range(count)])]
    ppermute x25, starting transfers between devices: 34.2 us -> 31.4 us  [swap(): return lax.ppermute(values, 'grid', [(i, i ^ flip) for i in range(count)])]
    pallas_call x1 -> x2, Pallas kernels: 8.69 us -> 8.08 us  [the longest x1 4.43 us: edge_product(): pl.pallas_call(functools.partial(edge_product_kernel, block, inner is not...]
  transfers between devices with their start and end apart: 27 -> 27, of which waited for: 9 -> 10; matrix products, arithmetic and copies ran while one was open for 0% -> 0% of each run, Pallas kernels for 35% -> 26%
where the time goes in v10:
time: 137 us
  Pallas kernels  60.5 us (44%)
  waiting for transfers between devices  39.2 us (29%)
  starting transfers between devices  35.3 us (26%)
    ppermute x25, waiting for transfers between devices, swap(): return lax.ppermute(values, 'grid', [(i, i ^ flip) for i in range(count)])  39.2 us
    ppermute x25, starting transfers between devices, swap(): return lax.ppermute(values, 'grid', [(i, i ^ flip) for i in range(count)])  31.4 us
    pallas_call x2, Pallas kernels, density_steps(): pl.pallas_call(density_kernel, grid=(steps,), in_specs=in_specs, out_spec...  12.9 us
    pallas_call x1, Pallas kernels, first_grad(): pl.pallas_call(functools.partial(first_grad_kernel, parts, block, tiles,...  12.3 us
    pallas_call x1, Pallas kernels, inner_steps(): pl.pallas_call(functools.partial(inner_kernel, rows, size), grid=(scenari...  11.5 us
    pallas_call x1, Pallas kernels, inner_product(): pl.pallas_call(functools.partial(inner_product_kernel, count), grid=(hidd...  8.17 us
    pallas_call x1, Pallas kernels, edge_product(): pl.pallas_call(functools.partial(edge_product_kernel, block, inner is not...  4.43 us
    pallas_call x1, Pallas kernels, edge_steps(): pl.pallas_call(edge_kernel, grid=(scenarios // size,), in_specs=density_s...  3.65 us
  transfers between devices with their start and end apart: 27, of which 10 were waited for; matrix products, arithmetic and copies ran while one was open for 0% of the time, Pallas kernels for 26%

profile of v10, /device:TPU:0, one launch (start us, length us, event | category | flops | bytes accessed | tf_op | source)
XLA Modules:
  0.0 136.5 jit_solution(669107828959066176)
XLA Ops:
  0.7 2.2 %mid_with_head.1 = (bf16[2064,128]{1,0:T(8,128)(2,1)S(1)}, s32[4]{0:T(128)S(1)}) custom-call(s32[4]{0:T(128)S(1)} %pad_add_fusion.place_ref, bf16[2048,128]{1,0:T(8,128)(2,1)} %mid_ref.1, f32[1,128]{1,0:T(1,128)} %bitcast.22, f32[384]{0:T(512)} %first_ref.1), custom_call_target="tpu_custom_call" | custom-call | flops 1 | bytes 1 | tf_op jit(solution)/shard_map/mid_with_head/pallas_call | solution.py:554
  2.9 3.0 %collective-permute-start.3 = (bf16[2064,128]{1,0:T(8,128)(2,1)S(1)}, bf16[2064,128]{1,0:T(8,128)(2,1)S(1)}, u32[]{:S(2)}, u32[]{:S(2)}) collective-permute-start(bf16[2064,128]{1,0:T(8,128)(2,1)S(1)} %get-tuple-element.57.refs_6_), channel_id=1, source_target_pairs={{0,2},{1,3},{2,0},{3,1},{4,6},{5,7},{6,4},{7,5},{8,10},{9,11},{10,... | collective-permute-start | bytes 1585160 | tf_op jit(solution)/shard_map/ppermute | solution.py:419
  6.0 11.5 %inner_density_steps.1 = (bf16[400,512]{1,0:T(8,128)(2,1)S(1)}, bf16[400,512]{1,0:T(8,128)(2,1)S(1)}, f32[4,384,128]{2,1,0:T(8,128)}, bf16[512,256]{1,0:T(8,128)...) custom-call(f32[12288,128]{1,0:T(8,128)} %bitcast.18, ...), custom_call_target="tpu_custom_call" | custom-call | flops 1 | bytes 1 | tf_op jit(solution)/shard_map/inner_density_steps/pallas_call | solution.py:237
  17.5 2.4 %collective-permute-start = (bf16[400,512]{1,0:T(8,128)(2,1)S(1)}, bf16[400,512]{1,0:T(8,128)(2,1)S(1)}, u32[]{:S(2)}, u32[]{:S(2)}) collective-permute-start(bf16[400,512]{1,0:T(8,128)(2,1)S(1)} %get-tuple-element.52), channel_id=1, source_target_pairs={{0,1},{1,2},{2,3},{3,4},{4,5},{5,6},{6,7},{7,8},{8,9},{9,10},{10,1... | collective-permute-start | bytes 1228808 | tf_op jit(solution)/shard_map/ppermute | solution.py:839
  21.5 8.2 %inner_product.1.dep_ref.refs_0_ = f32[4,384,512]{2,1,0:T(8,128)S(1)} custom-call(bf16[384,3072]{1,0:T(8,128)(2,1)S(1)} %get-tuple-element.56.inputs_ref.refs_1_, bf16[4096,2048]{1,0:T(8,128)(2,1)} %bottom_ref.1, bf16[4096,2048]{1,0:T(8,128)(2,1)} %bottom_ref.1, bf16[4096,2048]{1,0:T(8,128)(2,1)} %bottom_ref.1, bf16[4096,2048]{1,0:T(8,128)(2,1)} %bottom_ref.1, ...), custom_call_target="tpu_custom_call" | custom-call | flops 1 | bytes 1 | tf_op jit(solution)/shard_map/inner_product/pallas_call | solution.py:436
  29.7 3.6 %edge_density_steps.1 = (bf16[384,512]{1,0:T(8,128)(2,1)S(1)}, bf16[384,512]{1,0:T(8,128)(2,1)S(1)}) custom-call(f32[2,16,256]{2,1,0:T(8,128)S(1)} %copy-done.2, f32[4,384,128]{2,1,0:T(8,128)S(1)} %copy-done.1, bf16[512,256]{1,0:T(8,128)(2,1)S(1)} %get-tuple-element.50.band_ref, bf16[384,4096]{1,0:T(8,128)(2,1)S(1)} %copy-done, ...), custom_call_target="tpu_custom_call" | custom-call | flops 1 | bytes 1 | tf_op jit(solution)/shard_map/edge_density_steps/pallas_call | solution.py:366
  33.3 4.4 %edge_product.1 = (f32[2,4,96,512]{3,2,1,0:T(8,128)S(1)}, bf16[2,4,96,512]{3,2,1,0:T(8,128)(2,1)S(1)}) custom-call(s32[4]{0:T(128)S(1)} %get-tuple-element.54.place_ref.refs_0_, bf16[384,512]{1,0:T(8,128)(2,1)S(1)} %get-tuple-element.58.low_ref.refs_0_, bf16[384,512]{1,0:T(8,128)(2,1)S(1)} %get-tuple-element.59.high_ref.refs_2_, ...), custom_call_target="tpu_custom_call" | custom-call | flops 1 | bytes 1 | tf_op jit(solution)/shard_map/edge_product/pallas_call | solution.py:478
  41.6 3.6 %collective-permute-start.5 = (bf16[96,512]{1,0:T(8,128)(2,1)S(1)}, bf16[96,512]{1,0:T(8,128)(2,1)S(1)}, u32[]{:S(2)}, u32[]{:S(2)}) collective-permute-start(bf16[96,512]{1,0:T(8,128)(2,1)S(1)} %get-tuple-element.63), channel_id=1, source_target_pairs={{0,4},{1,5},{2,6},{3,7},{4,0},{5,1},{6,2},{7,3},{8,12},{9,13},{10,... | collective-permute-start | bytes 294920 | tf_op jit(solution)/shard_map/ppermute | solution.py:419
  45.2 2.6 %collective-permute-start.6 = (bf16[96,512]{1,0:T(8,128)(2,1)S(1)}, bf16[96,512]{1,0:T(8,128)(2,1)S(1)}, u32[]{:S(2)}, u32[]{:S(2)}) collective-permute-start(bf16[96,512]{1,0:T(8,128)(2,1)S(1)} %get-tuple-element.64), channel_id=1, source_target_pairs={{0,8},{1,9},{2,10},{3,11},{4,12},{5,13},{6,14},{7,15},{8,0},{9,1},... | collective-permute-start | bytes 294920 | tf_op jit(solution)/shard_map/ppermute | solution.py:419
  48.3 2.1 %collective-permute-start.9 = (bf16[96,512]{1,0:T(8,128)(2,1)S(1)}, bf16[96,512]{1,0:T(8,128)(2,1)S(1)}, u32[]{:S(2)}, u32[]{:S(2)}) collective-permute-start(bf16[96,512]{1,0:T(8,128)(2,1)S(1)} %get-tuple-element.67), channel_id=1, source_target_pairs={{0,6},{1,7},{2,4},{3,5},{4,2},{5,3},{6,0},{7,1},{8,14},{9,15},{10,... | collective-permute-start | bytes 294920 | tf_op jit(solution)/shard_map/ppermute | solution.py:419
  50.4 5.5 %collective-permute-done.6.refs_2_ = bf16[96,512]{1,0:T(8,128)(2,1)S(1)} collective-permute-done((bf16[96,512]{1,0:T(8,128)(2,1)S(1)}, bf16[96,512]{1,0:T(8,128)(2,1)S(1)}, u32[]{:S(2)}, u32[]{:S(2)}) %collective-permute-start.6) | collective-permute-done | bytes 98336 | tf_op jit(solution)/shard_map/ppermute | solution.py:419
  55.9 3.2 %collective-permute-start.11 = (bf16[96,512]{1,0:T(8,128)(2,1)S(1)}, bf16[96,512]{1,0:T(8,128)(2,1)S(1)}, u32[]{:S(2)}, u32[]{:S(2)}) collective-permute-start(bf16[96,512]{1,0:T(8,128)(2,1)S(1)} %get-tuple-element.69), channel_id=1, source_target_pairs={{0,14},{1,15},{2,12},{3,13},{4,10},{5,11},{6,8},{7,9},{8,6},{9,7},... | collective-permute-start | bytes 294920 | tf_op jit(solution)/shard_map/ppermute | solution.py:419
  59.1 5.5 %collective-permute-done.10.refs_6_ = bf16[96,512]{1,0:T(8,128)(2,1)S(1)} collective-permute-done((bf16[96,512]{1,0:T(8,128)(2,1)S(1)}, bf16[96,512]{1,0:T(8,128)(2,1)S(1)}, u32[]{:S(2)}, u32[]{:S(2)}) %collective-permute-start.10) | collective-permute-done | bytes 98336 | tf_op jit(solution)/shard_map/ppermute | solution.py:419
  64.7 2.1 %collective-permute-start.14 = (bf16[96,512]{1,0:T(8,128)(2,1)S(1)}, bf16[96,512]{1,0:T(8,128)(2,1)S(1)}, u32[]{:S(2)}, u32[]{:S(2)}) collective-permute-start(bf16[96,512]{1,0:T(8,128)(2,1)S(1)} %first_activation.1.dep_ref.refs_2_.refs_3_), channel_id=1, source_target_pairs={{0,12},{1,13},{2,14},{3,15},{4,8},{5,9},{6,10},{7,11},{8,4},{9,5},... | collective-permute-start | bytes 294920 | tf_op jit(solution)/shard_map/ppermute | solution.py:419
  69.2 6.4 %density_steps.2 = (f32[12288,128]{1,0:T(8,128)}, f32[8,128]{1,0:T(8,128)S(1)}) custom-call(f32[2,16,256]{2,1,0:T(8,128)S(1)} %copy-done.2, f32[4,384,128]{2,1,0:T(8,128)S(1)} %copy-done.1, bf16[512,256]{1,0:T(8,128)(2,1)S(1)} %get-tuple-element.50.band_ref, bf16[384,4096]{1,0:T(8,128)(2,1)S(1)} %copy-done, ...), custom_call_target="tpu_custom_call" | custom-call | flops 1 | bytes 1 | tf_op jit(solution)/shard_map/density_steps/pallas_call | solution.py:393
  75.7 2.4 %value_layers.1 = (f32[96,512]{1,0:T(8,128)S(1)}, f32[1,512]{1,0:T(1,128)S(1)}, bf16[2,2064,128]{2,1,0:T(8,128)(2,1)S(1)}, bf16[2,2064,128]{2,1,0:T(8,128)(2,1)S...) custom-call(s32[4]{0:T(128)S(1)} %get-tuple-element.54.place_ref.refs_0_, ...), custom_call_target="tpu_custom_call" | custom-call | flops 1 | bytes 1 | tf_op jit(solution)/shard_map/value_layers/pallas_call | solution.py:640
  78.1 6.5 %density_steps.3 = (f32[12288,128]{1,0:T(8,128)}, f32[8,128]{1,0:T(8,128)S(1)}) custom-call(f32[2,16,256]{2,1,0:T(8,128)S(1)} %copy-done.2, f32[4,384,128]{2,1,0:T(8,128)S(1)} %copy-done.1, bf16[512,256]{1,0:T(8,128)(2,1)S(1)} %get-tuple-element.50.band_ref, bf16[384,4096]{1,0:T(8,128)(2,1)S(1)} %copy-done, ...), custom_call_target="tpu_custom_call", output_to_operand_aliasing={{0}: (9, {})} | custom-call | flops 1 | bytes 1 | tf_op jit(solution)/shard_map/density_steps/pallas_call | solution.py:393
  86.1 1.9 %collective-permute-start.16 = (bf16[112,512]{1,0:T(8,128)(2,1)S(1)}, bf16[112,512]{1,0:T(8,128)(2,1)S(1)}, u32[]{:S(2)}, u32[]{:S(2)}) collective-permute-start(bf16[112,512]{1,0:T(8,128)(2,1)S(1)} %get-tuple-element.76), channel_id=1, source_target_pairs={{0,4},{1,5},{2,6},{3,7},{4,0},{5,1},{6,2},{7,3},{8,12},{9,13},{10,... | collective-permute-start | bytes 344072 | tf_op jit(solution)/shard_map/ppermute | solution.py:419
  91.5 8.0 %collective-permute-done.17.refs_1_ = bf16[112,512]{1,0:T(8,128)(2,1)S(1)} collective-permute-done((bf16[112,512]{1,0:T(8,128)(2,1)S(1)}, bf16[112,512]{1,0:T(8,128)(2,1)S(1)}, u32[]{:S(2)}, u32[]{:S(2)}) %collective-permute-start.17) | collective-permute-done | bytes 114720 | tf_op jit(solution)/shard_map/ppermute | solution.py:419
  101.4 2.0 %collective-permute-start.21 = (bf16[96,512]{1,0:T(8,128)(2,1)S(1)}, bf16[96,512]{1,0:T(8,128)(2,1)S(1)}, u32[]{:S(2)}, u32[]{:S(2)}) collective-permute-start(bf16[96,512]{1,0:T(8,128)(2,1)S(1)} %get-tuple-element.82.refs_3_.refs_0_), channel_id=1, source_target_pairs={{0,8},{1,9},{2,10},{3,11},{4,12},{5,13},{6,14},{7,15},{8,0},{9,1},... | collective-permute-start | bytes 294920 | tf_op jit(solution)/shard_map/ppermute | solution.py:419
  104.9 2.2 %collective-permute-done.22.refs_3_ = bf16[96,512]{1,0:T(8,128)(2,1)S(1)} collective-permute-done((bf16[96,512]{1,0:T(8,128)(2,1)S(1)}, bf16[96,512]{1,0:T(8,128)(2,1)S(1)}, u32[]{:S(2)}, u32[]{:S(2)}) %collective-permute-start.22) | collective-permute-done | bytes 98336 | tf_op jit(solution)/shard_map/ppermute | solution.py:419
  107.2 3.9 %collective-permute-done.21.refs_2_ = bf16[96,512]{1,0:T(8,128)(2,1)S(1)} collective-permute-done((bf16[96,512]{1,0:T(8,128)(2,1)S(1)}, bf16[96,512]{1,0:T(8,128)(2,1)S(1)}, u32[]{:S(2)}, u32[]{:S(2)}) %collective-permute-start.21) | collective-permute-done | bytes 98336 | tf_op jit(solution)/shard_map/ppermute | solution.py:419
  111.7 10.2 %collective-permute-done.25.refs_6_ = bf16[400,512]{1,0:T(8,128)(2,1)S(1)} collective-permute-done((bf16[400,512]{1,0:T(8,128)(2,1)S(1)}, bf16[400,512]{1,0:T(8,128)(2,1)S(1)}, u32[]{:S(2)}, u32[]{:S(2)}) %collective-permute-start.25) | collective-permute-done | bytes 409632 | tf_op jit(solution)/shard_map/ppermute | solution.py:419
  123.6 12.3 %first_gradient.1 = (bf16[4096,2048]{1,0:T(8,128)(2,1)}, f32[1,384]{1,0:T(1,128)S(1)}) custom-call(s32[4]{0:T(128)S(1)} %get-tuple-element.54.place_ref.refs_0_, bf16[512,384]{1,0:T(8,128)(2,1)S(1)} %get-tuple-element.83.refs_5_.refs_1_, bf16[3072,384]{1,0:T(8,128)(2,1)S(1)} %get-tuple-element.84.refs_2_, bf16[512,384]{1,0:T(8,128)(2,1)S(1)} %get-tuple-element.85.refs_3_, ...), custom_call_target="tpu_custom_call" | custom-call | flops 1 | bytes 1 | tf_op jit(solution)/shard_map/first_gradient/pallas_call | solution.py:803
  (54 shorter events, 19.8 us)
Async XLA Ops:
  2.9 18.5 %collective-permute-start.3 = (bf16[2064,128]{1,0:T(8,128)(2,1)S(1)}, bf16[2064,128]{1,0:T(8,128)(2,1)S(1)}, u32[]{:S(2)}, u32[]{:S(2)}) collective-permute-start(bf16[2064,128]{1,0:T(8,128)(2,1)S(1)} %get-tuple-element.57.refs_6_), channel_id=1, source_target_pairs={{0,2},{1,3},{2,0},{3,1},{4,6},{5,7},{6,4},{7,5},{8,10},{9,11},{10,... | collective-permute-start | bytes 1585160 | tf_op jit(solution)/shard_map/ppermute | solution.py:419
  6.0 15.5 %collective-permute-start.2 = (bf16[2064,128]{1,0:T(8,128)(2,1)S(1)}, bf16[2064,128]{1,0:T(8,128)(2,1)S(1)}, u32[]{:S(2)}, u32[]{:S(2)}) collective-permute-start(bf16[2064,128]{1,0:T(8,128)(2,1)S(1)} %get-tuple-element.57.refs_6_), channel_id=1, source_target_pairs={{0,1},{1,0},{2,3},{3,2},{4,5},{5,4},{6,7},{7,6},{8,9},{9,8},{10,11... | collective-permute-start | bytes 1585160 | tf_op jit(solution)/shard_map/ppermute | solution.py:419
  17.5 12.2 %collective-permute-start = (bf16[400,512]{1,0:T(8,128)(2,1)S(1)}, bf16[400,512]{1,0:T(8,128)(2,1)S(1)}, u32[]{:S(2)}, u32[]{:S(2)}) collective-permute-start(bf16[400,512]{1,0:T(8,128)(2,1)S(1)} %get-tuple-element.52), channel_id=1, source_target_pairs={{0,1},{1,2},{2,3},{3,4},{4,5},{5,6},{6,7},{7,8},{8,9},{9,10},{10,1... | collective-permute-start | bytes 1228808 | tf_op jit(solution)/shard_map/ppermute | solution.py:839
  19.9 9.7 %collective-permute-start.1 = (bf16[400,512]{1,0:T(8,128)(2,1)S(1)}, bf16[400,512]{1,0:T(8,128)(2,1)S(1)}, u32[]{:S(2)}, u32[]{:S(2)}) collective-permute-start(bf16[400,512]{1,0:T(8,128)(2,1)S(1)} %get-tuple-element.53), channel_id=1, source_target_pairs={{1,0},{2,1},{3,2},{4,3},{5,4},{6,5},{7,6},{8,7},{9,8},{10,9},{11,1... | collective-permute-start | bytes 1228808 | tf_op jit(solution)/shard_map/ppermute | solution.py:840
  39.0 36.7 %collective-permute-start.15 = (bf16[2064,128]{1,0:T(8,128)(2,1)S(1)}, bf16[2064,128]{1,0:T(8,128)(2,1)S(1)}, u32[]{:S(2)}, u32[]{:S(2)}) collective-permute-start(bf16[2064,128]{1,0:T(8,128)(2,1)S(1)} %collective-permute-done.3.refs_7_.refs_8_), channel_id=1, source_target_pairs={{0,1},{1,0},{2,3},{3,2},{4,5},{5,4},{6,7},{7,6},{8,9},{9,8},{10,11... | collective-permute-start | bytes 1585160 | tf_op jit(solution)/shard_map/ppermute | solution.py:419
  41.6 6.7 %collective-permute-start.5 = (bf16[96,512]{1,0:T(8,128)(2,1)S(1)}, bf16[96,512]{1,0:T(8,128)(2,1)S(1)}, u32[]{:S(2)}, u32[]{:S(2)}) collective-permute-start(bf16[96,512]{1,0:T(8,128)(2,1)S(1)} %get-tuple-element.63), channel_id=1, source_target_pairs={{0,4},{1,5},{2,6},{3,7},{4,0},{5,1},{6,2},{7,3},{8,12},{9,13},{10,... | collective-permute-start | bytes 294920 | tf_op jit(solution)/shard_map/ppermute | solution.py:419
  45.2 10.7 %collective-permute-start.6 = (bf16[96,512]{1,0:T(8,128)(2,1)S(1)}, bf16[96,512]{1,0:T(8,128)(2,1)S(1)}, u32[]{:S(2)}, u32[]{:S(2)}) collective-permute-start(bf16[96,512]{1,0:T(8,128)(2,1)S(1)} %get-tuple-element.64), channel_id=1, source_target_pairs={{0,8},{1,9},{2,10},{3,11},{4,12},{5,13},{6,14},{7,15},{8,0},{9,1},... | collective-permute-start | bytes 294920 | tf_op jit(solution)/shard_map/ppermute | solution.py:419
  47.8 8.1 %collective-permute-start.7 = (bf16[96,512]{1,0:T(8,128)(2,1)S(1)}, bf16[96,512]{1,0:T(8,128)(2,1)S(1)}, u32[]{:S(2)}, u32[]{:S(2)}) collective-permute-start(bf16[96,512]{1,0:T(8,128)(2,1)S(1)} %get-tuple-element.65), channel_id=1, source_target_pairs={{0,12},{1,13},{2,14},{3,15},{4,8},{5,9},{6,10},{7,11},{8,4},{9,5},... | collective-permute-start | bytes 294920 | tf_op jit(solution)/shard_map/ppermute | solution.py:419
  47.8 11.3 %collective-permute-start.8 = (bf16[96,512]{1,0:T(8,128)(2,1)S(1)}, bf16[96,512]{1,0:T(8,128)(2,1)S(1)}, u32[]{:S(2)}, u32[]{:S(2)}) collective-permute-start(bf16[96,512]{1,0:T(8,128)(2,1)S(1)} %get-tuple-element.66), channel_id=1, source_target_pairs={{0,2},{1,3},{2,0},{3,1},{4,6},{5,7},{6,4},{7,5},{8,10},{9,11},{10,... | collective-permute-start | bytes 294920 | tf_op jit(solution)/shard_map/ppermute | solution.py:419
  48.3 10.8 %collective-permute-start.9 = (bf16[96,512]{1,0:T(8,128)(2,1)S(1)}, bf16[96,512]{1,0:T(8,128)(2,1)S(1)}, u32[]{:S(2)}, u32[]{:S(2)}) collective-permute-start(bf16[96,512]{1,0:T(8,128)(2,1)S(1)} %get-tuple-element.67), channel_id=1, source_target_pairs={{0,6},{1,7},{2,4},{3,5},{4,2},{5,3},{6,0},{7,1},{8,14},{9,15},{10,... | collective-permute-start | bytes 294920 | tf_op jit(solution)/shard_map/ppermute | solution.py:419
  55.9 8.7 %collective-permute-start.10 = (bf16[96,512]{1,0:T(8,128)(2,1)S(1)}, bf16[96,512]{1,0:T(8,128)(2,1)S(1)}, u32[]{:S(2)}, u32[]{:S(2)}) collective-permute-start(bf16[96,512]{1,0:T(8,128)(2,1)S(1)} %get-tuple-element.68), channel_id=1, source_target_pairs={{0,10},{1,11},{2,8},{3,9},{4,14},{5,15},{6,12},{7,13},{8,2},{9,3},... | collective-permute-start | bytes 294920 | tf_op jit(solution)/shard_map/ppermute | solution.py:419
  55.9 8.7 %collective-permute-start.11 = (bf16[96,512]{1,0:T(8,128)(2,1)S(1)}, bf16[96,512]{1,0:T(8,128)(2,1)S(1)}, u32[]{:S(2)}, u32[]{:S(2)}) collective-permute-start(bf16[96,512]{1,0:T(8,128)(2,1)S(1)} %get-tuple-element.69), channel_id=1, source_target_pairs={{0,14},{1,15},{2,12},{3,13},{4,10},{5,11},{6,8},{7,9},{8,6},{9,7},... | collective-permute-start | bytes 294920 | tf_op jit(solution)/shard_map/ppermute | solution.py:419
  64.7 10.9 %collective-permute-start.14 = (bf16[96,512]{1,0:T(8,128)(2,1)S(1)}, bf16[96,512]{1,0:T(8,128)(2,1)S(1)}, u32[]{:S(2)}, u32[]{:S(2)}) collective-permute-start(bf16[96,512]{1,0:T(8,128)(2,1)S(1)} %first_activation.1.dep_ref.refs_2_.refs_3_), channel_id=1, source_target_pairs={{0,12},{1,13},{2,14},{3,15},{4,8},{5,9},{6,10},{7,11},{8,4},{9,5},... | collective-permute-start | bytes 294920 | tf_op jit(solution)/shard_map/ppermute | solution.py:419
  66.8 8.8 %collective-permute-start.13 = (bf16[96,512]{1,0:T(8,128)(2,1)S(1)}, bf16[96,512]{1,0:T(8,128)(2,1)S(1)}, u32[]{:S(2)}, u32[]{:S(2)}) collective-permute-start(bf16[96,512]{1,0:T(8,128)(2,1)S(1)} %first_activation.1.dep_ref.refs_2_.refs_3_), channel_id=1, source_target_pairs={{0,8},{1,9},{2,10},{3,11},{4,12},{5,13},{6,14},{7,15},{8,0},{9,1},... | collective-permute-start | bytes 294920 | tf_op jit(solution)/shard_map/ppermute | solution.py:419
  67.9 7.8 %collective-permute-start.12 = (bf16[96,512]{1,0:T(8,128)(2,1)S(1)}, bf16[96,512]{1,0:T(8,128)(2,1)S(1)}, u32[]{:S(2)}, u32[]{:S(2)}) collective-permute-start(bf16[96,512]{1,0:T(8,128)(2,1)S(1)} %first_activation.1.dep_ref.refs_2_.refs_3_), channel_id=1, source_target_pairs={{0,4},{1,5},{2,6},{3,7},{4,0},{5,1},{6,2},{7,3},{8,12},{9,13},{10,... | collective-permute-start | bytes 294920 | tf_op jit(solution)/shard_map/ppermute | solution.py:419
  78.1 6.6 %collective-permute-start.19 = (bf16[2,2064,128]{2,1,0:T(8,128)(2,1)S(1)}, bf16[2,2064,128]{2,1,0:T(8,128)(2,1)S(1)}, u32[]{:S(2)}, u32[]{:S(2)}) collective-permute-start(bf16[2,2064,128]{2,1,0:T(8,128)(2,1)S(1)} %get-tuple-element.80), channel_id=1, source_target_pairs={{0,1},{1,0},{2,3},{3,2},{4,5},{5,4},{6,7},{7,6},{8,9},{9,8},{10,11... | collective-permute-start | bytes 3170312 | tf_op jit(solution)/shard_map/ppermute | solution.py:419
  84.9 26.2 %collective-permute-start.23 = (bf16[2064,128]{1,0:T(8,128)(2,1)S(1)}, bf16[2064,128]{1,0:T(8,128)(2,1)S(1)}, u32[]{:S(2)}, u32[]{:S(2)}) collective-permute-start(bf16[2064,128]{1,0:T(8,128)(2,1)S(1)} %get-tuple-element.81.refs_5_), channel_id=1, source_target_pairs={{0,2},{1,3},{2,0},{3,1},{4,6},{5,7},{6,4},{7,5},{8,10},{9,11},{10,... | collective-permute-start | bytes 1585160 | tf_op jit(solution)/shard_map/ppermute | solution.py:419
  88.0 11.6 %collective-permute-start.17 = (bf16[112,512]{1,0:T(8,128)(2,1)S(1)}, bf16[112,512]{1,0:T(8,128)(2,1)S(1)}, u32[]{:S(2)}, u32[]{:S(2)}) collective-permute-start(bf16[112,512]{1,0:T(8,128)(2,1)S(1)} %get-tuple-element.77), channel_id=1, source_target_pairs={{0,8},{1,9},{2,10},{3,11},{4,12},{5,13},{6,14},{7,15},{8,0},{9,1},... | collective-permute-start | bytes 344072 | tf_op jit(solution)/shard_map/ppermute | solution.py:419
  88.9 10.6 %collective-permute-start.18 = (bf16[112,512]{1,0:T(8,128)(2,1)S(1)}, bf16[112,512]{1,0:T(8,128)(2,1)S(1)}, u32[]{:S(2)}, u32[]{:S(2)}) collective-permute-start(bf16[112,512]{1,0:T(8,128)(2,1)S(1)} %get-tuple-element.71.dep_ref), channel_id=1, source_target_pairs={{0,12},{1,13},{2,14},{3,15},{4,8},{5,9},{6,10},{7,11},{8,4},{9,5},... | collective-permute-start | bytes 344072 | tf_op jit(solution)/shard_map/ppermute | solution.py:419
  99.6 7.5 %collective-permute-start.22 = (bf16[96,512]{1,0:T(8,128)(2,1)S(1)}, bf16[96,512]{1,0:T(8,128)(2,1)S(1)}, u32[]{:S(2)}, u32[]{:S(2)}) collective-permute-start(bf16[96,512]{1,0:T(8,128)(2,1)S(1)} %get-tuple-element.82.refs_3_.refs_0_), channel_id=1, source_target_pairs={{0,12},{1,13},{2,14},{3,15},{4,8},{5,9},{6,10},{7,11},{8,4},{9,5},... | collective-permute-start | bytes 294920 | tf_op jit(solution)/shard_map/ppermute | solution.py:419
  101.4 9.7 %collective-permute-start.21 = (bf16[96,512]{1,0:T(8,128)(2,1)S(1)}, bf16[96,512]{1,0:T(8,128)(2,1)S(1)}, u32[]{:S(2)}, u32[]{:S(2)}) collective-permute-start(bf16[96,512]{1,0:T(8,128)(2,1)S(1)} %get-tuple-element.82.refs_3_.refs_0_), channel_id=1, source_target_pairs={{0,8},{1,9},{2,10},{3,11},{4,12},{5,13},{6,14},{7,15},{8,0},{9,1},... | collective-permute-start | bytes 294920 | tf_op jit(solution)/shard_map/ppermute | solution.py:419
  103.4 7.7 %collective-permute-start.20 = (bf16[96,512]{1,0:T(8,128)(2,1)S(1)}, bf16[96,512]{1,0:T(8,128)(2,1)S(1)}, u32[]{:S(2)}, u32[]{:S(2)}) collective-permute-start(bf16[96,512]{1,0:T(8,128)(2,1)S(1)} %get-tuple-element.82.refs_3_.refs_0_), channel_id=1, source_target_pairs={{0,4},{1,5},{2,6},{3,7},{4,0},{5,1},{6,2},{7,3},{8,12},{9,13},{10,... | collective-permute-start | bytes 294920 | tf_op jit(solution)/shard_map/ppermute | solution.py:419
  111.1 10.8 %collective-permute-start.25 = (bf16[400,512]{1,0:T(8,128)(2,1)S(1)}, bf16[400,512]{1,0:T(8,128)(2,1)S(1)}, u32[]{:S(2)}, u32[]{:S(2)}) collective-permute-start(bf16[400,512]{1,0:T(8,128)(2,1)S(1)} %stack_parts.1.refs_0_.refs_4_), channel_id=1, source_target_pairs={{0,2},{1,3},{2,0},{3,1},{4,6},{5,7},{6,4},{7,5},{8,10},{9,11},{10,... | collective-permute-start | bytes 1228808 | tf_op jit(solution)/shard_map/ppermute | solution.py:419
  111.7 11.1 %collective-permute-start.24 = (bf16[400,512]{1,0:T(8,128)(2,1)S(1)}, bf16[400,512]{1,0:T(8,128)(2,1)S(1)}, u32[]{:S(2)}, u32[]{:S(2)}) collective-permute-start(bf16[400,512]{1,0:T(8,128)(2,1)S(1)} %stack_parts.1.refs_0_.refs_4_), channel_id=1, source_target_pairs={{0,1},{1,0},{2,3},{3,2},{4,5},{5,4},{6,7},{7,6},{8,9},{9,8},{10,11... | collective-permute-start | bytes 1228808 | tf_op jit(solution)/shard_map/ppermute | solution.py:419
  (6 other events, 34.9 us)

commit v11 on v10

--- a/solution.py
+++ b/solution.py
@@ -751,25 +751,28 @@
 
 
 def turn_kernel(count, *refs):
-    for ref, out in zip(refs[:count], refs[-count:]):
-        out[...] = ref[...].T
+    out_ref = refs[-1]
+    at = 0
+    for ref in refs[:count]:
+        out_ref[pl.ds(at, ref.shape[1]), :] = ref[...].T
+        at += ref.shape[1]
 
 
 def transposed(arrays, deps):
+    cells = sum(array.shape[1] for array in arrays)
     return pl.pallas_call(
         functools.partial(turn_kernel, len(arrays)),
         in_specs=[vmem()] * len(arrays) + any_specs(deps),
-        out_shape=[jax.ShapeDtypeStruct(array.shape[::-1], array.dtype) for array in arrays],
+        out_shape=jax.ShapeDtypeStruct((cells, arrays[0].shape[0]), bf16),
         compiler_params=params(),
         cost_estimate=pl.CostEstimate(flops=1, bytes_accessed=1, transcendentals=0),
         name="transposed_inputs",
     )(*arrays, *deps)
 
 
-def first_grad_kernel(parts, block, tiles, count, *refs):
-    place_ref = refs[0]
-    lefts = refs[1 : 1 + count]
-    stacks = refs[1 + count : 5 + count]
+def first_grad_kernel(parts, block, tiles, *refs):
+    place_ref, left_ref = refs[:2]
+    stacks = refs[2:6]
     out_ref, value_ref, whole = refs[-3:]
     width = out_ref.shape[1]
     step = pl.program_id(0)
@@ -786,31 +789,26 @@
         value = tail[0:1] + tail[1:2]
         for q in range(4):
             values[q] = jnp.where(at == q, value, values[q])
-    value_ref[...] = jnp.concatenate(values, axis=1)
-    start = 0
-    for ref in lefts:
-        cells = ref.shape[0]
-        out_ref[pl.ds(start, cells), :] = jnp.dot(ref[...], whole[...], preferred_element_type=f32).astype(bf16)
-        start += cells
-
-
-def first_grad(place, lefts, stacks, parts, block, deps):
-    scenarios = lefts[0].shape[1]
-    cells = sum(left.shape[0] for left in lefts)
+    value_ref[...] = jnp.concatenate(values, axis=1).reshape(4 * block)
+    out_ref[...] = jnp.dot(left_ref[...], whole[...], preferred_element_type=f32).astype(bf16)
+
+
+def first_grad(place, left, stacks, parts, block, deps):
+    cells, scenarios = left.shape
     width = stacks[0].shape[1]
     tile = min(width, 256)
     tiles = width // tile
     return pl.pallas_call(
-        functools.partial(first_grad_kernel, parts, block, tiles, len(lefts)),
+        functools.partial(first_grad_kernel, parts, block, tiles),
         grid=(parts * tiles,),
-        in_specs=[smem()] + [vmem()] * (len(lefts) + 4) + any_specs(deps),
-        out_specs=[pl.BlockSpec((cells, tile), lambda i: (0, i)), pl.BlockSpec((1, scenarios), lambda i: (0, 0))],
-        out_shape=[pltpu.HBM((cells, parts * width), bf16), jax.ShapeDtypeStruct((1, scenarios), f32)],
+        in_specs=[smem()] + [vmem()] * 5 + any_specs(deps),
+        out_specs=[pl.BlockSpec((cells, tile), lambda i: (0, i)), pl.BlockSpec((scenarios,), lambda i: (0,))],
+        out_shape=[pltpu.HBM((cells, parts * width), bf16), jax.ShapeDtypeStruct((scenarios,), f32)],
         scratch_shapes=[pltpu.VMEM((scenarios, tile), bf16)],
         compiler_params=params(),
         cost_estimate=pl.CostEstimate(flops=1, bytes_accessed=1, transcendentals=0),
         name="first_gradient",
-    )(place, *lefts, *stacks, *deps)
+    )(place, left, *stacks, *deps)
 
 
 def local(hist, drift, shocks, shock_table, first_weight, mid_weight, head_weight, cotangent):
@@ -856,17 +854,16 @@
     own, value, mid_keep, mid_send, *sends = middle(place, cot, firsts, mids, 1, parts, width, [token, mids[1], mids[3]])
     received = [swap(piece, count, 4 * (k + 1)) for k, piece in enumerate(sends)]
     density, token = density_turn(1, sends[-1], density)
-    mid_keep, mid_send = mid_add(mid_keep, swap(mid_send, count, 1), [token])
-    back, tail = back_first(own, value, received, first, [token, mid_send])
+    back, tail = back_first(own, value, received, first, [token])
+    mid_keep, mid_send = mid_add(mid_keep, swap(mid_send, count, 1), [back])
     mid_other = swap(mid_send, count, 2)
-    lefts = transposed([low, high] if inner is None else [low, inner, high], [back])
+    left = transposed([low, high] if inner is None else [low, inner, high], [back])
     pieces = [back] + [swap(back, count, 4 * k) for k in range(1, parts)] + [tail]
-    stacks = [stack(pieces, [lefts[0], mid_other])]
+    stacks = [stack(pieces, [left, mid_other])]
     stacks += [swap(stacks[0], count, 1), swap(stacks[0], count, 2)]
     grad_mid, grad_head, token = mid_final(mid_keep, mid_other, [stacks[0]])
     stacks.append(swap(stacks[2], count, 1))
-    grad_first, value = first_grad(place, lefts, stacks, parts, block, [token])
-    value = value.reshape(scenarios)
+    grad_first, value = first_grad(place, left, stacks, parts, block, [token])
     return from_tiles(density, hist.shape), value, grad_first, grad_mid, grad_head[0]
 
 

time: 137 us -> 130 us (0.949)
  waiting for transfers between devices: 39.2 us -> 30.5 us
  starting transfers between devices: 35.3 us -> 37.3 us
    ppermute x25, waiting for transfers between devices: 39.2 us -> 30.5 us  [swap(): return lax.ppermute(values, 'grid', [(i, i ^ flip) for i in range(count)])]
    ppermute x25, starting transfers between devices: 31.4 us -> 33.4 us  [swap(): return lax.ppermute(values, 'grid', [(i, i ^ flip) for i in range(count)])]
  transfers between devices with their start and end apart: 27 -> 27, of which waited for: 10 -> 9; matrix products, arithmetic and copies ran while one was open for 0% -> 0% of each run, Pallas kernels for 26% -> 27%
where the time goes in v11:
time: 130 us; the launch traced here: 129 us
  Pallas kernels  60.5 us (47%)
  starting transfers between devices  37.3 us (29%)
  waiting for transfers between devices  30.5 us (23%)
    ppermute x25, starting transfers between devices, swap(): return lax.ppermute(values, 'grid', [(i, i ^ flip) for i in range(count)])  33.4 us
    ppermute x25, waiting for transfers between devices, swap(): return lax.ppermute(values, 'grid', [(i, i ^ flip) for i in range(count)])  30.5 us
    pallas_call x2, Pallas kernels, density_steps(): pl.pallas_call(density_kernel, grid=(steps,), in_specs=in_specs, out_spec...  12.9 us
    pallas_call x1, Pallas kernels, first_grad(): pl.pallas_call(functools.partial(first_grad_kernel, parts, block, tiles),...  12.2 us
    pallas_call x1, Pallas kernels, inner_steps(): pl.pallas_call(functools.partial(inner_kernel, rows, size), grid=(scenari...  11.5 us
    pallas_call x1, Pallas kernels, inner_product(): pl.pallas_call(functools.partial(inner_product_kernel, count), grid=(hidd...  8.17 us
    pallas_call x1, Pallas kernels, edge_product(): pl.pallas_call(functools.partial(edge_product_kernel, block, inner is not...  4.43 us
    pallas_call x1, Pallas kernels, edge_steps(): pl.pallas_call(edge_kernel, grid=(scenarios // size,), in_specs=density_s...  3.65 us
  transfers between devices with their start and end apart: 27, of which 9 were waited for; matrix products, arithmetic and copies ran while one was open for 0% of the time, Pallas kernels for 27%

profile of v11, /device:TPU:0, one launch (start us, length us, event | category | flops | bytes accessed | tf_op | source)
XLA Modules:
  0.0 129.2 jit_solution(10732639277557448375)
XLA Ops:
  0.7 2.2 %mid_with_head.1 = (bf16[2064,128]{1,0:T(8,128)(2,1)S(1)}, s32[4]{0:T(128)S(1)}) custom-call(s32[4]{0:T(128)S(1)} %pad_add_fusion.place_ref, bf16[2048,128]{1,0:T(8,128)(2,1)} %mid_ref.1, f32[1,128]{1,0:T(1,128)} %bitcast.22, f32[384]{0:T(512)} %first_ref.1), custom_call_target="tpu_custom_call" | custom-call | flops 1 | bytes 1 | tf_op jit(solution)/shard_map/mid_with_head/pallas_call | solution.py:554
  2.9 3.0 %collective-permute-start.3 = (bf16[2064,128]{1,0:T(8,128)(2,1)S(1)}, bf16[2064,128]{1,0:T(8,128)(2,1)S(1)}, u32[]{:S(2)}, u32[]{:S(2)}) collective-permute-start(bf16[2064,128]{1,0:T(8,128)(2,1)S(1)} %get-tuple-element.54.refs_6_), channel_id=1, source_target_pairs={{0,2},{1,3},{2,0},{3,1},{4,6},{5,7},{6,4},{7,5},{8,10},{9,11},{10,... | collective-permute-start | bytes 1585160 | tf_op jit(solution)/shard_map/ppermute | solution.py:419
  6.0 11.5 %inner_density_steps.1 = (bf16[400,512]{1,0:T(8,128)(2,1)S(1)}, bf16[400,512]{1,0:T(8,128)(2,1)S(1)}, f32[4,384,128]{2,1,0:T(8,128)}, bf16[512,256]{1,0:T(8,128)...) custom-call(f32[12288,128]{1,0:T(8,128)} %bitcast.18, ...), custom_call_target="tpu_custom_call" | custom-call | flops 1 | bytes 1 | tf_op jit(solution)/shard_map/inner_density_steps/pallas_call | solution.py:237
  17.5 2.4 %collective-permute-start = (bf16[400,512]{1,0:T(8,128)(2,1)S(1)}, bf16[400,512]{1,0:T(8,128)(2,1)S(1)}, u32[]{:S(2)}, u32[]{:S(2)}) collective-permute-start(bf16[400,512]{1,0:T(8,128)(2,1)S(1)} %get-tuple-element.49), channel_id=1, source_target_pairs={{0,1},{1,2},{2,3},{3,4},{4,5},{5,6},{6,7},{7,8},{8,9},{9,10},{10,1... | collective-permute-start | bytes 1228808 | tf_op jit(solution)/shard_map/ppermute | solution.py:837
  21.5 8.2 %inner_product.1.dep_ref.refs_0_ = f32[4,384,512]{2,1,0:T(8,128)S(1)} custom-call(bf16[384,3072]{1,0:T(8,128)(2,1)S(1)} %get-tuple-element.53.inputs_ref.refs_1_, bf16[4096,2048]{1,0:T(8,128)(2,1)} %bottom_ref.1, bf16[4096,2048]{1,0:T(8,128)(2,1)} %bottom_ref.1, bf16[4096,2048]{1,0:T(8,128)(2,1)} %bottom_ref.1, bf16[4096,2048]{1,0:T(8,128)(2,1)} %bottom_ref.1, ...), custom_call_target="tpu_custom_call" | custom-call | flops 1 | bytes 1 | tf_op jit(solution)/shard_map/inner_product/pallas_call | solution.py:436
  29.7 3.6 %edge_density_steps.1 = (bf16[384,512]{1,0:T(8,128)(2,1)S(1)}, bf16[384,512]{1,0:T(8,128)(2,1)S(1)}) custom-call(f32[2,16,256]{2,1,0:T(8,128)S(1)} %copy-done.2, f32[4,384,128]{2,1,0:T(8,128)S(1)} %copy-done.1, bf16[512,256]{1,0:T(8,128)(2,1)S(1)} %get-tuple-element.47.band_ref, bf16[384,4096]{1,0:T(8,128)(2,1)S(1)} %copy-done, ...), custom_call_target="tpu_custom_call" | custom-call | flops 1 | bytes 1 | tf_op jit(solution)/shard_map/edge_density_steps/pallas_call | solution.py:366
  33.3 4.4 %edge_product.1 = (f32[2,4,96,512]{3,2,1,0:T(8,128)S(1)}, bf16[2,4,96,512]{3,2,1,0:T(8,128)(2,1)S(1)}) custom-call(s32[4]{0:T(128)S(1)} %get-tuple-element.51.place_ref.refs_0_, bf16[384,512]{1,0:T(8,128)(2,1)S(1)} %get-tuple-element.55.low_ref.refs_0_, bf16[384,512]{1,0:T(8,128)(2,1)S(1)} %get-tuple-element.56.high_ref.refs_2_, ...), custom_call_target="tpu_custom_call" | custom-call | flops 1 | bytes 1 | tf_op jit(solution)/shard_map/edge_product/pallas_call | solution.py:478
  41.6 3.6 %collective-permute-start.5 = (bf16[96,512]{1,0:T(8,128)(2,1)S(1)}, bf16[96,512]{1,0:T(8,128)(2,1)S(1)}, u32[]{:S(2)}, u32[]{:S(2)}) collective-permute-start(bf16[96,512]{1,0:T(8,128)(2,1)S(1)} %get-tuple-element.60), channel_id=1, source_target_pairs={{0,4},{1,5},{2,6},{3,7},{4,0},{5,1},{6,2},{7,3},{8,12},{9,13},{10,... | collective-permute-start | bytes 294920 | tf_op jit(solution)/shard_map/ppermute | solution.py:419
  45.2 2.6 %collective-permute-start.6 = (bf16[96,512]{1,0:T(8,128)(2,1)S(1)}, bf16[96,512]{1,0:T(8,128)(2,1)S(1)}, u32[]{:S(2)}, u32[]{:S(2)}) collective-permute-start(bf16[96,512]{1,0:T(8,128)(2,1)S(1)} %get-tuple-element.61), channel_id=1, source_target_pairs={{0,8},{1,9},{2,10},{3,11},{4,12},{5,13},{6,14},{7,15},{8,0},{9,1},... | collective-permute-start | bytes 294920 | tf_op jit(solution)/shard_map/ppermute | solution.py:419
  48.3 2.1 %collective-permute-start.9 = (bf16[96,512]{1,0:T(8,128)(2,1)S(1)}, bf16[96,512]{1,0:T(8,128)(2,1)S(1)}, u32[]{:S(2)}, u32[]{:S(2)}) collective-permute-start(bf16[96,512]{1,0:T(8,128)(2,1)S(1)} %get-tuple-element.64), channel_id=1, source_target_pairs={{0,6},{1,7},{2,4},{3,5},{4,2},{5,3},{6,0},{7,1},{8,14},{9,15},{10,... | collective-permute-start | bytes 294920 | tf_op jit(solution)/shard_map/ppermute | solution.py:419
  50.4 5.5 %collective-permute-done.6.refs_2_ = bf16[96,512]{1,0:T(8,128)(2,1)S(1)} collective-permute-done((bf16[96,512]{1,0:T(8,128)(2,1)S(1)}, bf16[96,512]{1,0:T(8,128)(2,1)S(1)}, u32[]{:S(2)}, u32[]{:S(2)}) %collective-permute-start.6) | collective-permute-done | bytes 98336 | tf_op jit(solution)/shard_map/ppermute | solution.py:419
  55.9 3.2 %collective-permute-start.11 = (bf16[96,512]{1,0:T(8,128)(2,1)S(1)}, bf16[96,512]{1,0:T(8,128)(2,1)S(1)}, u32[]{:S(2)}, u32[]{:S(2)}) collective-permute-start(bf16[96,512]{1,0:T(8,128)(2,1)S(1)} %get-tuple-element.66), channel_id=1, source_target_pairs={{0,14},{1,15},{2,12},{3,13},{4,10},{5,11},{6,8},{7,9},{8,6},{9,7},... | collective-permute-start | bytes 294920 | tf_op jit(solution)/shard_map/ppermute | solution.py:419
  59.1 5.5 %collective-permute-done.10.refs_6_ = bf16[96,512]{1,0:T(8,128)(2,1)S(1)} collective-permute-done((bf16[96,512]{1,0:T(8,128)(2,1)S(1)}, bf16[96,512]{1,0:T(8,128)(2,1)S(1)}, u32[]{:S(2)}, u32[]{:S(2)}) %collective-permute-start.10) | collective-permute-done | bytes 98336 | tf_op jit(solution)/shard_map/ppermute | solution.py:419
  64.7 2.1 %collective-permute-start.14 = (bf16[96,512]{1,0:T(8,128)(2,1)S(1)}, bf16[96,512]{1,0:T(8,128)(2,1)S(1)}, u32[]{:S(2)}, u32[]{:S(2)}) collective-permute-start(bf16[96,512]{1,0:T(8,128)(2,1)S(1)} %first_activation.1.dep_ref.refs_2_.refs_3_), channel_id=1, source_target_pairs={{0,12},{1,13},{2,14},{3,15},{4,8},{5,9},{6,10},{7,11},{8,4},{9,5},... | collective-permute-start | bytes 294920 | tf_op jit(solution)/shard_map/ppermute | solution.py:419
  69.2 6.4 %density_steps.2 = (f32[12288,128]{1,0:T(8,128)}, f32[8,128]{1,0:T(8,128)S(1)}) custom-call(f32[2,16,256]{2,1,0:T(8,128)S(1)} %copy-done.2, f32[4,384,128]{2,1,0:T(8,128)S(1)} %copy-done.1, bf16[512,256]{1,0:T(8,128)(2,1)S(1)} %get-tuple-element.47.band_ref, bf16[384,4096]{1,0:T(8,128)(2,1)S(1)} %copy-done, ...), custom_call_target="tpu_custom_call" | custom-call | flops 1 | bytes 1 | tf_op jit(solution)/shard_map/density_steps/pallas_call | solution.py:393
  75.7 2.4 %value_layers.1 = (f32[96,512]{1,0:T(8,128)S(1)}, f32[1,512]{1,0:T(1,128)S(1)}, bf16[2,2064,128]{2,1,0:T(8,128)(2,1)S(1)}, bf16[2,2064,128]{2,1,0:T(8,128)(2,1)S...) custom-call(s32[4]{0:T(128)S(1)} %get-tuple-element.51.place_ref.refs_0_, ...), custom_call_target="tpu_custom_call" | custom-call | flops 1 | bytes 1 | tf_op jit(solution)/shard_map/value_layers/pallas_call | solution.py:640
  78.9 1.9 %collective-permute-start.17 = (bf16[112,512]{1,0:T(8,128)(2,1)S(1)}, bf16[112,512]{1,0:T(8,128)(2,1)S(1)}, u32[]{:S(2)}, u32[]{:S(2)}) collective-permute-start(bf16[112,512]{1,0:T(8,128)(2,1)S(1)} %get-tuple-element.74), channel_id=1, source_target_pairs={{0,8},{1,9},{2,10},{3,11},{4,12},{5,13},{6,14},{7,15},{8,0},{9,1},... | collective-permute-start | bytes 344072 | tf_op jit(solution)/shard_map/ppermute | solution.py:419
  82.6 6.5 %density_steps.3 = (f32[12288,128]{1,0:T(8,128)}, f32[8,128]{1,0:T(8,128)S(1)}) custom-call(f32[2,16,256]{2,1,0:T(8,128)S(1)} %copy-done.2, f32[4,384,128]{2,1,0:T(8,128)S(1)} %copy-done.1, bf16[512,256]{1,0:T(8,128)(2,1)S(1)} %get-tuple-element.47.band_ref, bf16[384,4096]{1,0:T(8,128)(2,1)S(1)} %copy-done, ...), custom_call_target="tpu_custom_call", output_to_operand_aliasing={{0}: (9, {})} | custom-call | flops 1 | bytes 1 | tf_op jit(solution)/shard_map/density_steps/pallas_call | solution.py:393
  91.1 2.3 %collective-permute-start.23 = (bf16[2064,128]{1,0:T(8,128)(2,1)S(1)}, bf16[2064,128]{1,0:T(8,128)(2,1)S(1)}, u32[]{:S(2)}, u32[]{:S(2)}) collective-permute-start(bf16[2064,128]{1,0:T(8,128)(2,1)S(1)} %get-tuple-element.80), channel_id=1, source_target_pairs={{0,2},{1,3},{2,0},{3,1},{4,6},{5,7},{6,4},{7,5},{8,10},{9,11},{10,... | collective-permute-start | bytes 1585160 | tf_op jit(solution)/shard_map/ppermute | solution.py:419
  94.9 2.2 %collective-permute-start.20 = (bf16[96,512]{1,0:T(8,128)(2,1)S(1)}, bf16[96,512]{1,0:T(8,128)(2,1)S(1)}, u32[]{:S(2)}, u32[]{:S(2)}) collective-permute-start(bf16[96,512]{1,0:T(8,128)(2,1)S(1)} %get-tuple-element.76.refs_3_.refs_0_), channel_id=1, source_target_pairs={{0,8},{1,9},{2,10},{3,11},{4,12},{5,13},{6,14},{7,15},{8,0},{9,1},... | collective-permute-start | bytes 294920 | tf_op jit(solution)/shard_map/ppermute | solution.py:419
  98.7 2.2 %collective-permute-done.21.refs_3_ = bf16[96,512]{1,0:T(8,128)(2,1)S(1)} collective-permute-done((bf16[96,512]{1,0:T(8,128)(2,1)S(1)}, bf16[96,512]{1,0:T(8,128)(2,1)S(1)}, u32[]{:S(2)}, u32[]{:S(2)}) %collective-permute-start.21) | collective-permute-done | bytes 98336 | tf_op jit(solution)/shard_map/ppermute | solution.py:419
  100.9 3.6 %collective-permute-done.20.refs_2_ = bf16[96,512]{1,0:T(8,128)(2,1)S(1)} collective-permute-done((bf16[96,512]{1,0:T(8,128)(2,1)S(1)}, bf16[96,512]{1,0:T(8,128)(2,1)S(1)}, u32[]{:S(2)}, u32[]{:S(2)}) %collective-permute-start.20) | collective-permute-done | bytes 98336 | tf_op jit(solution)/shard_map/ppermute | solution.py:419
  106.1 9.2 %collective-permute-done.25.refs_4_ = bf16[400,512]{1,0:T(8,128)(2,1)S(1)} collective-permute-done((bf16[400,512]{1,0:T(8,128)(2,1)S(1)}, bf16[400,512]{1,0:T(8,128)(2,1)S(1)}, u32[]{:S(2)}, u32[]{:S(2)}) %collective-permute-start.25) | collective-permute-done | bytes 409632 | tf_op jit(solution)/shard_map/ppermute | solution.py:419
  117.0 12.2 %first_gradient.1 = (bf16[4096,2048]{1,0:T(8,128)(2,1)}, f32[384]{0:T(512)}) custom-call(s32[4]{0:T(128)S(1)} %get-tuple-element.51.place_ref.refs_0_, bf16[4096,384]{1,0:T(8,128)(2,1)S(1)} %transposed_inputs.1.refs_5_.refs_1_, bf16[400,512]{1,0:T(8,128)(2,1)S(1)} %stack_parts.1.refs_0_.refs_2_, bf16[400,512]{1,0:T(8,128)(2,1)S(1)} %collective-permute-done.24.refs_3_, ...), custom_call_target="tpu_custom_call" | custom-call | flops 1 | bytes 1 | tf_op jit(solution)/shard_map/first_gradient/pallas_call | solution.py:801
  (53 shorter events, 19.3 us)
Async XLA Ops:
  2.9 18.5 %collective-permute-start.3 = (bf16[2064,128]{1,0:T(8,128)(2,1)S(1)}, bf16[2064,128]{1,0:T(8,128)(2,1)S(1)}, u32[]{:S(2)}, u32[]{:S(2)}) collective-permute-start(bf16[2064,128]{1,0:T(8,128)(2,1)S(1)} %get-tuple-element.54.refs_6_), channel_id=1, source_target_pairs={{0,2},{1,3},{2,0},{3,1},{4,6},{5,7},{6,4},{7,5},{8,10},{9,11},{10,... | collective-permute-start | bytes 1585160 | tf_op jit(solution)/shard_map/ppermute | solution.py:419
  6.0 15.5 %collective-permute-start.2 = (bf16[2064,128]{1,0:T(8,128)(2,1)S(1)}, bf16[2064,128]{1,0:T(8,128)(2,1)S(1)}, u32[]{:S(2)}, u32[]{:S(2)}) collective-permute-start(bf16[2064,128]{1,0:T(8,128)(2,1)S(1)} %get-tuple-element.54.refs_6_), channel_id=1, source_target_pairs={{0,1},{1,0},{2,3},{3,2},{4,5},{5,4},{6,7},{7,6},{8,9},{9,8},{10,11... | collective-permute-start | bytes 1585160 | tf_op jit(solution)/shard_map/ppermute | solution.py:419
  17.5 12.2 %collective-permute-start = (bf16[400,512]{1,0:T(8,128)(2,1)S(1)}, bf16[400,512]{1,0:T(8,128)(2,1)S(1)}, u32[]{:S(2)}, u32[]{:S(2)}) collective-permute-start(bf16[400,512]{1,0:T(8,128)(2,1)S(1)} %get-tuple-element.49), channel_id=1, source_target_pairs={{0,1},{1,2},{2,3},{3,4},{4,5},{5,6},{6,7},{7,8},{8,9},{9,10},{10,1... | collective-permute-start | bytes 1228808 | tf_op jit(solution)/shard_map/ppermute | solution.py:837
  19.9 9.7 %collective-permute-start.1 = (bf16[400,512]{1,0:T(8,128)(2,1)S(1)}, bf16[400,512]{1,0:T(8,128)(2,1)S(1)}, u32[]{:S(2)}, u32[]{:S(2)}) collective-permute-start(bf16[400,512]{1,0:T(8,128)(2,1)S(1)} %get-tuple-element.50), channel_id=1, source_target_pairs={{1,0},{2,1},{3,2},{4,3},{5,4},{6,5},{7,6},{8,7},{9,8},{10,9},{11,1... | collective-permute-start | bytes 1228808 | tf_op jit(solution)/shard_map/ppermute | solution.py:838
  39.0 36.7 %collective-permute-start.15 = (bf16[2064,128]{1,0:T(8,128)(2,1)S(1)}, bf16[2064,128]{1,0:T(8,128)(2,1)S(1)}, u32[]{:S(2)}, u32[]{:S(2)}) collective-permute-start(bf16[2064,128]{1,0:T(8,128)(2,1)S(1)} %collective-permute-done.3.refs_7_.refs_8_), channel_id=1, source_target_pairs={{0,1},{1,0},{2,3},{3,2},{4,5},{5,4},{6,7},{7,6},{8,9},{9,8},{10,11... | collective-permute-start | bytes 1585160 | tf_op jit(solution)/shard_map/ppermute | solution.py:419
  45.2 10.7 %collective-permute-start.6 = (bf16[96,512]{1,0:T(8,128)(2,1)S(1)}, bf16[96,512]{1,0:T(8,128)(2,1)S(1)}, u32[]{:S(2)}, u32[]{:S(2)}) collective-permute-start(bf16[96,512]{1,0:T(8,128)(2,1)S(1)} %get-tuple-element.61), channel_id=1, source_target_pairs={{0,8},{1,9},{2,10},{3,11},{4,12},{5,13},{6,14},{7,15},{8,0},{9,1},... | collective-permute-start | bytes 294920 | tf_op jit(solution)/shard_map/ppermute | solution.py:419
  47.8 8.1 %collective-permute-start.7 = (bf16[96,512]{1,0:T(8,128)(2,1)S(1)}, bf16[96,512]{1,0:T(8,128)(2,1)S(1)}, u32[]{:S(2)}, u32[]{:S(2)}) collective-permute-start(bf16[96,512]{1,0:T(8,128)(2,1)S(1)} %get-tuple-element.62), channel_id=1, source_target_pairs={{0,12},{1,13},{2,14},{3,15},{4,8},{5,9},{6,10},{7,11},{8,4},{9,5},... | collective-permute-start | bytes 294920 | tf_op jit(solution)/shard_map/ppermute | solution.py:419
  47.8 11.3 %collective-permute-start.8 = (bf16[96,512]{1,0:T(8,128)(2,1)S(1)}, bf16[96,512]{1,0:T(8,128)(2,1)S(1)}, u32[]{:S(2)}, u32[]{:S(2)}) collective-permute-start(bf16[96,512]{1,0:T(8,128)(2,1)S(1)} %get-tuple-element.63), channel_id=1, source_target_pairs={{0,2},{1,3},{2,0},{3,1},{4,6},{5,7},{6,4},{7,5},{8,10},{9,11},{10,... | collective-permute-start | bytes 294920 | tf_op jit(solution)/shard_map/ppermute | solution.py:419
  48.3 10.8 %collective-permute-start.9 = (bf16[96,512]{1,0:T(8,128)(2,1)S(1)}, bf16[96,512]{1,0:T(8,128)(2,1)S(1)}, u32[]{:S(2)}, u32[]{:S(2)}) collective-permute-start(bf16[96,512]{1,0:T(8,128)(2,1)S(1)} %get-tuple-element.64), channel_id=1, source_target_pairs={{0,6},{1,7},{2,4},{3,5},{4,2},{5,3},{6,0},{7,1},{8,14},{9,15},{10,... | collective-permute-start | bytes 294920 | tf_op jit(solution)/shard_map/ppermute | solution.py:419
  55.9 8.7 %collective-permute-start.10 = (bf16[96,512]{1,0:T(8,128)(2,1)S(1)}, bf16[96,512]{1,0:T(8,128)(2,1)S(1)}, u32[]{:S(2)}, u32[]{:S(2)}) collective-permute-start(bf16[96,512]{1,0:T(8,128)(2,1)S(1)} %get-tuple-element.65), channel_id=1, source_target_pairs={{0,10},{1,11},{2,8},{3,9},{4,14},{5,15},{6,12},{7,13},{8,2},{9,3},... | collective-permute-start | bytes 294920 | tf_op jit(solution)/shard_map/ppermute | solution.py:419
  55.9 8.7 %collective-permute-start.11 = (bf16[96,512]{1,0:T(8,128)(2,1)S(1)}, bf16[96,512]{1,0:T(8,128)(2,1)S(1)}, u32[]{:S(2)}, u32[]{:S(2)}) collective-permute-start(bf16[96,512]{1,0:T(8,128)(2,1)S(1)} %get-tuple-element.66), channel_id=1, source_target_pairs={{0,14},{1,15},{2,12},{3,13},{4,10},{5,11},{6,8},{7,9},{8,6},{9,7},... | collective-permute-start | bytes 294920 | tf_op jit(solution)/shard_map/ppermute | solution.py:419
  64.7 10.9 %collective-permute-start.14 = (bf16[96,512]{1,0:T(8,128)(2,1)S(1)}, bf16[96,512]{1,0:T(8,128)(2,1)S(1)}, u32[]{:S(2)}, u32[]{:S(2)}) collective-permute-start(bf16[96,512]{1,0:T(8,128)(2,1)S(1)} %first_activation.1.dep_ref.refs_2_.refs_3_), channel_id=1, source_target_pairs={{0,12},{1,13},{2,14},{3,15},{4,8},{5,9},{6,10},{7,11},{8,4},{9,5},... | collective-permute-start | bytes 294920 | tf_op jit(solution)/shard_map/ppermute | solution.py:419
  66.8 8.8 %collective-permute-start.13 = (bf16[96,512]{1,0:T(8,128)(2,1)S(1)}, bf16[96,512]{1,0:T(8,128)(2,1)S(1)}, u32[]{:S(2)}, u32[]{:S(2)}) collective-permute-start(bf16[96,512]{1,0:T(8,128)(2,1)S(1)} %first_activation.1.dep_ref.refs_2_.refs_3_), channel_id=1, source_target_pairs={{0,8},{1,9},{2,10},{3,11},{4,12},{5,13},{6,14},{7,15},{8,0},{9,1},... | collective-permute-start | bytes 294920 | tf_op jit(solution)/shard_map/ppermute | solution.py:419
  67.9 7.8 %collective-permute-start.12 = (bf16[96,512]{1,0:T(8,128)(2,1)S(1)}, bf16[96,512]{1,0:T(8,128)(2,1)S(1)}, u32[]{:S(2)}, u32[]{:S(2)}) collective-permute-start(bf16[96,512]{1,0:T(8,128)(2,1)S(1)} %first_activation.1.dep_ref.refs_2_.refs_3_), channel_id=1, source_target_pairs={{0,4},{1,5},{2,6},{3,7},{4,0},{5,1},{6,2},{7,3},{8,12},{9,13},{10,... | collective-permute-start | bytes 294920 | tf_op jit(solution)/shard_map/ppermute | solution.py:419
  78.1 12.8 %collective-permute-start.22 = (bf16[2,2064,128]{2,1,0:T(8,128)(2,1)S(1)}, bf16[2,2064,128]{2,1,0:T(8,128)(2,1)S(1)}, u32[]{:S(2)}, u32[]{:S(2)}) collective-permute-start(bf16[2,2064,128]{2,1,0:T(8,128)(2,1)S(1)} %get-tuple-element.79), channel_id=1, source_target_pairs={{0,1},{1,0},{2,3},{3,2},{4,5},{5,4},{6,7},{7,6},{8,9},{9,8},{10,11... | collective-permute-start | bytes 3170312 | tf_op jit(solution)/shard_map/ppermute | solution.py:419
  78.1 10.9 %collective-permute-start.16 = (bf16[112,512]{1,0:T(8,128)(2,1)S(1)}, bf16[112,512]{1,0:T(8,128)(2,1)S(1)}, u32[]{:S(2)}, u32[]{:S(2)}) collective-permute-start(bf16[112,512]{1,0:T(8,128)(2,1)S(1)} %get-tuple-element.73), channel_id=1, source_target_pairs={{0,4},{1,5},{2,6},{3,7},{4,0},{5,1},{6,2},{7,3},{8,12},{9,13},{10,... | collective-permute-start | bytes 344072 | tf_op jit(solution)/shard_map/ppermute | solution.py:419
  78.9 11.8 %collective-permute-start.17 = (bf16[112,512]{1,0:T(8,128)(2,1)S(1)}, bf16[112,512]{1,0:T(8,128)(2,1)S(1)}, u32[]{:S(2)}, u32[]{:S(2)}) collective-permute-start(bf16[112,512]{1,0:T(8,128)(2,1)S(1)} %get-tuple-element.74), channel_id=1, source_target_pairs={{0,8},{1,9},{2,10},{3,11},{4,12},{5,13},{6,14},{7,15},{8,0},{9,1},... | collective-permute-start | bytes 344072 | tf_op jit(solution)/shard_map/ppermute | solution.py:419
  80.8 10.0 %collective-permute-start.18 = (bf16[112,512]{1,0:T(8,128)(2,1)S(1)}, bf16[112,512]{1,0:T(8,128)(2,1)S(1)}, u32[]{:S(2)}, u32[]{:S(2)}) collective-permute-start(bf16[112,512]{1,0:T(8,128)(2,1)S(1)} %get-tuple-element.68.dep_ref), channel_id=1, source_target_pairs={{0,12},{1,13},{2,14},{3,15},{4,8},{5,9},{6,10},{7,11},{8,4},{9,5},... | collective-permute-start | bytes 344072 | tf_op jit(solution)/shard_map/ppermute | solution.py:419
  91.1 13.5 %collective-permute-start.23 = (bf16[2064,128]{1,0:T(8,128)(2,1)S(1)}, bf16[2064,128]{1,0:T(8,128)(2,1)S(1)}, u32[]{:S(2)}, u32[]{:S(2)}) collective-permute-start(bf16[2064,128]{1,0:T(8,128)(2,1)S(1)} %get-tuple-element.80), channel_id=1, source_target_pairs={{0,2},{1,3},{2,0},{3,1},{4,6},{5,7},{6,4},{7,5},{8,10},{9,11},{10,... | collective-permute-start | bytes 1585160 | tf_op jit(solution)/shard_map/ppermute | solution.py:419
  93.5 7.5 %collective-permute-start.21 = (bf16[96,512]{1,0:T(8,128)(2,1)S(1)}, bf16[96,512]{1,0:T(8,128)(2,1)S(1)}, u32[]{:S(2)}, u32[]{:S(2)}) collective-permute-start(bf16[96,512]{1,0:T(8,128)(2,1)S(1)} %get-tuple-element.76.refs_3_.refs_0_), channel_id=1, source_target_pairs={{0,12},{1,13},{2,14},{3,15},{4,8},{5,9},{6,10},{7,11},{8,4},{9,5},... | collective-permute-start | bytes 294920 | tf_op jit(solution)/shard_map/ppermute | solution.py:419
  94.9 9.7 %collective-permute-start.20 = (bf16[96,512]{1,0:T(8,128)(2,1)S(1)}, bf16[96,512]{1,0:T(8,128)(2,1)S(1)}, u32[]{:S(2)}, u32[]{:S(2)}) collective-permute-start(bf16[96,512]{1,0:T(8,128)(2,1)S(1)} %get-tuple-element.76.refs_3_.refs_0_), channel_id=1, source_target_pairs={{0,8},{1,9},{2,10},{3,11},{4,12},{5,13},{6,14},{7,15},{8,0},{9,1},... | collective-permute-start | bytes 294920 | tf_op jit(solution)/shard_map/ppermute | solution.py:419
  97.2 7.4 %collective-permute-start.19 = (bf16[96,512]{1,0:T(8,128)(2,1)S(1)}, bf16[96,512]{1,0:T(8,128)(2,1)S(1)}, u32[]{:S(2)}, u32[]{:S(2)}) collective-permute-start(bf16[96,512]{1,0:T(8,128)(2,1)S(1)} %get-tuple-element.76.refs_3_.refs_0_), channel_id=1, source_target_pairs={{0,4},{1,5},{2,6},{3,7},{4,0},{5,1},{6,2},{7,3},{8,12},{9,13},{10,... | collective-permute-start | bytes 294920 | tf_op jit(solution)/shard_map/ppermute | solution.py:419
  104.6 10.6 %collective-permute-start.25 = (bf16[400,512]{1,0:T(8,128)(2,1)S(1)}, bf16[400,512]{1,0:T(8,128)(2,1)S(1)}, u32[]{:S(2)}, u32[]{:S(2)}) collective-permute-start(bf16[400,512]{1,0:T(8,128)(2,1)S(1)} %stack_parts.1.refs_0_.refs_2_), channel_id=1, source_target_pairs={{0,2},{1,3},{2,0},{3,1},{4,6},{5,7},{6,4},{7,5},{8,10},{9,11},{10,... | collective-permute-start | bytes 1228808 | tf_op jit(solution)/shard_map/ppermute | solution.py:419
  106.1 10.1 %collective-permute-start.24 = (bf16[400,512]{1,0:T(8,128)(2,1)S(1)}, bf16[400,512]{1,0:T(8,128)(2,1)S(1)}, u32[]{:S(2)}, u32[]{:S(2)}) collective-permute-start(bf16[400,512]{1,0:T(8,128)(2,1)S(1)} %stack_parts.1.refs_0_.refs_2_), channel_id=1, source_target_pairs={{0,1},{1,0},{2,3},{3,2},{4,5},{5,4},{6,7},{7,6},{8,9},{9,8},{10,11... | collective-permute-start | bytes 1228808 | tf_op jit(solution)/shard_map/ppermute | solution.py:419
  (6 other events, 36.3 us)

commit v12 on v11

--- a/solution.py
+++ b/solution.py
@@ -166,8 +166,8 @@
 
 
 def inner_kernel(
-    rows, size, hist_ref, drift_hbm, levels_hbm, table_hbm, cot_hbm,
-    first_ref, last_ref, shift_ref, band_ref, cot_ref, rows_ref, inner_ref,
+    rows, size, place_ref, hist_ref, drift_hbm, levels_hbm, table_hbm, cot_hbm,
+    place_out_ref, first_ref, last_ref, shift_ref, band_ref, cot_ref, rows_ref, inner_ref,
     drift_ref, levels_ref, table_ref, cot_row, arrived, all_shifts, *scratch,
 ):
     step = pl.program_id(0)
@@ -175,6 +175,8 @@
 
     @pl.when(step == 0)
     def _():
+        for n in range(4):
+            place_out_ref[n] = place_ref[n]
         sources = ((drift_hbm, drift_ref), (levels_hbm, levels_ref), (table_hbm, table_ref), (cot_hbm, cot_row))
         copies = [pltpu.make_async_copy(*pair, arrived.at[n]) for n, pair in enumerate(sources)]
         for copy in copies:
@@ -225,7 +227,7 @@
     interleave([run(n) for n in range(count)])
 
 
-def inner_steps(tiles, drift, levels, table, cot):
+def inner_steps(place, tiles, drift, levels, table, cot):
     scenarios = levels.shape[1]
     rows, columns = drift.shape[1:]
     per = tiles.shape[0] // scenarios
@@ -237,8 +239,9 @@
     return pl.pallas_call(
         functools.partial(inner_kernel, rows, size),
         grid=(scenarios // size,),
-        in_specs=[pl.BlockSpec((size * per, LANES), lambda i: (i, 0))] + [pl.BlockSpec(memory_space=pltpu.HBM)] * 4,
-        out_specs=[pl.BlockSpec(sent.shape, lambda i: (0, 0))] * 2
+        in_specs=[smem(), pl.BlockSpec((size * per, LANES), lambda i: (i, 0))] + [pl.BlockSpec(memory_space=pltpu.HBM)] * 4,
+        out_specs=[smem()]
+        + [pl.BlockSpec(sent.shape, lambda i: (0, 0))] * 2
         + [
             pl.BlockSpec((4, size, LANES), lambda i: (0, i, 0)),
             pl.BlockSpec(band.shape, lambda i: (0, 0)),
@@ -247,6 +250,7 @@
             pl.BlockSpec((size, inner), lambda i: (i, 0)),
         ],
         out_shape=[
+            jax.ShapeDtypeStruct(place.shape, place.dtype),
             sent,
             sent,
             pltpu.HBM(shifts.shape, f32),
@@ -267,7 +271,7 @@
         compiler_params=params(),
         cost_estimate=pl.CostEstimate(flops=1, bytes_accessed=1, transcendentals=0),
         name="inner_density_steps",
-    )(tiles, drift, levels, table, cot)
+    )(place, tiles, drift, levels, table, cot)
 
 
 def halo_drift(ref, columns):
@@ -419,9 +423,12 @@
     return lax.ppermute(values, "grid", [(i, i ^ flip) for i in range(count)])
 
 
-def inner_product_kernel(count, inputs_ref, *refs):
+def inner_product_kernel(count, tiles, inputs_ref, *refs):
     weight = jnp.concatenate([ref[...] for ref in refs[:count]], axis=0)
-    refs[-1][pl.program_id(0)] = jnp.dot(inputs_ref[...], weight, preferred_element_type=f32)
+    step = pl.program_id(0)
+    tile = weight.shape[1]
+    column = pl.ds(pl.multiple_of(step % tiles * tile, tile), tile)
+    refs[-1][step // tiles, :, column] = jnp.dot(inputs_ref[...], weight, preferred_element_type=f32)
 
 
 def inner_product(inner, weight, width, deps):
@@ -430,12 +437,14 @@
     size = (total - cells) // 2
     count = cells // size
 
+    tile = min(width, 256)
+
     def spec(k):
-        return pl.BlockSpec((size, width), lambda n: (1 + k, n))
-
-    return pl.pallas_call(
-        functools.partial(inner_product_kernel, count),
-        grid=(hidden // width,),
+        return pl.BlockSpec((size, tile), lambda n: (1 + k, n))
+
+    return pl.pallas_call(
+        functools.partial(inner_product_kernel, count, width // tile),
+        grid=(hidden // tile,),
         in_specs=[vmem()] + [spec(k) for k in range(count)] + any_specs(deps),
         out_specs=vmem(),
         out_shape=jax.ShapeDtypeStruct((hidden // width, scenarios, width), f32),
@@ -445,7 +454,7 @@
     )(inner, *([weight] * count), *deps)
 
 
-def edge_product_kernel(block, with_inner, place_ref, low_ref, high_ref, top_ref, bottom_ref, *refs):
+def edge_product_kernel(block, with_inner, place_ref, head_ref, low_ref, high_ref, top_ref, bottom_ref, *refs):
     keep_ref, send_ref, total = refs[-3:]
     step = pl.program_id(0)
     left = jnp.concatenate([low_ref[...], high_ref[...]], axis=1)
@@ -456,22 +465,28 @@
     for out, half in ((keep_ref, core), (send_ref, 1 - core)):
         for side in range(2):
             start = pl.multiple_of((2 * half + side) * block, block)
-            out[side, step] = total[pl.ds(start, block), :].astype(out.dtype)
-
-
-def edge_product(place, low, high, weight, inner, parts, width):
+            out[side, step, pl.ds(0, block), :] = total[pl.ds(start, block), :].astype(out.dtype)
+    for side in range(2):
+        send_ref[side, step, pl.ds(block, EXTRA), :] = tail_rows(padded(head_ref[...], send_ref.shape[-1]))
+
+
+def padded(row, width):
+    return jnp.concatenate([row, jnp.zeros((1, width - row.shape[1]), f32)], axis=1)
+
+
+def edge_product(place, head, low, high, weight, inner, parts, width):
     scenarios, size = low.shape
     block = scenarios // 4
     last = weight.shape[0] // size - 1
-    shape = (2, parts, block, width)
     in_specs = [
         smem(),
+        pl.BlockSpec(head.shape, lambda n: (0, 0)),
         vmem(),
         vmem(),
         pl.BlockSpec((size, width), lambda n: (0, n)),
         pl.BlockSpec((size, width), lambda n: (last, n)),
     ]
-    args = [place, low, high, weight, weight]
+    args = [place, head, low, high, weight, weight]
     if inner is not None:
         in_specs.append(vmem())
         args.append(inner)
@@ -480,7 +495,10 @@
         grid=(parts,),
         in_specs=in_specs,
         out_specs=[vmem(), vmem()],
-        out_shape=[jax.ShapeDtypeStruct(shape, f32), jax.ShapeDtypeStruct(shape, bf16)],
+        out_shape=[
+            jax.ShapeDtypeStruct((2, parts, block, width), f32),
+            jax.ShapeDtypeStruct((2, parts, block + EXTRA, width), bf16),
+        ],
         scratch_shapes=[pltpu.VMEM((scenarios, width), f32)],
         compiler_params=params(),
         cost_estimate=pl.CostEstimate(flops=1, bytes_accessed=1, transcendentals=0),
@@ -496,71 +514,65 @@
     return [(side, part) for side in range(2) for part in range(parts) if side or part]
 
 
-def add_core_kernel(place_ref, mine_ref, other_ref, own_ref, *send_refs):
+def add_core_kernel(place_ref, head_ref, mine_ref, other_ref, own_ref, heads_ref, *send_refs):
     side, part = place_ref[1], place_ref[2]
-    own_ref[...] = mine_ref[side, part] + other_ref[side, part].astype(f32)
+    block = mine_ref.shape[2]
+    units = head_ref.shape[1]
+    rows = pl.ds(0, block)
+    tail = other_ref[0, 0, pl.ds(block, EXTRA), :].astype(f32)
+    core_head = tail[0:1] + tail[1:2]
+    own_head = padded(head_ref[...], core_head.shape[1])
+    heads_ref[0:1, :] = own_head[:, :units]
+    heads_ref[1:2, :] = core_head[:, :units]
+    own_ref[...] = mine_ref[side, part] + other_ref[side, part, rows, :].astype(f32)
     for (by_side, by_part), out in zip(other_places(mine_ref.shape[1]), send_refs):
         at = side ^ by_side, part ^ by_part
-        out[...] = (mine_ref[at] + other_ref[at].astype(f32)).astype(bf16)
-
-
-def add_core(place, mine, other):
-    parts, *piece = mine.shape[1:]
+        out[rows, :] = (mine_ref[at] + other_ref[(*at, rows, slice(None))].astype(f32)).astype(bf16)
+        if by_part == 0:
+            pieces = [piece for head in (own_head, core_head) for piece in two_halves(head)]
+            pieces.append(jnp.zeros((EXTRA - 4, own_head.shape[1]), bf16))
+            out[pl.ds(block, EXTRA), :] = jnp.concatenate(pieces, axis=0)
+
+
+def add_core(place, head, mine, other):
+    parts, block, width = mine.shape[1:]
+    sends = [
+        jax.ShapeDtypeStruct((block if by_part else block + EXTRA, width), bf16) for _, by_part in other_places(parts)
+    ]
     return pl.pallas_call(
         add_core_kernel,
-        in_specs=[smem(), vmem(), vmem()],
-        out_shape=[jax.ShapeDtypeStruct(piece, f32)] + [jax.ShapeDtypeStruct(piece, bf16)] * (2 * parts - 1),
+        in_specs=[smem(), vmem(), vmem(), vmem()],
+        out_shape=[jax.ShapeDtypeStruct((block, width), f32), jax.ShapeDtypeStruct((2, head.shape[1]), f32)] + sends,
         compiler_params=params(),
         cost_estimate=pl.CostEstimate(flops=1, bytes_accessed=1, transcendentals=0),
         name="add_core",
-    )(place, mine, other)
-
-
-def activate_kernel(count, *refs):
-    total = refs[0][...]
-    for ref in refs[1 : 1 + count]:
-        total = total + ref[...].astype(f32)
-    refs[-1][...] = jnp.tanh(total).astype(bf16)
-
-
-def activate(own, received, deps=()):
-    return pl.pallas_call(
-        functools.partial(activate_kernel, len(received)),
-        in_specs=[vmem()] * (1 + len(received)) + any_specs(deps),
-        out_shape=jax.ShapeDtypeStruct(own.shape, bf16),
+    )(place, head, mine, other)
+
+
+def activate_kernel(own_ref, heads_ref, *refs):
+    received, (first_ref, head_row_ref) = refs[:-2], refs[-2:]
+    block = own_ref.shape[0]
+    units = heads_ref.shape[1]
+    total = own_ref[...]
+    heads = [heads_ref[0:1, :], heads_ref[1:2, :]]
+    for ref in received:
+        total = total + ref[pl.ds(0, block), :].astype(f32)
+        if ref.shape[0] > block:
+            tail = ref[pl.ds(block, EXTRA), :].astype(f32)
+            heads += [(tail[0:1] + tail[1:2])[:, :units], (tail[2:3] + tail[3:4])[:, :units]]
+    first_ref[...] = jnp.tanh(total).astype(bf16)
+    head_row_ref[...] = jnp.concatenate(heads, axis=1)
+
+
+def activate(own, heads, received):
+    return pl.pallas_call(
+        activate_kernel,
+        in_specs=[vmem()] * (2 + len(received)),
+        out_shape=[jax.ShapeDtypeStruct(own.shape, bf16), jax.ShapeDtypeStruct((1, 4 * heads.shape[1]), f32)],
         compiler_params=params(),
         cost_estimate=pl.CostEstimate(flops=1, bytes_accessed=1, transcendentals=0),
         name="first_activation",
-    )(own, *received, *deps)
-
-
-def pack_kernel(place_ref, mid_ref, head_ref, first_ref, out_ref, place_out_ref, head_row, arrived):
-    for n in range(4):
-        place_out_ref[n] = place_ref[n]
-    hidden = mid_ref.shape[0]
-    copies = [
-        pltpu.make_async_copy(mid_ref, out_ref.at[pl.ds(0, hidden), :], arrived.at[0]),
-        pltpu.make_async_copy(head_ref, head_row, arrived.at[1]),
-    ]
-    for copy in copies:
-        copy.start()
-    copies[1].wait()
-    out_ref[pl.ds(hidden, EXTRA), :] = tail_rows(head_row[...])
-    copies[0].wait()
-
-
-def pack(place, mid_weight, head, first):
-    hidden, units = mid_weight.shape
-    return pl.pallas_call(
-        pack_kernel,
-        in_specs=[smem()] + [pl.BlockSpec(memory_space=pltpu.HBM)] * 3,
-        out_specs=[vmem(), smem()],
-        out_shape=[jax.ShapeDtypeStruct((hidden + EXTRA, units), bf16), jax.ShapeDtypeStruct(place.shape, place.dtype)],
-        scratch_shapes=[pltpu.VMEM(head.shape, f32), pltpu.SemaphoreType.DMA((2,))],
-        compiler_params=params(),
-        cost_estimate=pl.CostEstimate(flops=1, bytes_accessed=1, transcendentals=0),
-        name="mid_with_head",
-    )(place, *[pltpu.with_memory_space_constraint(array, pltpu.HBM) for array in (mid_weight, head)], first)
+    )(own, heads, *received)
 
 
 def two_halves(exact):
@@ -599,8 +611,8 @@
             total = term if total is None else total + term
     second_low = jnp.tanh(total).astype(bf16)
     second = second_low.astype(f32)
-    heads = jnp.concatenate([ref[pl.ds(pieces * width, EXTRA), :] for ref in mid_refs], axis=1)
-    head = heads[0:1].astype(f32) + heads[1:2].astype(f32)
+    head = refs[6 + pieces][...]
+    heads = tail_rows(head)
     rows = lax.dot_general(heads, second_low, (((1,), (1,)), ((), ())), preferred_element_type=f32)
     value = rows[0:1] + rows[1:2]
     if width > block:
@@ -634,12 +646,13 @@
         out[p // 2, pl.ds(pieces * width, EXTRA), :] = tail_rows(head_part[:, p * units : (p + 1) * units])
 
 
-def middle(place, cot, firsts, mids, chunks, parts, width, deps=()):
+def middle(place, cot, firsts, mids, head, chunks, parts, width, deps=()):
     block = firsts[0].shape[0]
-    partial = jax.ShapeDtypeStruct((2, *mids[0].shape), bf16)
+    hidden, units = mids[0].shape
+    partial = jax.ShapeDtypeStruct((2, hidden + EXTRA, units), bf16)
     return pl.pallas_call(
         functools.partial(middle_kernel, chunks, parts, width),
-        in_specs=[smem()] + [vmem()] * (1 + len(firsts) + 4) + any_specs(deps),
+        in_specs=[smem()] + [vmem()] * (1 + len(firsts) + 5) + any_specs(deps),
         out_shape=[
             jax.ShapeDtypeStruct((chunks * block, width), f32),
             jax.ShapeDtypeStruct((1, width), f32),
@@ -650,7 +663,7 @@
         compiler_params=params(),
         cost_estimate=pl.CostEstimate(flops=1, bytes_accessed=1, transcendentals=0),
         name="value_layers",
-    )(place, cot, *firsts, *mids, *deps)
+    )(place, cot, *firsts, *mids, head, *deps)
 
 
 def add_tail(left, right, hidden):
@@ -827,10 +840,9 @@
     place = jnp.stack([core, side, part, mine])
 
     small = [pltpu.with_memory_space_constraint(array, pltpu.HBM) for array in (drift, shocks.T, shock_table.T, cotangent)]
-    packed, place = pack(place, mid_weight, head_weight[None, :], small[-1])
-    mids = [packed]
+    mids = [mid_weight]
     mids += [swap(mids[0], count, 1), swap(mids[0], count, 2)]
-    first_rows, last_rows, shifts, band, cot, own_rows, inner = inner_steps(tiles, *small)
+    place, first_rows, last_rows, shifts, band, cot, own_rows, inner = inner_steps(place, tiles, *small)
     inner = inner if rows > 4 else None
     forward = [(i, i + 1) for i in range(count - 1)]
     backward = [(i + 1, i) for i in range(count - 1)]
@@ -839,19 +851,20 @@
     first_weight = pltpu.with_memory_space_constraint(first_weight, pltpu.HBM)
     product = None if inner is None else inner_product(inner, first_weight, width, mids[1:])
     low, high = edge_steps(drift, shifts, band, own_rows, below, above, own_rows if product is None else product)
-    keep, send = edge_product(place, low, high, first_weight, product, parts, width)
+    head = head_weight[None, :]
+    keep, send = edge_product(place, head, low, high, first_weight, product, parts, width)
     mids.append(swap(mids[2], count, 1))
 
     def density_turn(turn, dep, so_far):
         return density_steps(drift, shifts, band, own_rows, below, above, dep, so_far, turn, 2)
 
-    own, *sends = add_core(place, keep, swap(send, count, 1))
+    own, heads, *sends = add_core(place, head, keep, swap(send, count, 1))
     flips = [2 * by_side + 4 * by_part for by_side, by_part in other_places(parts)]
     received = [swap(piece, count, flip) for piece, flip in zip(sends, flips)]
-    first = activate(own, received)
+    first, head = activate(own, heads, received)
     firsts = [first] + [swap(first, count, 4 * k) for k in range(1, parts)]
     density, token = density_turn(0, first, None)
-    own, value, mid_keep, mid_send, *sends = middle(place, cot, firsts, mids, 1, parts, width, [token, mids[1], mids[3]])
+    own, value, mid_keep, mid_send, *sends = middle(place, cot, firsts, mids, head, 1, parts, width, [token, mids[1], mids[3]])
     received = [swap(piece, count, 4 * (k + 1)) for k, piece in enumerate(sends)]
     density, token = density_turn(1, sends[-1], density)
     back, tail = back_first(own, value, received, first, [token])

time: 130 us -> 129 us (level)
    pallas_call x4 -> x3, Pallas kernels: 11.1 us -> 10.7 us  [the longest x1 9.91 us: inner_product(): pl.pallas_call(functools.partial(inner_product_kernel, count, width // ti...]
  transfers between devices with their start and end apart: 27 -> 27, of which waited for: 9 -> 9; matrix products, arithmetic and copies ran while one was open for 0% -> 0% of each run, Pallas kernels for 27% -> 29%
where the time goes in v12:
time: 129 us
  Pallas kernels  60 us (47%)
  starting transfers between devices  37.2 us (29%)
  waiting for transfers between devices  30.7 us (24%)
    ppermute x25, starting transfers between devices, swap(): return lax.ppermute(values, 'grid', [(i, i ^ flip) for i in range(count)])  33.8 us
    ppermute x25, waiting for transfers between devices, swap(): return lax.ppermute(values, 'grid', [(i, i ^ flip) for i in range(count)])  30.7 us
    pallas_call x2, Pallas kernels, density_steps(): pl.pallas_call(density_kernel, grid=(steps,), in_specs=in_specs, out_spec...  12.8 us
    pallas_call x1, Pallas kernels, first_grad(): pl.pallas_call(functools.partial(first_grad_kernel, parts, block, tiles),...  12.2 us
    pallas_call x1, Pallas kernels, inner_steps(): pl.pallas_call(functools.partial(inner_kernel, rows, size), grid=(scenari...  11.5 us
    pallas_call x1, Pallas kernels, inner_product(): pl.pallas_call(functools.partial(inner_product_kernel, count, width // ti...  9.91 us
    pallas_call x1, Pallas kernels, edge_product(): pl.pallas_call(functools.partial(edge_product_kernel, block, inner is not...  4.44 us
    pallas_call x1, Pallas kernels, edge_steps(): pl.pallas_call(edge_kernel, grid=(scenarios // size,), in_specs=density_s...  3.63 us
  transfers between devices with their start and end apart: 27, of which 9 were waited for; matrix products, arithmetic and copies ran while one was open for 0% of the time, Pallas kernels for 29%

profile of v12, /device:TPU:0, one launch (start us, length us, event | category | flops | bytes accessed | tf_op | source)
XLA Modules:
  0.0 128.9 jit_solution(2555075810452880778)
XLA Ops:
  1.1 2.6 %collective-permute-start.3 = (bf16[2048,128]{1,0:T(8,128)(2,1)}, bf16[2048,128]{1,0:T(8,128)(2,1)S(1)}, u32[]{:S(2)}, u32[]{:S(2)}) collective-permute-start(bf16[2048,128]{1,0:T(8,128)(2,1)} %refs_6_.1), channel_id=1, source_target_pairs={{0,2},{1,3},{2,0},{3,1},{4,6},{5,7},{6,4},{7,5},{8,10},{9,11},{10,... | collective-permute-start | bytes 1572872 | tf_op jit(solution)/shard_map/ppermute | solution.py:423
  3.8 11.5 %inner_density_steps.1 = (s32[4]{0:T(128)S(1)}, bf16[400,512]{1,0:T(8,128)(2,1)S(1)}, bf16[400,512]{1,0:T(8,128)(2,1)S(1)}, f32[4,384,128]{2,1,0:T(8,128)}, bf16...) custom-call(s32[4]{0:T(128)S(1)} %pad_add_fusion.place_ref, ...), custom_call_target="tpu_custom_call" | custom-call | flops 1 | bytes 1 | tf_op jit(solution)/shard_map/inner_density_steps/pallas_call | solution.py:239
  15.4 2.1 %collective-permute-start = (bf16[400,512]{1,0:T(8,128)(2,1)S(1)}, bf16[400,512]{1,0:T(8,128)(2,1)S(1)}, u32[]{:S(2)}, u32[]{:S(2)}) collective-permute-start(bf16[400,512]{1,0:T(8,128)(2,1)S(1)} %get-tuple-element.51), channel_id=1, source_target_pairs={{0,1},{1,2},{2,3},{3,4},{4,5},{5,6},{6,7},{7,8},{8,9},{9,10},{10,1... | collective-permute-start | bytes 1228808 | tf_op jit(solution)/shard_map/ppermute | solution.py:849
  18.8 9.9 %inner_product.1.dep_ref.refs_0_ = f32[4,384,512]{2,1,0:T(8,128)S(1)} custom-call(bf16[384,3072]{1,0:T(8,128)(2,1)S(1)} %get-tuple-element.55.inputs_ref.refs_1_, bf16[4096,2048]{1,0:T(8,128)(2,1)} %bottom_ref.1, bf16[4096,2048]{1,0:T(8,128)(2,1)} %bottom_ref.1, bf16[4096,2048]{1,0:T(8,128)(2,1)} %bottom_ref.1, bf16[4096,2048]{1,0:T(8,128)(2,1)} %bottom_ref.1, ...), custom_call_target="tpu_custom_call" | custom-call | flops 1 | bytes 1 | tf_op jit(solution)/shard_map/inner_product/pallas_call | solution.py:445
  28.8 3.6 %edge_density_steps.1 = (bf16[384,512]{1,0:T(8,128)(2,1)S(1)}, bf16[384,512]{1,0:T(8,128)(2,1)S(1)}) custom-call(f32[2,16,256]{2,1,0:T(8,128)S(1)} %copy-done.2, f32[4,384,128]{2,1,0:T(8,128)S(1)} %copy-done.1, bf16[512,256]{1,0:T(8,128)(2,1)S(1)} %get-tuple-element.49.band_ref, bf16[384,4096]{1,0:T(8,128)(2,1)S(1)} %copy-done, ...), custom_call_target="tpu_custom_call" | custom-call | flops 1 | bytes 1 | tf_op jit(solution)/shard_map/edge_density_steps/pallas_call | solution.py:370
  32.4 4.4 %edge_product.1 = (f32[2,4,96,512]{3,2,1,0:T(8,128)S(1)}, bf16[2,4,112,512]{3,2,1,0:T(8,128)(2,1)S(1)}) custom-call(s32[4]{0:T(128)S(1)} %get-tuple-element.53.place_ref.refs_0_, f32[1,128]{1,0:T(1,128)S(1)} %bitcast.18, bf16[384,512]{1,0:T(8,128)(2,1)S(1)} %get-tuple-element.56.low_ref.refs_0_, bf16[384,512]{1,0:T(8,128)(2,1)S(1)} %get-tuple-element.57.high_ref.refs_2_, ...), custom_call_target="tpu_custom_call" | custom-call | flops 1 | bytes 1 | tf_op jit(solution)/shard_map/edge_product/pallas_call | solution.py:493
  38.2 2.0 %collective-permute-done.4.other_ref = bf16[2,4,112,512]{3,2,1,0:T(8,128)(2,1)S(1)} collective-permute-done((bf16[2,4,112,512]{3,2,1,0:T(8,128)(2,1)S(1)}, bf16[2,4,112,512]{3,2,1,0:T(8,128)(2,1)S(1)}, u32[]{:S(2)}, u32[]{:S(2)}) %collective-permute-start.4) | collective-permute-done | bytes 917536 | tf_op jit(solution)/shard_map/ppermute | solution.py:423
  40.9 4.0 %collective-permute-start.5 = (bf16[96,512]{1,0:T(8,128)(2,1)S(1)}, bf16[96,512]{1,0:T(8,128)(2,1)S(1)}, u32[]{:S(2)}, u32[]{:S(2)}) collective-permute-start(bf16[96,512]{1,0:T(8,128)(2,1)S(1)} %get-tuple-element.62), channel_id=1, source_target_pairs={{0,4},{1,5},{2,6},{3,7},{4,0},{5,1},{6,2},{7,3},{8,12},{9,13},{10,... | collective-permute-start | bytes 294920 | tf_op jit(solution)/shard_map/ppermute | solution.py:423
  44.9 2.6 %collective-permute-start.6 = (bf16[96,512]{1,0:T(8,128)(2,1)S(1)}, bf16[96,512]{1,0:T(8,128)(2,1)S(1)}, u32[]{:S(2)}, u32[]{:S(2)}) collective-permute-start(bf16[96,512]{1,0:T(8,128)(2,1)S(1)} %get-tuple-element.63), channel_id=1, source_target_pairs={{0,8},{1,9},{2,10},{3,11},{4,12},{5,13},{6,14},{7,15},{8,0},{9,1},... | collective-permute-start | bytes 294920 | tf_op jit(solution)/shard_map/ppermute | solution.py:423
  48.0 2.1 %collective-permute-start.9 = (bf16[96,512]{1,0:T(8,128)(2,1)S(1)}, bf16[96,512]{1,0:T(8,128)(2,1)S(1)}, u32[]{:S(2)}, u32[]{:S(2)}) collective-permute-start(bf16[96,512]{1,0:T(8,128)(2,1)S(1)} %get-tuple-element.66), channel_id=1, source_target_pairs={{0,6},{1,7},{2,4},{3,5},{4,2},{5,3},{6,0},{7,1},{8,14},{9,15},{10,... | collective-permute-start | bytes 294920 | tf_op jit(solution)/shard_map/ppermute | solution.py:423
  50.1 5.5 %collective-permute-done.6.refs_1_ = bf16[96,512]{1,0:T(8,128)(2,1)S(1)} collective-permute-done((bf16[96,512]{1,0:T(8,128)(2,1)S(1)}, bf16[96,512]{1,0:T(8,128)(2,1)S(1)}, u32[]{:S(2)}, u32[]{:S(2)}) %collective-permute-start.6) | collective-permute-done | bytes 98336 | tf_op jit(solution)/shard_map/ppermute | solution.py:423
  55.5 3.2 %collective-permute-start.11 = (bf16[96,512]{1,0:T(8,128)(2,1)S(1)}, bf16[96,512]{1,0:T(8,128)(2,1)S(1)}, u32[]{:S(2)}, u32[]{:S(2)}) collective-permute-start(bf16[96,512]{1,0:T(8,128)(2,1)S(1)} %get-tuple-element.68), channel_id=1, source_target_pairs={{0,14},{1,15},{2,12},{3,13},{4,10},{5,11},{6,8},{7,9},{8,6},{9,7},... | collective-permute-start | bytes 294920 | tf_op jit(solution)/shard_map/ppermute | solution.py:423
  58.8 5.5 %collective-permute-done.10.refs_5_ = bf16[96,512]{1,0:T(8,128)(2,1)S(1)} collective-permute-done((bf16[96,512]{1,0:T(8,128)(2,1)S(1)}, bf16[96,512]{1,0:T(8,128)(2,1)S(1)}, u32[]{:S(2)}, u32[]{:S(2)}) %collective-permute-start.10) | collective-permute-done | bytes 98336 | tf_op jit(solution)/shard_map/ppermute | solution.py:423
  64.4 2.1 %collective-permute-start.14 = (bf16[96,512]{1,0:T(8,128)(2,1)S(1)}, bf16[96,512]{1,0:T(8,128)(2,1)S(1)}, u32[]{:S(2)}, u32[]{:S(2)}) collective-permute-start(bf16[96,512]{1,0:T(8,128)(2,1)S(1)} %get-tuple-element.69.dep_ref.refs_2_.refs_3_), channel_id=1, source_target_pairs={{0,12},{1,13},{2,14},{3,15},{4,8},{5,9},{6,10},{7,11},{8,4},{9,5},... | collective-permute-start | bytes 294920 | tf_op jit(solution)/shard_map/ppermute | solution.py:423
  68.9 6.4 %density_steps.2 = (f32[12288,128]{1,0:T(8,128)}, f32[8,128]{1,0:T(8,128)S(1)}) custom-call(f32[2,16,256]{2,1,0:T(8,128)S(1)} %copy-done.2, f32[4,384,128]{2,1,0:T(8,128)S(1)} %copy-done.1, bf16[512,256]{1,0:T(8,128)(2,1)S(1)} %get-tuple-element.49.band_ref, bf16[384,4096]{1,0:T(8,128)(2,1)S(1)} %copy-done, ...), custom_call_target="tpu_custom_call" | custom-call | flops 1 | bytes 1 | tf_op jit(solution)/shard_map/density_steps/pallas_call | solution.py:397
  75.3 2.4 %value_layers.1 = (f32[96,512]{1,0:T(8,128)S(1)}, f32[1,512]{1,0:T(1,128)S(1)}, bf16[2,2064,128]{2,1,0:T(8,128)(2,1)S(1)}, bf16[2,2064,128]{2,1,0:T(8,128)(2,1)S...) custom-call(s32[4]{0:T(128)S(1)} %get-tuple-element.53.place_ref.refs_0_, ...), custom_call_target="tpu_custom_call" | custom-call | flops 1 | bytes 1 | tf_op jit(solution)/shard_map/value_layers/pallas_call | solution.py:653
  78.6 1.9 %collective-permute-start.17 = (bf16[112,512]{1,0:T(8,128)(2,1)S(1)}, bf16[112,512]{1,0:T(8,128)(2,1)S(1)}, u32[]{:S(2)}, u32[]{:S(2)}) collective-permute-start(bf16[112,512]{1,0:T(8,128)(2,1)S(1)} %get-tuple-element.78), channel_id=1, source_target_pairs={{0,8},{1,9},{2,10},{3,11},{4,12},{5,13},{6,14},{7,15},{8,0},{9,1},... | collective-permute-start | bytes 344072 | tf_op jit(solution)/shard_map/ppermute | solution.py:423
  82.3 6.4 %density_steps.3 = (f32[12288,128]{1,0:T(8,128)}, f32[8,128]{1,0:T(8,128)S(1)}) custom-call(f32[2,16,256]{2,1,0:T(8,128)S(1)} %copy-done.2, f32[4,384,128]{2,1,0:T(8,128)S(1)} %copy-done.1, bf16[512,256]{1,0:T(8,128)(2,1)S(1)} %get-tuple-element.49.band_ref, bf16[384,4096]{1,0:T(8,128)(2,1)S(1)} %copy-done, ...), custom_call_target="tpu_custom_call", output_to_operand_aliasing={{0}: (9, {})} | custom-call | flops 1 | bytes 1 | tf_op jit(solution)/shard_map/density_steps/pallas_call | solution.py:397
  90.8 2.3 %collective-permute-start.23 = (bf16[2064,128]{1,0:T(8,128)(2,1)S(1)}, bf16[2064,128]{1,0:T(8,128)(2,1)S(1)}, u32[]{:S(2)}, u32[]{:S(2)}) collective-permute-start(bf16[2064,128]{1,0:T(8,128)(2,1)S(1)} %get-tuple-element.84), channel_id=1, source_target_pairs={{0,2},{1,3},{2,0},{3,1},{4,6},{5,7},{6,4},{7,5},{8,10},{9,11},{10,... | collective-permute-start | bytes 1585160 | tf_op jit(solution)/shard_map/ppermute | solution.py:423
  94.6 2.2 %collective-permute-start.20 = (bf16[96,512]{1,0:T(8,128)(2,1)S(1)}, bf16[96,512]{1,0:T(8,128)(2,1)S(1)}, u32[]{:S(2)}, u32[]{:S(2)}) collective-permute-start(bf16[96,512]{1,0:T(8,128)(2,1)S(1)} %get-tuple-element.80.refs_3_.refs_0_), channel_id=1, source_target_pairs={{0,8},{1,9},{2,10},{3,11},{4,12},{5,13},{6,14},{7,15},{8,0},{9,1},... | collective-permute-start | bytes 294920 | tf_op jit(solution)/shard_map/ppermute | solution.py:423
  98.4 2.2 %collective-permute-done.21.refs_3_ = bf16[96,512]{1,0:T(8,128)(2,1)S(1)} collective-permute-done((bf16[96,512]{1,0:T(8,128)(2,1)S(1)}, bf16[96,512]{1,0:T(8,128)(2,1)S(1)}, u32[]{:S(2)}, u32[]{:S(2)}) %collective-permute-start.21) | collective-permute-done | bytes 98336 | tf_op jit(solution)/shard_map/ppermute | solution.py:423
  100.6 3.6 %collective-permute-done.20.refs_2_ = bf16[96,512]{1,0:T(8,128)(2,1)S(1)} collective-permute-done((bf16[96,512]{1,0:T(8,128)(2,1)S(1)}, bf16[96,512]{1,0:T(8,128)(2,1)S(1)}, u32[]{:S(2)}, u32[]{:S(2)}) %collective-permute-start.20) | collective-permute-done | bytes 98336 | tf_op jit(solution)/shard_map/ppermute | solution.py:423
  105.7 9.2 %collective-permute-done.25.refs_4_ = bf16[400,512]{1,0:T(8,128)(2,1)S(1)} collective-permute-done((bf16[400,512]{1,0:T(8,128)(2,1)S(1)}, bf16[400,512]{1,0:T(8,128)(2,1)S(1)}, u32[]{:S(2)}, u32[]{:S(2)}) %collective-permute-start.25) | collective-permute-done | bytes 409632 | tf_op jit(solution)/shard_map/ppermute | solution.py:423
  116.6 12.2 %first_gradient.1 = (bf16[4096,2048]{1,0:T(8,128)(2,1)}, f32[384]{0:T(512)}) custom-call(s32[4]{0:T(128)S(1)} %get-tuple-element.53.place_ref.refs_0_, bf16[4096,384]{1,0:T(8,128)(2,1)S(1)} %transposed_inputs.1.refs_5_.refs_1_, bf16[400,512]{1,0:T(8,128)(2,1)S(1)} %stack_parts.1.refs_0_.refs_2_, bf16[400,512]{1,0:T(8,128)(2,1)S(1)} %collective-permute-done.24.refs_3_, ...), custom_call_target="tpu_custom_call" | custom-call | flops 1 | bytes 1 | tf_op jit(solution)/shard_map/first_gradient/pallas_call | solution.py:814
  (56 shorter events, 17.9 us)
Async XLA Ops:
  0.6 18.1 %collective-permute-start.2 = (bf16[2048,128]{1,0:T(8,128)(2,1)}, bf16[2048,128]{1,0:T(8,128)(2,1)S(1)}, u32[]{:S(2)}, u32[]{:S(2)}) collective-permute-start(bf16[2048,128]{1,0:T(8,128)(2,1)} %refs_6_.1), channel_id=1, source_target_pairs={{0,1},{1,0},{2,3},{3,2},{4,5},{5,4},{6,7},{7,6},{8,9},{9,8},{10,11... | collective-permute-start | bytes 1572872 | tf_op jit(solution)/shard_map/ppermute | solution.py:423
  1.1 17.6 %collective-permute-start.3 = (bf16[2048,128]{1,0:T(8,128)(2,1)}, bf16[2048,128]{1,0:T(8,128)(2,1)S(1)}, u32[]{:S(2)}, u32[]{:S(2)}) collective-permute-start(bf16[2048,128]{1,0:T(8,128)(2,1)} %refs_6_.1), channel_id=1, source_target_pairs={{0,2},{1,3},{2,0},{3,1},{4,6},{5,7},{6,4},{7,5},{8,10},{9,11},{10,... | collective-permute-start | bytes 1572872 | tf_op jit(solution)/shard_map/ppermute | solution.py:423
  15.4 13.4 %collective-permute-start = (bf16[400,512]{1,0:T(8,128)(2,1)S(1)}, bf16[400,512]{1,0:T(8,128)(2,1)S(1)}, u32[]{:S(2)}, u32[]{:S(2)}) collective-permute-start(bf16[400,512]{1,0:T(8,128)(2,1)S(1)} %get-tuple-element.51), channel_id=1, source_target_pairs={{0,1},{1,2},{2,3},{3,4},{4,5},{5,6},{6,7},{7,8},{8,9},{9,10},{10,1... | collective-permute-start | bytes 1228808 | tf_op jit(solution)/shard_map/ppermute | solution.py:849
  17.5 11.3 %collective-permute-start.1 = (bf16[400,512]{1,0:T(8,128)(2,1)S(1)}, bf16[400,512]{1,0:T(8,128)(2,1)S(1)}, u32[]{:S(2)}, u32[]{:S(2)}) collective-permute-start(bf16[400,512]{1,0:T(8,128)(2,1)S(1)} %get-tuple-element.52), channel_id=1, source_target_pairs={{1,0},{2,1},{3,2},{4,3},{5,4},{6,5},{7,6},{8,7},{9,8},{10,9},{11,1... | collective-permute-start | bytes 1228808 | tf_op jit(solution)/shard_map/ppermute | solution.py:850
  38.1 37.2 %collective-permute-start.15 = (bf16[2048,128]{1,0:T(8,128)(2,1)S(1)}, bf16[2048,128]{1,0:T(8,128)(2,1)S(1)}, u32[]{:S(2)}, u32[]{:S(2)}) collective-permute-start(bf16[2048,128]{1,0:T(8,128)(2,1)S(1)} %collective-permute-done.3.refs_7_.refs_8_), channel_id=1, source_target_pairs={{0,1},{1,0},{2,3},{3,2},{4,5},{5,4},{6,7},{7,6},{8,9},{9,8},{10,11... | collective-permute-start | bytes 1572872 | tf_op jit(solution)/shard_map/ppermute | solution.py:423
  44.9 10.7 %collective-permute-start.6 = (bf16[96,512]{1,0:T(8,128)(2,1)S(1)}, bf16[96,512]{1,0:T(8,128)(2,1)S(1)}, u32[]{:S(2)}, u32[]{:S(2)}) collective-permute-start(bf16[96,512]{1,0:T(8,128)(2,1)S(1)} %get-tuple-element.63), channel_id=1, source_target_pairs={{0,8},{1,9},{2,10},{3,11},{4,12},{5,13},{6,14},{7,15},{8,0},{9,1},... | collective-permute-start | bytes 294920 | tf_op jit(solution)/shard_map/ppermute | solution.py:423
  47.4 8.1 %collective-permute-start.7 = (bf16[96,512]{1,0:T(8,128)(2,1)S(1)}, bf16[96,512]{1,0:T(8,128)(2,1)S(1)}, u32[]{:S(2)}, u32[]{:S(2)}) collective-permute-start(bf16[96,512]{1,0:T(8,128)(2,1)S(1)} %get-tuple-element.64), channel_id=1, source_target_pairs={{0,12},{1,13},{2,14},{3,15},{4,8},{5,9},{6,10},{7,11},{8,4},{9,5},... | collective-permute-start | bytes 294920 | tf_op jit(solution)/shard_map/ppermute | solution.py:423
  47.5 16.8 %collective-permute-start.8 = (bf16[112,512]{1,0:T(8,128)(2,1)S(1)}, bf16[112,512]{1,0:T(8,128)(2,1)S(1)}, u32[]{:S(2)}, u32[]{:S(2)}) collective-permute-start(bf16[112,512]{1,0:T(8,128)(2,1)S(1)} %get-tuple-element.65), channel_id=1, source_target_pairs={{0,2},{1,3},{2,0},{3,1},{4,6},{5,7},{6,4},{7,5},{8,10},{9,11},{10,... | collective-permute-start | bytes 344072 | tf_op jit(solution)/shard_map/ppermute | solution.py:423
  48.0 10.8 %collective-permute-start.9 = (bf16[96,512]{1,0:T(8,128)(2,1)S(1)}, bf16[96,512]{1,0:T(8,128)(2,1)S(1)}, u32[]{:S(2)}, u32[]{:S(2)}) collective-permute-start(bf16[96,512]{1,0:T(8,128)(2,1)S(1)} %get-tuple-element.66), channel_id=1, source_target_pairs={{0,6},{1,7},{2,4},{3,5},{4,2},{5,3},{6,0},{7,1},{8,14},{9,15},{10,... | collective-permute-start | bytes 294920 | tf_op jit(solution)/shard_map/ppermute | solution.py:423
  55.5 8.7 %collective-permute-start.10 = (bf16[96,512]{1,0:T(8,128)(2,1)S(1)}, bf16[96,512]{1,0:T(8,128)(2,1)S(1)}, u32[]{:S(2)}, u32[]{:S(2)}) collective-permute-start(bf16[96,512]{1,0:T(8,128)(2,1)S(1)} %get-tuple-element.67), channel_id=1, source_target_pairs={{0,10},{1,11},{2,8},{3,9},{4,14},{5,15},{6,12},{7,13},{8,2},{9,3},... | collective-permute-start | bytes 294920 | tf_op jit(solution)/shard_map/ppermute | solution.py:423
  55.5 8.7 %collective-permute-start.11 = (bf16[96,512]{1,0:T(8,128)(2,1)S(1)}, bf16[96,512]{1,0:T(8,128)(2,1)S(1)}, u32[]{:S(2)}, u32[]{:S(2)}) collective-permute-start(bf16[96,512]{1,0:T(8,128)(2,1)S(1)} %get-tuple-element.68), channel_id=1, source_target_pairs={{0,14},{1,15},{2,12},{3,13},{4,10},{5,11},{6,8},{7,9},{8,6},{9,7},... | collective-permute-start | bytes 294920 | tf_op jit(solution)/shard_map/ppermute | solution.py:423
  64.4 10.9 %collective-permute-start.14 = (bf16[96,512]{1,0:T(8,128)(2,1)S(1)}, bf16[96,512]{1,0:T(8,128)(2,1)S(1)}, u32[]{:S(2)}, u32[]{:S(2)}) collective-permute-start(bf16[96,512]{1,0:T(8,128)(2,1)S(1)} %get-tuple-element.69.dep_ref.refs_2_.refs_3_), channel_id=1, source_target_pairs={{0,12},{1,13},{2,14},{3,15},{4,8},{5,9},{6,10},{7,11},{8,4},{9,5},... | collective-permute-start | bytes 294920 | tf_op jit(solution)/shard_map/ppermute | solution.py:423
  66.5 8.8 %collective-permute-start.13 = (bf16[96,512]{1,0:T(8,128)(2,1)S(1)}, bf16[96,512]{1,0:T(8,128)(2,1)S(1)}, u32[]{:S(2)}, u32[]{:S(2)}) collective-permute-start(bf16[96,512]{1,0:T(8,128)(2,1)S(1)} %get-tuple-element.69.dep_ref.refs_2_.refs_3_), channel_id=1, source_target_pairs={{0,8},{1,9},{2,10},{3,11},{4,12},{5,13},{6,14},{7,15},{8,0},{9,1},... | collective-permute-start | bytes 294920 | tf_op jit(solution)/shard_map/ppermute | solution.py:423
  67.6 7.7 %collective-permute-start.12 = (bf16[96,512]{1,0:T(8,128)(2,1)S(1)}, bf16[96,512]{1,0:T(8,128)(2,1)S(1)}, u32[]{:S(2)}, u32[]{:S(2)}) collective-permute-start(bf16[96,512]{1,0:T(8,128)(2,1)S(1)} %get-tuple-element.69.dep_ref.refs_2_.refs_3_), channel_id=1, source_target_pairs={{0,4},{1,5},{2,6},{3,7},{4,0},{5,1},{6,2},{7,3},{8,12},{9,13},{10,... | collective-permute-start | bytes 294920 | tf_op jit(solution)/shard_map/ppermute | solution.py:423
  77.7 12.8 %collective-permute-start.22 = (bf16[2,2064,128]{2,1,0:T(8,128)(2,1)S(1)}, bf16[2,2064,128]{2,1,0:T(8,128)(2,1)S(1)}, u32[]{:S(2)}, u32[]{:S(2)}) collective-permute-start(bf16[2,2064,128]{2,1,0:T(8,128)(2,1)S(1)} %get-tuple-element.83), channel_id=1, source_target_pairs={{0,1},{1,0},{2,3},{3,2},{4,5},{5,4},{6,7},{7,6},{8,9},{9,8},{10,11... | collective-permute-start | bytes 3170312 | tf_op jit(solution)/shard_map/ppermute | solution.py:423
  77.8 10.9 %collective-permute-start.16 = (bf16[112,512]{1,0:T(8,128)(2,1)S(1)}, bf16[112,512]{1,0:T(8,128)(2,1)S(1)}, u32[]{:S(2)}, u32[]{:S(2)}) collective-permute-start(bf16[112,512]{1,0:T(8,128)(2,1)S(1)} %get-tuple-element.77), channel_id=1, source_target_pairs={{0,4},{1,5},{2,6},{3,7},{4,0},{5,1},{6,2},{7,3},{8,12},{9,13},{10,... | collective-permute-start | bytes 344072 | tf_op jit(solution)/shard_map/ppermute | solution.py:423
  78.6 11.9 %collective-permute-start.17 = (bf16[112,512]{1,0:T(8,128)(2,1)S(1)}, bf16[112,512]{1,0:T(8,128)(2,1)S(1)}, u32[]{:S(2)}, u32[]{:S(2)}) collective-permute-start(bf16[112,512]{1,0:T(8,128)(2,1)S(1)} %get-tuple-element.78), channel_id=1, source_target_pairs={{0,8},{1,9},{2,10},{3,11},{4,12},{5,13},{6,14},{7,15},{8,0},{9,1},... | collective-permute-start | bytes 344072 | tf_op jit(solution)/shard_map/ppermute | solution.py:423
  80.5 10.0 %collective-permute-start.18 = (bf16[112,512]{1,0:T(8,128)(2,1)S(1)}, bf16[112,512]{1,0:T(8,128)(2,1)S(1)}, u32[]{:S(2)}, u32[]{:S(2)}) collective-permute-start(bf16[112,512]{1,0:T(8,128)(2,1)S(1)} %get-tuple-element.72.dep_ref), channel_id=1, source_target_pairs={{0,12},{1,13},{2,14},{3,15},{4,8},{5,9},{6,10},{7,11},{8,4},{9,5},... | collective-permute-start | bytes 344072 | tf_op jit(solution)/shard_map/ppermute | solution.py:423
  90.8 13.4 %collective-permute-start.23 = (bf16[2064,128]{1,0:T(8,128)(2,1)S(1)}, bf16[2064,128]{1,0:T(8,128)(2,1)S(1)}, u32[]{:S(2)}, u32[]{:S(2)}) collective-permute-start(bf16[2064,128]{1,0:T(8,128)(2,1)S(1)} %get-tuple-element.84), channel_id=1, source_target_pairs={{0,2},{1,3},{2,0},{3,1},{4,6},{5,7},{6,4},{7,5},{8,10},{9,11},{10,... | collective-permute-start | bytes 1585160 | tf_op jit(solution)/shard_map/ppermute | solution.py:423
  93.1 7.5 %collective-permute-start.21 = (bf16[96,512]{1,0:T(8,128)(2,1)S(1)}, bf16[96,512]{1,0:T(8,128)(2,1)S(1)}, u32[]{:S(2)}, u32[]{:S(2)}) collective-permute-start(bf16[96,512]{1,0:T(8,128)(2,1)S(1)} %get-tuple-element.80.refs_3_.refs_0_), channel_id=1, source_target_pairs={{0,12},{1,13},{2,14},{3,15},{4,8},{5,9},{6,10},{7,11},{8,4},{9,5},... | collective-permute-start | bytes 294920 | tf_op jit(solution)/shard_map/ppermute | solution.py:423
  94.6 9.6 %collective-permute-start.20 = (bf16[96,512]{1,0:T(8,128)(2,1)S(1)}, bf16[96,512]{1,0:T(8,128)(2,1)S(1)}, u32[]{:S(2)}, u32[]{:S(2)}) collective-permute-start(bf16[96,512]{1,0:T(8,128)(2,1)S(1)} %get-tuple-element.80.refs_3_.refs_0_), channel_id=1, source_target_pairs={{0,8},{1,9},{2,10},{3,11},{4,12},{5,13},{6,14},{7,15},{8,0},{9,1},... | collective-permute-start | bytes 294920 | tf_op jit(solution)/shard_map/ppermute | solution.py:423
  96.8 7.4 %collective-permute-start.19 = (bf16[96,512]{1,0:T(8,128)(2,1)S(1)}, bf16[96,512]{1,0:T(8,128)(2,1)S(1)}, u32[]{:S(2)}, u32[]{:S(2)}) collective-permute-start(bf16[96,512]{1,0:T(8,128)(2,1)S(1)} %get-tuple-element.80.refs_3_.refs_0_), channel_id=1, source_target_pairs={{0,4},{1,5},{2,6},{3,7},{4,0},{5,1},{6,2},{7,3},{8,12},{9,13},{10,... | collective-permute-start | bytes 294920 | tf_op jit(solution)/shard_map/ppermute | solution.py:423
  104.3 10.6 %collective-permute-start.25 = (bf16[400,512]{1,0:T(8,128)(2,1)S(1)}, bf16[400,512]{1,0:T(8,128)(2,1)S(1)}, u32[]{:S(2)}, u32[]{:S(2)}) collective-permute-start(bf16[400,512]{1,0:T(8,128)(2,1)S(1)} %stack_parts.1.refs_0_.refs_2_), channel_id=1, source_target_pairs={{0,2},{1,3},{2,0},{3,1},{4,6},{5,7},{6,4},{7,5},{8,10},{9,11},{10,... | collective-permute-start | bytes 1228808 | tf_op jit(solution)/shard_map/ppermute | solution.py:423
  105.7 10.1 %collective-permute-start.24 = (bf16[400,512]{1,0:T(8,128)(2,1)S(1)}, bf16[400,512]{1,0:T(8,128)(2,1)S(1)}, u32[]{:S(2)}, u32[]{:S(2)}) collective-permute-start(bf16[400,512]{1,0:T(8,128)(2,1)S(1)} %stack_parts.1.refs_0_.refs_2_), channel_id=1, source_target_pairs={{0,1},{1,0},{2,3},{3,2},{4,5},{5,4},{6,7},{7,6},{8,9},{9,8},{10,11... | collective-permute-start | bytes 1228808 | tf_op jit(solution)/shard_map/ppermute | solution.py:423
  (8 other events, 56.6 us)

commit v13 on v12

--- a/solution.py
+++ b/solution.py
@@ -437,7 +437,7 @@
     size = (total - cells) // 2
     count = cells // size
 
-    tile = min(width, 256)
+    tile = width
 
     def spec(k):
         return pl.BlockSpec((size, tile), lambda n: (1 + k, n))
@@ -511,10 +511,11 @@
 
 
 def other_places(parts):
-    return [(side, part) for side in range(2) for part in range(parts) if side or part]
-
-
-def add_core_kernel(place_ref, head_ref, mine_ref, other_ref, own_ref, heads_ref, *send_refs):
+    return [(side, part) for part in reversed(range(parts)) for side in range(2) if side or part]
+
+
+def add_core_kernel(dep_count, place_ref, head_ref, mine_ref, other_ref, *refs):
+    own_ref, heads_ref, *send_refs = refs[dep_count:]
     side, part = place_ref[1], place_ref[2]
     block = mine_ref.shape[2]
     units = head_ref.shape[1]
@@ -534,19 +535,19 @@
             out[pl.ds(block, EXTRA), :] = jnp.concatenate(pieces, axis=0)
 
 
-def add_core(place, head, mine, other):
+def add_core(place, head, mine, other, deps):
     parts, block, width = mine.shape[1:]
     sends = [
         jax.ShapeDtypeStruct((block if by_part else block + EXTRA, width), bf16) for _, by_part in other_places(parts)
     ]
     return pl.pallas_call(
-        add_core_kernel,
-        in_specs=[smem(), vmem(), vmem(), vmem()],
+        functools.partial(add_core_kernel, len(deps)),
+        in_specs=[smem(), vmem(), vmem(), vmem()] + any_specs(deps),
         out_shape=[jax.ShapeDtypeStruct((block, width), f32), jax.ShapeDtypeStruct((2, head.shape[1]), f32)] + sends,
         compiler_params=params(),
         cost_estimate=pl.CostEstimate(flops=1, bytes_accessed=1, transcendentals=0),
         name="add_core",
-    )(place, head, mine, other)
+    )(place, head, mine, other, *deps)
 
 
 def activate_kernel(own_ref, heads_ref, *refs):
@@ -858,7 +859,7 @@
     def density_turn(turn, dep, so_far):
         return density_steps(drift, shifts, band, own_rows, below, above, dep, so_far, turn, 2)
 
-    own, heads, *sends = add_core(place, head, keep, swap(send, count, 1))
+    own, heads, *sends = add_core(place, head, keep, swap(send, count, 1), [mids[3]])
     flips = [2 * by_side + 4 * by_part for by_side, by_part in other_places(parts)]
     received = [swap(piece, count, flip) for piece, flip in zip(sends, flips)]
     first, head = activate(own, heads, received)

time: 129 us -> 130 us (level)
  starting transfers between devices: 37.2 us -> 45.3 us
  waiting for transfers between devices: 30.7 us -> 24.6 us
  Pallas kernels: 60 us -> 58.2 us
    ppermute x25, starting transfers between devices: 33.8 us -> 41.9 us  [swap(): return lax.ppermute(values, 'grid', [(i, i ^ flip) for i in range(count)])]
    ppermute x25, waiting for transfers between devices: 30.7 us -> 24.6 us  [swap(): return lax.ppermute(values, 'grid', [(i, i ^ flip) for i in range(count)])]
    pallas_call x1, Pallas kernels: 9.91 us -> 8.17 us  [inner_product(): pl.pallas_call(functools.partial(inner_product_kernel, count, width // ti...]
  transfers between devices with their start and end apart: 27 -> 27, of which waited for: 9 -> 10; matrix products, arithmetic and copies ran while one was open for 0% -> 0% of each run, Pallas kernels for 29% -> 27%
where the time goes in v13:
time: 130 us; the launch traced here: 129 us
  Pallas kernels  58.2 us (45%)
  starting transfers between devices  45.3 us (35%)
  waiting for transfers between devices  24.6 us (19%)
    ppermute x25, starting transfers between devices, swap(): return lax.ppermute(values, 'grid', [(i, i ^ flip) for i in range(count)])  41.9 us
    ppermute x25, waiting for transfers between devices, swap(): return lax.ppermute(values, 'grid', [(i, i ^ flip) for i in range(count)])  24.6 us
    pallas_call x2, Pallas kernels, density_steps(): pl.pallas_call(density_kernel, grid=(steps,), in_specs=in_specs, out_spec...  12.8 us
    pallas_call x1, Pallas kernels, first_grad(): pl.pallas_call(functools.partial(first_grad_kernel, parts, block, tiles),...  12.2 us
    pallas_call x1, Pallas kernels, inner_steps(): pl.pallas_call(functools.partial(inner_kernel, rows, size), grid=(scenari...  11.5 us
    pallas_call x1, Pallas kernels, inner_product(): pl.pallas_call(functools.partial(inner_product_kernel, count, width // ti...  8.17 us
    pallas_call x1, Pallas kernels, edge_product(): pl.pallas_call(functools.partial(edge_product_kernel, block, inner is not...  4.44 us
    pallas_call x1, Pallas kernels, edge_steps(): pl.pallas_call(edge_kernel, grid=(scenarios // size,), in_specs=density_s...  3.63 us
  transfers between devices with their start and end apart: 27, of which 10 were waited for; matrix products, arithmetic and copies ran while one was open for 0% of the time, Pallas kernels for 27%

profile of v13, /device:TPU:0, one launch (start us, length us, event | category | flops | bytes accessed | tf_op | source)
XLA Modules:
  0.0 129.1 jit_solution(17474433366283570017)
XLA Ops:
  1.1 2.6 %collective-permute-start.3 = (bf16[2048,128]{1,0:T(8,128)(2,1)}, bf16[2048,128]{1,0:T(8,128)(2,1)S(1)}, u32[]{:S(2)}, u32[]{:S(2)}) collective-permute-start(bf16[2048,128]{1,0:T(8,128)(2,1)} %refs_6_.1), channel_id=1, source_target_pairs={{0,2},{1,3},{2,0},{3,1},{4,6},{5,7},{6,4},{7,5},{8,10},{9,11},{10,... | collective-permute-start | bytes 1572872 | tf_op jit(solution)/shard_map/ppermute | solution.py:423
  3.8 11.5 %inner_density_steps.1 = (s32[4]{0:T(128)S(1)}, bf16[400,512]{1,0:T(8,128)(2,1)S(1)}, bf16[400,512]{1,0:T(8,128)(2,1)S(1)}, f32[4,384,128]{2,1,0:T(8,128)}, bf16...) custom-call(s32[4]{0:T(128)S(1)} %pad_add_fusion.place_ref, ...), custom_call_target="tpu_custom_call" | custom-call | flops 1 | bytes 1 | tf_op jit(solution)/shard_map/inner_density_steps/pallas_call | solution.py:239
  15.4 2.1 %collective-permute-start = (bf16[400,512]{1,0:T(8,128)(2,1)S(1)}, bf16[400,512]{1,0:T(8,128)(2,1)S(1)}, u32[]{:S(2)}, u32[]{:S(2)}) collective-permute-start(bf16[400,512]{1,0:T(8,128)(2,1)S(1)} %get-tuple-element.51), channel_id=1, source_target_pairs={{0,1},{1,2},{2,3},{3,4},{4,5},{5,6},{6,7},{7,8},{8,9},{9,10},{10,1... | collective-permute-start | bytes 1228808 | tf_op jit(solution)/shard_map/ppermute | solution.py:850
  18.8 8.2 %inner_product.1.dep_ref.refs_0_ = f32[4,384,512]{2,1,0:T(8,128)S(1)} custom-call(bf16[384,3072]{1,0:T(8,128)(2,1)S(1)} %get-tuple-element.55.inputs_ref.refs_1_, bf16[4096,2048]{1,0:T(8,128)(2,1)} %bottom_ref.1, bf16[4096,2048]{1,0:T(8,128)(2,1)} %bottom_ref.1, bf16[4096,2048]{1,0:T(8,128)(2,1)} %bottom_ref.1, bf16[4096,2048]{1,0:T(8,128)(2,1)} %bottom_ref.1, ...), custom_call_target="tpu_custom_call" | custom-call | flops 1 | bytes 1 | tf_op jit(solution)/shard_map/inner_product/pallas_call | solution.py:445
  27.1 3.6 %edge_density_steps.1 = (bf16[384,512]{1,0:T(8,128)(2,1)S(1)}, bf16[384,512]{1,0:T(8,128)(2,1)S(1)}) custom-call(f32[2,16,256]{2,1,0:T(8,128)S(1)} %copy-done.2, f32[4,384,128]{2,1,0:T(8,128)S(1)} %copy-done.1, bf16[512,256]{1,0:T(8,128)(2,1)S(1)} %get-tuple-element.49.band_ref, bf16[384,4096]{1,0:T(8,128)(2,1)S(1)} %copy-done, ...), custom_call_target="tpu_custom_call" | custom-call | flops 1 | bytes 1 | tf_op jit(solution)/shard_map/edge_density_steps/pallas_call | solution.py:370
  30.7 4.4 %edge_product.1 = (f32[2,4,96,512]{3,2,1,0:T(8,128)S(1)}, bf16[2,4,112,512]{3,2,1,0:T(8,128)(2,1)S(1)}) custom-call(s32[4]{0:T(128)S(1)} %get-tuple-element.53.place_ref.refs_0_, f32[1,128]{1,0:T(1,128)S(1)} %bitcast.18, bf16[384,512]{1,0:T(8,128)(2,1)S(1)} %get-tuple-element.56.low_ref.refs_0_, bf16[384,512]{1,0:T(8,128)(2,1)S(1)} %get-tuple-element.57.high_ref.refs_2_, ...), custom_call_target="tpu_custom_call" | custom-call | flops 1 | bytes 1 | tf_op jit(solution)/shard_map/edge_product/pallas_call | solution.py:493
  36.4 2.8 %collective-permute-done.5.refs_0_.refs_9_.refs_13_ = bf16[2048,128]{1,0:T(8,128)(2,1)S(1)} collective-permute-done((bf16[2048,128]{1,0:T(8,128)(2,1)S(1)}, bf16[2048,128]{1,0:T(8,128)(2,1)S(1)}, u32[]{:S(2)}, u32[]{:S(2)}) %collective-permute-start.5) | collective-permute-done | bytes 524320 | tf_op jit(solution)/shard_map/ppermute | solution.py:423
  39.9 6.0 %collective-permute-start.6 = (bf16[96,512]{1,0:T(8,128)(2,1)S(1)}, bf16[96,512]{1,0:T(8,128)(2,1)S(1)}, u32[]{:S(2)}, u32[]{:S(2)}) collective-permute-start(bf16[96,512]{1,0:T(8,128)(2,1)S(1)} %get-tuple-element.62), channel_id=1, source_target_pairs={{0,12},{1,13},{2,14},{3,15},{4,8},{5,9},{6,10},{7,11},{8,4},{9,5},... | collective-permute-start | bytes 294920 | tf_op jit(solution)/shard_map/ppermute | solution.py:423
  48.4 1.9 %collective-permute-start.9 = (bf16[96,512]{1,0:T(8,128)(2,1)S(1)}, bf16[96,512]{1,0:T(8,128)(2,1)S(1)}, u32[]{:S(2)}, u32[]{:S(2)}) collective-permute-start(bf16[96,512]{1,0:T(8,128)(2,1)S(1)} %get-tuple-element.65), channel_id=1, source_target_pairs={{0,10},{1,11},{2,8},{3,9},{4,14},{5,15},{6,12},{7,13},{8,2},{9,3},... | collective-permute-start | bytes 294920 | tf_op jit(solution)/shard_map/ppermute | solution.py:423
  50.3 7.6 %collective-permute-start.10 = (bf16[96,512]{1,0:T(8,128)(2,1)S(1)}, bf16[96,512]{1,0:T(8,128)(2,1)S(1)}, u32[]{:S(2)}, u32[]{:S(2)}) collective-permute-start(bf16[96,512]{1,0:T(8,128)(2,1)S(1)} %get-tuple-element.66), channel_id=1, source_target_pairs={{0,4},{1,5},{2,6},{3,7},{4,0},{5,1},{6,2},{7,3},{8,12},{9,13},{10,... | collective-permute-start | bytes 294920 | tf_op jit(solution)/shard_map/ppermute | solution.py:423
  57.9 3.0 %collective-permute-start.11 = (bf16[96,512]{1,0:T(8,128)(2,1)S(1)}, bf16[96,512]{1,0:T(8,128)(2,1)S(1)}, u32[]{:S(2)}, u32[]{:S(2)}) collective-permute-start(bf16[96,512]{1,0:T(8,128)(2,1)S(1)} %get-tuple-element.67), channel_id=1, source_target_pairs={{0,6},{1,7},{2,4},{3,5},{4,2},{5,3},{6,0},{7,1},{8,14},{9,15},{10,... | collective-permute-start | bytes 294920 | tf_op jit(solution)/shard_map/ppermute | solution.py:423
  62.8 2.2 %collective-permute-done.10.refs_4_ = bf16[96,512]{1,0:T(8,128)(2,1)S(1)} collective-permute-done((bf16[96,512]{1,0:T(8,128)(2,1)S(1)}, bf16[96,512]{1,0:T(8,128)(2,1)S(1)}, u32[]{:S(2)}, u32[]{:S(2)}) %collective-permute-start.10) | collective-permute-done | bytes 98336 | tf_op jit(solution)/shard_map/ppermute | solution.py:423
  65.5 3.1 %collective-permute-start.15 = (bf16[96,512]{1,0:T(8,128)(2,1)S(1)}, bf16[96,512]{1,0:T(8,128)(2,1)S(1)}, u32[]{:S(2)}, u32[]{:S(2)}) collective-permute-start(bf16[96,512]{1,0:T(8,128)(2,1)S(1)} %get-tuple-element.69.dep_ref.refs_2_.refs_3_), channel_id=1, source_target_pairs={{0,12},{1,13},{2,14},{3,15},{4,8},{5,9},{6,10},{7,11},{8,4},{9,5},... | collective-permute-start | bytes 294920 | tf_op jit(solution)/shard_map/ppermute | solution.py:423
  69.9 6.4 %density_steps.2 = (f32[12288,128]{1,0:T(8,128)}, f32[8,128]{1,0:T(8,128)S(1)}) custom-call(f32[2,16,256]{2,1,0:T(8,128)S(1)} %copy-done.2, f32[4,384,128]{2,1,0:T(8,128)S(1)} %copy-done.1, bf16[512,256]{1,0:T(8,128)(2,1)S(1)} %get-tuple-element.49.band_ref, bf16[384,4096]{1,0:T(8,128)(2,1)S(1)} %copy-done, ...), custom_call_target="tpu_custom_call" | custom-call | flops 1 | bytes 1 | tf_op jit(solution)/shard_map/density_steps/pallas_call | solution.py:397
  76.4 2.4 %value_layers.1 = (f32[96,512]{1,0:T(8,128)S(1)}, f32[1,512]{1,0:T(1,128)S(1)}, bf16[2,2064,128]{2,1,0:T(8,128)(2,1)S(1)}, bf16[2,2064,128]{2,1,0:T(8,128)(2,1)S...) custom-call(s32[4]{0:T(128)S(1)} %get-tuple-element.53.place_ref.refs_0_, ...), custom_call_target="tpu_custom_call" | custom-call | flops 1 | bytes 1 | tf_op jit(solution)/shard_map/value_layers/pallas_call | solution.py:654
  79.5 2.9 %collective-permute-start.17 = (bf16[112,512]{1,0:T(8,128)(2,1)S(1)}, bf16[112,512]{1,0:T(8,128)(2,1)S(1)}, u32[]{:S(2)}, u32[]{:S(2)}) collective-permute-start(bf16[112,512]{1,0:T(8,128)(2,1)S(1)} %get-tuple-element.78), channel_id=1, source_target_pairs={{0,8},{1,9},{2,10},{3,11},{4,12},{5,13},{6,14},{7,15},{8,0},{9,1},... | collective-permute-start | bytes 344072 | tf_op jit(solution)/shard_map/ppermute | solution.py:423
  83.3 6.4 %density_steps.3 = (f32[12288,128]{1,0:T(8,128)}, f32[8,128]{1,0:T(8,128)S(1)}) custom-call(f32[2,16,256]{2,1,0:T(8,128)S(1)} %copy-done.2, f32[4,384,128]{2,1,0:T(8,128)S(1)} %copy-done.1, bf16[512,256]{1,0:T(8,128)(2,1)S(1)} %get-tuple-element.49.band_ref, bf16[384,4096]{1,0:T(8,128)(2,1)S(1)} %copy-done, ...), custom_call_target="tpu_custom_call", output_to_operand_aliasing={{0}: (9, {})} | custom-call | flops 1 | bytes 1 | tf_op jit(solution)/shard_map/density_steps/pallas_call | solution.py:397
  89.7 1.7 %collective-permute-done.17.refs_1_ = bf16[112,512]{1,0:T(8,128)(2,1)S(1)} collective-permute-done((bf16[112,512]{1,0:T(8,128)(2,1)S(1)}, bf16[112,512]{1,0:T(8,128)(2,1)S(1)}, u32[]{:S(2)}, u32[]{:S(2)}) %collective-permute-start.17) | collective-permute-done | bytes 114720 | tf_op jit(solution)/shard_map/ppermute | solution.py:423
  91.7 1.7 %collective-permute-start.23 = (bf16[2064,128]{1,0:T(8,128)(2,1)S(1)}, bf16[2064,128]{1,0:T(8,128)(2,1)S(1)}, u32[]{:S(2)}, u32[]{:S(2)}) collective-permute-start(bf16[2064,128]{1,0:T(8,128)(2,1)S(1)} %get-tuple-element.84), channel_id=1, source_target_pairs={{0,2},{1,3},{2,0},{3,1},{4,6},{5,7},{6,4},{7,5},{8,10},{9,11},{10,... | collective-permute-start | bytes 1585160 | tf_op jit(solution)/shard_map/ppermute | solution.py:423
  93.4 2.4 %collective-permute-start.21 = (bf16[96,512]{1,0:T(8,128)(2,1)S(1)}, bf16[96,512]{1,0:T(8,128)(2,1)S(1)}, u32[]{:S(2)}, u32[]{:S(2)}) collective-permute-start(bf16[96,512]{1,0:T(8,128)(2,1)S(1)} %get-tuple-element.80.refs_3_.refs_0_), channel_id=1, source_target_pairs={{0,12},{1,13},{2,14},{3,15},{4,8},{5,9},{6,10},{7,11},{8,4},{9,5},... | collective-permute-start | bytes 294920 | tf_op jit(solution)/shard_map/ppermute | solution.py:423
  98.7 1.8 %collective-permute-done.21.refs_3_ = bf16[96,512]{1,0:T(8,128)(2,1)S(1)} collective-permute-done((bf16[96,512]{1,0:T(8,128)(2,1)S(1)}, bf16[96,512]{1,0:T(8,128)(2,1)S(1)}, u32[]{:S(2)}, u32[]{:S(2)}) %collective-permute-start.21) | collective-permute-done | bytes 98336 | tf_op jit(solution)/shard_map/ppermute | solution.py:423
  100.5 4.6 %collective-permute-done.20.refs_2_ = bf16[96,512]{1,0:T(8,128)(2,1)S(1)} collective-permute-done((bf16[96,512]{1,0:T(8,128)(2,1)S(1)}, bf16[96,512]{1,0:T(8,128)(2,1)S(1)}, u32[]{:S(2)}, u32[]{:S(2)}) %collective-permute-start.20) | collective-permute-done | bytes 98336 | tf_op jit(solution)/shard_map/ppermute | solution.py:423
  106.5 8.6 %collective-permute-done.25.refs_4_ = bf16[400,512]{1,0:T(8,128)(2,1)S(1)} collective-permute-done((bf16[400,512]{1,0:T(8,128)(2,1)S(1)}, bf16[400,512]{1,0:T(8,128)(2,1)S(1)}, u32[]{:S(2)}, u32[]{:S(2)}) %collective-permute-start.25) | collective-permute-done | bytes 409632 | tf_op jit(solution)/shard_map/ppermute | solution.py:423
  116.8 12.2 %first_gradient.1 = (bf16[4096,2048]{1,0:T(8,128)(2,1)}, f32[384]{0:T(512)}) custom-call(s32[4]{0:T(128)S(1)} %get-tuple-element.53.place_ref.refs_0_, bf16[4096,384]{1,0:T(8,128)(2,1)S(1)} %transposed_inputs.1.refs_5_.refs_1_, bf16[400,512]{1,0:T(8,128)(2,1)S(1)} %stack_parts.1.refs_0_.refs_2_, bf16[400,512]{1,0:T(8,128)(2,1)S(1)} %collective-permute-done.24.refs_3_, ...), custom_call_target="tpu_custom_call" | custom-call | flops 1 | bytes 1 | tf_op jit(solution)/shard_map/first_gradient/pallas_call | solution.py:815
  (56 shorter events, 18.1 us)
Async XLA Ops:
  0.6 18.1 %collective-permute-start.2 = (bf16[2048,128]{1,0:T(8,128)(2,1)}, bf16[2048,128]{1,0:T(8,128)(2,1)S(1)}, u32[]{:S(2)}, u32[]{:S(2)}) collective-permute-start(bf16[2048,128]{1,0:T(8,128)(2,1)} %refs_6_.1), channel_id=1, source_target_pairs={{0,1},{1,0},{2,3},{3,2},{4,5},{5,4},{6,7},{7,6},{8,9},{9,8},{10,11... | collective-permute-start | bytes 1572872 | tf_op jit(solution)/shard_map/ppermute | solution.py:423
  1.1 17.6 %collective-permute-start.3 = (bf16[2048,128]{1,0:T(8,128)(2,1)}, bf16[2048,128]{1,0:T(8,128)(2,1)S(1)}, u32[]{:S(2)}, u32[]{:S(2)}) collective-permute-start(bf16[2048,128]{1,0:T(8,128)(2,1)} %refs_6_.1), channel_id=1, source_target_pairs={{0,2},{1,3},{2,0},{3,1},{4,6},{5,7},{6,4},{7,5},{8,10},{9,11},{10,... | collective-permute-start | bytes 1572872 | tf_op jit(solution)/shard_map/ppermute | solution.py:423
  15.4 11.6 %collective-permute-start = (bf16[400,512]{1,0:T(8,128)(2,1)S(1)}, bf16[400,512]{1,0:T(8,128)(2,1)S(1)}, u32[]{:S(2)}, u32[]{:S(2)}) collective-permute-start(bf16[400,512]{1,0:T(8,128)(2,1)S(1)} %get-tuple-element.51), channel_id=1, source_target_pairs={{0,1},{1,2},{2,3},{3,4},{4,5},{5,6},{6,7},{7,8},{8,9},{9,10},{10,1... | collective-permute-start | bytes 1228808 | tf_op jit(solution)/shard_map/ppermute | solution.py:850
  17.5 9.5 %collective-permute-start.1 = (bf16[400,512]{1,0:T(8,128)(2,1)S(1)}, bf16[400,512]{1,0:T(8,128)(2,1)S(1)}, u32[]{:S(2)}, u32[]{:S(2)}) collective-permute-start(bf16[400,512]{1,0:T(8,128)(2,1)S(1)} %get-tuple-element.52), channel_id=1, source_target_pairs={{1,0},{2,1},{3,2},{4,3},{5,4},{6,5},{7,6},{8,7},{9,8},{10,9},{11,1... | collective-permute-start | bytes 1228808 | tf_op jit(solution)/shard_map/ppermute | solution.py:851
  39.9 10.4 %collective-permute-start.6 = (bf16[96,512]{1,0:T(8,128)(2,1)S(1)}, bf16[96,512]{1,0:T(8,128)(2,1)S(1)}, u32[]{:S(2)}, u32[]{:S(2)}) collective-permute-start(bf16[96,512]{1,0:T(8,128)(2,1)S(1)} %get-tuple-element.62), channel_id=1, source_target_pairs={{0,12},{1,13},{2,14},{3,15},{4,8},{5,9},{6,10},{7,11},{8,4},{9,5},... | collective-permute-start | bytes 294920 | tf_op jit(solution)/shard_map/ppermute | solution.py:423
  45.9 12.0 %collective-permute-start.7 = (bf16[96,512]{1,0:T(8,128)(2,1)S(1)}, bf16[96,512]{1,0:T(8,128)(2,1)S(1)}, u32[]{:S(2)}, u32[]{:S(2)}) collective-permute-start(bf16[96,512]{1,0:T(8,128)(2,1)S(1)} %get-tuple-element.63), channel_id=1, source_target_pairs={{0,14},{1,15},{2,12},{3,13},{4,10},{5,11},{6,8},{7,9},{8,6},{9,7},... | collective-permute-start | bytes 294920 | tf_op jit(solution)/shard_map/ppermute | solution.py:423
  45.9 19.4 %collective-permute-start.12 = (bf16[112,512]{1,0:T(8,128)(2,1)S(1)}, bf16[112,512]{1,0:T(8,128)(2,1)S(1)}, u32[]{:S(2)}, u32[]{:S(2)}) collective-permute-start(bf16[112,512]{1,0:T(8,128)(2,1)S(1)} %get-tuple-element.68), channel_id=1, source_target_pairs={{0,2},{1,3},{2,0},{3,1},{4,6},{5,7},{6,4},{7,5},{8,10},{9,11},{10,... | collective-permute-start | bytes 344072 | tf_op jit(solution)/shard_map/ppermute | solution.py:423
  47.4 14.2 %collective-permute-start.8 = (bf16[96,512]{1,0:T(8,128)(2,1)S(1)}, bf16[96,512]{1,0:T(8,128)(2,1)S(1)}, u32[]{:S(2)}, u32[]{:S(2)}) collective-permute-start(bf16[96,512]{1,0:T(8,128)(2,1)S(1)} %get-tuple-element.64), channel_id=1, source_target_pairs={{0,8},{1,9},{2,10},{3,11},{4,12},{5,13},{6,14},{7,15},{8,0},{9,1},... | collective-permute-start | bytes 294920 | tf_op jit(solution)/shard_map/ppermute | solution.py:423
  48.4 14.4 %collective-permute-start.9 = (bf16[96,512]{1,0:T(8,128)(2,1)S(1)}, bf16[96,512]{1,0:T(8,128)(2,1)S(1)}, u32[]{:S(2)}, u32[]{:S(2)}) collective-permute-start(bf16[96,512]{1,0:T(8,128)(2,1)S(1)} %get-tuple-element.65), channel_id=1, source_target_pairs={{0,10},{1,11},{2,8},{3,9},{4,14},{5,15},{6,12},{7,13},{8,2},{9,3},... | collective-permute-start | bytes 294920 | tf_op jit(solution)/shard_map/ppermute | solution.py:423
  50.3 14.7 %collective-permute-start.10 = (bf16[96,512]{1,0:T(8,128)(2,1)S(1)}, bf16[96,512]{1,0:T(8,128)(2,1)S(1)}, u32[]{:S(2)}, u32[]{:S(2)}) collective-permute-start(bf16[96,512]{1,0:T(8,128)(2,1)S(1)} %get-tuple-element.66), channel_id=1, source_target_pairs={{0,4},{1,5},{2,6},{3,7},{4,0},{5,1},{6,2},{7,3},{8,12},{9,13},{10,... | collective-permute-start | bytes 294920 | tf_op jit(solution)/shard_map/ppermute | solution.py:423
  57.9 7.4 %collective-permute-start.11 = (bf16[96,512]{1,0:T(8,128)(2,1)S(1)}, bf16[96,512]{1,0:T(8,128)(2,1)S(1)}, u32[]{:S(2)}, u32[]{:S(2)}) collective-permute-start(bf16[96,512]{1,0:T(8,128)(2,1)S(1)} %get-tuple-element.67), channel_id=1, source_target_pairs={{0,6},{1,7},{2,4},{3,5},{4,2},{5,3},{6,0},{7,1},{8,14},{9,15},{10,... | collective-permute-start | bytes 294920 | tf_op jit(solution)/shard_map/ppermute | solution.py:423
  65.5 10.9 %collective-permute-start.15 = (bf16[96,512]{1,0:T(8,128)(2,1)S(1)}, bf16[96,512]{1,0:T(8,128)(2,1)S(1)}, u32[]{:S(2)}, u32[]{:S(2)}) collective-permute-start(bf16[96,512]{1,0:T(8,128)(2,1)S(1)} %get-tuple-element.69.dep_ref.refs_2_.refs_3_), channel_id=1, source_target_pairs={{0,12},{1,13},{2,14},{3,15},{4,8},{5,9},{6,10},{7,11},{8,4},{9,5},... | collective-permute-start | bytes 294920 | tf_op jit(solution)/shard_map/ppermute | solution.py:423
  68.5 7.8 %collective-permute-start.14 = (bf16[96,512]{1,0:T(8,128)(2,1)S(1)}, bf16[96,512]{1,0:T(8,128)(2,1)S(1)}, u32[]{:S(2)}, u32[]{:S(2)}) collective-permute-start(bf16[96,512]{1,0:T(8,128)(2,1)S(1)} %get-tuple-element.69.dep_ref.refs_2_.refs_3_), channel_id=1, source_target_pairs={{0,8},{1,9},{2,10},{3,11},{4,12},{5,13},{6,14},{7,15},{8,0},{9,1},... | collective-permute-start | bytes 294920 | tf_op jit(solution)/shard_map/ppermute | solution.py:423
  68.5 7.8 %collective-permute-start.13 = (bf16[96,512]{1,0:T(8,128)(2,1)S(1)}, bf16[96,512]{1,0:T(8,128)(2,1)S(1)}, u32[]{:S(2)}, u32[]{:S(2)}) collective-permute-start(bf16[96,512]{1,0:T(8,128)(2,1)S(1)} %get-tuple-element.69.dep_ref.refs_2_.refs_3_), channel_id=1, source_target_pairs={{0,4},{1,5},{2,6},{3,7},{4,0},{5,1},{6,2},{7,3},{8,12},{9,13},{10,... | collective-permute-start | bytes 294920 | tf_op jit(solution)/shard_map/ppermute | solution.py:423
  78.8 12.7 %collective-permute-start.22 = (bf16[2,2064,128]{2,1,0:T(8,128)(2,1)S(1)}, bf16[2,2064,128]{2,1,0:T(8,128)(2,1)S(1)}, u32[]{:S(2)}, u32[]{:S(2)}) collective-permute-start(bf16[2,2064,128]{2,1,0:T(8,128)(2,1)S(1)} %get-tuple-element.83), channel_id=1, source_target_pairs={{0,1},{1,0},{2,3},{3,2},{4,5},{5,4},{6,7},{7,6},{8,9},{9,8},{10,11... | collective-permute-start | bytes 3170312 | tf_op jit(solution)/shard_map/ppermute | solution.py:423
  78.8 10.9 %collective-permute-start.16 = (bf16[112,512]{1,0:T(8,128)(2,1)S(1)}, bf16[112,512]{1,0:T(8,128)(2,1)S(1)}, u32[]{:S(2)}, u32[]{:S(2)}) collective-permute-start(bf16[112,512]{1,0:T(8,128)(2,1)S(1)} %get-tuple-element.77), channel_id=1, source_target_pairs={{0,4},{1,5},{2,6},{3,7},{4,0},{5,1},{6,2},{7,3},{8,12},{9,13},{10,... | collective-permute-start | bytes 344072 | tf_op jit(solution)/shard_map/ppermute | solution.py:423
  79.5 11.8 %collective-permute-start.17 = (bf16[112,512]{1,0:T(8,128)(2,1)S(1)}, bf16[112,512]{1,0:T(8,128)(2,1)S(1)}, u32[]{:S(2)}, u32[]{:S(2)}) collective-permute-start(bf16[112,512]{1,0:T(8,128)(2,1)S(1)} %get-tuple-element.78), channel_id=1, source_target_pairs={{0,8},{1,9},{2,10},{3,11},{4,12},{5,13},{6,14},{7,15},{8,0},{9,1},... | collective-permute-start | bytes 344072 | tf_op jit(solution)/shard_map/ppermute | solution.py:423
  82.5 8.9 %collective-permute-start.18 = (bf16[112,512]{1,0:T(8,128)(2,1)S(1)}, bf16[112,512]{1,0:T(8,128)(2,1)S(1)}, u32[]{:S(2)}, u32[]{:S(2)}) collective-permute-start(bf16[112,512]{1,0:T(8,128)(2,1)S(1)} %get-tuple-element.72.dep_ref), channel_id=1, source_target_pairs={{0,12},{1,13},{2,14},{3,15},{4,8},{5,9},{6,10},{7,11},{8,4},{9,5},... | collective-permute-start | bytes 344072 | tf_op jit(solution)/shard_map/ppermute | solution.py:423
  91.7 13.4 %collective-permute-start.23 = (bf16[2064,128]{1,0:T(8,128)(2,1)S(1)}, bf16[2064,128]{1,0:T(8,128)(2,1)S(1)}, u32[]{:S(2)}, u32[]{:S(2)}) collective-permute-start(bf16[2064,128]{1,0:T(8,128)(2,1)S(1)} %get-tuple-element.84), channel_id=1, source_target_pairs={{0,2},{1,3},{2,0},{3,1},{4,6},{5,7},{6,4},{7,5},{8,10},{9,11},{10,... | collective-permute-start | bytes 1585160 | tf_op jit(solution)/shard_map/ppermute | solution.py:423
  93.4 7.1 %collective-permute-start.21 = (bf16[96,512]{1,0:T(8,128)(2,1)S(1)}, bf16[96,512]{1,0:T(8,128)(2,1)S(1)}, u32[]{:S(2)}, u32[]{:S(2)}) collective-permute-start(bf16[96,512]{1,0:T(8,128)(2,1)S(1)} %get-tuple-element.80.refs_3_.refs_0_), channel_id=1, source_target_pairs={{0,12},{1,13},{2,14},{3,15},{4,8},{5,9},{6,10},{7,11},{8,4},{9,5},... | collective-permute-start | bytes 294920 | tf_op jit(solution)/shard_map/ppermute | solution.py:423
  95.9 9.2 %collective-permute-start.20 = (bf16[96,512]{1,0:T(8,128)(2,1)S(1)}, bf16[96,512]{1,0:T(8,128)(2,1)S(1)}, u32[]{:S(2)}, u32[]{:S(2)}) collective-permute-start(bf16[96,512]{1,0:T(8,128)(2,1)S(1)} %get-tuple-element.80.refs_3_.refs_0_), channel_id=1, source_target_pairs={{0,8},{1,9},{2,10},{3,11},{4,12},{5,13},{6,14},{7,15},{8,0},{9,1},... | collective-permute-start | bytes 294920 | tf_op jit(solution)/shard_map/ppermute | solution.py:423
  97.5 7.6 %collective-permute-start.19 = (bf16[96,512]{1,0:T(8,128)(2,1)S(1)}, bf16[96,512]{1,0:T(8,128)(2,1)S(1)}, u32[]{:S(2)}, u32[]{:S(2)}) collective-permute-start(bf16[96,512]{1,0:T(8,128)(2,1)S(1)} %get-tuple-element.80.refs_3_.refs_0_), channel_id=1, source_target_pairs={{0,4},{1,5},{2,6},{3,7},{4,0},{5,1},{6,2},{7,3},{8,12},{9,13},{10,... | collective-permute-start | bytes 294920 | tf_op jit(solution)/shard_map/ppermute | solution.py:423
  105.1 10.0 %collective-permute-start.25 = (bf16[400,512]{1,0:T(8,128)(2,1)S(1)}, bf16[400,512]{1,0:T(8,128)(2,1)S(1)}, u32[]{:S(2)}, u32[]{:S(2)}) collective-permute-start(bf16[400,512]{1,0:T(8,128)(2,1)S(1)} %stack_parts.1.refs_0_.refs_2_), channel_id=1, source_target_pairs={{0,2},{1,3},{2,0},{3,1},{4,6},{5,7},{6,4},{7,5},{8,10},{9,11},{10,... | collective-permute-start | bytes 1228808 | tf_op jit(solution)/shard_map/ppermute | solution.py:423
  106.5 9.5 %collective-permute-start.24 = (bf16[400,512]{1,0:T(8,128)(2,1)S(1)}, bf16[400,512]{1,0:T(8,128)(2,1)S(1)}, u32[]{:S(2)}, u32[]{:S(2)}) collective-permute-start(bf16[400,512]{1,0:T(8,128)(2,1)S(1)} %stack_parts.1.refs_0_.refs_2_), channel_id=1, source_target_pairs={{0,1},{1,0},{2,3},{3,2},{4,5},{5,4},{6,7},{7,6},{8,9},{9,8},{10,11... | collective-permute-start | bytes 1228808 | tf_op jit(solution)/shard_map/ppermute | solution.py:423
  (8 other events, 47.9 us)

commit v14 on v12

--- a/solution.py
+++ b/solution.py
@@ -437,7 +437,7 @@
     size = (total - cells) // 2
     count = cells // size
 
-    tile = min(width, 256)
+    tile = width
 
     def spec(k):
         return pl.BlockSpec((size, tile), lambda n: (1 + k, n))

time: 129 us -> 128 us (level)
  Pallas kernels: 60 us -> 58.3 us
    pallas_call x1, Pallas kernels: 9.91 us -> 8.17 us  [inner_product(): pl.pallas_call(functools.partial(inner_product_kernel, count, width // ti...]
  transfers between devices with their start and end apart: 27 -> 27, of which waited for: 9 -> 9; matrix products, arithmetic and copies ran while one was open for 0% -> 0% of each run, Pallas kernels for 29% -> 28%
where the time goes in v14:
time: 128 us; the launch traced here: 127 us
  Pallas kernels  58.3 us (46%)
  starting transfers between devices  37.2 us (29%)
  waiting for transfers between devices  30.7 us (24%)
    ppermute x25, starting transfers between devices, swap(): return lax.ppermute(values, 'grid', [(i, i ^ flip) for i in range(count)])  33.8 us
    ppermute x25, waiting for transfers between devices, swap(): return lax.ppermute(values, 'grid', [(i, i ^ flip) for i in range(count)])  30.7 us
    pallas_call x2, Pallas kernels, density_steps(): pl.pallas_call(density_kernel, grid=(steps,), in_specs=in_specs, out_spec...  12.8 us
    pallas_call x1, Pallas kernels, first_grad(): pl.pallas_call(functools.partial(first_grad_kernel, parts, block, tiles),...  12.2 us
    pallas_call x1, Pallas kernels, inner_steps(): pl.pallas_call(functools.partial(inner_kernel, rows, size), grid=(scenari...  11.5 us
    pallas_call x1, Pallas kernels, inner_product(): pl.pallas_call(functools.partial(inner_product_kernel, count, width // ti...  8.17 us
    pallas_call x1, Pallas kernels, edge_product(): pl.pallas_call(functools.partial(edge_product_kernel, block, inner is not...  4.44 us
    pallas_call x1, Pallas kernels, edge_steps(): pl.pallas_call(edge_kernel, grid=(scenarios // size,), in_specs=density_s...  3.63 us
  transfers between devices with their start and end apart: 27, of which 9 were waited for; matrix products, arithmetic and copies ran while one was open for 0% of the time, Pallas kernels for 28%

profile of v14, /device:TPU:0, one launch (start us, length us, event | category | flops | bytes accessed | tf_op | source)
XLA Modules:
  0.0 127.1 jit_solution(9359738363763049755)
XLA Ops:
  1.1 2.6 %collective-permute-start.3 = (bf16[2048,128]{1,0:T(8,128)(2,1)}, bf16[2048,128]{1,0:T(8,128)(2,1)S(1)}, u32[]{:S(2)}, u32[]{:S(2)}) collective-permute-start(bf16[2048,128]{1,0:T(8,128)(2,1)} %refs_6_.1), channel_id=1, source_target_pairs={{0,2},{1,3},{2,0},{3,1},{4,6},{5,7},{6,4},{7,5},{8,10},{9,11},{10,... | collective-permute-start | bytes 1572872 | tf_op jit(solution)/shard_map/ppermute | solution.py:423
  3.8 11.5 %inner_density_steps.1 = (s32[4]{0:T(128)S(1)}, bf16[400,512]{1,0:T(8,128)(2,1)S(1)}, bf16[400,512]{1,0:T(8,128)(2,1)S(1)}, f32[4,384,128]{2,1,0:T(8,128)}, bf16...) custom-call(s32[4]{0:T(128)S(1)} %pad_add_fusion.place_ref, ...), custom_call_target="tpu_custom_call" | custom-call | flops 1 | bytes 1 | tf_op jit(solution)/shard_map/inner_density_steps/pallas_call | solution.py:239
  15.4 2.1 %collective-permute-start = (bf16[400,512]{1,0:T(8,128)(2,1)S(1)}, bf16[400,512]{1,0:T(8,128)(2,1)S(1)}, u32[]{:S(2)}, u32[]{:S(2)}) collective-permute-start(bf16[400,512]{1,0:T(8,128)(2,1)S(1)} %get-tuple-element.51), channel_id=1, source_target_pairs={{0,1},{1,2},{2,3},{3,4},{4,5},{5,6},{6,7},{7,8},{8,9},{9,10},{10,1... | collective-permute-start | bytes 1228808 | tf_op jit(solution)/shard_map/ppermute | solution.py:849
  18.8 8.2 %inner_product.1.dep_ref.refs_0_ = f32[4,384,512]{2,1,0:T(8,128)S(1)} custom-call(bf16[384,3072]{1,0:T(8,128)(2,1)S(1)} %get-tuple-element.55.inputs_ref.refs_1_, bf16[4096,2048]{1,0:T(8,128)(2,1)} %bottom_ref.1, bf16[4096,2048]{1,0:T(8,128)(2,1)} %bottom_ref.1, bf16[4096,2048]{1,0:T(8,128)(2,1)} %bottom_ref.1, bf16[4096,2048]{1,0:T(8,128)(2,1)} %bottom_ref.1, ...), custom_call_target="tpu_custom_call" | custom-call | flops 1 | bytes 1 | tf_op jit(solution)/shard_map/inner_product/pallas_call | solution.py:445
  27.1 3.6 %edge_density_steps.1 = (bf16[384,512]{1,0:T(8,128)(2,1)S(1)}, bf16[384,512]{1,0:T(8,128)(2,1)S(1)}) custom-call(f32[2,16,256]{2,1,0:T(8,128)S(1)} %copy-done.2, f32[4,384,128]{2,1,0:T(8,128)S(1)} %copy-done.1, bf16[512,256]{1,0:T(8,128)(2,1)S(1)} %get-tuple-element.49.band_ref, bf16[384,4096]{1,0:T(8,128)(2,1)S(1)} %copy-done, ...), custom_call_target="tpu_custom_call" | custom-call | flops 1 | bytes 1 | tf_op jit(solution)/shard_map/edge_density_steps/pallas_call | solution.py:370
  30.7 4.4 %edge_product.1 = (f32[2,4,96,512]{3,2,1,0:T(8,128)S(1)}, bf16[2,4,112,512]{3,2,1,0:T(8,128)(2,1)S(1)}) custom-call(s32[4]{0:T(128)S(1)} %get-tuple-element.53.place_ref.refs_0_, f32[1,128]{1,0:T(1,128)S(1)} %bitcast.18, bf16[384,512]{1,0:T(8,128)(2,1)S(1)} %get-tuple-element.56.low_ref.refs_0_, bf16[384,512]{1,0:T(8,128)(2,1)S(1)} %get-tuple-element.57.high_ref.refs_2_, ...), custom_call_target="tpu_custom_call" | custom-call | flops 1 | bytes 1 | tf_op jit(solution)/shard_map/edge_product/pallas_call | solution.py:493
  36.4 2.0 %collective-permute-done.4.other_ref = bf16[2,4,112,512]{3,2,1,0:T(8,128)(2,1)S(1)} collective-permute-done((bf16[2,4,112,512]{3,2,1,0:T(8,128)(2,1)S(1)}, bf16[2,4,112,512]{3,2,1,0:T(8,128)(2,1)S(1)}, u32[]{:S(2)}, u32[]{:S(2)}) %collective-permute-start.4) | collective-permute-done | bytes 917536 | tf_op jit(solution)/shard_map/ppermute | solution.py:423
  39.1 4.0 %collective-permute-start.5 = (bf16[96,512]{1,0:T(8,128)(2,1)S(1)}, bf16[96,512]{1,0:T(8,128)(2,1)S(1)}, u32[]{:S(2)}, u32[]{:S(2)}) collective-permute-start(bf16[96,512]{1,0:T(8,128)(2,1)S(1)} %get-tuple-element.62), channel_id=1, source_target_pairs={{0,4},{1,5},{2,6},{3,7},{4,0},{5,1},{6,2},{7,3},{8,12},{9,13},{10,... | collective-permute-start | bytes 294920 | tf_op jit(solution)/shard_map/ppermute | solution.py:423
  43.1 2.6 %collective-permute-start.6 = (bf16[96,512]{1,0:T(8,128)(2,1)S(1)}, bf16[96,512]{1,0:T(8,128)(2,1)S(1)}, u32[]{:S(2)}, u32[]{:S(2)}) collective-permute-start(bf16[96,512]{1,0:T(8,128)(2,1)S(1)} %get-tuple-element.63), channel_id=1, source_target_pairs={{0,8},{1,9},{2,10},{3,11},{4,12},{5,13},{6,14},{7,15},{8,0},{9,1},... | collective-permute-start | bytes 294920 | tf_op jit(solution)/shard_map/ppermute | solution.py:423
  46.2 2.1 %collective-permute-start.9 = (bf16[96,512]{1,0:T(8,128)(2,1)S(1)}, bf16[96,512]{1,0:T(8,128)(2,1)S(1)}, u32[]{:S(2)}, u32[]{:S(2)}) collective-permute-start(bf16[96,512]{1,0:T(8,128)(2,1)S(1)} %get-tuple-element.66), channel_id=1, source_target_pairs={{0,6},{1,7},{2,4},{3,5},{4,2},{5,3},{6,0},{7,1},{8,14},{9,15},{10,... | collective-permute-start | bytes 294920 | tf_op jit(solution)/shard_map/ppermute | solution.py:423
  48.3 5.5 %collective-permute-done.6.refs_1_ = bf16[96,512]{1,0:T(8,128)(2,1)S(1)} collective-permute-done((bf16[96,512]{1,0:T(8,128)(2,1)S(1)}, bf16[96,512]{1,0:T(8,128)(2,1)S(1)}, u32[]{:S(2)}, u32[]{:S(2)}) %collective-permute-start.6) | collective-permute-done | bytes 98336 | tf_op jit(solution)/shard_map/ppermute | solution.py:423
  53.8 3.2 %collective-permute-start.11 = (bf16[96,512]{1,0:T(8,128)(2,1)S(1)}, bf16[96,512]{1,0:T(8,128)(2,1)S(1)}, u32[]{:S(2)}, u32[]{:S(2)}) collective-permute-start(bf16[96,512]{1,0:T(8,128)(2,1)S(1)} %get-tuple-element.68), channel_id=1, source_target_pairs={{0,14},{1,15},{2,12},{3,13},{4,10},{5,11},{6,8},{7,9},{8,6},{9,7},... | collective-permute-start | bytes 294920 | tf_op jit(solution)/shard_map/ppermute | solution.py:423
  57.0 5.5 %collective-permute-done.10.refs_5_ = bf16[96,512]{1,0:T(8,128)(2,1)S(1)} collective-permute-done((bf16[96,512]{1,0:T(8,128)(2,1)S(1)}, bf16[96,512]{1,0:T(8,128)(2,1)S(1)}, u32[]{:S(2)}, u32[]{:S(2)}) %collective-permute-start.10) | collective-permute-done | bytes 98336 | tf_op jit(solution)/shard_map/ppermute | solution.py:423
  62.7 2.1 %collective-permute-start.14 = (bf16[96,512]{1,0:T(8,128)(2,1)S(1)}, bf16[96,512]{1,0:T(8,128)(2,1)S(1)}, u32[]{:S(2)}, u32[]{:S(2)}) collective-permute-start(bf16[96,512]{1,0:T(8,128)(2,1)S(1)} %get-tuple-element.69.dep_ref.refs_2_.refs_3_), channel_id=1, source_target_pairs={{0,12},{1,13},{2,14},{3,15},{4,8},{5,9},{6,10},{7,11},{8,4},{9,5},... | collective-permute-start | bytes 294920 | tf_op jit(solution)/shard_map/ppermute | solution.py:423
  67.1 6.4 %density_steps.2 = (f32[12288,128]{1,0:T(8,128)}, f32[8,128]{1,0:T(8,128)S(1)}) custom-call(f32[2,16,256]{2,1,0:T(8,128)S(1)} %copy-done.2, f32[4,384,128]{2,1,0:T(8,128)S(1)} %copy-done.1, bf16[512,256]{1,0:T(8,128)(2,1)S(1)} %get-tuple-element.49.band_ref, bf16[384,4096]{1,0:T(8,128)(2,1)S(1)} %copy-done, ...), custom_call_target="tpu_custom_call" | custom-call | flops 1 | bytes 1 | tf_op jit(solution)/shard_map/density_steps/pallas_call | solution.py:397
  73.6 2.4 %value_layers.1 = (f32[96,512]{1,0:T(8,128)S(1)}, f32[1,512]{1,0:T(1,128)S(1)}, bf16[2,2064,128]{2,1,0:T(8,128)(2,1)S(1)}, bf16[2,2064,128]{2,1,0:T(8,128)(2,1)S...) custom-call(s32[4]{0:T(128)S(1)} %get-tuple-element.53.place_ref.refs_0_, ...), custom_call_target="tpu_custom_call" | custom-call | flops 1 | bytes 1 | tf_op jit(solution)/shard_map/value_layers/pallas_call | solution.py:653
  76.8 1.9 %collective-permute-start.17 = (bf16[112,512]{1,0:T(8,128)(2,1)S(1)}, bf16[112,512]{1,0:T(8,128)(2,1)S(1)}, u32[]{:S(2)}, u32[]{:S(2)}) collective-permute-start(bf16[112,512]{1,0:T(8,128)(2,1)S(1)} %get-tuple-element.78), channel_id=1, source_target_pairs={{0,8},{1,9},{2,10},{3,11},{4,12},{5,13},{6,14},{7,15},{8,0},{9,1},... | collective-permute-start | bytes 344072 | tf_op jit(solution)/shard_map/ppermute | solution.py:423
  80.5 6.4 %density_steps.3 = (f32[12288,128]{1,0:T(8,128)}, f32[8,128]{1,0:T(8,128)S(1)}) custom-call(f32[2,16,256]{2,1,0:T(8,128)S(1)} %copy-done.2, f32[4,384,128]{2,1,0:T(8,128)S(1)} %copy-done.1, bf16[512,256]{1,0:T(8,128)(2,1)S(1)} %get-tuple-element.49.band_ref, bf16[384,4096]{1,0:T(8,128)(2,1)S(1)} %copy-done, ...), custom_call_target="tpu_custom_call", output_to_operand_aliasing={{0}: (9, {})} | custom-call | flops 1 | bytes 1 | tf_op jit(solution)/shard_map/density_steps/pallas_call | solution.py:397
  89.1 2.3 %collective-permute-start.23 = (bf16[2064,128]{1,0:T(8,128)(2,1)S(1)}, bf16[2064,128]{1,0:T(8,128)(2,1)S(1)}, u32[]{:S(2)}, u32[]{:S(2)}) collective-permute-start(bf16[2064,128]{1,0:T(8,128)(2,1)S(1)} %get-tuple-element.84), channel_id=1, source_target_pairs={{0,2},{1,3},{2,0},{3,1},{4,6},{5,7},{6,4},{7,5},{8,10},{9,11},{10,... | collective-permute-start | bytes 1585160 | tf_op jit(solution)/shard_map/ppermute | solution.py:423
  92.9 2.2 %collective-permute-start.20 = (bf16[96,512]{1,0:T(8,128)(2,1)S(1)}, bf16[96,512]{1,0:T(8,128)(2,1)S(1)}, u32[]{:S(2)}, u32[]{:S(2)}) collective-permute-start(bf16[96,512]{1,0:T(8,128)(2,1)S(1)} %get-tuple-element.80.refs_3_.refs_0_), channel_id=1, source_target_pairs={{0,8},{1,9},{2,10},{3,11},{4,12},{5,13},{6,14},{7,15},{8,0},{9,1},... | collective-permute-start | bytes 294920 | tf_op jit(solution)/shard_map/ppermute | solution.py:423
  96.6 2.2 %collective-permute-done.21.refs_3_ = bf16[96,512]{1,0:T(8,128)(2,1)S(1)} collective-permute-done((bf16[96,512]{1,0:T(8,128)(2,1)S(1)}, bf16[96,512]{1,0:T(8,128)(2,1)S(1)}, u32[]{:S(2)}, u32[]{:S(2)}) %collective-permute-start.21) | collective-permute-done | bytes 98336 | tf_op jit(solution)/shard_map/ppermute | solution.py:423
  98.9 3.6 %collective-permute-done.20.refs_2_ = bf16[96,512]{1,0:T(8,128)(2,1)S(1)} collective-permute-done((bf16[96,512]{1,0:T(8,128)(2,1)S(1)}, bf16[96,512]{1,0:T(8,128)(2,1)S(1)}, u32[]{:S(2)}, u32[]{:S(2)}) %collective-permute-start.20) | collective-permute-done | bytes 98336 | tf_op jit(solution)/shard_map/ppermute | solution.py:423
  104.0 9.2 %collective-permute-done.25.refs_4_ = bf16[400,512]{1,0:T(8,128)(2,1)S(1)} collective-permute-done((bf16[400,512]{1,0:T(8,128)(2,1)S(1)}, bf16[400,512]{1,0:T(8,128)(2,1)S(1)}, u32[]{:S(2)}, u32[]{:S(2)}) %collective-permute-start.25) | collective-permute-done | bytes 409632 | tf_op jit(solution)/shard_map/ppermute | solution.py:423
  114.9 12.2 %first_gradient.1 = (bf16[4096,2048]{1,0:T(8,128)(2,1)}, f32[384]{0:T(512)}) custom-call(s32[4]{0:T(128)S(1)} %get-tuple-element.53.place_ref.refs_0_, bf16[4096,384]{1,0:T(8,128)(2,1)S(1)} %transposed_inputs.1.refs_5_.refs_1_, bf16[400,512]{1,0:T(8,128)(2,1)S(1)} %stack_parts.1.refs_0_.refs_2_, bf16[400,512]{1,0:T(8,128)(2,1)S(1)} %collective-permute-done.24.refs_3_, ...), custom_call_target="tpu_custom_call" | custom-call | flops 1 | bytes 1 | tf_op jit(solution)/shard_map/first_gradient/pallas_call | solution.py:814
  (56 shorter events, 17.9 us)
Async XLA Ops:
  0.6 18.1 %collective-permute-start.2 = (bf16[2048,128]{1,0:T(8,128)(2,1)}, bf16[2048,128]{1,0:T(8,128)(2,1)S(1)}, u32[]{:S(2)}, u32[]{:S(2)}) collective-permute-start(bf16[2048,128]{1,0:T(8,128)(2,1)} %refs_6_.1), channel_id=1, source_target_pairs={{0,1},{1,0},{2,3},{3,2},{4,5},{5,4},{6,7},{7,6},{8,9},{9,8},{10,11... | collective-permute-start | bytes 1572872 | tf_op jit(solution)/shard_map/ppermute | solution.py:423
  1.1 17.6 %collective-permute-start.3 = (bf16[2048,128]{1,0:T(8,128)(2,1)}, bf16[2048,128]{1,0:T(8,128)(2,1)S(1)}, u32[]{:S(2)}, u32[]{:S(2)}) collective-permute-start(bf16[2048,128]{1,0:T(8,128)(2,1)} %refs_6_.1), channel_id=1, source_target_pairs={{0,2},{1,3},{2,0},{3,1},{4,6},{5,7},{6,4},{7,5},{8,10},{9,11},{10,... | collective-permute-start | bytes 1572872 | tf_op jit(solution)/shard_map/ppermute | solution.py:423
  15.4 11.6 %collective-permute-start = (bf16[400,512]{1,0:T(8,128)(2,1)S(1)}, bf16[400,512]{1,0:T(8,128)(2,1)S(1)}, u32[]{:S(2)}, u32[]{:S(2)}) collective-permute-start(bf16[400,512]{1,0:T(8,128)(2,1)S(1)} %get-tuple-element.51), channel_id=1, source_target_pairs={{0,1},{1,2},{2,3},{3,4},{4,5},{5,6},{6,7},{7,8},{8,9},{9,10},{10,1... | collective-permute-start | bytes 1228808 | tf_op jit(solution)/shard_map/ppermute | solution.py:849
  17.5 9.5 %collective-permute-start.1 = (bf16[400,512]{1,0:T(8,128)(2,1)S(1)}, bf16[400,512]{1,0:T(8,128)(2,1)S(1)}, u32[]{:S(2)}, u32[]{:S(2)}) collective-permute-start(bf16[400,512]{1,0:T(8,128)(2,1)S(1)} %get-tuple-element.52), channel_id=1, source_target_pairs={{1,0},{2,1},{3,2},{4,3},{5,4},{6,5},{7,6},{8,7},{9,8},{10,9},{11,1... | collective-permute-start | bytes 1228808 | tf_op jit(solution)/shard_map/ppermute | solution.py:850
  36.3 37.2 %collective-permute-start.15 = (bf16[2048,128]{1,0:T(8,128)(2,1)S(1)}, bf16[2048,128]{1,0:T(8,128)(2,1)S(1)}, u32[]{:S(2)}, u32[]{:S(2)}) collective-permute-start(bf16[2048,128]{1,0:T(8,128)(2,1)S(1)} %collective-permute-done.3.refs_7_.refs_8_), channel_id=1, source_target_pairs={{0,1},{1,0},{2,3},{3,2},{4,5},{5,4},{6,7},{7,6},{8,9},{9,8},{10,11... | collective-permute-start | bytes 1572872 | tf_op jit(solution)/shard_map/ppermute | solution.py:423
  43.1 10.7 %collective-permute-start.6 = (bf16[96,512]{1,0:T(8,128)(2,1)S(1)}, bf16[96,512]{1,0:T(8,128)(2,1)S(1)}, u32[]{:S(2)}, u32[]{:S(2)}) collective-permute-start(bf16[96,512]{1,0:T(8,128)(2,1)S(1)} %get-tuple-element.63), channel_id=1, source_target_pairs={{0,8},{1,9},{2,10},{3,11},{4,12},{5,13},{6,14},{7,15},{8,0},{9,1},... | collective-permute-start | bytes 294920 | tf_op jit(solution)/shard_map/ppermute | solution.py:423
  45.7 8.1 %collective-permute-start.7 = (bf16[96,512]{1,0:T(8,128)(2,1)S(1)}, bf16[96,512]{1,0:T(8,128)(2,1)S(1)}, u32[]{:S(2)}, u32[]{:S(2)}) collective-permute-start(bf16[96,512]{1,0:T(8,128)(2,1)S(1)} %get-tuple-element.64), channel_id=1, source_target_pairs={{0,12},{1,13},{2,14},{3,15},{4,8},{5,9},{6,10},{7,11},{8,4},{9,5},... | collective-permute-start | bytes 294920 | tf_op jit(solution)/shard_map/ppermute | solution.py:423
  45.7 16.8 %collective-permute-start.8 = (bf16[112,512]{1,0:T(8,128)(2,1)S(1)}, bf16[112,512]{1,0:T(8,128)(2,1)S(1)}, u32[]{:S(2)}, u32[]{:S(2)}) collective-permute-start(bf16[112,512]{1,0:T(8,128)(2,1)S(1)} %get-tuple-element.65), channel_id=1, source_target_pairs={{0,2},{1,3},{2,0},{3,1},{4,6},{5,7},{6,4},{7,5},{8,10},{9,11},{10,... | collective-permute-start | bytes 344072 | tf_op jit(solution)/shard_map/ppermute | solution.py:423
  46.2 10.8 %collective-permute-start.9 = (bf16[96,512]{1,0:T(8,128)(2,1)S(1)}, bf16[96,512]{1,0:T(8,128)(2,1)S(1)}, u32[]{:S(2)}, u32[]{:S(2)}) collective-permute-start(bf16[96,512]{1,0:T(8,128)(2,1)S(1)} %get-tuple-element.66), channel_id=1, source_target_pairs={{0,6},{1,7},{2,4},{3,5},{4,2},{5,3},{6,0},{7,1},{8,14},{9,15},{10,... | collective-permute-start | bytes 294920 | tf_op jit(solution)/shard_map/ppermute | solution.py:423
  53.8 8.7 %collective-permute-start.10 = (bf16[96,512]{1,0:T(8,128)(2,1)S(1)}, bf16[96,512]{1,0:T(8,128)(2,1)S(1)}, u32[]{:S(2)}, u32[]{:S(2)}) collective-permute-start(bf16[96,512]{1,0:T(8,128)(2,1)S(1)} %get-tuple-element.67), channel_id=1, source_target_pairs={{0,10},{1,11},{2,8},{3,9},{4,14},{5,15},{6,12},{7,13},{8,2},{9,3},... | collective-permute-start | bytes 294920 | tf_op jit(solution)/shard_map/ppermute | solution.py:423
  53.8 8.7 %collective-permute-start.11 = (bf16[96,512]{1,0:T(8,128)(2,1)S(1)}, bf16[96,512]{1,0:T(8,128)(2,1)S(1)}, u32[]{:S(2)}, u32[]{:S(2)}) collective-permute-start(bf16[96,512]{1,0:T(8,128)(2,1)S(1)} %get-tuple-element.68), channel_id=1, source_target_pairs={{0,14},{1,15},{2,12},{3,13},{4,10},{5,11},{6,8},{7,9},{8,6},{9,7},... | collective-permute-start | bytes 294920 | tf_op jit(solution)/shard_map/ppermute | solution.py:423
  62.7 10.9 %collective-permute-start.14 = (bf16[96,512]{1,0:T(8,128)(2,1)S(1)}, bf16[96,512]{1,0:T(8,128)(2,1)S(1)}, u32[]{:S(2)}, u32[]{:S(2)}) collective-permute-start(bf16[96,512]{1,0:T(8,128)(2,1)S(1)} %get-tuple-element.69.dep_ref.refs_2_.refs_3_), channel_id=1, source_target_pairs={{0,12},{1,13},{2,14},{3,15},{4,8},{5,9},{6,10},{7,11},{8,4},{9,5},... | collective-permute-start | bytes 294920 | tf_op jit(solution)/shard_map/ppermute | solution.py:423
  64.8 8.8 %collective-permute-start.13 = (bf16[96,512]{1,0:T(8,128)(2,1)S(1)}, bf16[96,512]{1,0:T(8,128)(2,1)S(1)}, u32[]{:S(2)}, u32[]{:S(2)}) collective-permute-start(bf16[96,512]{1,0:T(8,128)(2,1)S(1)} %get-tuple-element.69.dep_ref.refs_2_.refs_3_), channel_id=1, source_target_pairs={{0,8},{1,9},{2,10},{3,11},{4,12},{5,13},{6,14},{7,15},{8,0},{9,1},... | collective-permute-start | bytes 294920 | tf_op jit(solution)/shard_map/ppermute | solution.py:423
  65.8 7.7 %collective-permute-start.12 = (bf16[96,512]{1,0:T(8,128)(2,1)S(1)}, bf16[96,512]{1,0:T(8,128)(2,1)S(1)}, u32[]{:S(2)}, u32[]{:S(2)}) collective-permute-start(bf16[96,512]{1,0:T(8,128)(2,1)S(1)} %get-tuple-element.69.dep_ref.refs_2_.refs_3_), channel_id=1, source_target_pairs={{0,4},{1,5},{2,6},{3,7},{4,0},{5,1},{6,2},{7,3},{8,12},{9,13},{10,... | collective-permute-start | bytes 294920 | tf_op jit(solution)/shard_map/ppermute | solution.py:423
  76.0 12.8 %collective-permute-start.22 = (bf16[2,2064,128]{2,1,0:T(8,128)(2,1)S(1)}, bf16[2,2064,128]{2,1,0:T(8,128)(2,1)S(1)}, u32[]{:S(2)}, u32[]{:S(2)}) collective-permute-start(bf16[2,2064,128]{2,1,0:T(8,128)(2,1)S(1)} %get-tuple-element.83), channel_id=1, source_target_pairs={{0,1},{1,0},{2,3},{3,2},{4,5},{5,4},{6,7},{7,6},{8,9},{9,8},{10,11... | collective-permute-start | bytes 3170312 | tf_op jit(solution)/shard_map/ppermute | solution.py:423
  76.1 10.9 %collective-permute-start.16 = (bf16[112,512]{1,0:T(8,128)(2,1)S(1)}, bf16[112,512]{1,0:T(8,128)(2,1)S(1)}, u32[]{:S(2)}, u32[]{:S(2)}) collective-permute-start(bf16[112,512]{1,0:T(8,128)(2,1)S(1)} %get-tuple-element.77), channel_id=1, source_target_pairs={{0,4},{1,5},{2,6},{3,7},{4,0},{5,1},{6,2},{7,3},{8,12},{9,13},{10,... | collective-permute-start | bytes 344072 | tf_op jit(solution)/shard_map/ppermute | solution.py:423
  76.8 11.9 %collective-permute-start.17 = (bf16[112,512]{1,0:T(8,128)(2,1)S(1)}, bf16[112,512]{1,0:T(8,128)(2,1)S(1)}, u32[]{:S(2)}, u32[]{:S(2)}) collective-permute-start(bf16[112,512]{1,0:T(8,128)(2,1)S(1)} %get-tuple-element.78), channel_id=1, source_target_pairs={{0,8},{1,9},{2,10},{3,11},{4,12},{5,13},{6,14},{7,15},{8,0},{9,1},... | collective-permute-start | bytes 344072 | tf_op jit(solution)/shard_map/ppermute | solution.py:423
  78.7 10.0 %collective-permute-start.18 = (bf16[112,512]{1,0:T(8,128)(2,1)S(1)}, bf16[112,512]{1,0:T(8,128)(2,1)S(1)}, u32[]{:S(2)}, u32[]{:S(2)}) collective-permute-start(bf16[112,512]{1,0:T(8,128)(2,1)S(1)} %get-tuple-element.72.dep_ref), channel_id=1, source_target_pairs={{0,12},{1,13},{2,14},{3,15},{4,8},{5,9},{6,10},{7,11},{8,4},{9,5},... | collective-permute-start | bytes 344072 | tf_op jit(solution)/shard_map/ppermute | solution.py:423
  89.1 13.4 %collective-permute-start.23 = (bf16[2064,128]{1,0:T(8,128)(2,1)S(1)}, bf16[2064,128]{1,0:T(8,128)(2,1)S(1)}, u32[]{:S(2)}, u32[]{:S(2)}) collective-permute-start(bf16[2064,128]{1,0:T(8,128)(2,1)S(1)} %get-tuple-element.84), channel_id=1, source_target_pairs={{0,2},{1,3},{2,0},{3,1},{4,6},{5,7},{6,4},{7,5},{8,10},{9,11},{10,... | collective-permute-start | bytes 1585160 | tf_op jit(solution)/shard_map/ppermute | solution.py:423
  91.4 7.5 %collective-permute-start.21 = (bf16[96,512]{1,0:T(8,128)(2,1)S(1)}, bf16[96,512]{1,0:T(8,128)(2,1)S(1)}, u32[]{:S(2)}, u32[]{:S(2)}) collective-permute-start(bf16[96,512]{1,0:T(8,128)(2,1)S(1)} %get-tuple-element.80.refs_3_.refs_0_), channel_id=1, source_target_pairs={{0,12},{1,13},{2,14},{3,15},{4,8},{5,9},{6,10},{7,11},{8,4},{9,5},... | collective-permute-start | bytes 294920 | tf_op jit(solution)/shard_map/ppermute | solution.py:423
  92.9 9.6 %collective-permute-start.20 = (bf16[96,512]{1,0:T(8,128)(2,1)S(1)}, bf16[96,512]{1,0:T(8,128)(2,1)S(1)}, u32[]{:S(2)}, u32[]{:S(2)}) collective-permute-start(bf16[96,512]{1,0:T(8,128)(2,1)S(1)} %get-tuple-element.80.refs_3_.refs_0_), channel_id=1, source_target_pairs={{0,8},{1,9},{2,10},{3,11},{4,12},{5,13},{6,14},{7,15},{8,0},{9,1},... | collective-permute-start | bytes 294920 | tf_op jit(solution)/shard_map/ppermute | solution.py:423
  95.1 7.4 %collective-permute-start.19 = (bf16[96,512]{1,0:T(8,128)(2,1)S(1)}, bf16[96,512]{1,0:T(8,128)(2,1)S(1)}, u32[]{:S(2)}, u32[]{:S(2)}) collective-permute-start(bf16[96,512]{1,0:T(8,128)(2,1)S(1)} %get-tuple-element.80.refs_3_.refs_0_), channel_id=1, source_target_pairs={{0,4},{1,5},{2,6},{3,7},{4,0},{5,1},{6,2},{7,3},{8,12},{9,13},{10,... | collective-permute-start | bytes 294920 | tf_op jit(solution)/shard_map/ppermute | solution.py:423
  102.6 10.6 %collective-permute-start.25 = (bf16[400,512]{1,0:T(8,128)(2,1)S(1)}, bf16[400,512]{1,0:T(8,128)(2,1)S(1)}, u32[]{:S(2)}, u32[]{:S(2)}) collective-permute-start(bf16[400,512]{1,0:T(8,128)(2,1)S(1)} %stack_parts.1.refs_0_.refs_2_), channel_id=1, source_target_pairs={{0,2},{1,3},{2,0},{3,1},{4,6},{5,7},{6,4},{7,5},{8,10},{9,11},{10,... | collective-permute-start | bytes 1228808 | tf_op jit(solution)/shard_map/ppermute | solution.py:423
  104.0 10.1 %collective-permute-start.24 = (bf16[400,512]{1,0:T(8,128)(2,1)S(1)}, bf16[400,512]{1,0:T(8,128)(2,1)S(1)}, u32[]{:S(2)}, u32[]{:S(2)}) collective-permute-start(bf16[400,512]{1,0:T(8,128)(2,1)S(1)} %stack_parts.1.refs_0_.refs_2_), channel_id=1, source_target_pairs={{0,1},{1,0},{2,3},{3,2},{4,5},{5,4},{6,7},{7,6},{8,9},{9,8},{10,11... | collective-permute-start | bytes 1228808 | tf_op jit(solution)/shard_map/ppermute | solution.py:423
  (8 other events, 51.4 us)
